TPU v7x, 32 devices: a whole 2x2x4 slice. The times are simulated.
32 devices in a mesh: fx: 8 (over z, x), wy: 4 (over y, core).
Axes of the slice: x: 2, y: 2, z: 4, core: 2. Of those that a mesh axis runs over, the one named last changes fastest.
Arguments:
- displacement: float32 [3, 16, 16, 128], P(None, 'fx', 'wy'), may hold values from -6 to 6
- velocity: float32 [3, 16, 16, 128], P(None, 'fx', 'wy'), may hold values from -3 to 3
- jitter: float32 [3, 16, 16, 128], P(None, 'fx', 'wy'), may hold values from -0.3 to 0.3
- bond_masks: int32 [16, 16, 9, 128, 128], P('fx', 'wy'), may hold values from 0 to 1, as said below
- pressure: float32 [128, 128, 128], P('fx', 'wy'), may hold values from -6 to 6
- pressure_prev: float32 [128, 128, 128], P('fx', 'wy'), may hold values from -6 to 6
- speed_sq: float32 [128, 128, 128], P('fx', 'wy'), may hold values from 0.03 to 0.3
- route_device: int32 [16384, 1], P(('fx', 'wy')), may hold values from 0 to 31; in each aligned block of 512 rows (0 to 511, 512 to 1023, ...) at most 64 rows name the same one
- route_tile: int32 [16384], P(('fx', 'wy')), may hold values from 0 to 7
Outputs:
- displacement_out: float32 [3, 16, 16, 128], P(None, 'fx', 'wy')
- velocity_out: float32 [3, 16, 16, 128], P(None, 'fx', 'wy')
- pressure_out: float32 [128, 128, 128], P('fx', 'wy')
Inputs may be any that keep to these rules, and one draw needn't show every extreme that they name: `bond_masks`: 0 or 1. Bonds to a neighbour tile beyond the wall's edge are 0, and some neighbour tiles have all bonds 0. `route_device`: among the 512 rows of one device, no device is named more than 64 times, and one is named exactly 64 times.
All inputs are finite; a program needn't handle non-finite values.
Results may differ from a plain program's by a relative error of at most 0.0001.
Values sent between devices are 32-bit elements; how exact they have to be, the bound alone decides.
No kernel may reach another device: no remote copies, remote signals or barrier semaphores. Data moves between devices by JAX's collectives and lax.ppermute only.
A program may use at most 64 MiB of HBM per device.

v0:
```python
import jax
import jax.numpy as jnp
from jax import lax
from jax.sharding import PartitionSpec as P

STEPS = 2


STIFFNESS = 0.02
LOADING = 0.05
REACH_SQ = 9.0


def padded_2(x, sides, width):
    for axis, dim in sides:
        peers, length = (lax.axis_size(axis), x.shape[dim])
        up = [(i, (i + 1) % peers) for i in range(peers - 1)]
        down = [(j, i) for i, j in up]
        last = lax.slice_in_dim(x, length - width, length, axis=dim)
        first = lax.slice_in_dim(x, 0, width, axis=dim)
        before = lax.ppermute(last, axis, up)
        after = lax.ppermute(first, axis, down)
        x = jnp.concatenate([before, x, after], axis=dim)
    return x


def lattice(count):
    index = jnp.arange(count, dtype=jnp.int32)
    return jnp.stack([index % 8, index // 8 % 4, index // 32]).astype(jnp.float32)


def offsets():
    table = []
    for slot in range(9):
        table.append([8.0 * (slot // 3 - 1), 4.0 * (slot % 3 - 1), 0.0])
    return jnp.array(table, dtype=jnp.float32)


def neighbours(padded, rows, cols):
    pieces = []
    for slot in range(9):
        pieces.append(padded[:, slot // 3 : slot // 3 + rows, slot % 3 : slot % 3 + cols, :])
    return jnp.stack(pieces)


def bond_weights(jitter_pad, masks):
    rows, cols, count = (masks.shape[0], masks.shape[1], masks.shape[3])
    base = lattice(count)
    own = base[:, None, None, :] + jitter_pad[:, 1 : rows + 1, 1 : cols + 1, :]
    other = (
        base[None, :, None, None, :]
        + offsets()[:, :, None, None, None]
        + neighbours(jitter_pad, rows, cols)
    )
    other = jnp.transpose(other, (1, 2, 3, 0, 4))
    dist_sq = jnp.zeros(masks.shape, jnp.float32)
    for comp in range(3):
        diff = other[comp][:, :, :, None, :] - own[comp][:, :, None, :, None]
        dist_sq = dist_sq + diff * diff
    return masks.astype(jnp.float32) * jnp.maximum(1.0 - dist_sq / REACH_SQ, 0.0)


def bond_forces(weights, disp_pad):
    rows, cols = (weights.shape[0], weights.shape[1])
    own = disp_pad[:, 1 : rows + 1, 1 : cols + 1, :]
    other = neighbours(disp_pad, rows, cols)
    pulled = jnp.einsum("abkij,kcabj->cabi", weights, other, precision=lax.Precision.HIGHEST)
    totals = jnp.sum(weights, axis=(2, 4))
    return STIFFNESS * (pulled - totals[None] * own)


def fluid_step(padded, pressure, previous, speed_sq):
    beside = padded[2:, 1:-1, 1:-1] + padded[:-2, 1:-1, 1:-1]
    beside = beside + padded[1:-1, 2:, 1:-1] + padded[1:-1, :-2, 1:-1]
    beside = beside + padded[1:-1, 1:-1, 2:] + padded[1:-1, 1:-1, :-2]
    return 2.0 * pressure - previous + speed_sq * (beside - 6.0 * pressure)


def per_device(
    displacement,
    velocity,
    jitter,
    bond_masks,
    pressure,
    pressure_prev,
    speed_sq,
    route_device,
    route_tile,
):
    rows, cols, count = (displacement.shape[1], displacement.shape[2], displacement.shape[3])
    tiles = rows * cols
    faces = pressure.shape[0] * pressure.shape[1]
    fx_count = lax.axis_size("fx")
    wy_count = lax.axis_size("wy")
    devices = fx_count * wy_count
    capacity = 4 * faces // devices
    jitter_pad = padded_2(jitter, (("fx", 1), ("wy", 2)), 1)
    target = route_device[:, 0]
    hits = (target[:, None] == jnp.arange(devices, dtype=jnp.int32)[None, :]).astype(jnp.int32)
    rank = jnp.sum(hits * (jnp.cumsum(hits, axis=0) - 1), axis=1)
    position = target * capacity + rank
    labels = (
        jnp.full((devices * capacity,), -1.0, jnp.float32)
        .at[position]
        .set(route_tile.astype(jnp.float32))
    )
    tile_ids = jnp.arange(tiles, dtype=jnp.int32).astype(jnp.float32)
    for step in range(STEPS):
        padded = padded_2(pressure, (("fx", 0), ("wy", 1)), 1)
        padded = jnp.pad(padded, ((0, 0), (0, 0), (1, 1)))
        fresh = fluid_step(padded, pressure, pressure_prev, speed_sq)
        pressure_prev, pressure = (pressure, fresh)
        outgoing = (
            jnp.zeros((devices * capacity, count), jnp.float32)
            .at[position]
            .set(pressure.reshape(faces, count))
        )
        got_rows, got_labels = (
            lax.all_to_all(
                outgoing.reshape(devices, capacity, count),
                ("fx", "wy"),
                split_axis=0,
                concat_axis=0,
                tiled=True,
            ),
            lax.all_to_all(
                labels.reshape(devices, capacity),
                ("fx", "wy"),
                split_axis=0,
                concat_axis=0,
                tiled=True,
            ),
        )
        flat_rows = got_rows.reshape(devices * capacity, count)
        flat_labels = got_labels.reshape(devices * capacity)
        picks = (flat_labels[:, None] == tile_ids[None, :]).astype(jnp.float32)
        loads = jnp.einsum("mt,mp->tp", picks, flat_rows, precision=lax.Precision.HIGHEST).reshape(
            rows, cols, count
        )
        disp_pad = padded_2(displacement, (("fx", 1), ("wy", 2)), 1)
        weights = bond_weights(jitter_pad, bond_masks)
        forces = bond_forces(weights, disp_pad)
        forces = forces.at[0].add(LOADING * loads)
        velocity = velocity + forces
        displacement = displacement + velocity
    return (displacement, velocity, pressure)


def solution(mesh):
    placed = (
        P(None, "fx", "wy", None),
        P(None, "fx", "wy", None),
        P(None, "fx", "wy", None),
        P("fx", "wy", None, None, None),
        P("fx", "wy", None),
        P("fx", "wy", None),
        P("fx", "wy", None),
        P(("fx", "wy"), None),
        P(("fx", "wy")),
    )
    return jax.shard_map(
        per_device,
        mesh=mesh,
        in_specs=placed,
        out_specs=(P(None, "fx", "wy", None), P(None, "fx", "wy", None), P("fx", "wy", None)),
        check_vma=False,
    )
```

profile of v0, /device:TPU:0, one launch (start us, length us, event | category | flops | bytes accessed | tf_op | source)
XLA Modules:
  0.0 150.3 jit_solution(11752543189071070963)
XLA Ops:
  2.6 5.5 %collective-permute-start.4 = (f32[3,1,4,128]{3,2,1,0:T(4,128)S(1)}, f32[3,1,4,128]{3,2,1,0:T(4,128)S(1)}, u32[]{:S(2)}, u32[]{:S(2)}) collective-permute-start(f32[3,1,4,128]{3,2,1,0:T(4,128)S(1)} %get-tuple-element.64), channel_id=1, source_target_pairs={{0,4},{4,8},{8,12},{12,16},{16,20},{20,24},{24,28},{1,5},{5,9},{9,... | collective-permute-start | bytes 18440 | tf_op jit(solution)/shard_map/ppermute | solution.py:21
  8.8 1.3 collective-permute-start.1
  10.1 5.4 %collective-permute-start = (f32[3,1,4,128]{3,0,2,1:T(4,128)S(1)}, f32[3,1,4,128]{3,0,2,1:T(4,128)S(1)}, u32[]{:S(2)}, u32[]{:S(2)}) collective-permute-start(f32[3,1,4,128]{3,0,2,1:T(4,128)S(1)} %get-tuple-element.59), channel_id=1, source_target_pairs={{0,4},{4,8},{8,12},{12,16},{16,20},{20,24},{24,28},{1,5},{5,9},{9,... | collective-permute-start | bytes 18440 | tf_op jit(solution)/shard_map/ppermute | solution.py:21
  21.9 2.4 %scatter_custom_fusion = f32[2048]{0:T(1024)S(1)} fusion(s32[512]{0:T(512)S(1)} %bitcast.194, f32[512]{0:T(512)S(1)} %convert_element_type.40, f32[]{:T(128)} %constant.140.clone.1), kind=kCustom, calls=%fused_computation.175 | custom fusion | bytes 8196 | tf_op jit(solution)/shard_map/scatter | solution.py:105
  25.1 8.3 %all-to-all-start = ((f32[32,1,64]{2,1,0:T(1,128)}), f32[32,1,64]{2,1,0:T(1,128)S(1)}, u32[]{:S(2)}, u32[]{:S(2)}) async-start(f32[32,1,64]{2,1,0:T(1,128)} %all_to_all.13), calls=%async_computation | async-start | bytes 32768 | tf_op jit(solution)/shard_map/all_to_all | solution.py:126
  34.2 3.7 %collective-permute-start.9 = (f32[1,32,128]{2,1,0:T(8,128)S(1)}, f32[1,32,128]{2,1,0:T(8,128)S(1)}, u32[]{:S(2)}, u32[]{:S(2)}) collective-permute-start(f32[1,32,128]{2,1,0:T(8,128)S(1)} %get-tuple-element.44), channel_id=1, source_target_pairs={{0,4},{4,8},{8,12},{12,16},{16,20},{20,24},{24,28},{1,5},{5,9},{9,... | collective-permute-start | bytes 49160 | tf_op jit(solution)/shard_map/ppermute | solution.py:21
  38.7 1.3 collective-permute-start.7
  40.0 3.0 %collective-permute-start.6 = (f32[3,4,1,128]{3,2,1,0:T(1,128)S(1)}, f32[3,4,1,128]{3,2,1,0:T(1,128)S(1)}, u32[]{:S(2)}, u32[]{:S(2)}) collective-permute-start(f32[3,4,1,128]{3,2,1,0:T(1,128)S(1)} %get-tuple-element.55), channel_id=1, source_target_pairs={{0,1},{1,2},{2,3},{4,5},{5,6},{6,7},{8,9},{9,10},{10,11},{12,13},{... | collective-permute-start | bytes 18440 | tf_op jit(solution)/shard_map/ppermute | solution.py:21
  43.8 1.3 collective-permute-start.3
  45.1 3.6 %collective-permute-start.2 = (f32[3,4,1,128]{3,0,2,1:T(4,128)S(1)}, f32[3,4,1,128]{3,0,2,1:T(4,128)S(1)}, u32[]{:S(2)}, u32[]{:S(2)}) collective-permute-start(f32[3,4,1,128]{3,0,2,1:T(4,128)S(1)} %get-tuple-element.53), channel_id=1, source_target_pairs={{0,1},{1,2},{2,3},{4,5},{5,6},{6,7},{8,9},{9,10},{10,11},{12,13},{... | collective-permute-start | bytes 18440 | tf_op jit(solution)/shard_map/ppermute | solution.py:21
  52.2 3.6 %collective-permute-start.11 = (f32[18,1,128]{2,1,0:T(1,128)S(1)}, f32[18,1,128]{2,1,0:T(1,128)S(1)}, u32[]{:S(2)}, u32[]{:S(2)}) collective-permute-start(f32[18,1,128]{2,1,0:T(1,128)S(1)} %get-tuple-element.39), channel_id=1, source_target_pairs={{0,1},{1,2},{2,3},{4,5},{5,6},{6,7},{8,9},{9,10},{10,11},{12,13},{... | collective-permute-start | bytes 27656 | tf_op jit(solution)/shard_map/ppermute | solution.py:21
  55.8 1.3 collective-permute-start.10
  57.2 1.9 %collective-permute-done.10 = f32[18,1,128]{2,1,0:T(1,128)S(1)} collective-permute-done((f32[18,1,128]{2,1,0:T(1,128)S(1)}, f32[18,1,128]{2,1,0:T(1,128)S(1)}, u32[]{:S(2)}, u32[]{:S(2)}) %collective-permute-start.10) | collective-permute-done | bytes 9248 | tf_op jit(solution)/shard_map/ppermute | solution.py:22
  59.5 1.5 %fusion.19 = f32[16,32,128]{2,1,0:T(8,128)S(1)} fusion(f32[16,32,128]{2,1,0:T(8,128)} %param.21, f32[18,34,130]{2,1,0:T(8,128)S(1)} %select_maximum_fusion.4, f32[18,32,128]{2,1,0:T(8,128)S(1)} %constant_dynamic-update-slice_fusion.24, f32[18,1,128]{2,1,0:T(1,128)S(1)} %collective-permute-done.11, f32[18,1,128]{2,1,0:T(1,128)S(1)} %collective-permute-done.10, ...), kind=kLoop, calls=%fused_computation.45 | loop fusion | flops 983040 | bytes 1918976 | tf_op jit(solution)/shard_map/add | solution.py:76
  61.0 2.7 %scatter_custom_fusion.1 = f32[2048,128]{1,0:T(8,128)} fusion(s32[512]{0:T(512)S(1)} %bitcast.195, f32[512,128]{1,0:T(8,128)S(1)} %bitcast.184, f32[]{:T(128)} %constant.138.clone.1), kind=kCustom, calls=%fused_computation.24 | custom fusion | bytes 1048580 | tf_op jit(solution)/shard_map/scatter | solution.py:116
  63.7 5.7 %all-to-all-start.1 = ((f32[32,64,128]{2,1,0:T(8,128)}), f32[32,64,128]{2,1,0:T(8,128)S(1)}, u32[]{:S(2)}, u32[]{:S(2)}) async-start(f32[32,64,128]{2,1,0:T(8,128)} %bitcast.39), calls=%async_computation.1 | async-start | bytes 2097152 | tf_op jit(solution)/shard_map/all_to_all | solution.py:119
  69.6 4.2 %fusion.59 = (f32[2,4,128]{2,1,0:T(4,128)S(1)}, f32[2,4,9,128,128]{4,3,2,1,0:T(8,128)S(1)}) fusion(f32[2,4,128]{2,1,0:T(4,128)S(1)} %get-tuple-element.61, f32[2,4,9,128]{3,2,1,0:T(8,128)S(1)} %copy.49, f32[2,4,128]{2,1,0:T(4,128)S(1)} %get-tuple-element.62, f32[2,4,9,128]{3,2,1,0:T(8,128)S(1)} %copy.48, f32[2,4,128]{2,1,0:T(4,128)S(1)} %get-tuple-element.60, ...), kind=kLoop, calls=%fused_computation.192 | loop fusion | flops 16514048 | bytes 9564160 | tf_op jit(solution)/shard_map/reduce_sum | solution.py:68
  73.8 3.8 %collective-permute-start.17 = (f32[1,32,128]{2,1,0:T(8,128)S(1)}, f32[1,32,128]{2,1,0:T(8,128)S(1)}, u32[]{:S(2)}, u32[]{:S(2)}) collective-permute-start(f32[1,32,128]{2,1,0:T(8,128)S(1)} %get-tuple-element.41), channel_id=1, source_target_pairs={{0,4},{4,8},{8,12},{12,16},{16,20},{20,24},{24,28},{1,5},{5,9},{9,... | collective-permute-start | bytes 49160 | tf_op jit(solution)/shard_map/ppermute | solution.py:21
  77.6 1.3 collective-permute-start.16
  79.0 4.4 %fusion.3 = f32[3,2,4,128]{3,0,2,1:T(4,128)S(1)} fusion(f32[9,3,2,4,128]{4,1,0,3,2:T(4,128)S(1)} %constant_dynamic-update-slice_fusion.3, f32[2,4,9,128,128]{4,3,2,1,0:T(8,128)S(1)} %get-tuple-element.36, f32[2,4,128]{2,1,0:T(4,128)S(1)} %get-tuple-element.35, f32[3,2,4,128]{3,2,1,0:T(4,128)S(1)} %copy-done.3), kind=kOutput, calls=%fused_computation.8 | convolution fusion | flops 42476544 | bytes 4857856 | tf_op jit(solution)/shard_map/abkij,kcabj->cabi/dot_general | solution.py:67
  84.7 1.8 %collective-permute-start.19 = (f32[18,1,128]{2,1,0:T(1,128)S(1)}, f32[18,1,128]{2,1,0:T(1,128)S(1)}, u32[]{:S(2)}, u32[]{:S(2)}) collective-permute-start(f32[18,1,128]{2,1,0:T(1,128)S(1)} %get-tuple-element.37), channel_id=1, source_target_pairs={{0,1},{1,2},{2,3},{4,5},{5,6},{6,7},{8,9},{9,10},{10,11},{12,13},{... | collective-permute-start | bytes 27656 | tf_op jit(solution)/shard_map/ppermute | solution.py:21
  86.4 1.3 collective-permute-start.18
  87.7 8.1 %all-to-all-done.1 = f32[32,64,128]{2,1,0:T(8,128)S(1)} async-done(((f32[32,64,128]{2,1,0:T(8,128)}), f32[32,64,128]{2,1,0:T(8,128)S(1)}, u32[]{:S(2)}, u32[]{:S(2)}) %all-to-all-start.1) | async-done | bytes 1048608 | tf_op jit(solution)/shard_map/all_to_all | solution.py:119
  96.4 3.2 %collective-permute-start.12 = (f32[3,1,4,128]{3,0,2,1:T(4,128)S(1)}, f32[3,1,4,128]{3,0,2,1:T(4,128)S(1)}, u32[]{:S(2)}, u32[]{:S(2)}) collective-permute-start(f32[3,1,4,128]{3,0,2,1:T(4,128)S(1)} %get-tuple-element.56), channel_id=1, source_target_pairs={{0,4},{4,8},{8,12},{12,16},{16,20},{20,24},{24,28},{1,5},{5,9},{9,... | collective-permute-start | bytes 18440 | tf_op jit(solution)/shard_map/ppermute | solution.py:21
  99.6 1.3 collective-permute-start.13
  101.3 3.9 %collective-permute-done.13 = f32[3,1,4,128]{3,0,2,1:T(4,128)S(1)} collective-permute-done((f32[3,1,4,128]{3,0,2,1:T(4,128)S(1)}, f32[3,1,4,128]{3,0,2,1:T(4,128)S(1)}, u32[]{:S(2)}, u32[]{:S(2)}) %collective-permute-start.13) | collective-permute-done | bytes 6176 | tf_op jit(solution)/shard_map/ppermute | solution.py:22
  105.2 1.3 collective-permute-start.15
  106.5 3.2 %collective-permute-start.14 = (f32[3,4,1,128]{3,0,2,1:T(4,128)S(1)}, f32[3,4,1,128]{3,0,2,1:T(4,128)S(1)}, u32[]{:S(2)}, u32[]{:S(2)}) collective-permute-start(f32[3,4,1,128]{3,0,2,1:T(4,128)S(1)} %get-tuple-element.51), channel_id=1, source_target_pairs={{0,1},{1,2},{2,3},{4,5},{5,6},{6,7},{8,9},{9,10},{10,11},{12,13},{... | collective-permute-start | bytes 18440 | tf_op jit(solution)/shard_map/ppermute | solution.py:21
  109.9 2.7 %scatter_custom_fusion.2 = f32[2048,128]{1,0:T(8,128)} fusion(s32[512]{0:T(512)S(1)} %bitcast.196, f32[512,128]{1,0:T(8,128)S(1)} %bitcast.187, f32[]{:T(128)} %constant.138.clone.1), kind=kCustom, calls=%fused_computation.22 | custom fusion | bytes 1048580 | tf_op jit(solution)/shard_map/scatter | solution.py:116
  112.7 9.6 %all-to-all-start.2 = ((f32[32,64,128]{2,1,0:T(8,128)}), f32[32,64,128]{2,1,0:T(8,128)S(1)}, u32[]{:S(2)}, u32[]{:S(2)}) async-start(f32[32,64,128]{2,1,0:T(8,128)} %bitcast.56), calls=%async_computation.2 | async-start | bytes 2097152 | tf_op jit(solution)/shard_map/all_to_all | solution.py:119
  122.4 6.6 %fusion = f32[2,4,3,128,1]{3,2,0,1,4:T(4,128)S(1)} fusion(f32[2,4,9,128,128]{4,3,2,1,0:T(8,128)} %copy-done, f32[9,3,2,4,128]{4,1,3,2,0:T(4,128)S(1)} %constant_dynamic-update-slice_fusion.27), kind=kOutput, calls=%fused_computation.3 | convolution fusion | flops 42467328 | bytes 4841472 | tf_op jit(solution)/shard_map/abkij,kcabj->cabi/dot_general | solution.py:67
  129.1 19.4 %all-to-all-done.2 = f32[32,64,128]{2,1,0:T(8,128)S(1)} async-done(((f32[32,64,128]{2,1,0:T(8,128)}), f32[32,64,128]{2,1,0:T(8,128)S(1)}, u32[]{:S(2)}, u32[]{:S(2)}) %all-to-all-start.2) | async-done | bytes 1048608 | tf_op jit(solution)/shard_map/all_to_all | solution.py:119
  (118 shorter events, 20.1 us)
Async XLA Ops:
  0.6 68.8 %copy-start.3 = (f32[3,2,4,128]{3,2,1,0:T(4,128)S(1)}, f32[3,2,4,128]{3,2,1,0:T(4,128)}, u32[]{:S(2)}) copy-start(f32[3,2,4,128]{3,2,1,0:T(4,128)} %param.15) | copy-start | bytes 36868
  1.4 37.3 %collective-permute-start.5 = (f32[3,1,4,128]{3,2,1,0:T(4,128)S(1)}, f32[3,1,4,128]{3,2,1,0:T(4,128)S(1)}, u32[]{:S(2)}, u32[]{:S(2)}) collective-permute-start(f32[3,1,4,128]{3,2,1,0:T(4,128)S(1)} %get-tuple-element.63), channel_id=1, source_target_pairs={{4,0},{8,4},{12,8},{16,12},{20,16},{24,20},{28,24},{5,1},{9,5},{13... | collective-permute-start | bytes 18440 | tf_op jit(solution)/shard_map/ppermute | solution.py:22
  2.6 31.6 %collective-permute-start.4 = (f32[3,1,4,128]{3,2,1,0:T(4,128)S(1)}, f32[3,1,4,128]{3,2,1,0:T(4,128)S(1)}, u32[]{:S(2)}, u32[]{:S(2)}) collective-permute-start(f32[3,1,4,128]{3,2,1,0:T(4,128)S(1)} %get-tuple-element.64), channel_id=1, source_target_pairs={{0,4},{4,8},{8,12},{12,16},{16,20},{20,24},{24,28},{1,5},{5,9},{9,... | collective-permute-start | bytes 18440 | tf_op jit(solution)/shard_map/ppermute | solution.py:21
  8.8 34.9 %collective-permute-start.1 = (f32[3,1,4,128]{3,0,2,1:T(4,128)S(1)}, f32[3,1,4,128]{3,0,2,1:T(4,128)S(1)}, u32[]{:S(2)}, u32[]{:S(2)}) collective-permute-start(f32[3,1,4,128]{3,0,2,1:T(4,128)S(1)} %get-tuple-element.58), channel_id=1, source_target_pairs={{4,0},{8,4},{12,8},{16,12},{20,16},{24,20},{28,24},{5,1},{9,5},{13... | collective-permute-start | bytes 18440 | tf_op jit(solution)/shard_map/ppermute | solution.py:22
  10.1 29.9 %collective-permute-start = (f32[3,1,4,128]{3,0,2,1:T(4,128)S(1)}, f32[3,1,4,128]{3,0,2,1:T(4,128)S(1)}, u32[]{:S(2)}, u32[]{:S(2)}) collective-permute-start(f32[3,1,4,128]{3,0,2,1:T(4,128)S(1)} %get-tuple-element.59), channel_id=1, source_target_pairs={{0,4},{4,8},{8,12},{12,16},{16,20},{20,24},{24,28},{1,5},{5,9},{9,... | collective-permute-start | bytes 18440 | tf_op jit(solution)/shard_map/ppermute | solution.py:21
  16.3 35.8 %collective-permute-start.8 = (f32[1,32,128]{2,1,0:T(8,128)S(1)}, f32[1,32,128]{2,1,0:T(8,128)S(1)}, u32[]{:S(2)}, u32[]{:S(2)}) collective-permute-start(f32[1,32,128]{2,1,0:T(8,128)S(1)} %get-tuple-element.43), channel_id=1, source_target_pairs={{4,0},{8,4},{12,8},{16,12},{20,16},{24,20},{28,24},{5,1},{9,5},{13... | collective-permute-start | bytes 49160 | tf_op jit(solution)/shard_map/ppermute | solution.py:22
  25.1 38.7 %all-to-all-start = ((f32[32,1,64]{2,1,0:T(1,128)}), f32[32,1,64]{2,1,0:T(1,128)S(1)}, u32[]{:S(2)}, u32[]{:S(2)}) async-start(f32[32,1,64]{2,1,0:T(1,128)} %all_to_all.13), calls=%async_computation | async-start | bytes 32768 | tf_op jit(solution)/shard_map/all_to_all | solution.py:126
  34.2 16.9 %collective-permute-start.9 = (f32[1,32,128]{2,1,0:T(8,128)S(1)}, f32[1,32,128]{2,1,0:T(8,128)S(1)}, u32[]{:S(2)}, u32[]{:S(2)}) collective-permute-start(f32[1,32,128]{2,1,0:T(8,128)S(1)} %get-tuple-element.44), channel_id=1, source_target_pairs={{0,4},{4,8},{8,12},{12,16},{16,20},{20,24},{24,28},{1,5},{5,9},{9,... | collective-permute-start | bytes 49160 | tf_op jit(solution)/shard_map/ppermute | solution.py:21
  38.7 10.8 %collective-permute-start.7 = (f32[3,4,1,128]{3,2,1,0:T(1,128)S(1)}, f32[3,4,1,128]{3,2,1,0:T(1,128)S(1)}, u32[]{:S(2)}, u32[]{:S(2)}) collective-permute-start(f32[3,4,1,128]{3,2,1,0:T(1,128)S(1)} %get-tuple-element.54), channel_id=1, source_target_pairs={{1,0},{2,1},{3,2},{5,4},{6,5},{7,6},{9,8},{10,9},{11,10},{13,12},{... | collective-permute-start | bytes 18440 | tf_op jit(solution)/shard_map/ppermute | solution.py:22
  40.0 5.1 %collective-permute-start.6 = (f32[3,4,1,128]{3,2,1,0:T(1,128)S(1)}, f32[3,4,1,128]{3,2,1,0:T(1,128)S(1)}, u32[]{:S(2)}, u32[]{:S(2)}) collective-permute-start(f32[3,4,1,128]{3,2,1,0:T(1,128)S(1)} %get-tuple-element.55), channel_id=1, source_target_pairs={{0,1},{1,2},{2,3},{4,5},{5,6},{6,7},{8,9},{9,10},{10,11},{12,13},{... | collective-permute-start | bytes 18440 | tf_op jit(solution)/shard_map/ppermute | solution.py:21
  43.8 13.3 %collective-permute-start.3 = (f32[3,4,1,128]{3,0,2,1:T(4,128)S(1)}, f32[3,4,1,128]{3,0,2,1:T(4,128)S(1)}, u32[]{:S(2)}, u32[]{:S(2)}) collective-permute-start(f32[3,4,1,128]{3,0,2,1:T(4,128)S(1)} %get-tuple-element.52), channel_id=1, source_target_pairs={{1,0},{2,1},{3,2},{5,4},{6,5},{7,6},{9,8},{10,9},{11,10},{13,12},{... | collective-permute-start | bytes 18440 | tf_op jit(solution)/shard_map/ppermute | solution.py:22
  45.1 6.0 %collective-permute-start.2 = (f32[3,4,1,128]{3,0,2,1:T(4,128)S(1)}, f32[3,4,1,128]{3,0,2,1:T(4,128)S(1)}, u32[]{:S(2)}, u32[]{:S(2)}) collective-permute-start(f32[3,4,1,128]{3,0,2,1:T(4,128)S(1)} %get-tuple-element.53), channel_id=1, source_target_pairs={{0,1},{1,2},{2,3},{4,5},{5,6},{6,7},{8,9},{9,10},{10,11},{12,13},{... | collective-permute-start | bytes 18440 | tf_op jit(solution)/shard_map/ppermute | solution.py:21
  52.2 5.0 %collective-permute-start.11 = (f32[18,1,128]{2,1,0:T(1,128)S(1)}, f32[18,1,128]{2,1,0:T(1,128)S(1)}, u32[]{:S(2)}, u32[]{:S(2)}) collective-permute-start(f32[18,1,128]{2,1,0:T(1,128)S(1)} %get-tuple-element.39), channel_id=1, source_target_pairs={{0,1},{1,2},{2,3},{4,5},{5,6},{6,7},{8,9},{9,10},{10,11},{12,13},{... | collective-permute-start | bytes 27656 | tf_op jit(solution)/shard_map/ppermute | solution.py:21
  55.8 3.3 %collective-permute-start.10 = (f32[18,1,128]{2,1,0:T(1,128)S(1)}, f32[18,1,128]{2,1,0:T(1,128)S(1)}, u32[]{:S(2)}, u32[]{:S(2)}) collective-permute-start(f32[18,1,128]{2,1,0:T(1,128)S(1)} %get-tuple-element.40), channel_id=1, source_target_pairs={{1,0},{2,1},{3,2},{5,4},{6,5},{7,6},{9,8},{10,9},{11,10},{13,12},{... | collective-permute-start | bytes 27656 | tf_op jit(solution)/shard_map/ppermute | solution.py:22
  63.7 32.1 %all-to-all-start.1 = ((f32[32,64,128]{2,1,0:T(8,128)}), f32[32,64,128]{2,1,0:T(8,128)S(1)}, u32[]{:S(2)}, u32[]{:S(2)}) async-start(f32[32,64,128]{2,1,0:T(8,128)} %bitcast.39), calls=%async_computation.1 | async-start | bytes 2097152 | tf_op jit(solution)/shard_map/all_to_all | solution.py:119
  73.8 5.2 %copy-start = (f32[2,4,9,128,128]{4,3,2,1,0:T(8,128)}, f32[2,4,9,128,128]{4,3,2,1,0:T(8,128)S(1)}, u32[]{:S(2)}) copy-start(f32[2,4,9,128,128]{4,3,2,1,0:T(8,128)S(1)} %get-tuple-element.36) | copy-start | bytes 14155780
  73.8 22.6 %copy-start.5 = (f32[3,2,4,128]{3,2,1,0:T(4,128)S(1)}, f32[3,2,4,128]{3,2,1,0:T(4,128)}, u32[]{:S(2)}) copy-start(f32[3,2,4,128]{3,2,1,0:T(4,128)} %param.16) | copy-start | bytes 36868
  73.8 35.9 %copy-start.1 = (f32[16,32,128]{2,1,0:T(8,128)S(1)}, f32[16,32,128]{2,1,0:T(8,128)}, u32[]{:S(2)}) copy-start(f32[16,32,128]{2,1,0:T(8,128)} %param.19) | copy-start | bytes 786436
  73.8 35.9 %copy-start.2 = (f32[16,32,128]{2,1,0:T(8,128)S(1)}, f32[16,32,128]{2,1,0:T(8,128)}, u32[]{:S(2)}) copy-start(f32[16,32,128]{2,1,0:T(8,128)} %param.21) | copy-start | bytes 786436
  73.8 10.8 %collective-permute-start.17 = (f32[1,32,128]{2,1,0:T(8,128)S(1)}, f32[1,32,128]{2,1,0:T(8,128)S(1)}, u32[]{:S(2)}, u32[]{:S(2)}) collective-permute-start(f32[1,32,128]{2,1,0:T(8,128)S(1)} %get-tuple-element.41), channel_id=1, source_target_pairs={{0,4},{4,8},{8,12},{12,16},{16,20},{20,24},{24,28},{1,5},{5,9},{9,... | collective-permute-start | bytes 49160 | tf_op jit(solution)/shard_map/ppermute | solution.py:21
  77.6 7.0 %collective-permute-start.16 = (f32[1,32,128]{2,1,0:T(8,128)S(1)}, f32[1,32,128]{2,1,0:T(8,128)S(1)}, u32[]{:S(2)}, u32[]{:S(2)}) collective-permute-start(f32[1,32,128]{2,1,0:T(8,128)S(1)} %get-tuple-element.42), channel_id=1, source_target_pairs={{4,0},{8,4},{12,8},{16,12},{20,16},{24,20},{28,24},{5,1},{9,5},{13... | collective-permute-start | bytes 49160 | tf_op jit(solution)/shard_map/ppermute | solution.py:22
  84.7 16.3 %collective-permute-start.19 = (f32[18,1,128]{2,1,0:T(1,128)S(1)}, f32[18,1,128]{2,1,0:T(1,128)S(1)}, u32[]{:S(2)}, u32[]{:S(2)}) collective-permute-start(f32[18,1,128]{2,1,0:T(1,128)S(1)} %get-tuple-element.37), channel_id=1, source_target_pairs={{0,1},{1,2},{2,3},{4,5},{5,6},{6,7},{8,9},{9,10},{10,11},{12,13},{... | collective-permute-start | bytes 27656 | tf_op jit(solution)/shard_map/ppermute | solution.py:21
  86.4 14.5 %collective-permute-start.18 = (f32[18,1,128]{2,1,0:T(1,128)S(1)}, f32[18,1,128]{2,1,0:T(1,128)S(1)}, u32[]{:S(2)}, u32[]{:S(2)}) collective-permute-start(f32[18,1,128]{2,1,0:T(1,128)S(1)} %get-tuple-element.38), channel_id=1, source_target_pairs={{1,0},{2,1},{3,2},{5,4},{6,5},{7,6},{9,8},{10,9},{11,10},{13,12},{... | collective-permute-start | bytes 27656 | tf_op jit(solution)/shard_map/ppermute | solution.py:22
  96.4 4.9 %collective-permute-start.12 = (f32[3,1,4,128]{3,0,2,1:T(4,128)S(1)}, f32[3,1,4,128]{3,0,2,1:T(4,128)S(1)}, u32[]{:S(2)}, u32[]{:S(2)}) collective-permute-start(f32[3,1,4,128]{3,0,2,1:T(4,128)S(1)} %get-tuple-element.56), channel_id=1, source_target_pairs={{0,4},{4,8},{8,12},{12,16},{16,20},{20,24},{24,28},{1,5},{5,9},{9,... | collective-permute-start | bytes 18440 | tf_op jit(solution)/shard_map/ppermute | solution.py:21
  99.6 5.5 %collective-permute-start.13 = (f32[3,1,4,128]{3,0,2,1:T(4,128)S(1)}, f32[3,1,4,128]{3,0,2,1:T(4,128)S(1)}, u32[]{:S(2)}, u32[]{:S(2)}) collective-permute-start(f32[3,1,4,128]{3,0,2,1:T(4,128)S(1)} %get-tuple-element.57), channel_id=1, source_target_pairs={{4,0},{8,4},{12,8},{16,12},{20,16},{24,20},{28,24},{5,1},{9,5},{13... | collective-permute-start | bytes 18440 | tf_op jit(solution)/shard_map/ppermute | solution.py:22
  105.2 17.1 %collective-permute-start.15 = (f32[3,4,1,128]{3,0,2,1:T(4,128)S(1)}, f32[3,4,1,128]{3,0,2,1:T(4,128)S(1)}, u32[]{:S(2)}, u32[]{:S(2)}) collective-permute-start(f32[3,4,1,128]{3,0,2,1:T(4,128)S(1)} %get-tuple-element.50), channel_id=1, source_target_pairs={{1,0},{2,1},{3,2},{5,4},{6,5},{7,6},{9,8},{10,9},{11,10},{13,12},{... | collective-permute-start | bytes 18440 | tf_op jit(solution)/shard_map/ppermute | solution.py:22
  106.5 15.8 %collective-permute-start.14 = (f32[3,4,1,128]{3,0,2,1:T(4,128)S(1)}, f32[3,4,1,128]{3,0,2,1:T(4,128)S(1)}, u32[]{:S(2)}, u32[]{:S(2)}) collective-permute-start(f32[3,4,1,128]{3,0,2,1:T(4,128)S(1)} %get-tuple-element.51), channel_id=1, source_target_pairs={{0,1},{1,2},{2,3},{4,5},{5,6},{6,7},{8,9},{9,10},{10,11},{12,13},{... | collective-permute-start | bytes 18440 | tf_op jit(solution)/shard_map/ppermute | solution.py:21
  109.9 39.1 %copy-start.4 = (f32[16,32,128]{2,1,0:T(8,128)}, f32[16,32,128]{2,1,0:T(8,128)S(1)}, u32[]{:S(2)}) copy-start(f32[16,32,128]{2,1,0:T(8,128)S(1)} %fusion.13) | copy-start | bytes 786436
  112.7 35.8 %all-to-all-start.2 = ((f32[32,64,128]{2,1,0:T(8,128)}), f32[32,64,128]{2,1,0:T(8,128)S(1)}, u32[]{:S(2)}, u32[]{:S(2)}) async-start(f32[32,64,128]{2,1,0:T(8,128)} %bitcast.56), calls=%async_computation.2 | async-start | bytes 2097152 | tf_op jit(solution)/shard_map/all_to_all | solution.py:119
where the time goes:
time: 152 us; the launch traced here: 150 us
  starting transfers between devices  73.4 us (48%)
  waiting for transfers between devices  33.4 us (22%)
  local copies, waits for them, and re-layouts  15.5 us (10%)
  other arithmetic  14.7 us (10%)
  matrix products  12 us (8%)
    ppermute x10, starting transfers between devices, padded_2(): before = lax.ppermute(last, axis, up)  36.9 us
    all_to_all x2, waiting for transfers between devices, per_device(): lax.all_to_all(outgoing.reshape(devices, capacity, count), ('fx', 'wy'),...  27.5 us
    all_to_all x2, starting transfers between devices, per_device(): lax.all_to_all(outgoing.reshape(devices, capacity, count), ('fx', 'wy'),...  15.3 us
    ppermute x10, starting transfers between devices, padded_2(): after = lax.ppermute(first, axis, down)  12.9 us
    dot_general x2, matrix products, bond_forces(): jnp.einsum('abkij,kcabj->cabi', weights, other, precision=lax.Precision.H...  11 us
    all_to_all x1, starting transfers between devices, per_device(): lax.all_to_all(labels.reshape(devices, capacity), ('fx', 'wy'), split_axi...  8.34 us
    ppermute x10, waiting for transfers between devices, padded_2(): after = lax.ppermute(first, axis, down)  5.8 us
    scatter x2, local copies, waits for them, and re-layouts, per_device(): outgoing = jnp.zeros((devices * capacity, count), jnp.float32).at[positio...  5.43 us
  transfers between devices with their start and end apart: 23, of which 4 were waited for; matrix products, arithmetic and copies ran while one was open for 26% of the time, Pallas kernels for 0%

commit v1 on v0

v1 whole, which is shorter than its diff:
```python
import functools

import jax
import jax.numpy as jnp
from jax import lax
from jax.experimental import pallas as pl
from jax.experimental.pallas import tpu as pltpu
from jax.sharding import PartitionSpec as P

STIFFNESS = 0.02
LOADING = 0.05
REACH = 3.0
LANES = 128
SUB = 8
VMEM_BYTES = 48 * 1024 * 1024

F32 = jnp.float32
BF16 = jnp.bfloat16


def whole(ndim):
    return pl.BlockSpec(memory_space=pltpu.VMEM)


def params(*semantics):
    return pltpu.CompilerParams(vmem_limit_bytes=VMEM_BYTES)


def even_at(axis):
    return lax.rem(lax.axis_index(axis), 2) == 0


def pair_list(count, first):
    pairs = []
    for low in range(first, count - 1, 2):
        pairs.extend([(low, low + 1), (low + 1, low)])
    return pairs


def exchange(axis, to_even, to_odd):
    count = lax.axis_size(axis)
    got_even = lax.ppermute(to_even, axis, pair_list(count, 0))
    got_odd = lax.ppermute(to_odd, axis, pair_list(count, 1))
    return got_even, got_odd


def place_edges(even, low, high, to_even, to_odd):
    @pl.when(even)
    def _():
        high(to_even)
        low(to_odd)

    @pl.when(jnp.logical_not(even))
    def _():
        low(to_even)
        high(to_odd)


def before_after(even, got_even, got_odd):
    a, b = got_even[...], got_odd[...]
    return jnp.where(even, b, a), jnp.where(even, a, b)


def pack_wy_kernel(p_lo, p_hi, q_lo, q_hi, s_lo, s_hi, jit, disp, to_even, to_odd):
    cx = p_lo.shape[0]
    rows, cols = jit.shape[1], jit.shape[2]

    def edge(p, q, s, near, far, h):
        def write(out):
            out[0:cx, :] = p[:, near, :]
            out[cx : 2 * cx, :] = p[:, far, :]
            out[2 * cx : 3 * cx, :] = q[:, near, :]
            out[3 * cx : 4 * cx, :] = s[:, near, :]
            at = 4 * cx
            for field in (jit, disp):
                for c in range(3):
                    for l in range(rows):
                        out[at : at + 1, :] = field[c, l, h : h + 1, :]
                        at += 1
            for spare in range(at, out.shape[0]):
                out[spare : spare + 1, :] = jnp.zeros((1, LANES), F32)

        return write

    place_edges(
        even_at("wy"),
        edge(p_lo, q_lo, s_lo, 0, 1, 0),
        edge(p_hi, q_hi, s_hi, SUB - 1, SUB - 2, cols - 1),
        to_even,
        to_odd,
    )


def pad8(count):
    return (count + 7) // 8 * 8


def pack_wy(p, q, s, jit, disp):
    cx, cy = p.shape[0], p.shape[1]
    rows = jit.shape[1]
    size = pad8(4 * cx + 6 * rows)
    first = pl.BlockSpec((cx, SUB, LANES), lambda i: (0, 0, 0))
    last = pl.BlockSpec((cx, SUB, LANES), lambda i: (0, cy // SUB - 1, 0))
    small = pl.BlockSpec(jit.shape, lambda i: (0, 0, 0, 0))
    out = jax.ShapeDtypeStruct((size, LANES), F32)
    spec = pl.BlockSpec((size, LANES), lambda i: (0, 0))
    return pl.pallas_call(
        pack_wy_kernel,
        grid=(1,),
        in_specs=[first, last, first, last, first, last, small, small],
        out_specs=[spec, spec],
        out_shape=[out, out],
        compiler_params=params(),
        name="pack_wy",
    )(p, p, q, q, s, s, jit, disp)


def pack_fx_kernel(
    cx, p_lo, p_hi, q_lo, q_hi, s_lo, s_hi, jit, disp, got_even, got_odd, to_even, to_odd
):
    cy = p_lo.shape[1]
    rows, cols = jit.shape[1], jit.shape[2]
    before, after = before_after(even_at("wy"), got_even, got_odd)

    def edge(p, q, s, near, far, x, l):
        def write(out):
            out[0:cy, :] = p[near]
            out[cy : 2 * cy, :] = p[far]
            out[2 * cy : 3 * cy, :] = q[0]
            out[3 * cy : 4 * cy, :] = s[0]
            at = 4 * cy
            for f, field in enumerate((jit, disp)):
                for c in range(3):
                    side = 4 * cx + (f * 3 + c) * rows + l
                    out[at : at + 1, :] = before[side : side + 1]
                    out[at + 1 : at + 1 + cols, :] = field[c, l]
                    out[at + 1 + cols : at + 2 + cols, :] = after[side : side + 1]
                    at += cols + 2
            out[at : at + 1, :] = before[x : x + 1]
            out[at + 1 : at + 2, :] = after[x : x + 1]
            for spare in range(at + 2, out.shape[0]):
                out[spare : spare + 1, :] = jnp.zeros((1, LANES), F32)

        return write

    place_edges(
        even_at("fx"),
        edge(p_lo, q_lo, s_lo, 0, 1, 0, 0),
        edge(p_hi, q_hi, s_hi, 1, 0, cx - 1, rows - 1),
        to_even,
        to_odd,
    )


def pack_fx(p, q, s, jit, disp, got_even, got_odd):
    cx, cy = p.shape[0], p.shape[1]
    cols = jit.shape[2]
    size = pad8(4 * cy + 6 * (cols + 2) + 2)

    def at(depth, index):
        return pl.BlockSpec((depth, cy, LANES), lambda i: (index, 0, 0))

    small = pl.BlockSpec(jit.shape, lambda i: (0, 0, 0, 0))
    message = pl.BlockSpec(got_even.shape, lambda i: (0, 0))
    out = jax.ShapeDtypeStruct((size, LANES), F32)
    spec = pl.BlockSpec((size, LANES), lambda i: (0, 0))
    return pl.pallas_call(
        functools.partial(pack_fx_kernel, cx),
        grid=(1,),
        in_specs=[at(2, 0), at(2, cx // 2 - 1), at(1, 0), at(1, cx - 1), at(1, 0), at(1, cx - 1)]
        + [small, small, message, message],
        out_specs=[spec, spec],
        out_shape=[out, out],
        compiler_params=params(),
        name="pack_fx",
    )(p, p, q, q, s, s, jit, disp, got_even, got_odd)


def along_z(v):
    lane = lax.broadcasted_iota(jnp.int32, v.shape, 1)
    up = jnp.where(lane == LANES - 1, 0.0, pltpu.roll(v, LANES - 1, 1))
    down = jnp.where(lane == 0, 0.0, pltpu.roll(v, 1, 1))
    return up + down


def update(v, old, speed, beside):
    return 2.0 * v - old + speed * (beside + along_z(v) - 6.0 * v)


def two_terms(v):
    high = v.astype(BF16)
    return high, (v - high.astype(F32)).astype(BF16)


def grid_kernel(p, q, s, wye, wyo, fxe, fxo, target, out, slots, s0, s1, rhs, part1, part2):
    cx, cy = p.shape[0], p.shape[1]
    ahead, behind = SUB, SUB + cy
    fx_count = part1.shape[0] // 2 - 1
    cols = 4
    tall = part2.shape[0]
    high = part1.shape[1] - 2 * SUB
    wy_count = high // cols
    before_y, after_y = before_after(even_at("wy"), wye, wyo)
    before_x, after_x = before_after(even_at("fx"), fxe, fxo)
    corner = 4 * cy + 6 * (cols + 2)

    s0[1 : cx + 1, ahead:behind, :] = p[...]
    for x, side in ((0, before_x), (cx + 1, after_x)):
        s0[x, ahead:behind, :] = side[0:cy]
        s0[x, ahead - 1 : ahead, :] = side[corner : corner + 1]
        s0[x, behind : behind + 1, :] = side[corner + 1 : corner + 2]
    s0[1 : cx + 1, ahead - 1, :] = before_y[0:cx]
    s0[1 : cx + 1, behind, :] = after_y[0:cx]

    for side, y, inner in ((before_y, ahead - 1, ahead), (after_y, behind, behind - 1)):
        near, far = side[0:cx], side[cx : 2 * cx]
        old, speed = side[2 * cx : 3 * cx], side[3 * cx : 4 * cx]
        beside = s0[0:cx, y, :] + s0[2 : cx + 2, y, :] + far + s0[1 : cx + 1, inner, :]
        s1[1 : cx + 1, y, :] = update(near, old, speed, beside)
    for side, x, inner in ((before_x, 0, 1), (after_x, cx + 1, cx)):
        near, far = side[0:cy], side[cy : 2 * cy]
        old, speed = side[2 * cy : 3 * cy], side[3 * cy : 4 * cy]
        beside = s0[x, ahead - 1 : behind - 1, :] + s0[x, ahead + 1 : behind + 1, :]
        beside = beside + far + s0[inner, ahead:behind, :]
        s1[x, ahead:behind, :] = update(near, old, speed, beside)

    def sweep(now, old, x):
        beside = now[x, ahead:behind, :] + now[x + 2, ahead:behind, :]
        beside = beside + now[x + 1, ahead - 1 : behind - 1, :]
        beside = beside + now[x + 1, ahead + 1 : behind + 1, :]
        return update(now[x + 1, ahead:behind, :], old, s[x], beside)

    for x in range(cx):
        fresh = sweep(s0, q[x], x)
        s1[x + 1, ahead:behind, :] = fresh
        a, b = two_terms(fresh)
        rhs[x * cy : (x + 1) * cy, 0:LANES] = a
        rhs[x * cy : (x + 1) * cy, LANES : 2 * LANES] = b
    for x in range(cx):
        fresh = sweep(s1, p[x], x)
        out[x] = fresh
        a, b = two_terms(fresh)
        rhs[x * cy : (x + 1) * cy, 2 * LANES : 3 * LANES] = a
        rhs[x * cy : (x + 1) * cy, 3 * LANES : 4 * LANES] = b

    part1[...] = jnp.zeros(part1.shape, F32)
    part2[:, 0:SUB, :] = jnp.zeros((tall, SUB, LANES), F32)
    chunk = 256
    for first in range(0, tall * high, chunk):
        tile = lax.broadcasted_iota(jnp.int32, (chunk, LANES), 0) + first
        picks = []
        for piece in range(target.shape[0]):
            picks.append(jnp.where(tile == target[piece : piece + 1, :], 1.0, 0.0).astype(BF16))
        sums = jnp.dot(jnp.concatenate(picks, axis=1), rhs[...], preferred_element_type=F32)
        one = sums[:, 0:LANES] + sums[:, LANES : 2 * LANES]
        two = sums[:, 2 * LANES : 3 * LANES] + sums[:, 3 * LANES : 4 * LANES]
        l = first // high
        part1[1 + l : 1 + l + chunk // high, SUB : SUB + high, :] = one.reshape(-1, high, LANES)
        part2[l : l + chunk // high, SUB : SUB + high, :] = two.reshape(-1, high, LANES)
    lower = lax.broadcasted_iota(jnp.int32, (SUB, LANES), 0) < cols + 2
    for a in range(fx_count):
        for b in range(wy_count):
            for l in range(4):
                h = SUB + cols * b
                one = part1[2 * a + l, h - 1 : h - 1 + SUB, :]
                h = h + 2 * (l % 2) - 6
                two = part2[2 * a + l // 2, h : h + SUB, :]
                slots[a * wy_count + b, l * SUB : (l + 1) * SUB, :] = jnp.where(lower, one, two)


def grid_steps(p, q, s, wy_got, fx_got, target, fx_count, wy_count):
    cx, cy = p.shape[0], p.shape[1]
    tall, high = fx_count * 2, wy_count * 4
    devices = fx_count * wy_count
    return pl.pallas_call(
        grid_kernel,
        in_specs=[whole(0)] * 8,
        out_specs=[whole(0)] * 2,
        out_shape=[
            jax.ShapeDtypeStruct(p.shape, F32),
            jax.ShapeDtypeStruct((devices, 4 * SUB, LANES), F32),
        ],
        scratch_shapes=[
            pltpu.VMEM((cx + 2, cy + 2 * SUB, LANES), F32),
            pltpu.VMEM((cx + 2, cy + 2 * SUB, LANES), F32),
            pltpu.VMEM((cx * cy, 4 * LANES), BF16),
            pltpu.VMEM((tall + 2, high + 2 * SUB, LANES), F32),
            pltpu.VMEM((tall, high + 2 * SUB, LANES), F32),
        ],
        compiler_params=params(),
        name="grid_steps",
    )(p, q, s, *wy_got, *fx_got, target)


def reached(g):
    groups = []
    for dh in (-1, 0, 1):
        if (dh == -1 and g % 4 == 3) or (dh == 1 and g % 4 == 0):
            continue
        groups.append((False, dh))
        groups.append((True, dh))
    return groups


STORED = sum(len(reached(g)) for g in range(LANES // SUB))


def tile_rows(ref, c, l, h, first_sub):
    mid, ends = {}, {}
    for dh in (-1, 0, 1):
        at = h + 1 + dh
        mid[dh] = jnp.broadcast_to(ref[c, l + 1, pl.ds(at, 1), :], (SUB, LANES))
        before = jnp.broadcast_to(ref[c, l, pl.ds(at, 1), :], (SUB, LANES))
        after = jnp.broadcast_to(ref[c, l + 2, pl.ds(at, 1), :], (SUB, LANES))
        ends[dh] = jnp.where(first_sub, before, after)
    return mid, ends


def fill_padded(pad, own, before_y, after_y, before_x, after_x, at_y, at_x):
    rows, cols = own.shape[1], own.shape[2]
    for c in range(3):
        for l in range(rows):
            row = at_y + c * rows + l
            pad[c, l + 1, 0:1, :] = before_y[row : row + 1]
            pad[c, l + 1, 1 : cols + 1, :] = own[c, l]
            pad[c, l + 1, cols + 1 : cols + 2, :] = after_y[row : row + 1]
        row = at_x + c * (cols + 2)
        pad[c, 0, 0 : cols + 2, :] = before_x[row : row + cols + 2]
        pad[c, rows + 1, 0 : cols + 2, :] = after_x[row : row + cols + 2]


def lane_sums(acc, count):
    ones = jnp.ones((2 * SUB, LANES), BF16)
    result = []
    for c in range(count):
        high, low = two_terms(acc[c])
        both = jnp.concatenate([high, low], axis=0)
        sums = lax.dot_general(
            ones, both, (((1,), (1,)), ((), ())), preferred_element_type=F32
        )
        result.append(sums[0:1, 0:LANES] + sums[0:1, LANES : 2 * LANES])
    return result


def wall_kernel(
    cx, cy, masks, jit, disp, vel, wye, wyo, fxe, fxo, weights, vel1, base1, totals, to_even, to_odd,
    jpad, dpad, acc,
):
    rows, cols = jit.shape[1], jit.shape[2]
    l, h = pl.program_id(0), pl.program_id(1)
    first_sub = lax.broadcasted_iota(jnp.int32, (SUB, LANES), 0) < SUB // 2

    @pl.when((l == 0) & (h == 0))
    def _():
        before_y, after_y = before_after(even_at("wy"), wye, wyo)
        before_x, after_x = before_after(even_at("fx"), fxe, fxo)
        fill_padded(jpad, jit, before_y, after_y, before_x, after_x, 4 * cx, 4 * cy)
        fill_padded(
            dpad, disp, before_y, after_y, before_x, after_x,
            4 * cx + 3 * rows, 4 * cy + 3 * (cols + 2),
        )

    index = lax.broadcasted_iota(jnp.int32, (1, LANES), 1)
    lattice = (index % 8, index // 8 % 4, index // 32)
    lattice = [v.astype(F32) * (1.0 / REACH) for v in lattice]
    span = 8.0 / REACH
    rise = 4.0 / REACH
    others, own = [], []
    for c in range(3):
        mid, ends = tile_rows(jpad, c, l, h, first_sub)
        for dh in (-1, 0, 1):
            mid[dh] = mid[dh] * (1.0 / REACH) + lattice[c]
            ends[dh] = ends[dh] * (1.0 / REACH) + lattice[c]
            if c == 0:
                ends[dh] = ends[dh] + jnp.where(first_sub, -span, span)
            if c == 1:
                mid[dh] = mid[dh] + rise * dh
                ends[dh] = ends[dh] + rise * dh
        own.append(mid[0])
        others.append((mid, ends))
    pulls = [tile_rows(dpad, c, l, h, first_sub) for c in range(3)]
    columns = jnp.transpose(
        jnp.concatenate([own[0], own[1], own[2]], axis=0)
    )

    place = 0
    for g in range(LANES // SUB):
        mine = [
            jnp.broadcast_to(columns[g * SUB : (g + 1) * SUB, c * SUB : c * SUB + 1], (SUB, LANES))
            for c in range(3)
        ]
        sums = [jnp.zeros((SUB, LANES), F32) for _ in range(4)]
        span_g = slice(g * SUB, (g + 1) * SUB)
        for ends, dh in reached(g):
            if ends:
                mask = jnp.where(first_sub, masks[0, 0, 1 + dh, span_g, :], masks[0, 0, 7 + dh, span_g, :])
            else:
                mask = masks[0, 0, 4 + dh, span_g, :]
            weight = mask.astype(F32)
            for c in range(3):
                diff = others[c][ends][dh] - mine[c]
                weight = weight - diff * diff
            weight = jnp.maximum(weight, 0.0)
            weights[0, 0, place] = weight
            place += 1
            for c in range(3):
                sums[c] = sums[c] + weight * pulls[c][ends][dh]
            sums[3] = sums[3] + weight
        for c in range(4):
            acc[c, span_g, :] = sums[c]
    pulled = lane_sums(acc, 4)
    totals[l, pl.ds(h, 1), :] = pulled[3]
    for c in range(3):
        mine = dpad[c, l + 1, pl.ds(h + 1, 1), :]
        force = STIFFNESS * (pulled[c] - pulled[3] * mine)
        fresh = vel[c, l, pl.ds(h, 1), :] + force
        vel1[c, l, pl.ds(h, 1), :] = fresh
        base1[c, l, pl.ds(h, 1), :] = mine + fresh

    @pl.when((l == rows - 1) & (h == cols - 1))
    def _():
        def edge(at):
            def write(out):
                for c in range(3):
                    for k in range(rows):
                        out[c * rows + k : c * rows + k + 1, :] = base1[c, k, at : at + 1, :]
                for spare in range(3 * rows, out.shape[0]):
                    out[spare : spare + 1, :] = jnp.zeros((1, LANES), F32)

            return write

        place_edges(even_at("wy"), edge(0), edge(cols - 1), to_even, to_odd)


def wall_first(cx, cy, masks, jit, disp, vel, wy_got, fx_got):
    rows, cols = jit.shape[1], jit.shape[2]
    field = pl.BlockSpec(jit.shape, lambda l, h: (0, 0, 0, 0))
    wy_spec = pl.BlockSpec(wy_got[0].shape, lambda l, h: (0, 0))
    fx_spec = pl.BlockSpec(fx_got[0].shape, lambda l, h: (0, 0))
    edge = (pad8(3 * rows), LANES)
    edge_spec = pl.BlockSpec(edge, lambda l, h: (0, 0))
    return pl.pallas_call(
        functools.partial(wall_kernel, cx, cy),
        grid=(rows, cols),
        in_specs=[
            pl.BlockSpec((1, 1, 9, LANES, LANES), lambda l, h: (l, h, 0, 0, 0)),
            field, field, field, wy_spec, wy_spec, fx_spec, fx_spec,
        ],
        out_specs=[
            pl.BlockSpec((1, 1, STORED, SUB, LANES), lambda l, h: (l, h, 0, 0, 0)),
            field, field,
            pl.BlockSpec((rows, cols, LANES), lambda l, h: (0, 0, 0)),
            edge_spec, edge_spec,
        ],
        out_shape=[
            jax.ShapeDtypeStruct((rows, cols, STORED, SUB, LANES), F32),
            jax.ShapeDtypeStruct(jit.shape, F32),
            jax.ShapeDtypeStruct(jit.shape, F32),
            jax.ShapeDtypeStruct((rows, cols, LANES), F32),
            jax.ShapeDtypeStruct(edge, F32),
            jax.ShapeDtypeStruct(edge, F32),
        ],
        scratch_shapes=[
            pltpu.VMEM((3, rows + 2, SUB, LANES), F32),
            pltpu.VMEM((3, rows + 2, SUB, LANES), F32),
            pltpu.VMEM((4, LANES, LANES), F32),
        ],
        compiler_params=params(),
        name="wall_first",
    )(masks, jit, disp, vel, *wy_got, *fx_got)


def pack_base_kernel(base1, got_even, got_odd, to_even, to_odd):
    rows, cols = base1.shape[1], base1.shape[2]
    before, after = before_after(even_at("wy"), got_even, got_odd)

    def edge(l):
        def write(out):
            at = 0
            for c in range(3):
                side = c * rows + l
                out[at : at + 1, :] = before[side : side + 1]
                out[at + 1 : at + 1 + cols, :] = base1[c, l]
                out[at + 1 + cols : at + 2 + cols, :] = after[side : side + 1]
                at += cols + 2
            for spare in range(at, out.shape[0]):
                out[spare : spare + 1, :] = jnp.zeros((1, LANES), F32)

        return write

    place_edges(even_at("fx"), edge(0), edge(rows - 1), to_even, to_odd)


def pack_base(base1, got):
    cols = base1.shape[2]
    out = jax.ShapeDtypeStruct((pad8(3 * (cols + 2)), LANES), F32)
    return pl.pallas_call(
        pack_base_kernel,
        in_specs=[whole(0)] * 3,
        out_specs=[whole(0)] * 2,
        out_shape=[out, out],
        compiler_params=params(),
        name="pack_base",
    )(base1, *got)


def last_kernel(
    weights, got, base1, vel1, totals, wye, wyo, fxe, fxo, disp_out, vel_out, dpad, loads, acc
):
    rows, cols = base1.shape[1], base1.shape[2]
    l, h = pl.program_id(0), pl.program_id(1)
    first_sub = lax.broadcasted_iota(jnp.int32, (SUB, LANES), 0) < SUB // 2

    @pl.when((l == 0) & (h == 0))
    def _():
        before_y, after_y = before_after(even_at("wy"), wye, wyo)
        before_x, after_x = before_after(even_at("fx"), fxe, fxo)
        fill_padded(dpad, base1, before_y, after_y, before_x, after_x, 0, 0)
        total = got[0]
        for d in range(1, got.shape[0]):
            total = total + got[d]
        loads[...] = total
        for k in range(rows + 2):
            here = total[k * SUB : k * SUB + cols + 2, :]
            dpad[0, k, 0 : cols + 2, :] = dpad[0, k, 0 : cols + 2, :] + LOADING * here

    pulls = [tile_rows(dpad, c, l, h, first_sub) for c in range(3)]
    place = 0
    for g in range(LANES // SUB):
        sums = [jnp.zeros((SUB, LANES), F32) for _ in range(3)]
        for ends, dh in reached(g):
            weight = weights[0, 0, place]
            place += 1
            for c in range(3):
                sums[c] = sums[c] + weight * pulls[c][ends][dh]
        for c in range(3):
            acc[c, g * SUB : (g + 1) * SUB, :] = sums[c]
    pulled = lane_sums(acc, 3)
    for c in range(3):
        mine = dpad[c, l + 1, pl.ds(h + 1, 1), :]
        force = STIFFNESS * (pulled[c] - totals[l, pl.ds(h, 1), :] * mine)
        if c == 0:
            one = loads[pl.ds((l + 1) * SUB + h + 1, 1), :]
            two = loads[pl.ds((2 * l + h // 2) * SUB + cols + 2 + h % 2, 1), :]
            force = force + LOADING * (one + two)
        fresh = vel1[c, l, pl.ds(h, 1), :] + force
        vel_out[c, l, pl.ds(h, 1), :] = fresh
        disp_out[c, l, pl.ds(h, 1), :] = mine + fresh


def wall_last(weights, got, base1, vel1, totals, wy_got, fx_got):
    rows, cols = base1.shape[1], base1.shape[2]
    field = pl.BlockSpec(base1.shape, lambda l, h: (0, 0, 0, 0))

    def flat(v):
        return pl.BlockSpec(v.shape, lambda l, h: (0,) * v.ndim)

    return pl.pallas_call(
        last_kernel,
        grid=(rows, cols),
        in_specs=[
            pl.BlockSpec((1, 1, STORED, SUB, LANES), lambda l, h: (l, h, 0, 0, 0)),
            flat(got), field, field, flat(totals),
            flat(wy_got[0]), flat(wy_got[1]), flat(fx_got[0]), flat(fx_got[1]),
        ],
        out_specs=[field, field],
        out_shape=[jax.ShapeDtypeStruct(base1.shape, F32)] * 2,
        scratch_shapes=[
            pltpu.VMEM((3, rows + 2, SUB, LANES), F32),
            pltpu.VMEM((4 * SUB, LANES), F32),
            pltpu.VMEM((3, LANES, LANES), F32),
        ],
        compiler_params=params(),
        name="wall_last",
    )(weights, got, base1, vel1, totals, *wy_got, *fx_got)


def per_device(
    displacement,
    velocity,
    jitter,
    bond_masks,
    pressure,
    pressure_prev,
    speed_sq,
    route_device,
    route_tile,
):
    fx_count, wy_count = lax.axis_size("fx"), lax.axis_size("wy")
    cols = displacement.shape[2]
    device = route_device.reshape(-1, LANES)
    tile = route_tile.reshape(-1, LANES)
    length = (device // wy_count) * 2 + tile // cols
    height = (device % wy_count) * cols + tile % cols
    target = length * (wy_count * cols) + height

    sends = pack_wy(pressure, pressure_prev, speed_sq, jitter, displacement)
    wy_got = exchange("wy", *sends)
    sends = pack_fx(pressure, pressure_prev, speed_sq, jitter, displacement, *wy_got)
    fx_got = exchange("fx", *sends)
    pressure_out, slots = grid_steps(
        pressure, pressure_prev, speed_sq, wy_got, fx_got, target, fx_count, wy_count
    )
    got = lax.all_to_all(slots, ("fx", "wy"), split_axis=0, concat_axis=0, tiled=True)
    weights, vel1, base1, totals, *sends = wall_first(
        pressure.shape[0], pressure.shape[1],
        bond_masks, jitter, displacement, velocity, wy_got, fx_got
    )
    base_wy = exchange("wy", *sends)
    sends = pack_base(base1, base_wy)
    base_fx = exchange("fx", *sends)
    disp_out, vel_out = wall_last(weights, got, base1, vel1, totals, base_wy, base_fx)
    return (disp_out, vel_out, pressure_out)


def solution(mesh):
    placed = (
        P(None, "fx", "wy", None),
        P(None, "fx", "wy", None),
        P(None, "fx", "wy", None),
        P("fx", "wy", None, None, None),
        P("fx", "wy", None),
        P("fx", "wy", None),
        P("fx", "wy", None),
        P(("fx", "wy"), None),
        P(("fx", "wy")),
    )
    return jax.shard_map(
        per_device,
        mesh=mesh,
        in_specs=placed,
        out_specs=(P(None, "fx", "wy", None), P(None, "fx", "wy", None), P("fx", "wy", None)),
        check_vma=False,
    )
```

time: 152 us -> 49 us (0.32)
  the two profiles are of different devices: /device:TPU:0 before, /device:TPU:12 now
where the time goes in v1:
time: 49 us; the launch traced here: 48.4 us
  starting transfers between devices  18.1 us (37%)
  waiting for transfers between devices  13.5 us (28%)
  Pallas kernels  11 us (22%)
  local copies, waits for them, and re-layouts  4.27 us (9%)
  between operations  0.79 us (2%)
  other arithmetic  0.71 us (1%)
    ppermute x4, waiting for transfers between devices, exchange(): got_odd = lax.ppermute(to_odd, axis, pair_list(count, 1))  13.5 us
    ppermute x4, starting transfers between devices, exchange(): got_odd = lax.ppermute(to_odd, axis, pair_list(count, 1))  9.71 us
    pallas_call x1, Pallas kernels, wall_first(): pl.pallas_call(functools.partial(wall_kernel, cx, cy), grid=(rows, cols),...  6.95 us
    all_to_all x1, starting transfers between devices, per_device(): lax.all_to_all(slots, ('fx', 'wy'), split_axis=0, concat_axis=0, tiled=True)  5.06 us
    unnamed x16, local copies, waits for them, and re-layouts  4.27 us
    ppermute x4, starting transfers between devices, exchange(): got_even = lax.ppermute(to_even, axis, pair_list(count, 0))  3.36 us
    pallas_call x1, Pallas kernels, wall_last(): pl.pallas_call(last_kernel, grid=(rows, cols), in_specs=[pl.BlockSpec((1,...  2.35 us
    pallas_call x1, Pallas kernels, grid_steps(): pl.pallas_call(grid_kernel, in_specs=[whole(0)] * 8, out_specs=[whole(0)]...  1.62 us
  transfers between devices with their start and end apart: 9, of which 4 were waited for; matrix products, arithmetic and copies ran while one was open for 1% of the time, Pallas kernels for 14%

profile of v1, /device:TPU:12, one launch (start us, length us, event | category | flops | bytes accessed | tf_op | source)
XLA Modules:
  0.0 48.4 jit_solution(12581126324172737040)
XLA Ops:
  0.6 0.0 copy-start
  0.6 0.9 %copy-done = f32[16,32,128]{2,1,0:T(8,128)S(1)} copy-done((f32[16,32,128]{2,1,0:T(8,128)S(1)}, f32[16,32,128]{2,1,0:T(8,128)}, u32[]{:S(2)}) %copy-start) | copy-done | bytes 262168
  1.6 0.9 %copy-done.1 = f32[16,32,128]{2,1,0:T(8,128)S(1)} copy-done((f32[16,32,128]{2,1,0:T(8,128)S(1)}, f32[16,32,128]{2,1,0:T(8,128)}, u32[]{:S(2)}) %copy-start.1) | copy-done | bytes 262168
  2.5 0.9 %copy-done.2 = f32[16,32,128]{2,1,0:T(8,128)S(1)} copy-done((f32[16,32,128]{2,1,0:T(8,128)S(1)}, f32[16,32,128]{2,1,0:T(8,128)}, u32[]{:S(2)}) %copy-start.2) | copy-done | bytes 262168
  3.5 0.7 %copy-done.3 = f32[3,2,4,128]{3,2,1,0:T(4,128)S(1)} copy-done((f32[3,2,4,128]{3,2,1,0:T(4,128)S(1)}, f32[3,2,4,128]{3,2,1,0:T(4,128)}, u32[]{:S(2)}) %copy-start.3) | copy-done | bytes 12312
  4.2 0.7 %copy-done.5 = f32[3,2,4,128]{3,2,1,0:T(4,128)S(1)} copy-done((f32[3,2,4,128]{3,2,1,0:T(4,128)S(1)}, f32[3,2,4,128]{3,2,1,0:T(4,128)}, u32[]{:S(2)}) %copy-start.5) | copy-done | bytes 12312
  4.9 0.1 pack_wy.1
  5.0 0.1 collective-permute-start
  5.1 2.5 %collective-permute-start.1 = (f32[80,128]{1,0:T(8,128)S(1)}, f32[80,128]{1,0:T(8,128)S(1)}, u32[]{:S(2)}, u32[]{:S(2)}) collective-permute-start(f32[80,128]{1,0:T(8,128)S(1)} %get-tuple-element.20), channel_id=1, source_target_pairs={{1,2},{2,1},{5,6},{6,5},{9,10},{10,9},{13,14},{14,13},{17,18},{18,... | collective-permute-start | bytes 122888 | tf_op jit(solution)/shard_map/ppermute | solution.py:43
  7.6 0.0 collective-permute-done.got_even.wye
  7.6 2.8 %collective-permute-done.1.got_odd.wyo = f32[80,128]{1,0:T(8,128)S(1)} collective-permute-done((f32[80,128]{1,0:T(8,128)S(1)}, f32[80,128]{1,0:T(8,128)S(1)}, u32[]{:S(2)}, u32[]{:S(2)}) %collective-permute-start.1) | collective-permute-done | bytes 40992 | tf_op jit(solution)/shard_map/ppermute | solution.py:43
  10.4 1.6 %collective-permute-start.2 = (f32[168,128]{1,0:T(8,128)S(1)}, f32[168,128]{1,0:T(8,128)S(1)}, u32[]{:S(2)}, u32[]{:S(2)}) collective-permute-start(f32[168,128]{1,0:T(8,128)S(1)} %get-tuple-element.21), channel_id=1, source_target_pairs={{0,4},{4,0},{8,12},{12,8},{16,20},{20,16},{24,28},{28,24},{1,5},{5... | collective-permute-start | bytes 258056 | tf_op jit(solution)/shard_map/ppermute | solution.py:42
  12.0 2.3 %collective-permute-start.3 = (f32[168,128]{1,0:T(8,128)S(1)}, f32[168,128]{1,0:T(8,128)S(1)}, u32[]{:S(2)}, u32[]{:S(2)}) collective-permute-start(f32[168,128]{1,0:T(8,128)S(1)} %get-tuple-element.22), channel_id=1, source_target_pairs={{4,8},{8,4},{12,16},{16,12},{20,24},{24,20},{5,9},{9,5},{13,17},{1... | collective-permute-start | bytes 258056 | tf_op jit(solution)/shard_map/ppermute | solution.py:43
  14.3 0.7 %fusion.3.target = s32[4,128]{1,0:T(4,128)S(1)} fusion(s32[4,128]{1,0:T(4,128)} %bitcast.17, s32[512]{0:T(512)} %param.17), kind=kLoop, calls=%fused_computation.13 | loop fusion | flops 22528 | bytes 6144 | tf_op jit(solution)/shard_map/add | solution.py:595
  15.0 0.0 collective-permute-done.2.fxe
  15.0 4.2 %collective-permute-done.3.fxo = f32[168,128]{1,0:T(8,128)S(1)} collective-permute-done((f32[168,128]{1,0:T(8,128)S(1)}, f32[168,128]{1,0:T(8,128)S(1)}, u32[]{:S(2)}, u32[]{:S(2)}) %collective-permute-start.3) | collective-permute-done | bytes 86048 | tf_op jit(solution)/shard_map/ppermute | solution.py:43
  19.2 1.6 %grid_steps.1 = (f32[16,32,128]{2,1,0:T(8,128)}, f32[32,32,128]{2,1,0:T(8,128)}) custom-call(f32[16,32,128]{2,1,0:T(8,128)S(1)} %copy-done, f32[16,32,128]{2,1,0:T(8,128)S(1)} %copy-done.1, f32[16,32,128]{2,1,0:T(8,128)S(1)} %copy-done.2, f32[80,128]{1,0:T(8,128)S(1)} %collective-permute-done.got_even.wye, f32[80,128]{1,0:T(8,128)S(1)} %collective-permute-done.1.got_odd.wyo, ...), custom_call_target="tpu_custom_call" | custom-call | tf_op jit(solution)/shard_map/grid_steps/pallas_call | solution.py:275
  20.9 5.1 %all-to-all-start = ((f32[32,32,128]{2,1,0:T(8,128)}), f32[32,32,128]{2,1,0:T(8,128)S(1)}, u32[]{:S(2)}, u32[]{:S(2)}) async-start(f32[32,32,128]{2,1,0:T(8,128)} %get-tuple-element.24), calls=%async_computation | async-start | bytes 1048576 | tf_op jit(solution)/shard_map/all_to_all | solution.py:604
  25.9 0.0 copy-done.4
  25.9 0.0 copy-done.6
  25.9 0.0 copy-done.7
  25.9 6.9 %wall_first.1 = (f32[2,4,80,8,128]{4,3,2,1,0:T(8,128)S(1)}, f32[3,2,4,128]{3,2,1,0:T(4,128)S(1)}, f32[3,2,4,128]{3,2,1,0:T(4,128)S(1)}, f32[2,4,128]{2,1,0:T(4,1...) custom-call(s32[2,4,9,128,128]{4,3,2,1,0:T(8,128)} %masks.1, f32[3,2,4,128]{3,2,1,0:T(4,128)S(1)} %copy-done.4, ...), custom_call_target="tpu_custom_call" | custom-call | tf_op jit(solution)/shard_map/wall_first/pallas_call | solution.py:442
  32.9 0.2 collective-permute-start.4
  33.1 2.4 %collective-permute-start.5 = (f32[8,128]{1,0:T(8,128)S(1)}, f32[8,128]{1,0:T(8,128)S(1)}, u32[]{:S(2)}, u32[]{:S(2)}) collective-permute-start(f32[8,128]{1,0:T(8,128)S(1)} %get-tuple-element.29), channel_id=1, source_target_pairs={{1,2},{2,1},{5,6},{6,5},{9,10},{10,9},{13,14},{14,13},{17,18},{18,... | collective-permute-start | bytes 12296 | tf_op jit(solution)/shard_map/ppermute | solution.py:43
  35.6 0.0 collective-permute-done.4.got_even.wye
  35.6 2.5 %collective-permute-done.5.got_odd.wyo = f32[8,128]{1,0:T(8,128)S(1)} collective-permute-done((f32[8,128]{1,0:T(8,128)S(1)}, f32[8,128]{1,0:T(8,128)S(1)}, u32[]{:S(2)}, u32[]{:S(2)}) %collective-permute-start.5) | collective-permute-done | bytes 4128 | tf_op jit(solution)/shard_map/ppermute | solution.py:43
  38.0 1.5 %collective-permute-start.6 = (f32[24,128]{1,0:T(8,128)S(1)}, f32[24,128]{1,0:T(8,128)S(1)}, u32[]{:S(2)}, u32[]{:S(2)}) collective-permute-start(f32[24,128]{1,0:T(8,128)S(1)} %get-tuple-element.30), channel_id=1, source_target_pairs={{0,4},{4,0},{8,12},{12,8},{16,20},{20,16},{24,28},{28,24},{1,5},{5... | collective-permute-start | bytes 36872 | tf_op jit(solution)/shard_map/ppermute | solution.py:42
  39.6 2.5 %collective-permute-start.7 = (f32[24,128]{1,0:T(8,128)S(1)}, f32[24,128]{1,0:T(8,128)S(1)}, u32[]{:S(2)}, u32[]{:S(2)}) collective-permute-start(f32[24,128]{1,0:T(8,128)S(1)} %get-tuple-element.31), channel_id=1, source_target_pairs={{4,8},{8,4},{12,16},{16,12},{20,24},{24,20},{5,9},{9,5},{13,17},{1... | collective-permute-start | bytes 36872 | tf_op jit(solution)/shard_map/ppermute | solution.py:43
  42.0 0.0 collective-permute-done.6.fxe
  42.1 4.0 %collective-permute-done.7.fxo = f32[24,128]{1,0:T(8,128)S(1)} collective-permute-done((f32[24,128]{1,0:T(8,128)S(1)}, f32[24,128]{1,0:T(8,128)S(1)}, u32[]{:S(2)}, u32[]{:S(2)}) %collective-permute-start.7) | collective-permute-done | bytes 12320 | tf_op jit(solution)/shard_map/ppermute | solution.py:43
  46.0 0.0 all-to-all-done.got
  46.1 2.4 %wall_last.1 = (f32[3,2,4,128]{3,2,1,0:T(4,128)}, f32[3,2,4,128]{3,2,1,0:T(4,128)}) custom-call(f32[2,4,80,8,128]{4,3,2,1,0:T(8,128)S(1)} %get-tuple-element.23.weights, f32[32,32,128]{2,1,0:T(8,128)S(1)} %all-to-all-done.got, f32[3,2,4,128]{3,2,1,0:T(4,128)S(1)} %get-tuple-element.25.base1, f32[3,2,4,128]{3,2,1,0:T(4,128)S(1)} %get-tuple-element.26.vel1, ...), custom_call_target="tpu_custom_call" | custom-call | tf_op jit(solution)/shard_map/wall_last/pallas_call | solution.py:558
  (9 shorter events, 0.0 us)
Async XLA Ops:
  0.6 1.0 %copy-start = (f32[16,32,128]{2,1,0:T(8,128)S(1)}, f32[16,32,128]{2,1,0:T(8,128)}, u32[]{:S(2)}) copy-start(f32[16,32,128]{2,1,0:T(8,128)} %p.1) | copy-start | bytes 786436
  1.6 0.9 %copy-start.1 = (f32[16,32,128]{2,1,0:T(8,128)S(1)}, f32[16,32,128]{2,1,0:T(8,128)}, u32[]{:S(2)}) copy-start(f32[16,32,128]{2,1,0:T(8,128)} %q.1) | copy-start | bytes 786436
  2.5 0.9 %copy-start.2 = (f32[16,32,128]{2,1,0:T(8,128)S(1)}, f32[16,32,128]{2,1,0:T(8,128)}, u32[]{:S(2)}) copy-start(f32[16,32,128]{2,1,0:T(8,128)} %s.1) | copy-start | bytes 786436
  3.5 0.7 %copy-start.3 = (f32[3,2,4,128]{3,2,1,0:T(4,128)S(1)}, f32[3,2,4,128]{3,2,1,0:T(4,128)}, u32[]{:S(2)}) copy-start(f32[3,2,4,128]{3,2,1,0:T(4,128)} %jit.5) | copy-start | bytes 36868
  4.2 0.7 %copy-start.5 = (f32[3,2,4,128]{3,2,1,0:T(4,128)S(1)}, f32[3,2,4,128]{3,2,1,0:T(4,128)}, u32[]{:S(2)}) copy-start(f32[3,2,4,128]{3,2,1,0:T(4,128)} %disp.5) | copy-start | bytes 36868
  4.9 21.0 %copy-start.4 = (f32[3,2,4,128]{3,2,1,0:T(4,128)S(1)}, f32[3,2,4,128]{3,2,1,0:T(4,128)}, u32[]{:S(2)}) copy-start(f32[3,2,4,128]{3,2,1,0:T(4,128)} %jit.5) | copy-start | bytes 36868
  4.9 21.0 %copy-start.6 = (f32[3,2,4,128]{3,2,1,0:T(4,128)S(1)}, f32[3,2,4,128]{3,2,1,0:T(4,128)}, u32[]{:S(2)}) copy-start(f32[3,2,4,128]{3,2,1,0:T(4,128)} %disp.5) | copy-start | bytes 36868
  4.9 21.0 %copy-start.7 = (f32[3,2,4,128]{3,2,1,0:T(4,128)S(1)}, f32[3,2,4,128]{3,2,1,0:T(4,128)}, u32[]{:S(2)}) copy-start(f32[3,2,4,128]{3,2,1,0:T(4,128)} %vel.1) | copy-start | bytes 36868
  5.0 2.6 %collective-permute-start = (f32[80,128]{1,0:T(8,128)S(1)}, f32[80,128]{1,0:T(8,128)S(1)}, u32[]{:S(2)}, u32[]{:S(2)}) collective-permute-start(f32[80,128]{1,0:T(8,128)S(1)} %get-tuple-element.19), channel_id=1, source_target_pairs={{0,1},{1,0},{2,3},{3,2},{4,5},{5,4},{6,7},{7,6},{8,9},{9,8},{10,11... | collective-permute-start | bytes 122888 | tf_op jit(solution)/shard_map/ppermute | solution.py:42
  5.1 5.3 %collective-permute-start.1 = (f32[80,128]{1,0:T(8,128)S(1)}, f32[80,128]{1,0:T(8,128)S(1)}, u32[]{:S(2)}, u32[]{:S(2)}) collective-permute-start(f32[80,128]{1,0:T(8,128)S(1)} %get-tuple-element.20), channel_id=1, source_target_pairs={{1,2},{2,1},{5,6},{6,5},{9,10},{10,9},{13,14},{14,13},{17,18},{18,... | collective-permute-start | bytes 122888 | tf_op jit(solution)/shard_map/ppermute | solution.py:43
  10.4 4.6 %collective-permute-start.2 = (f32[168,128]{1,0:T(8,128)S(1)}, f32[168,128]{1,0:T(8,128)S(1)}, u32[]{:S(2)}, u32[]{:S(2)}) collective-permute-start(f32[168,128]{1,0:T(8,128)S(1)} %get-tuple-element.21), channel_id=1, source_target_pairs={{0,4},{4,0},{8,12},{12,8},{16,20},{20,16},{24,28},{28,24},{1,5},{5... | collective-permute-start | bytes 258056 | tf_op jit(solution)/shard_map/ppermute | solution.py:42
  12.0 7.3 %collective-permute-start.3 = (f32[168,128]{1,0:T(8,128)S(1)}, f32[168,128]{1,0:T(8,128)S(1)}, u32[]{:S(2)}, u32[]{:S(2)}) collective-permute-start(f32[168,128]{1,0:T(8,128)S(1)} %get-tuple-element.22), channel_id=1, source_target_pairs={{4,8},{8,4},{12,16},{16,12},{20,24},{24,20},{5,9},{9,5},{13,17},{1... | collective-permute-start | bytes 258056 | tf_op jit(solution)/shard_map/ppermute | solution.py:43
  20.9 25.2 %all-to-all-start = ((f32[32,32,128]{2,1,0:T(8,128)}), f32[32,32,128]{2,1,0:T(8,128)S(1)}, u32[]{:S(2)}, u32[]{:S(2)}) async-start(f32[32,32,128]{2,1,0:T(8,128)} %get-tuple-element.24), calls=%async_computation | async-start | bytes 1048576 | tf_op jit(solution)/shard_map/all_to_all | solution.py:604
  32.9 2.6 %collective-permute-start.4 = (f32[8,128]{1,0:T(8,128)S(1)}, f32[8,128]{1,0:T(8,128)S(1)}, u32[]{:S(2)}, u32[]{:S(2)}) collective-permute-start(f32[8,128]{1,0:T(8,128)S(1)} %get-tuple-element.28), channel_id=1, source_target_pairs={{0,1},{1,0},{2,3},{3,2},{4,5},{5,4},{6,7},{7,6},{8,9},{9,8},{10,11... | collective-permute-start | bytes 12296 | tf_op jit(solution)/shard_map/ppermute | solution.py:42
  33.1 4.9 %collective-permute-start.5 = (f32[8,128]{1,0:T(8,128)S(1)}, f32[8,128]{1,0:T(8,128)S(1)}, u32[]{:S(2)}, u32[]{:S(2)}) collective-permute-start(f32[8,128]{1,0:T(8,128)S(1)} %get-tuple-element.29), channel_id=1, source_target_pairs={{1,2},{2,1},{5,6},{6,5},{9,10},{10,9},{13,14},{14,13},{17,18},{18,... | collective-permute-start | bytes 12296 | tf_op jit(solution)/shard_map/ppermute | solution.py:43
  38.0 4.0 %collective-permute-start.6 = (f32[24,128]{1,0:T(8,128)S(1)}, f32[24,128]{1,0:T(8,128)S(1)}, u32[]{:S(2)}, u32[]{:S(2)}) collective-permute-start(f32[24,128]{1,0:T(8,128)S(1)} %get-tuple-element.30), channel_id=1, source_target_pairs={{0,4},{4,0},{8,12},{12,8},{16,20},{20,16},{24,28},{28,24},{1,5},{5... | collective-permute-start | bytes 36872 | tf_op jit(solution)/shard_map/ppermute | solution.py:42
  39.6 6.5 %collective-permute-start.7 = (f32[24,128]{1,0:T(8,128)S(1)}, f32[24,128]{1,0:T(8,128)S(1)}, u32[]{:S(2)}, u32[]{:S(2)}) collective-permute-start(f32[24,128]{1,0:T(8,128)S(1)} %get-tuple-element.31), channel_id=1, source_target_pairs={{4,8},{8,4},{12,16},{16,12},{20,24},{24,20},{5,9},{9,5},{13,17},{1... | collective-permute-start | bytes 36872 | tf_op jit(solution)/shard_map/ppermute | solution.py:43

commit v2 on v1

--- a/solution.py
+++ b/solution.py
@@ -18,11 +18,11 @@
 BF16 = jnp.bfloat16
 
 
-def whole(ndim):
+def whole():
     return pl.BlockSpec(memory_space=pltpu.VMEM)
 
 
-def params(*semantics):
+def params():
     return pltpu.CompilerParams(vmem_limit_bytes=VMEM_BYTES)
 
 
@@ -39,8 +39,8 @@
 
 def exchange(axis, to_even, to_odd):
     count = lax.axis_size(axis)
+    got_odd = lax.ppermute(to_odd, axis, pair_list(count, 1))
     got_even = lax.ppermute(to_even, axis, pair_list(count, 0))
-    got_odd = lax.ppermute(to_odd, axis, pair_list(count, 1))
     return got_even, got_odd
 
 
@@ -61,9 +61,23 @@
     return jnp.where(even, b, a), jnp.where(even, a, b)
 
 
-def pack_wy_kernel(p_lo, p_hi, q_lo, q_hi, s_lo, s_hi, jit, disp, to_even, to_odd):
-    cx = p_lo.shape[0]
-    rows, cols = jit.shape[1], jit.shape[2]
+def pack_wy_kernel(p, q, s, jit_in, disp_in, to_even, to_odd, edges, walls, sems):
+    cx, cy = p.shape[0], p.shape[1]
+    rows, cols = jit_in.shape[1], jit_in.shape[2]
+    copies = []
+    for k, field in enumerate((p, q, s)):
+        for side, first in enumerate((0, cy - SUB)):
+            source = field.at[:, first : first + SUB, :]
+            copies.append((source, edges.at[2 * k + side], sems.at[2 * k + side]))
+    copies.append((jit_in, walls.at[0], sems.at[6]))
+    copies.append((disp_in, walls.at[1], sems.at[7]))
+    copies = [pltpu.make_async_copy(*copy) for copy in copies]
+    for copy in copies:
+        copy.start()
+    for copy in copies:
+        copy.wait()
+    p_lo, p_hi, q_lo, q_hi, s_lo, s_hi = [edges.at[k] for k in range(6)]
+    jit, disp = walls.at[0], walls.at[1]
 
     def edge(p, q, s, near, far, h):
         def write(out):
@@ -96,23 +110,23 @@
 
 
 def pack_wy(p, q, s, jit, disp):
-    cx, cy = p.shape[0], p.shape[1]
+    cx = p.shape[0]
     rows = jit.shape[1]
     size = pad8(4 * cx + 6 * rows)
-    first = pl.BlockSpec((cx, SUB, LANES), lambda i: (0, 0, 0))
-    last = pl.BlockSpec((cx, SUB, LANES), lambda i: (0, cy // SUB - 1, 0))
-    small = pl.BlockSpec(jit.shape, lambda i: (0, 0, 0, 0))
     out = jax.ShapeDtypeStruct((size, LANES), F32)
-    spec = pl.BlockSpec((size, LANES), lambda i: (0, 0))
     return pl.pallas_call(
         pack_wy_kernel,
-        grid=(1,),
-        in_specs=[first, last, first, last, first, last, small, small],
-        out_specs=[spec, spec],
+        in_specs=[pl.BlockSpec(memory_space=pltpu.HBM)] * 5,
+        out_specs=[whole()] * 2,
         out_shape=[out, out],
+        scratch_shapes=[
+            pltpu.VMEM((6, cx, SUB, LANES), F32),
+            pltpu.VMEM((2,) + jit.shape, F32),
+            pltpu.SemaphoreType.DMA((8,)),
+        ],
         compiler_params=params(),
         name="pack_wy",
-    )(p, p, q, q, s, s, jit, disp)
+    )(p, q, s, jit, disp)
 
 
 def pack_fx_kernel(
@@ -274,8 +288,8 @@
     devices = fx_count * wy_count
     return pl.pallas_call(
         grid_kernel,
-        in_specs=[whole(0)] * 8,
-        out_specs=[whole(0)] * 2,
+        in_specs=[whole()] * 8,
+        out_specs=[whole()] * 2,
         out_shape=[
             jax.ShapeDtypeStruct(p.shape, F32),
             jax.ShapeDtypeStruct((devices, 4 * SUB, LANES), F32),
@@ -308,10 +322,10 @@
 def tile_rows(ref, c, l, h, first_sub):
     mid, ends = {}, {}
     for dh in (-1, 0, 1):
-        at = h + 1 + dh
-        mid[dh] = jnp.broadcast_to(ref[c, l + 1, pl.ds(at, 1), :], (SUB, LANES))
-        before = jnp.broadcast_to(ref[c, l, pl.ds(at, 1), :], (SUB, LANES))
-        after = jnp.broadcast_to(ref[c, l + 2, pl.ds(at, 1), :], (SUB, LANES))
+        at = pl.ds(h + 1 + dh, 1)
+        mid[dh] = jnp.broadcast_to(ref[c, l + 1, at, :], (SUB, LANES))
+        before = jnp.broadcast_to(ref[c, l, at, :], (SUB, LANES))
+        after = jnp.broadcast_to(ref[c, l + 2, at, :], (SUB, LANES))
         ends[dh] = jnp.where(first_sub, before, after)
     return mid, ends
 
@@ -329,17 +343,23 @@
         pad[c, rows + 1, 0 : cols + 2, :] = after_x[row : row + cols + 2]
 
 
-def lane_sums(acc, count):
+def lane_sums(acc, l, cols, count):
     ones = jnp.ones((2 * SUB, LANES), BF16)
-    result = []
-    for c in range(count):
-        high, low = two_terms(acc[c])
-        both = jnp.concatenate([high, low], axis=0)
+    result = [[] for _ in range(count)]
+    for h in range(cols):
+        terms = []
+        for c in range(count):
+            terms.extend(two_terms(acc[l, h, c]))
         sums = lax.dot_general(
-            ones, both, (((1,), (1,)), ((), ())), preferred_element_type=F32
-        )
-        result.append(sums[0:1, 0:LANES] + sums[0:1, LANES : 2 * LANES])
-    return result
+            ones,
+            jnp.concatenate(terms, axis=0),
+            (((1,), (1,)), ((), ())),
+            preferred_element_type=F32,
+        )[0:1]
+        for c in range(count):
+            at = 2 * c * LANES
+            result[c].append(sums[:, at : at + LANES] + sums[:, at + LANES : at + 2 * LANES])
+    return [jnp.concatenate(parts, axis=0) for parts in result]
 
 
 def wall_kernel(
@@ -347,111 +367,101 @@
     jpad, dpad, acc,
 ):
     rows, cols = jit.shape[1], jit.shape[2]
-    l, h = pl.program_id(0), pl.program_id(1)
     first_sub = lax.broadcasted_iota(jnp.int32, (SUB, LANES), 0) < SUB // 2
-
-    @pl.when((l == 0) & (h == 0))
-    def _():
-        before_y, after_y = before_after(even_at("wy"), wye, wyo)
-        before_x, after_x = before_after(even_at("fx"), fxe, fxo)
-        fill_padded(jpad, jit, before_y, after_y, before_x, after_x, 4 * cx, 4 * cy)
-        fill_padded(
-            dpad, disp, before_y, after_y, before_x, after_x,
-            4 * cx + 3 * rows, 4 * cy + 3 * (cols + 2),
-        )
-
+    before_y, after_y = before_after(even_at("wy"), wye, wyo)
+    before_x, after_x = before_after(even_at("fx"), fxe, fxo)
+    fill_padded(jpad, jit, before_y, after_y, before_x, after_x, 4 * cx, 4 * cy)
+    fill_padded(
+        dpad, disp, before_y, after_y, before_x, after_x,
+        4 * cx + 3 * rows, 4 * cy + 3 * (cols + 2),
+    )
     index = lax.broadcasted_iota(jnp.int32, (1, LANES), 1)
     lattice = (index % 8, index // 8 % 4, index // 32)
     lattice = [v.astype(F32) * (1.0 / REACH) for v in lattice]
     span = 8.0 / REACH
     rise = 4.0 / REACH
-    others, own = [], []
-    for c in range(3):
-        mid, ends = tile_rows(jpad, c, l, h, first_sub)
-        for dh in (-1, 0, 1):
-            mid[dh] = mid[dh] * (1.0 / REACH) + lattice[c]
-            ends[dh] = ends[dh] * (1.0 / REACH) + lattice[c]
-            if c == 0:
-                ends[dh] = ends[dh] + jnp.where(first_sub, -span, span)
-            if c == 1:
-                mid[dh] = mid[dh] + rise * dh
-                ends[dh] = ends[dh] + rise * dh
-        own.append(mid[0])
-        others.append((mid, ends))
-    pulls = [tile_rows(dpad, c, l, h, first_sub) for c in range(3)]
-    columns = jnp.transpose(
-        jnp.concatenate([own[0], own[1], own[2]], axis=0)
-    )
-
-    place = 0
-    for g in range(LANES // SUB):
-        mine = [
-            jnp.broadcast_to(columns[g * SUB : (g + 1) * SUB, c * SUB : c * SUB + 1], (SUB, LANES))
-            for c in range(3)
-        ]
-        sums = [jnp.zeros((SUB, LANES), F32) for _ in range(4)]
-        span_g = slice(g * SUB, (g + 1) * SUB)
-        for ends, dh in reached(g):
-            if ends:
-                mask = jnp.where(first_sub, masks[0, 0, 1 + dh, span_g, :], masks[0, 0, 7 + dh, span_g, :])
-            else:
-                mask = masks[0, 0, 4 + dh, span_g, :]
-            weight = mask.astype(F32)
+
+    def one_tile(l, h):
+        others, own = [], []
+        for c in range(3):
+            mid, ends = tile_rows(jpad, c, l, h, first_sub)
+            for dh in (-1, 0, 1):
+                mid[dh] = mid[dh] * (1.0 / REACH) + lattice[c]
+                ends[dh] = ends[dh] * (1.0 / REACH) + lattice[c]
+                if c == 0:
+                    ends[dh] = ends[dh] + jnp.where(first_sub, -span, span)
+                if c == 1:
+                    mid[dh] = mid[dh] + rise * dh
+                    ends[dh] = ends[dh] + rise * dh
+            own.append(mid[0])
+            others.append((mid, ends))
+        pulls = [tile_rows(dpad, c, l, h, first_sub) for c in range(3)]
+        sub = lax.broadcasted_iota(jnp.int32, (SUB, LANES), 0)
+        columns = jnp.transpose(
+            jnp.where(sub == 0, own[0], jnp.where(sub == 1, own[1], own[2]))
+        )
+        place = 0
+        for g in range(LANES // SUB):
+            span_g = slice(g * SUB, (g + 1) * SUB)
+            mine = [
+                jnp.broadcast_to(columns[span_g, c : c + 1], (SUB, LANES)) for c in range(3)
+            ]
+            sums = [None] * 4
+            for ends, dh in reached(g):
+                if ends:
+                    mask = jnp.where(
+                        first_sub,
+                        masks[l, h, 1 + dh, span_g, :],
+                        masks[l, h, 7 + dh, span_g, :],
+                    )
+                else:
+                    mask = masks[l, h, 4 + dh, span_g, :]
+                weight = mask.astype(F32)
+                for c in range(3):
+                    diff = others[c][ends][dh] - mine[c]
+                    weight = weight - diff * diff
+                weight = jnp.maximum(weight, 0.0)
+                weights[l, h, place] = weight
+                place += 1
+                terms = [weight * pulls[c][ends][dh] for c in range(3)] + [weight]
+                sums = [t if v is None else v + t for v, t in zip(sums, terms)]
+            for c in range(4):
+                acc[l, h, c, span_g, :] = sums[c]
+
+    @pl.loop(0, cols)
+    def _(h):
+        for l in range(rows):
+            one_tile(l, h)
+
+    for l in range(rows):
+        pulled = lane_sums(acc, l, cols, 4)
+        totals[l] = pulled[3]
+        for c in range(3):
+            mine = disp[c, l]
+            fresh = vel[c, l] + STIFFNESS * (pulled[c] - pulled[3] * mine)
+            vel1[c, l] = fresh
+            base1[c, l] = mine + fresh
+
+    def edge(at):
+        def write(out):
             for c in range(3):
-                diff = others[c][ends][dh] - mine[c]
-                weight = weight - diff * diff
-            weight = jnp.maximum(weight, 0.0)
-            weights[0, 0, place] = weight
-            place += 1
-            for c in range(3):
-                sums[c] = sums[c] + weight * pulls[c][ends][dh]
-            sums[3] = sums[3] + weight
-        for c in range(4):
-            acc[c, span_g, :] = sums[c]
-    pulled = lane_sums(acc, 4)
-    totals[l, pl.ds(h, 1), :] = pulled[3]
-    for c in range(3):
-        mine = dpad[c, l + 1, pl.ds(h + 1, 1), :]
-        force = STIFFNESS * (pulled[c] - pulled[3] * mine)
-        fresh = vel[c, l, pl.ds(h, 1), :] + force
-        vel1[c, l, pl.ds(h, 1), :] = fresh
-        base1[c, l, pl.ds(h, 1), :] = mine + fresh
-
-    @pl.when((l == rows - 1) & (h == cols - 1))
-    def _():
-        def edge(at):
-            def write(out):
-                for c in range(3):
-                    for k in range(rows):
-                        out[c * rows + k : c * rows + k + 1, :] = base1[c, k, at : at + 1, :]
-                for spare in range(3 * rows, out.shape[0]):
-                    out[spare : spare + 1, :] = jnp.zeros((1, LANES), F32)
-
-            return write
-
-        place_edges(even_at("wy"), edge(0), edge(cols - 1), to_even, to_odd)
+                for k in range(rows):
+                    out[c * rows + k : c * rows + k + 1, :] = base1[c, k, at : at + 1, :]
+            for spare in range(3 * rows, out.shape[0]):
+                out[spare : spare + 1, :] = jnp.zeros((1, LANES), F32)
+
+        return write
+
+    place_edges(even_at("wy"), edge(0), edge(cols - 1), to_even, to_odd)
 
 
 def wall_first(cx, cy, masks, jit, disp, vel, wy_got, fx_got):
     rows, cols = jit.shape[1], jit.shape[2]
-    field = pl.BlockSpec(jit.shape, lambda l, h: (0, 0, 0, 0))
-    wy_spec = pl.BlockSpec(wy_got[0].shape, lambda l, h: (0, 0))
-    fx_spec = pl.BlockSpec(fx_got[0].shape, lambda l, h: (0, 0))
     edge = (pad8(3 * rows), LANES)
-    edge_spec = pl.BlockSpec(edge, lambda l, h: (0, 0))
     return pl.pallas_call(
         functools.partial(wall_kernel, cx, cy),
-        grid=(rows, cols),
-        in_specs=[
-            pl.BlockSpec((1, 1, 9, LANES, LANES), lambda l, h: (l, h, 0, 0, 0)),
-            field, field, field, wy_spec, wy_spec, fx_spec, fx_spec,
-        ],
-        out_specs=[
-            pl.BlockSpec((1, 1, STORED, SUB, LANES), lambda l, h: (l, h, 0, 0, 0)),
-            field, field,
-            pl.BlockSpec((rows, cols, LANES), lambda l, h: (0, 0, 0)),
-            edge_spec, edge_spec,
-        ],
+        in_specs=[whole()] * 8,
+        out_specs=[whole()] * 6,
         out_shape=[
             jax.ShapeDtypeStruct((rows, cols, STORED, SUB, LANES), F32),
             jax.ShapeDtypeStruct(jit.shape, F32),
@@ -463,7 +473,7 @@
         scratch_shapes=[
             pltpu.VMEM((3, rows + 2, SUB, LANES), F32),
             pltpu.VMEM((3, rows + 2, SUB, LANES), F32),
-            pltpu.VMEM((4, LANES, LANES), F32),
+            pltpu.VMEM((rows, cols, 4, LANES, LANES), F32),
         ],
         compiler_params=params(),
         name="wall_first",
@@ -496,8 +506,8 @@
     out = jax.ShapeDtypeStruct((pad8(3 * (cols + 2)), LANES), F32)
     return pl.pallas_call(
         pack_base_kernel,
-        in_specs=[whole(0)] * 3,
-        out_specs=[whole(0)] * 2,
+        in_specs=[whole()] * 3,
+        out_specs=[whole()] * 2,
         out_shape=[out, out],
         compiler_params=params(),
         name="pack_base",
@@ -508,67 +518,68 @@
     weights, got, base1, vel1, totals, wye, wyo, fxe, fxo, disp_out, vel_out, dpad, loads, acc
 ):
     rows, cols = base1.shape[1], base1.shape[2]
-    l, h = pl.program_id(0), pl.program_id(1)
     first_sub = lax.broadcasted_iota(jnp.int32, (SUB, LANES), 0) < SUB // 2
-
-    @pl.when((l == 0) & (h == 0))
-    def _():
-        before_y, after_y = before_after(even_at("wy"), wye, wyo)
-        before_x, after_x = before_after(even_at("fx"), fxe, fxo)
-        fill_padded(dpad, base1, before_y, after_y, before_x, after_x, 0, 0)
-        total = got[0]
-        for d in range(1, got.shape[0]):
-            total = total + got[d]
-        loads[...] = total
-        for k in range(rows + 2):
-            here = total[k * SUB : k * SUB + cols + 2, :]
-            dpad[0, k, 0 : cols + 2, :] = dpad[0, k, 0 : cols + 2, :] + LOADING * here
-
-    pulls = [tile_rows(dpad, c, l, h, first_sub) for c in range(3)]
-    place = 0
-    for g in range(LANES // SUB):
-        sums = [jnp.zeros((SUB, LANES), F32) for _ in range(3)]
-        for ends, dh in reached(g):
-            weight = weights[0, 0, place]
-            place += 1
+    before_y, after_y = before_after(even_at("wy"), wye, wyo)
+    before_x, after_x = before_after(even_at("fx"), fxe, fxo)
+    fill_padded(dpad, base1, before_y, after_y, before_x, after_x, 0, 0)
+    total = got[0]
+    for d in range(1, got.shape[0]):
+        total = total + got[d]
+    loads[...] = total
+    for k in range(rows + 2):
+        here = total[k * SUB : k * SUB + cols + 2, :]
+        dpad[0, k, 0 : cols + 2, :] = dpad[0, k, 0 : cols + 2, :] + LOADING * here
+
+    def one_tile(l, h):
+        pulls = [tile_rows(dpad, c, l, h, first_sub) for c in range(3)]
+        place = 0
+        for g in range(LANES // SUB):
+            sums = [None] * 3
+            for ends, dh in reached(g):
+                weight = weights[l, h, place]
+                place += 1
+                terms = [weight * pulls[c][ends][dh] for c in range(3)]
+                sums = [t if v is None else v + t for v, t in zip(sums, terms)]
             for c in range(3):
-                sums[c] = sums[c] + weight * pulls[c][ends][dh]
+                acc[l, h, c, g * SUB : (g + 1) * SUB, :] = sums[c]
+
+    @pl.loop(0, cols)
+    def _(h):
+        for l in range(rows):
+            one_tile(l, h)
+
+    for l in range(rows):
+        pulled = lane_sums(acc, l, cols, 3)
         for c in range(3):
-            acc[c, g * SUB : (g + 1) * SUB, :] = sums[c]
-    pulled = lane_sums(acc, 3)
-    for c in range(3):
-        mine = dpad[c, l + 1, pl.ds(h + 1, 1), :]
-        force = STIFFNESS * (pulled[c] - totals[l, pl.ds(h, 1), :] * mine)
-        if c == 0:
-            one = loads[pl.ds((l + 1) * SUB + h + 1, 1), :]
-            two = loads[pl.ds((2 * l + h // 2) * SUB + cols + 2 + h % 2, 1), :]
-            force = force + LOADING * (one + two)
-        fresh = vel1[c, l, pl.ds(h, 1), :] + force
-        vel_out[c, l, pl.ds(h, 1), :] = fresh
-        disp_out[c, l, pl.ds(h, 1), :] = mine + fresh
+            mine = dpad[c, l + 1, 1 : cols + 1, :]
+            force = STIFFNESS * (pulled[c] - totals[l] * mine)
+            if c == 0:
+                at = (l + 1) * SUB + 1
+                force = force + LOADING * loads[at : at + cols, :]
+                for half in range(2):
+                    at = (2 * l + half) * SUB + cols + 2
+                    two = loads[at : at + 2, :]
+                    span = slice(2 * half, 2 * half + 2)
+                    fresh = vel1[c, l, span, :] + force[span] + LOADING * two
+                    vel_out[c, l, span, :] = fresh
+                    disp_out[c, l, span, :] = mine[span] + fresh
+            else:
+                fresh = vel1[c, l] + force
+                vel_out[c, l] = fresh
+                disp_out[c, l] = mine + fresh
 
 
 def wall_last(weights, got, base1, vel1, totals, wy_got, fx_got):
     rows, cols = base1.shape[1], base1.shape[2]
-    field = pl.BlockSpec(base1.shape, lambda l, h: (0, 0, 0, 0))
-
-    def flat(v):
-        return pl.BlockSpec(v.shape, lambda l, h: (0,) * v.ndim)
-
     return pl.pallas_call(
         last_kernel,
-        grid=(rows, cols),
-        in_specs=[
-            pl.BlockSpec((1, 1, STORED, SUB, LANES), lambda l, h: (l, h, 0, 0, 0)),
-            flat(got), field, field, flat(totals),
-            flat(wy_got[0]), flat(wy_got[1]), flat(fx_got[0]), flat(fx_got[1]),
-        ],
-        out_specs=[field, field],
+        in_specs=[whole()] * 9,
+        out_specs=[whole()] * 2,
         out_shape=[jax.ShapeDtypeStruct(base1.shape, F32)] * 2,
         scratch_shapes=[
             pltpu.VMEM((3, rows + 2, SUB, LANES), F32),
             pltpu.VMEM((4 * SUB, LANES), F32),
-            pltpu.VMEM((3, LANES, LANES), F32),
+            pltpu.VMEM((rows, cols, 3, LANES, LANES), F32),
         ],
         compiler_params=params(),
         name="wall_last",

time: 49 us -> 49.1 us (level)
  Pallas kernels: 11 us -> 8.85 us
  local copies, waits for them, and re-layouts: 4.27 us -> 6.37 us
    pallas_call x5, Pallas kernels: 11 us -> 8.82 us  [the longest x1 5.3 us: wall_first(): pl.pallas_call(functools.partial(wall_kernel, cx, cy), in_specs=[whole()]...]
    unnamed x16, local copies, waits for them, and re-layouts: 4.27 us -> 6.37 us
  transfers between devices with their start and end apart: 9 -> 9, of which waited for: 4 -> 4; matrix products, arithmetic and copies ran while one was open for 1% -> 1% of each run, Pallas kernels for 14% -> 11%
where the time goes in v2:
time: 49.1 us; the launch traced here: 48.4 us
  starting transfers between devices  18.1 us (37%)
  waiting for transfers between devices  13.6 us (28%)
  Pallas kernels  8.85 us (18%)
  local copies, waits for them, and re-layouts  6.37 us (13%)
  between operations  0.77 us (2%)
  other arithmetic  0.71 us (1%)
    ppermute x4, waiting for transfers between devices, exchange(): got_odd = lax.ppermute(to_odd, axis, pair_list(count, 1))  13.6 us
    ppermute x4, starting transfers between devices, exchange(): got_odd = lax.ppermute(to_odd, axis, pair_list(count, 1))  9.67 us
    unnamed x16, local copies, waits for them, and re-layouts  6.37 us
    pallas_call x1, Pallas kernels, wall_first(): pl.pallas_call(functools.partial(wall_kernel, cx, cy), in_specs=[whole()]...  5.3 us
    all_to_all x1, starting transfers between devices, per_device(): lax.all_to_all(slots, ('fx', 'wy'), split_axis=0, concat_axis=0, tiled=True)  5.06 us
    ppermute x4, starting transfers between devices, exchange(): got_even = lax.ppermute(to_even, axis, pair_list(count, 0))  3.35 us
    pallas_call x1, Pallas kernels, wall_last(): pl.pallas_call(last_kernel, in_specs=[whole()] * 9, out_specs=[whole()] *...  1.67 us
    pallas_call x1, Pallas kernels, grid_steps(): pl.pallas_call(grid_kernel, in_specs=[whole()] * 8, out_specs=[whole()] *...  1.61 us
  transfers between devices with their start and end apart: 9, of which 4 were waited for; matrix products, arithmetic and copies ran while one was open for 1% of the time, Pallas kernels for 11%

profile of v2, /device:TPU:12, one launch (start us, length us, event | category | flops | bytes accessed | tf_op | source)
XLA Modules:
  0.0 48.4 jit_solution(8203691850308402254)
XLA Ops:
  0.6 0.9 %copy-done = f32[16,32,128]{2,1,0:T(8,128)S(1)} copy-done((f32[16,32,128]{2,1,0:T(8,128)S(1)}, f32[16,32,128]{2,1,0:T(8,128)}, u32[]{:S(2)}) %copy-start) | copy-done | bytes 262168
  1.6 0.9 %copy-done.1 = f32[16,32,128]{2,1,0:T(8,128)S(1)} copy-done((f32[16,32,128]{2,1,0:T(8,128)S(1)}, f32[16,32,128]{2,1,0:T(8,128)}, u32[]{:S(2)}) %copy-start.1) | copy-done | bytes 262168
  2.5 0.9 %copy-done.2 = f32[16,32,128]{2,1,0:T(8,128)S(1)} copy-done((f32[16,32,128]{2,1,0:T(8,128)S(1)}, f32[16,32,128]{2,1,0:T(8,128)}, u32[]{:S(2)}) %copy-start.2) | copy-done | bytes 262168
  3.5 0.7 %copy-done.3 = f32[3,2,4,128]{3,2,1,0:T(4,128)S(1)} copy-done((f32[3,2,4,128]{3,2,1,0:T(4,128)S(1)}, f32[3,2,4,128]{3,2,1,0:T(4,128)}, u32[]{:S(2)}) %copy-start.3) | copy-done | bytes 12312
  4.2 0.7 %copy-done.5 = f32[3,2,4,128]{3,2,1,0:T(4,128)S(1)} copy-done((f32[3,2,4,128]{3,2,1,0:T(4,128)S(1)}, f32[3,2,4,128]{3,2,1,0:T(4,128)}, u32[]{:S(2)}) %copy-start.5) | copy-done | bytes 12312
  4.9 0.2 pack_wy.1
  5.1 0.1 collective-permute-start
  5.2 2.5 %collective-permute-start.1 = (f32[80,128]{1,0:T(8,128)S(1)}, f32[80,128]{1,0:T(8,128)S(1)}, u32[]{:S(2)}, u32[]{:S(2)}) collective-permute-start(f32[80,128]{1,0:T(8,128)S(1)} %get-tuple-element.20), channel_id=1, source_target_pairs={{1,2},{2,1},{5,6},{6,5},{9,10},{10,9},{13,14},{14,13},{17,18},{18,... | collective-permute-start | bytes 122888 | tf_op jit(solution)/shard_map/ppermute | solution.py:42
  7.7 0.0 collective-permute-done.got_even.wye
  7.7 2.8 %collective-permute-done.1.got_odd.wyo = f32[80,128]{1,0:T(8,128)S(1)} collective-permute-done((f32[80,128]{1,0:T(8,128)S(1)}, f32[80,128]{1,0:T(8,128)S(1)}, u32[]{:S(2)}, u32[]{:S(2)}) %collective-permute-start.1) | collective-permute-done | bytes 40992 | tf_op jit(solution)/shard_map/ppermute | solution.py:42
  10.6 1.6 %collective-permute-start.2 = (f32[168,128]{1,0:T(8,128)S(1)}, f32[168,128]{1,0:T(8,128)S(1)}, u32[]{:S(2)}, u32[]{:S(2)}) collective-permute-start(f32[168,128]{1,0:T(8,128)S(1)} %get-tuple-element.21), channel_id=1, source_target_pairs={{0,4},{4,0},{8,12},{12,8},{16,20},{20,16},{24,28},{28,24},{1,5},{5... | collective-permute-start | bytes 258056 | tf_op jit(solution)/shard_map/ppermute | solution.py:43
  12.1 2.3 %collective-permute-start.3 = (f32[168,128]{1,0:T(8,128)S(1)}, f32[168,128]{1,0:T(8,128)S(1)}, u32[]{:S(2)}, u32[]{:S(2)}) collective-permute-start(f32[168,128]{1,0:T(8,128)S(1)} %get-tuple-element.22), channel_id=1, source_target_pairs={{4,8},{8,4},{12,16},{16,12},{20,24},{24,20},{5,9},{9,5},{13,17},{1... | collective-permute-start | bytes 258056 | tf_op jit(solution)/shard_map/ppermute | solution.py:42
  14.4 0.7 %fusion.3.target = s32[4,128]{1,0:T(4,128)S(1)} fusion(s32[4,128]{1,0:T(4,128)} %bitcast.17, s32[512]{0:T(512)} %param.17), kind=kLoop, calls=%fused_computation.13 | loop fusion | flops 22528 | bytes 6144 | tf_op jit(solution)/shard_map/add | solution.py:606
  15.2 0.0 collective-permute-done.2.fxe
  15.2 4.2 %collective-permute-done.3.fxo = f32[168,128]{1,0:T(8,128)S(1)} collective-permute-done((f32[168,128]{1,0:T(8,128)S(1)}, f32[168,128]{1,0:T(8,128)S(1)}, u32[]{:S(2)}, u32[]{:S(2)}) %collective-permute-start.3) | collective-permute-done | bytes 86048 | tf_op jit(solution)/shard_map/ppermute | solution.py:42
  19.4 1.6 %grid_steps.1 = (f32[16,32,128]{2,1,0:T(8,128)}, f32[32,32,128]{2,1,0:T(8,128)}) custom-call(f32[16,32,128]{2,1,0:T(8,128)S(1)} %copy-done, f32[16,32,128]{2,1,0:T(8,128)S(1)} %copy-done.1, f32[16,32,128]{2,1,0:T(8,128)S(1)} %copy-done.2, f32[80,128]{1,0:T(8,128)S(1)} %collective-permute-done.got_even.wye, f32[80,128]{1,0:T(8,128)S(1)} %collective-permute-done.1.got_odd.wyo, ...), custom_call_target="tpu_custom_call" | custom-call | tf_op jit(solution)/shard_map/grid_steps/pallas_call | solution.py:289
  21.0 5.1 %all-to-all-start = ((f32[32,32,128]{2,1,0:T(8,128)}), f32[32,32,128]{2,1,0:T(8,128)S(1)}, u32[]{:S(2)}, u32[]{:S(2)}) async-start(f32[32,32,128]{2,1,0:T(8,128)} %get-tuple-element.24), calls=%async_computation | async-start | bytes 1048576 | tf_op jit(solution)/shard_map/all_to_all | solution.py:615
  26.1 0.0 copy-start.4
  26.1 0.7 %copy-done.4 = f32[3,2,4,128]{3,2,1,0:T(4,128)S(1)} copy-done((f32[3,2,4,128]{3,2,1,0:T(4,128)S(1)}, f32[3,2,4,128]{3,2,1,0:T(4,128)}, u32[]{:S(2)}) %copy-start.4) | copy-done | bytes 12312
  26.8 0.7 %copy-done.6 = f32[3,2,4,128]{3,2,1,0:T(4,128)S(1)} copy-done((f32[3,2,4,128]{3,2,1,0:T(4,128)S(1)}, f32[3,2,4,128]{3,2,1,0:T(4,128)}, u32[]{:S(2)}) %copy-start.6) | copy-done | bytes 12312
  27.5 0.7 %copy-done.7 = f32[3,2,4,128]{3,2,1,0:T(4,128)S(1)} copy-done((f32[3,2,4,128]{3,2,1,0:T(4,128)S(1)}, f32[3,2,4,128]{3,2,1,0:T(4,128)}, u32[]{:S(2)}) %copy-start.7) | copy-done | bytes 12312
  28.2 5.3 %wall_first.1 = (f32[2,4,80,8,128]{4,3,2,1,0:T(8,128)S(1)}, f32[3,2,4,128]{3,2,1,0:T(4,128)S(1)}, f32[3,2,4,128]{3,2,1,0:T(4,128)S(1)}, f32[2,4,128]{2,1,0:T(4,1...) custom-call(s32[2,4,9,128,128]{4,3,2,1,0:T(8,128)} %masks.1, f32[3,2,4,128]{3,2,1,0:T(4,128)S(1)} %copy-done.4, ...), custom_call_target="tpu_custom_call" | custom-call | tf_op jit(solution)/shard_map/wall_first/pallas_call | solution.py:461
  33.5 0.2 collective-permute-start.4
  33.7 2.4 %collective-permute-start.5 = (f32[8,128]{1,0:T(8,128)S(1)}, f32[8,128]{1,0:T(8,128)S(1)}, u32[]{:S(2)}, u32[]{:S(2)}) collective-permute-start(f32[8,128]{1,0:T(8,128)S(1)} %get-tuple-element.29), channel_id=1, source_target_pairs={{1,2},{2,1},{5,6},{6,5},{9,10},{10,9},{13,14},{14,13},{17,18},{18,... | collective-permute-start | bytes 12296 | tf_op jit(solution)/shard_map/ppermute | solution.py:42
  36.1 0.0 collective-permute-done.4.got_even.wye
  36.2 2.5 %collective-permute-done.5.got_odd.wyo = f32[8,128]{1,0:T(8,128)S(1)} collective-permute-done((f32[8,128]{1,0:T(8,128)S(1)}, f32[8,128]{1,0:T(8,128)S(1)}, u32[]{:S(2)}, u32[]{:S(2)}) %collective-permute-start.5) | collective-permute-done | bytes 4128 | tf_op jit(solution)/shard_map/ppermute | solution.py:42
  38.7 1.5 %collective-permute-start.6 = (f32[24,128]{1,0:T(8,128)S(1)}, f32[24,128]{1,0:T(8,128)S(1)}, u32[]{:S(2)}, u32[]{:S(2)}) collective-permute-start(f32[24,128]{1,0:T(8,128)S(1)} %get-tuple-element.30), channel_id=1, source_target_pairs={{0,4},{4,0},{8,12},{12,8},{16,20},{20,16},{24,28},{28,24},{1,5},{5... | collective-permute-start | bytes 36872 | tf_op jit(solution)/shard_map/ppermute | solution.py:43
  40.2 2.4 %collective-permute-start.7 = (f32[24,128]{1,0:T(8,128)S(1)}, f32[24,128]{1,0:T(8,128)S(1)}, u32[]{:S(2)}, u32[]{:S(2)}) collective-permute-start(f32[24,128]{1,0:T(8,128)S(1)} %get-tuple-element.31), channel_id=1, source_target_pairs={{4,8},{8,4},{12,16},{16,12},{20,24},{24,20},{5,9},{9,5},{13,17},{1... | collective-permute-start | bytes 36872 | tf_op jit(solution)/shard_map/ppermute | solution.py:42
  42.6 0.0 collective-permute-done.6.fxe
  42.7 4.0 %collective-permute-done.7.fxo = f32[24,128]{1,0:T(8,128)S(1)} collective-permute-done((f32[24,128]{1,0:T(8,128)S(1)}, f32[24,128]{1,0:T(8,128)S(1)}, u32[]{:S(2)}, u32[]{:S(2)}) %collective-permute-start.7) | collective-permute-done | bytes 12320 | tf_op jit(solution)/shard_map/ppermute | solution.py:42
  46.7 0.0 all-to-all-done.got
  46.7 1.7 %wall_last.1 = (f32[3,2,4,128]{3,2,1,0:T(4,128)}, f32[3,2,4,128]{3,2,1,0:T(4,128)}) custom-call(f32[2,4,80,8,128]{4,3,2,1,0:T(8,128)S(1)} %get-tuple-element.23.weights, f32[32,32,128]{2,1,0:T(8,128)S(1)} %all-to-all-done.got, f32[3,2,4,128]{3,2,1,0:T(4,128)S(1)} %get-tuple-element.25.base1, f32[3,2,4,128]{3,2,1,0:T(4,128)S(1)} %get-tuple-element.26.vel1, ...), custom_call_target="tpu_custom_call" | custom-call | tf_op jit(solution)/shard_map/wall_last/pallas_call | solution.py:574
  (9 shorter events, 0.0 us)
Async XLA Ops:
  0.6 1.0 %copy-start = (f32[16,32,128]{2,1,0:T(8,128)S(1)}, f32[16,32,128]{2,1,0:T(8,128)}, u32[]{:S(2)}) copy-start(f32[16,32,128]{2,1,0:T(8,128)} %p.3) | copy-start | bytes 786436
  1.6 0.9 %copy-start.1 = (f32[16,32,128]{2,1,0:T(8,128)S(1)}, f32[16,32,128]{2,1,0:T(8,128)}, u32[]{:S(2)}) copy-start(f32[16,32,128]{2,1,0:T(8,128)} %q.3) | copy-start | bytes 786436
  2.5 0.9 %copy-start.2 = (f32[16,32,128]{2,1,0:T(8,128)S(1)}, f32[16,32,128]{2,1,0:T(8,128)}, u32[]{:S(2)}) copy-start(f32[16,32,128]{2,1,0:T(8,128)} %s.3) | copy-start | bytes 786436
  3.5 0.7 %copy-start.3 = (f32[3,2,4,128]{3,2,1,0:T(4,128)S(1)}, f32[3,2,4,128]{3,2,1,0:T(4,128)}, u32[]{:S(2)}) copy-start(f32[3,2,4,128]{3,2,1,0:T(4,128)} %jit.3) | copy-start | bytes 36868
  4.2 0.7 %copy-start.5 = (f32[3,2,4,128]{3,2,1,0:T(4,128)S(1)}, f32[3,2,4,128]{3,2,1,0:T(4,128)}, u32[]{:S(2)}) copy-start(f32[3,2,4,128]{3,2,1,0:T(4,128)} %disp.3) | copy-start | bytes 36868
  5.1 2.6 %collective-permute-start = (f32[80,128]{1,0:T(8,128)S(1)}, f32[80,128]{1,0:T(8,128)S(1)}, u32[]{:S(2)}, u32[]{:S(2)}) collective-permute-start(f32[80,128]{1,0:T(8,128)S(1)} %get-tuple-element.19), channel_id=1, source_target_pairs={{0,1},{1,0},{2,3},{3,2},{4,5},{5,4},{6,7},{7,6},{8,9},{9,8},{10,11... | collective-permute-start | bytes 122888 | tf_op jit(solution)/shard_map/ppermute | solution.py:43
  5.2 5.3 %collective-permute-start.1 = (f32[80,128]{1,0:T(8,128)S(1)}, f32[80,128]{1,0:T(8,128)S(1)}, u32[]{:S(2)}, u32[]{:S(2)}) collective-permute-start(f32[80,128]{1,0:T(8,128)S(1)} %get-tuple-element.20), channel_id=1, source_target_pairs={{1,2},{2,1},{5,6},{6,5},{9,10},{10,9},{13,14},{14,13},{17,18},{18,... | collective-permute-start | bytes 122888 | tf_op jit(solution)/shard_map/ppermute | solution.py:42
  10.6 4.6 %collective-permute-start.2 = (f32[168,128]{1,0:T(8,128)S(1)}, f32[168,128]{1,0:T(8,128)S(1)}, u32[]{:S(2)}, u32[]{:S(2)}) collective-permute-start(f32[168,128]{1,0:T(8,128)S(1)} %get-tuple-element.21), channel_id=1, source_target_pairs={{0,4},{4,0},{8,12},{12,8},{16,20},{20,16},{24,28},{28,24},{1,5},{5... | collective-permute-start | bytes 258056 | tf_op jit(solution)/shard_map/ppermute | solution.py:43
  12.1 7.3 %collective-permute-start.3 = (f32[168,128]{1,0:T(8,128)S(1)}, f32[168,128]{1,0:T(8,128)S(1)}, u32[]{:S(2)}, u32[]{:S(2)}) collective-permute-start(f32[168,128]{1,0:T(8,128)S(1)} %get-tuple-element.22), channel_id=1, source_target_pairs={{4,8},{8,4},{12,16},{16,12},{20,24},{24,20},{5,9},{9,5},{13,17},{1... | collective-permute-start | bytes 258056 | tf_op jit(solution)/shard_map/ppermute | solution.py:42
  21.0 25.7 %all-to-all-start = ((f32[32,32,128]{2,1,0:T(8,128)}), f32[32,32,128]{2,1,0:T(8,128)S(1)}, u32[]{:S(2)}, u32[]{:S(2)}) async-start(f32[32,32,128]{2,1,0:T(8,128)} %get-tuple-element.24), calls=%async_computation | async-start | bytes 1048576 | tf_op jit(solution)/shard_map/all_to_all | solution.py:615
  26.1 0.7 %copy-start.4 = (f32[3,2,4,128]{3,2,1,0:T(4,128)S(1)}, f32[3,2,4,128]{3,2,1,0:T(4,128)}, u32[]{:S(2)}) copy-start(f32[3,2,4,128]{3,2,1,0:T(4,128)} %jit.3) | copy-start | bytes 36868
  26.8 0.7 %copy-start.6 = (f32[3,2,4,128]{3,2,1,0:T(4,128)S(1)}, f32[3,2,4,128]{3,2,1,0:T(4,128)}, u32[]{:S(2)}) copy-start(f32[3,2,4,128]{3,2,1,0:T(4,128)} %disp.3) | copy-start | bytes 36868
  27.5 0.7 %copy-start.7 = (f32[3,2,4,128]{3,2,1,0:T(4,128)S(1)}, f32[3,2,4,128]{3,2,1,0:T(4,128)}, u32[]{:S(2)}) copy-start(f32[3,2,4,128]{3,2,1,0:T(4,128)} %vel.1) | copy-start | bytes 36868
  33.5 2.6 %collective-permute-start.4 = (f32[8,128]{1,0:T(8,128)S(1)}, f32[8,128]{1,0:T(8,128)S(1)}, u32[]{:S(2)}, u32[]{:S(2)}) collective-permute-start(f32[8,128]{1,0:T(8,128)S(1)} %get-tuple-element.28), channel_id=1, source_target_pairs={{0,1},{1,0},{2,3},{3,2},{4,5},{5,4},{6,7},{7,6},{8,9},{9,8},{10,11... | collective-permute-start | bytes 12296 | tf_op jit(solution)/shard_map/ppermute | solution.py:43
  33.7 5.0 %collective-permute-start.5 = (f32[8,128]{1,0:T(8,128)S(1)}, f32[8,128]{1,0:T(8,128)S(1)}, u32[]{:S(2)}, u32[]{:S(2)}) collective-permute-start(f32[8,128]{1,0:T(8,128)S(1)} %get-tuple-element.29), channel_id=1, source_target_pairs={{1,2},{2,1},{5,6},{6,5},{9,10},{10,9},{13,14},{14,13},{17,18},{18,... | collective-permute-start | bytes 12296 | tf_op jit(solution)/shard_map/ppermute | solution.py:42
  38.7 4.0 %collective-permute-start.6 = (f32[24,128]{1,0:T(8,128)S(1)}, f32[24,128]{1,0:T(8,128)S(1)}, u32[]{:S(2)}, u32[]{:S(2)}) collective-permute-start(f32[24,128]{1,0:T(8,128)S(1)} %get-tuple-element.30), channel_id=1, source_target_pairs={{0,4},{4,0},{8,12},{12,8},{16,20},{20,16},{24,28},{28,24},{1,5},{5... | collective-permute-start | bytes 36872 | tf_op jit(solution)/shard_map/ppermute | solution.py:43
  40.2 6.5 %collective-permute-start.7 = (f32[24,128]{1,0:T(8,128)S(1)}, f32[24,128]{1,0:T(8,128)S(1)}, u32[]{:S(2)}, u32[]{:S(2)}) collective-permute-start(f32[24,128]{1,0:T(8,128)S(1)} %get-tuple-element.31), channel_id=1, source_target_pairs={{4,8},{8,4},{12,16},{16,12},{20,24},{24,20},{5,9},{9,5},{13,17},{1... | collective-permute-start | bytes 36872 | tf_op jit(solution)/shard_map/ppermute | solution.py:42

commit v3 on v2

--- a/solution.py
+++ b/solution.py
@@ -13,6 +13,8 @@
 LANES = 128
 SUB = 8
 VMEM_BYTES = 48 * 1024 * 1024
+ALL_VMEM = 67_000_000
+HBM = pl.BlockSpec(memory_space=pltpu.HBM)
 
 F32 = jnp.float32
 BF16 = jnp.bfloat16
@@ -22,8 +24,8 @@
     return pl.BlockSpec(memory_space=pltpu.VMEM)
 
 
-def params():
-    return pltpu.CompilerParams(vmem_limit_bytes=VMEM_BYTES)
+def params(limit=VMEM_BYTES):
+    return pltpu.CompilerParams(vmem_limit_bytes=limit)
 
 
 def even_at(axis):
@@ -61,35 +63,39 @@
     return jnp.where(even, b, a), jnp.where(even, a, b)
 
 
-def pack_wy_kernel(p, q, s, jit_in, disp_in, to_even, to_odd, edges, walls, sems):
+def pack_wy_kernel(
+    p, q, s, jit_in, disp_in, vel_in, wy_even, wy_odd, fx_even, fx_odd, wall, edges, ends, sems
+):
     cx, cy = p.shape[0], p.shape[1]
     rows, cols = jit_in.shape[1], jit_in.shape[2]
-    copies = []
+    pairs = []
     for k, field in enumerate((p, q, s)):
         for side, first in enumerate((0, cy - SUB)):
-            source = field.at[:, first : first + SUB, :]
-            copies.append((source, edges.at[2 * k + side], sems.at[2 * k + side]))
-    copies.append((jit_in, walls.at[0], sems.at[6]))
-    copies.append((disp_in, walls.at[1], sems.at[7]))
-    copies = [pltpu.make_async_copy(*copy) for copy in copies]
+            pairs.append((field.at[:, first : first + SUB, :], edges.at[2 * k + side]))
+    pairs.append((p.at[0:2], ends.at[0, 0:2]))
+    pairs.append((p.at[cx - 2 : cx], ends.at[1, 0:2]))
+    for k, field in enumerate((q, s)):
+        pairs.append((field.at[0], ends.at[0, 2 + k]))
+        pairs.append((field.at[cx - 1], ends.at[1, 2 + k]))
+    for k, field in enumerate((jit_in, disp_in, vel_in)):
+        pairs.append((field, wall.at[k]))
+    copies = [pltpu.make_async_copy(a, b, sems.at[k]) for k, (a, b) in enumerate(pairs)]
     for copy in copies:
         copy.start()
     for copy in copies:
         copy.wait()
-    p_lo, p_hi, q_lo, q_hi, s_lo, s_hi = [edges.at[k] for k in range(6)]
-    jit, disp = walls.at[0], walls.at[1]
-
-    def edge(p, q, s, near, far, h):
+
+    def edge(side, near, far, h):
         def write(out):
-            out[0:cx, :] = p[:, near, :]
-            out[cx : 2 * cx, :] = p[:, far, :]
-            out[2 * cx : 3 * cx, :] = q[:, near, :]
-            out[3 * cx : 4 * cx, :] = s[:, near, :]
+            out[0:cx, :] = edges[side, :, near, :]
+            out[cx : 2 * cx, :] = edges[side, :, far, :]
+            out[2 * cx : 3 * cx, :] = edges[2 + side, :, near, :]
+            out[3 * cx : 4 * cx, :] = edges[4 + side, :, near, :]
             at = 4 * cx
-            for field in (jit, disp):
+            for field in range(2):
                 for c in range(3):
                     for l in range(rows):
-                        out[at : at + 1, :] = field[c, l, h : h + 1, :]
+                        out[at : at + 1, :] = wall[field, c, l, h : h + 1, :]
                         at += 1
             for spare in range(at, out.shape[0]):
                 out[spare : spare + 1, :] = jnp.zeros((1, LANES), F32)
@@ -98,96 +104,84 @@
 
     place_edges(
         even_at("wy"),
-        edge(p_lo, q_lo, s_lo, 0, 1, 0),
-        edge(p_hi, q_hi, s_hi, SUB - 1, SUB - 2, cols - 1),
-        to_even,
-        to_odd,
+        edge(0, 0, 1, 0),
+        edge(1, SUB - 1, SUB - 2, cols - 1),
+        wy_even,
+        wy_odd,
     )
+
+    def end(side, near, far, l):
+        def write(out):
+            out[0:cy, :] = ends[side, near]
+            out[cy : 2 * cy, :] = ends[side, far]
+            out[2 * cy : 3 * cy, :] = ends[side, 2]
+            out[3 * cy : 4 * cy, :] = ends[side, 3]
+            at = 4 * cy
+            for field in range(2):
+                for c in range(3):
+                    out[at + 1 : at + 1 + cols, :] = wall[field, c, l]
+                    at += cols + 2
+
+        return write
+
+    place_edges(even_at("fx"), end(0, 0, 1, 0), end(1, 1, 0, rows - 1), fx_even, fx_odd)
 
 
 def pad8(count):
     return (count + 7) // 8 * 8
 
 
-def pack_wy(p, q, s, jit, disp):
-    cx = p.shape[0]
-    rows = jit.shape[1]
-    size = pad8(4 * cx + 6 * rows)
-    out = jax.ShapeDtypeStruct((size, LANES), F32)
+def pack_wy(p, q, s, jit, disp, vel):
+    cx, cy = p.shape[0], p.shape[1]
+    rows, cols = jit.shape[1], jit.shape[2]
+    wy_out = jax.ShapeDtypeStruct((pad8(4 * cx + 6 * rows), LANES), F32)
+    fx_out = jax.ShapeDtypeStruct((pad8(4 * cy + 6 * (cols + 2) + 2), LANES), F32)
     return pl.pallas_call(
         pack_wy_kernel,
-        in_specs=[pl.BlockSpec(memory_space=pltpu.HBM)] * 5,
-        out_specs=[whole()] * 2,
-        out_shape=[out, out],
+        in_specs=[HBM] * 6,
+        out_specs=[whole()] * 5,
+        out_shape=[wy_out, wy_out, fx_out, fx_out, jax.ShapeDtypeStruct((3,) + jit.shape, F32)],
         scratch_shapes=[
             pltpu.VMEM((6, cx, SUB, LANES), F32),
-            pltpu.VMEM((2,) + jit.shape, F32),
-            pltpu.SemaphoreType.DMA((8,)),
+            pltpu.VMEM((2, 4, cy, LANES), F32),
+            pltpu.SemaphoreType.DMA((15,)),
         ],
-        compiler_params=params(),
+        compiler_params=params(ALL_VMEM),
         name="pack_wy",
-    )(p, q, s, jit, disp)
-
-
-def pack_fx_kernel(
-    cx, p_lo, p_hi, q_lo, q_hi, s_lo, s_hi, jit, disp, got_even, got_odd, to_even, to_odd
-):
-    cy = p_lo.shape[1]
-    rows, cols = jit.shape[1], jit.shape[2]
+    )(p, q, s, jit, disp, vel)
+
+
+def pack_fx_kernel(cx, cy, rows, cols, part_even, part_odd, got_even, got_odd, to_even, to_odd):
     before, after = before_after(even_at("wy"), got_even, got_odd)
-
-    def edge(p, q, s, near, far, x, l):
+    to_even[...] = part_even[...]
+    to_odd[...] = part_odd[...]
+
+    def corners(x, l):
         def write(out):
-            out[0:cy, :] = p[near]
-            out[cy : 2 * cy, :] = p[far]
-            out[2 * cy : 3 * cy, :] = q[0]
-            out[3 * cy : 4 * cy, :] = s[0]
             at = 4 * cy
-            for f, field in enumerate((jit, disp)):
-                for c in range(3):
-                    side = 4 * cx + (f * 3 + c) * rows + l
-                    out[at : at + 1, :] = before[side : side + 1]
-                    out[at + 1 : at + 1 + cols, :] = field[c, l]
-                    out[at + 1 + cols : at + 2 + cols, :] = after[side : side + 1]
-                    at += cols + 2
+            for k in range(6):
+                side = 4 * cx + k * rows + l
+                out[at : at + 1, :] = before[side : side + 1]
+                out[at + 1 + cols : at + 2 + cols, :] = after[side : side + 1]
+                at += cols + 2
             out[at : at + 1, :] = before[x : x + 1]
             out[at + 1 : at + 2, :] = after[x : x + 1]
-            for spare in range(at + 2, out.shape[0]):
-                out[spare : spare + 1, :] = jnp.zeros((1, LANES), F32)
 
         return write
 
-    place_edges(
-        even_at("fx"),
-        edge(p_lo, q_lo, s_lo, 0, 1, 0, 0),
-        edge(p_hi, q_hi, s_hi, 1, 0, cx - 1, rows - 1),
-        to_even,
-        to_odd,
-    )
-
-
-def pack_fx(p, q, s, jit, disp, got_even, got_odd):
-    cx, cy = p.shape[0], p.shape[1]
-    cols = jit.shape[2]
-    size = pad8(4 * cy + 6 * (cols + 2) + 2)
-
-    def at(depth, index):
-        return pl.BlockSpec((depth, cy, LANES), lambda i: (index, 0, 0))
-
-    small = pl.BlockSpec(jit.shape, lambda i: (0, 0, 0, 0))
-    message = pl.BlockSpec(got_even.shape, lambda i: (0, 0))
-    out = jax.ShapeDtypeStruct((size, LANES), F32)
-    spec = pl.BlockSpec((size, LANES), lambda i: (0, 0))
+    place_edges(even_at("fx"), corners(0, 0), corners(cx - 1, rows - 1), to_even, to_odd)
+
+
+def pack_fx(sizes, parts, got):
+    out = jax.ShapeDtypeStruct(parts[0].shape, F32)
     return pl.pallas_call(
-        functools.partial(pack_fx_kernel, cx),
-        grid=(1,),
-        in_specs=[at(2, 0), at(2, cx // 2 - 1), at(1, 0), at(1, cx - 1), at(1, 0), at(1, cx - 1)]
-        + [small, small, message, message],
-        out_specs=[spec, spec],
+        functools.partial(pack_fx_kernel, *sizes),
+        in_specs=[whole()] * 4,
+        out_specs=[whole()] * 2,
         out_shape=[out, out],
         compiler_params=params(),
         name="pack_fx",
-    )(p, p, q, q, s, s, jit, disp, got_even, got_odd)
+    )(*parts, *got)
 
 
 def along_z(v):
@@ -311,36 +305,89 @@
     for dh in (-1, 0, 1):
         if (dh == -1 and g % 4 == 3) or (dh == 1 and g % 4 == 0):
             continue
-        groups.append((False, dh))
-        groups.append((True, dh))
+        groups.append(dh)
     return groups
 
 
 STORED = sum(len(reached(g)) for g in range(LANES // SUB))
 
 
-def tile_rows(ref, c, l, h, first_sub):
-    mid, ends = {}, {}
+def mid_rows(ref, c, l, h):
+    rows = {}
+    for dh in (-1, 0, 1):
+        row = ref[c, l + 1, pl.ds(h + 1 + dh, 1), :]
+        rows[dh] = jnp.broadcast_to(row, (SUB, LANES))
+    return rows
+
+
+def end_rows(ref, c, l, h, first_sub):
+    rows = {}
     for dh in (-1, 0, 1):
         at = pl.ds(h + 1 + dh, 1)
-        mid[dh] = jnp.broadcast_to(ref[c, l + 1, at, :], (SUB, LANES))
         before = jnp.broadcast_to(ref[c, l, at, :], (SUB, LANES))
         after = jnp.broadcast_to(ref[c, l + 2, at, :], (SUB, LANES))
-        ends[dh] = jnp.where(first_sub, before, after)
-    return mid, ends
-
-
-def fill_padded(pad, own, before_y, after_y, before_x, after_x, at_y, at_x):
+        rows[dh] = jnp.where(first_sub, before, after)
+    return rows
+
+
+def fill_y(pad, own, before, after, at):
     rows, cols = own.shape[1], own.shape[2]
     for c in range(3):
         for l in range(rows):
-            row = at_y + c * rows + l
-            pad[c, l + 1, 0:1, :] = before_y[row : row + 1]
+            row = at + c * rows + l
+            pad[c, l + 1, 0:1, :] = before[row : row + 1]
             pad[c, l + 1, 1 : cols + 1, :] = own[c, l]
-            pad[c, l + 1, cols + 1 : cols + 2, :] = after_y[row : row + 1]
-        row = at_x + c * (cols + 2)
-        pad[c, 0, 0 : cols + 2, :] = before_x[row : row + cols + 2]
-        pad[c, rows + 1, 0 : cols + 2, :] = after_x[row : row + cols + 2]
+            pad[c, l + 1, cols + 1 : cols + 2, :] = after[row : row + 1]
+
+
+def fill_x(pad, rows, cols, before, after, at):
+    for c in range(3):
+        row = at + c * (cols + 2)
+        pad[c, 0, 0 : cols + 2, :] = before[row : row + cols + 2]
+        pad[c, rows + 1, 0 : cols + 2, :] = after[row : row + cols + 2]
+
+
+def lattice_rows():
+    index = lax.broadcasted_iota(jnp.int32, (1, LANES), 1)
+    places = (index % 8, index // 8 % 4, index // 32)
+    return [v.astype(F32) * (1.0 / REACH) for v in places]
+
+
+SPAN = 8.0 / REACH
+RISE = 4.0 / REACH
+
+
+def mine_columns(ref, lattice, l, h):
+    sub = lax.broadcasted_iota(jnp.int32, (SUB, LANES), 0)
+    own = []
+    for c in range(3):
+        row = ref[c, l + 1, pl.ds(h + 1, 1), :] * (1.0 / REACH) + lattice[c]
+        own.append(jnp.broadcast_to(row, (SUB, LANES)))
+    return jnp.transpose(jnp.where(sub == 0, own[0], jnp.where(sub == 1, own[1], own[2])))
+
+
+def bond_row(weight, others, mine):
+    for c in range(3):
+        diff = others[c] - mine[c]
+        weight = weight - diff * diff
+    return jnp.maximum(weight, 0.0)
+
+
+def tile_pass(l, h, columns, others, pulls, mask_at, weights, sums_in, acc):
+    place = 0
+    for g in range(LANES // SUB):
+        span = slice(g * SUB, (g + 1) * SUB)
+        mine = [jnp.broadcast_to(columns[span, c : c + 1], (SUB, LANES)) for c in range(3)]
+        sums = [None if sums_in is None else sums_in[l, h, c, span, :] for c in range(4)]
+        for dh in reached(g):
+            here = [others[c][dh] for c in range(3)]
+            weight = bond_row(mask_at(dh, span, place), here, mine)
+            weights[l, h, place] = weight
+            place += 1
+            terms = [weight * pulls[c][dh] for c in range(3)] + [weight]
+            sums = [t if v is None else v + t for v, t in zip(sums, terms)]
+        for c in range(4):
+            acc[l, h, c, span, :] = sums[c]
 
 
 def lane_sums(acc, l, cols, count):
@@ -362,71 +409,100 @@
     return [jnp.concatenate(parts, axis=0) for parts in result]
 
 
+def center_kernel(
+    cx, masks_in, wall, wye, wyo, weights, acc, end_masks, jpad, dpad, masks, sems
+):
+    rows, cols = wall.shape[2], wall.shape[3]
+    copies = {}
+    for h in range(cols):
+        for l in range(rows):
+            copies[l, h] = pltpu.make_async_copy(
+                masks_in.at[l, h], masks.at[l, h], sems.at[l * cols + h]
+            )
+            copies[l, h].start()
+    first_sub = lax.broadcasted_iota(jnp.int32, (SUB, LANES), 0) < SUB // 2
+    before, after = before_after(even_at("wy"), wye, wyo)
+    fill_y(jpad, wall.at[0], before, after, 4 * cx)
+    fill_y(dpad, wall.at[1], before, after, 4 * cx + 3 * rows)
+    lattice = lattice_rows()
+
+    def one_tile(l, h):
+        columns = mine_columns(jpad, lattice, l, h)
+        others = []
+        for c in range(3):
+            mid = mid_rows(jpad, c, l, h)
+            for dh in (-1, 0, 1):
+                mid[dh] = mid[dh] * (1.0 / REACH) + lattice[c]
+                if c == 1:
+                    mid[dh] = mid[dh] + RISE * dh
+            others.append(mid)
+        pulls = [mid_rows(dpad, c, l, h) for c in range(3)]
+
+        def mask_at(dh, span, place):
+            before = masks[l, h, 1 + dh, span, :]
+            after = masks[l, h, 7 + dh, span, :]
+            end_masks[l, h, place] = jnp.where(first_sub, before, after).astype(F32)
+            return masks[l, h, 4 + dh, span, :].astype(F32)
+
+        tile_pass(l, h, columns, others, pulls, mask_at, weights, None, acc)
+
+    for h in range(cols):
+        for l in range(rows):
+            copies[l, h].wait()
+            one_tile(l, h)
+
+
+def wall_center(cx, masks, wall, wy_got):
+    rows, cols = wall.shape[2], wall.shape[3]
+    stored = jax.ShapeDtypeStruct((rows, cols, STORED, SUB, LANES), F32)
+    return pl.pallas_call(
+        functools.partial(center_kernel, cx),
+        in_specs=[HBM] + [whole()] * 3,
+        out_specs=[whole()] * 3,
+        out_shape=[stored, jax.ShapeDtypeStruct((rows, cols, 4, LANES, LANES), F32), stored],
+        scratch_shapes=[
+            pltpu.VMEM((3, rows + 2, SUB, LANES), F32),
+            pltpu.VMEM((3, rows + 2, SUB, LANES), F32),
+            pltpu.VMEM(masks.shape, jnp.int32),
+            pltpu.SemaphoreType.DMA((rows * cols,)),
+        ],
+        compiler_params=params(),
+        name="wall_center",
+    )(masks, wall, *wy_got)
+
+
 def wall_kernel(
-    cx, cy, masks, jit, disp, vel, wye, wyo, fxe, fxo, weights, vel1, base1, totals, to_even, to_odd,
+    cx, cy, wall, wye, wyo, fxe, fxo, part, end_masks, weights, vel1, base1, totals, to_even, to_odd,
     jpad, dpad, acc,
 ):
-    rows, cols = jit.shape[1], jit.shape[2]
+    rows, cols = wall.shape[2], wall.shape[3]
     first_sub = lax.broadcasted_iota(jnp.int32, (SUB, LANES), 0) < SUB // 2
-    before_y, after_y = before_after(even_at("wy"), wye, wyo)
-    before_x, after_x = before_after(even_at("fx"), fxe, fxo)
-    fill_padded(jpad, jit, before_y, after_y, before_x, after_x, 4 * cx, 4 * cy)
-    fill_padded(
-        dpad, disp, before_y, after_y, before_x, after_x,
-        4 * cx + 3 * rows, 4 * cy + 3 * (cols + 2),
-    )
-    index = lax.broadcasted_iota(jnp.int32, (1, LANES), 1)
-    lattice = (index % 8, index // 8 % 4, index // 32)
-    lattice = [v.astype(F32) * (1.0 / REACH) for v in lattice]
-    span = 8.0 / REACH
-    rise = 4.0 / REACH
+    before, after = before_after(even_at("wy"), wye, wyo)
+    fill_y(jpad, wall.at[0], before, after, 4 * cx)
+    fill_y(dpad, wall.at[1], before, after, 4 * cx + 3 * rows)
+    before, after = before_after(even_at("fx"), fxe, fxo)
+    fill_x(jpad, rows, cols, before, after, 4 * cy)
+    fill_x(dpad, rows, cols, before, after, 4 * cy + 3 * (cols + 2))
+    lattice = lattice_rows()
 
     def one_tile(l, h):
-        others, own = [], []
+        columns = mine_columns(jpad, lattice, l, h)
+        others = []
         for c in range(3):
-            mid, ends = tile_rows(jpad, c, l, h, first_sub)
+            ends = end_rows(jpad, c, l, h, first_sub)
             for dh in (-1, 0, 1):
-                mid[dh] = mid[dh] * (1.0 / REACH) + lattice[c]
                 ends[dh] = ends[dh] * (1.0 / REACH) + lattice[c]
                 if c == 0:
-                    ends[dh] = ends[dh] + jnp.where(first_sub, -span, span)
+                    ends[dh] = ends[dh] + jnp.where(first_sub, -SPAN, SPAN)
                 if c == 1:
-                    mid[dh] = mid[dh] + rise * dh
-                    ends[dh] = ends[dh] + rise * dh
-            own.append(mid[0])
-            others.append((mid, ends))
-        pulls = [tile_rows(dpad, c, l, h, first_sub) for c in range(3)]
-        sub = lax.broadcasted_iota(jnp.int32, (SUB, LANES), 0)
-        columns = jnp.transpose(
-            jnp.where(sub == 0, own[0], jnp.where(sub == 1, own[1], own[2]))
-        )
-        place = 0
-        for g in range(LANES // SUB):
-            span_g = slice(g * SUB, (g + 1) * SUB)
-            mine = [
-                jnp.broadcast_to(columns[span_g, c : c + 1], (SUB, LANES)) for c in range(3)
-            ]
-            sums = [None] * 4
-            for ends, dh in reached(g):
-                if ends:
-                    mask = jnp.where(
-                        first_sub,
-                        masks[l, h, 1 + dh, span_g, :],
-                        masks[l, h, 7 + dh, span_g, :],
-                    )
-                else:
-                    mask = masks[l, h, 4 + dh, span_g, :]
-                weight = mask.astype(F32)
-                for c in range(3):
-                    diff = others[c][ends][dh] - mine[c]
-                    weight = weight - diff * diff
-                weight = jnp.maximum(weight, 0.0)
-                weights[l, h, place] = weight
-                place += 1
-                terms = [weight * pulls[c][ends][dh] for c in range(3)] + [weight]
-                sums = [t if v is None else v + t for v, t in zip(sums, terms)]
-            for c in range(4):
-                acc[l, h, c, span_g, :] = sums[c]
+                    ends[dh] = ends[dh] + RISE * dh
+            others.append(ends)
+        pulls = [end_rows(dpad, c, l, h, first_sub) for c in range(3)]
+
+        def mask_at(dh, span, place):
+            return end_masks[l, h, place]
+
+        tile_pass(l, h, columns, others, pulls, mask_at, weights, part, acc)
 
     @pl.loop(0, cols)
     def _(h):
@@ -437,8 +513,8 @@
         pulled = lane_sums(acc, l, cols, 4)
         totals[l] = pulled[3]
         for c in range(3):
-            mine = disp[c, l]
-            fresh = vel[c, l] + STIFFNESS * (pulled[c] - pulled[3] * mine)
+            mine = wall[1, c, l]
+            fresh = wall[2, c, l] + STIFFNESS * (pulled[c] - pulled[3] * mine)
             vel1[c, l] = fresh
             base1[c, l] = mine + fresh
 
@@ -455,17 +531,18 @@
     place_edges(even_at("wy"), edge(0), edge(cols - 1), to_even, to_odd)
 
 
-def wall_first(cx, cy, masks, jit, disp, vel, wy_got, fx_got):
-    rows, cols = jit.shape[1], jit.shape[2]
+def wall_first(cx, cy, wall, wy_got, fx_got, part, end_masks):
+    rows, cols = wall.shape[2], wall.shape[3]
     edge = (pad8(3 * rows), LANES)
+    field = jax.ShapeDtypeStruct(wall.shape[1:], F32)
     return pl.pallas_call(
         functools.partial(wall_kernel, cx, cy),
-        in_specs=[whole()] * 8,
+        in_specs=[whole()] * 7,
         out_specs=[whole()] * 6,
         out_shape=[
             jax.ShapeDtypeStruct((rows, cols, STORED, SUB, LANES), F32),
-            jax.ShapeDtypeStruct(jit.shape, F32),
-            jax.ShapeDtypeStruct(jit.shape, F32),
+            field,
+            field,
             jax.ShapeDtypeStruct((rows, cols, LANES), F32),
             jax.ShapeDtypeStruct(edge, F32),
             jax.ShapeDtypeStruct(edge, F32),
@@ -477,7 +554,7 @@
         ],
         compiler_params=params(),
         name="wall_first",
-    )(masks, jit, disp, vel, *wy_got, *fx_got)
+    )(wall, *wy_got, *fx_got, part, end_masks)
 
 
 def pack_base_kernel(base1, got_even, got_odd, to_even, to_odd):
@@ -515,13 +592,15 @@
 
 
 def last_kernel(
-    weights, got, base1, vel1, totals, wye, wyo, fxe, fxo, disp_out, vel_out, dpad, loads, acc
+    weights, end_weights, got, base1, vel1, totals, wye, wyo, fxe, fxo, disp_out, vel_out,
+    dpad, loads, acc,
 ):
     rows, cols = base1.shape[1], base1.shape[2]
     first_sub = lax.broadcasted_iota(jnp.int32, (SUB, LANES), 0) < SUB // 2
-    before_y, after_y = before_after(even_at("wy"), wye, wyo)
-    before_x, after_x = before_after(even_at("fx"), fxe, fxo)
-    fill_padded(dpad, base1, before_y, after_y, before_x, after_x, 0, 0)
+    before, after = before_after(even_at("wy"), wye, wyo)
+    fill_y(dpad, base1, before, after, 0)
+    before, after = before_after(even_at("fx"), fxe, fxo)
+    fill_x(dpad, rows, cols, before, after, 0)
     total = got[0]
     for d in range(1, got.shape[0]):
         total = total + got[d]
@@ -531,15 +610,18 @@
         dpad[0, k, 0 : cols + 2, :] = dpad[0, k, 0 : cols + 2, :] + LOADING * here
 
     def one_tile(l, h):
-        pulls = [tile_rows(dpad, c, l, h, first_sub) for c in range(3)]
+        mids = [mid_rows(dpad, c, l, h) for c in range(3)]
+        ends = [end_rows(dpad, c, l, h, first_sub) for c in range(3)]
         place = 0
         for g in range(LANES // SUB):
             sums = [None] * 3
-            for ends, dh in reached(g):
-                weight = weights[l, h, place]
+            for dh in reached(g):
+                for weight, pulls in (
+                    (weights[l, h, place], mids), (end_weights[l, h, place], ends)
+                ):
+                    terms = [weight * pulls[c][dh] for c in range(3)]
+                    sums = [t if v is None else v + t for v, t in zip(sums, terms)]
                 place += 1
-                terms = [weight * pulls[c][ends][dh] for c in range(3)]
-                sums = [t if v is None else v + t for v, t in zip(sums, terms)]
             for c in range(3):
                 acc[l, h, c, g * SUB : (g + 1) * SUB, :] = sums[c]
 
@@ -569,11 +651,11 @@
                 disp_out[c, l] = mine + fresh
 
 
-def wall_last(weights, got, base1, vel1, totals, wy_got, fx_got):
+def wall_last(weights, end_weights, got, base1, vel1, totals, wy_got, fx_got):
     rows, cols = base1.shape[1], base1.shape[2]
     return pl.pallas_call(
         last_kernel,
-        in_specs=[whole()] * 9,
+        in_specs=[whole()] * 10,
         out_specs=[whole()] * 2,
         out_shape=[jax.ShapeDtypeStruct(base1.shape, F32)] * 2,
         scratch_shapes=[
@@ -583,7 +665,7 @@
         ],
         compiler_params=params(),
         name="wall_last",
-    )(weights, got, base1, vel1, totals, *wy_got, *fx_got)
+    )(weights, end_weights, got, base1, vel1, totals, *wy_got, *fx_got)
 
 
 def per_device(
@@ -605,22 +687,28 @@
     height = (device % wy_count) * cols + tile % cols
     target = length * (wy_count * cols) + height
 
-    sends = pack_wy(pressure, pressure_prev, speed_sq, jitter, displacement)
+    cx, cy = pressure.shape[0], pressure.shape[1]
+    rows = displacement.shape[1]
+    *sends, part_even, part_odd, wall = pack_wy(
+        pressure, pressure_prev, speed_sq, jitter, displacement, velocity
+    )
     wy_got = exchange("wy", *sends)
-    sends = pack_fx(pressure, pressure_prev, speed_sq, jitter, displacement, *wy_got)
+    sends = pack_fx((cx, cy, rows, cols), (part_even, part_odd), wy_got)
     fx_got = exchange("fx", *sends)
+    weights, part, end_masks = wall_center(cx, bond_masks, wall, wy_got)
     pressure_out, slots = grid_steps(
         pressure, pressure_prev, speed_sq, wy_got, fx_got, target, fx_count, wy_count
     )
     got = lax.all_to_all(slots, ("fx", "wy"), split_axis=0, concat_axis=0, tiled=True)
-    weights, vel1, base1, totals, *sends = wall_first(
-        pressure.shape[0], pressure.shape[1],
-        bond_masks, jitter, displacement, velocity, wy_got, fx_got
+    end_weights, vel1, base1, totals, *sends = wall_first(
+        cx, cy, wall, wy_got, fx_got, part, end_masks
     )
     base_wy = exchange("wy", *sends)
     sends = pack_base(base1, base_wy)
     base_fx = exchange("fx", *sends)
-    disp_out, vel_out = wall_last(weights, got, base1, vel1, totals, base_wy, base_fx)
+    disp_out, vel_out = wall_last(
+        weights, end_weights, got, base1, vel1, totals, base_wy, base_fx
+    )
     return (disp_out, vel_out, pressure_out)
 
 

time: 49.1 us -> 49.3 us (level)
  Pallas kernels: 8.85 us -> 10.8 us
  local copies, waits for them, and re-layouts: 6.37 us -> 4.63 us
    pallas_call x3 -> x4, Pallas kernels: 1.92 us -> 6.91 us  [the longest x1 3.29 us: wall_center(): pl.pallas_call(functools.partial(center_kernel, cx), in_specs=[HBM] + [wh...]
    pallas_call x1, Pallas kernels: 5.3 us -> 2.27 us  [wall_first(): pl.pallas_call(functools.partial(wall_kernel, cx, cy), in_specs=[whole()]...]
    unnamed x16 -> x12, local copies, waits for them, and re-layouts: 6.37 us -> 4.63 us
where the time goes in v3:
time: 49.3 us; the launch traced here: 48.8 us
  starting transfers between devices  18.2 us (37%)
  waiting for transfers between devices  13.7 us (28%)
  Pallas kernels  10.8 us (22%)
  local copies, waits for them, and re-layouts  4.63 us (9%)
  between operations  0.78 us (2%)
  other arithmetic  0.71 us (1%)
    ppermute x4, waiting for transfers between devices, exchange(): got_odd = lax.ppermute(to_odd, axis, pair_list(count, 1))  13.7 us
    ppermute x4, starting transfers between devices, exchange(): got_odd = lax.ppermute(to_odd, axis, pair_list(count, 1))  9.74 us
    all_to_all x1, starting transfers between devices, per_device(): lax.all_to_all(slots, ('fx', 'wy'), split_axis=0, concat_axis=0, tiled=True)  5.06 us
    unnamed x12, local copies, waits for them, and re-layouts  4.63 us
    ppermute x4, starting transfers between devices, exchange(): got_even = lax.ppermute(to_even, axis, pair_list(count, 0))  3.36 us
    pallas_call x1, Pallas kernels, wall_center(): pl.pallas_call(functools.partial(center_kernel, cx), in_specs=[HBM] + [wh...  3.29 us
    pallas_call x1, Pallas kernels, wall_first(): pl.pallas_call(functools.partial(wall_kernel, cx, cy), in_specs=[whole()]...  2.27 us
    pallas_call x1, Pallas kernels, pack_wy(): pl.pallas_call(pack_wy_kernel, in_specs=[HBM] * 6, out_specs=[whole()] *...  1.92 us
  transfers between devices with their start and end apart: 9, of which 4 were waited for; matrix products, arithmetic and copies ran while one was open for 1% of the time, Pallas kernels for 11%

profile of v3, /device:TPU:12, one launch (start us, length us, event | category | flops | bytes accessed | tf_op | source)
XLA Modules:
  0.0 48.8 jit_solution(6899336733126962665)
XLA Ops:
  0.6 1.9 %pack_wy.1 = (f32[80,128]{1,0:T(8,128)}, f32[80,128]{1,0:T(8,128)}, f32[168,128]{1,0:T(8,128)}, f32[168,128]{1,0:T(8,128)}, f32[3,3,2,4,128]{4,3,2,1,0:T(4,128)}) custom-call(f32[16,32,128]{2,1,0:T(8,128)} %p.3, f32[16,32,128]{2,1,0:T(8,128)} %q.3, f32[16,32,128]{2,1,0:T(8,128)} %s.3, f32[3,2,4,128]{3,2,1,0:T(4,128)} %jit_in.1, f32[3,2,4,128]{3,2,1,0:T(4,128)} %disp_in.1, ...), custom_call_target="tpu_custom_call" | custom-call | tf_op jit(solution)/shard_map/pack_wy/pallas_call | solution.py:139
  2.6 0.0 copy-start.3
  2.6 0.1 collective-permute-start
  2.6 2.5 %collective-permute-start.1 = (f32[80,128]{1,0:T(8,128)}, f32[80,128]{1,0:T(8,128)S(1)}, u32[]{:S(2)}, u32[]{:S(2)}) collective-permute-start(f32[80,128]{1,0:T(8,128)} %get-tuple-element.27), channel_id=1, source_target_pairs={{1,2},{2,1},{5,6},{6,5},{9,10},{10,9},{13,14},{14,13},{17,18},{18,... | collective-permute-start | bytes 122888 | tf_op jit(solution)/shard_map/ppermute | solution.py:44
  5.2 0.0 collective-permute-done.wye.got_even
  5.2 3.0 %collective-permute-done.1.wyo.got_odd = f32[80,128]{1,0:T(8,128)S(1)} collective-permute-done((f32[80,128]{1,0:T(8,128)}, f32[80,128]{1,0:T(8,128)S(1)}, u32[]{:S(2)}, u32[]{:S(2)}) %collective-permute-start.1) | collective-permute-done | bytes 40992 | tf_op jit(solution)/shard_map/ppermute | solution.py:44
  8.2 0.0 copy-start.4
  8.2 0.9 %copy-done.4 = f32[168,128]{1,0:T(8,128)S(1)} copy-done((f32[168,128]{1,0:T(8,128)S(1)}, f32[168,128]{1,0:T(8,128)}, u32[]{:S(2)}) %copy-start.4) | copy-done | bytes 86040
  9.1 0.9 %copy-done.5 = f32[168,128]{1,0:T(8,128)S(1)} copy-done((f32[168,128]{1,0:T(8,128)S(1)}, f32[168,128]{1,0:T(8,128)}, u32[]{:S(2)}) %copy-start.5) | copy-done | bytes 86040
  10.0 1.6 %collective-permute-start.2 = (f32[168,128]{1,0:T(8,128)S(1)}, f32[168,128]{1,0:T(8,128)S(1)}, u32[]{:S(2)}, u32[]{:S(2)}) collective-permute-start(f32[168,128]{1,0:T(8,128)S(1)} %get-tuple-element.31), channel_id=1, source_target_pairs={{0,4},{4,0},{8,12},{12,8},{16,20},{20,16},{24,28},{28,24},{1,5},{5... | collective-permute-start | bytes 258056 | tf_op jit(solution)/shard_map/ppermute | solution.py:45
  11.5 2.3 %collective-permute-start.3 = (f32[168,128]{1,0:T(8,128)S(1)}, f32[168,128]{1,0:T(8,128)S(1)}, u32[]{:S(2)}, u32[]{:S(2)}) collective-permute-start(f32[168,128]{1,0:T(8,128)S(1)} %get-tuple-element.32), channel_id=1, source_target_pairs={{4,8},{8,4},{12,16},{16,12},{20,24},{24,20},{5,9},{9,5},{13,17},{1... | collective-permute-start | bytes 258056 | tf_op jit(solution)/shard_map/ppermute | solution.py:44
  13.9 0.7 %fusion.3.target = s32[4,128]{1,0:T(4,128)S(1)} fusion(s32[4,128]{1,0:T(4,128)} %bitcast.17, s32[512]{0:T(512)} %param.17), kind=kLoop, calls=%fused_computation.13 | loop fusion | flops 22528 | bytes 6144 | tf_op jit(solution)/shard_map/add | solution.py:688
  14.6 0.0 collective-permute-done.2.fxe
  14.6 4.2 %collective-permute-done.3.fxo = f32[168,128]{1,0:T(8,128)S(1)} collective-permute-done((f32[168,128]{1,0:T(8,128)S(1)}, f32[168,128]{1,0:T(8,128)S(1)}, u32[]{:S(2)}, u32[]{:S(2)}) %collective-permute-start.3) | collective-permute-done | bytes 86048 | tf_op jit(solution)/shard_map/ppermute | solution.py:44
  18.8 0.9 %copy-done = f32[16,32,128]{2,1,0:T(8,128)S(1)} copy-done((f32[16,32,128]{2,1,0:T(8,128)S(1)}, f32[16,32,128]{2,1,0:T(8,128)}, u32[]{:S(2)}) %copy-start) | copy-done | bytes 262168
  19.8 0.9 %copy-done.1 = f32[16,32,128]{2,1,0:T(8,128)S(1)} copy-done((f32[16,32,128]{2,1,0:T(8,128)S(1)}, f32[16,32,128]{2,1,0:T(8,128)}, u32[]{:S(2)}) %copy-start.1) | copy-done | bytes 262168
  20.7 0.9 %copy-done.2 = f32[16,32,128]{2,1,0:T(8,128)S(1)} copy-done((f32[16,32,128]{2,1,0:T(8,128)S(1)}, f32[16,32,128]{2,1,0:T(8,128)}, u32[]{:S(2)}) %copy-start.2) | copy-done | bytes 262168
  21.7 1.6 %grid_steps.1 = (f32[16,32,128]{2,1,0:T(8,128)}, f32[32,32,128]{2,1,0:T(8,128)}) custom-call(f32[16,32,128]{2,1,0:T(8,128)S(1)} %copy-done, f32[16,32,128]{2,1,0:T(8,128)S(1)} %copy-done.1, f32[16,32,128]{2,1,0:T(8,128)S(1)} %copy-done.2, f32[80,128]{1,0:T(8,128)S(1)} %collective-permute-done.wye.got_even, f32[80,128]{1,0:T(8,128)S(1)} %collective-permute-done.1.wyo.got_odd, ...), custom_call_target="tpu_custom_call" | custom-call | tf_op jit(solution)/shard_map/grid_steps/pallas_call | solution.py:283
  23.3 5.1 %all-to-all-start = ((f32[32,32,128]{2,1,0:T(8,128)}), f32[32,32,128]{2,1,0:T(8,128)S(1)}, u32[]{:S(2)}, u32[]{:S(2)}) async-start(f32[32,32,128]{2,1,0:T(8,128)} %get-tuple-element.36), calls=%async_computation | async-start | bytes 1048576 | tf_op jit(solution)/shard_map/all_to_all | solution.py:702
  28.4 0.0 copy-done.3
  28.4 3.3 %wall_center.1 = (f32[2,4,40,8,128]{4,3,2,1,0:T(8,128)S(1)}, f32[2,4,4,128,128]{4,3,2,1,0:T(8,128)S(1)}, f32[2,4,40,8,128]{4,3,2,1,0:T(8,128)S(1)}) custom-call(s32[2,4,9,128,128]{4,3,2,1,0:T(8,128)} %masks_in.1, f32[3,3,2,4,128]{4,3,2,1,0:T(4,128)S(1)} %copy-done.3, f32[80,128]{1,0:T(8,128)S(1)} %collective-permute-done.wye.got_even, ...), custom_call_target="tpu_custom_call" | custom-call | tf_op jit(solution)/shard_map/wall_center/pallas_call | solution.py:458
  31.7 2.3 %wall_first.1 = (f32[2,4,40,8,128]{4,3,2,1,0:T(8,128)S(1)}, f32[3,2,4,128]{3,2,1,0:T(4,128)S(1)}, f32[3,2,4,128]{3,2,1,0:T(4,128)S(1)}, f32[2,4,128]{2,1,0:T(4,1...) custom-call(f32[3,3,2,4,128]{4,3,2,1,0:T(4,128)S(1)} %copy-done.3, f32[80,128]{1,0:T(8,128)S(1)} %collective-permute-done.wye.got_even, ...), custom_call_target="tpu_custom_call" | custom-call | tf_op jit(solution)/shard_map/wall_first/pallas_call | solution.py:538
  33.9 0.2 collective-permute-start.4
  34.2 2.4 %collective-permute-start.5 = (f32[8,128]{1,0:T(8,128)S(1)}, f32[8,128]{1,0:T(8,128)S(1)}, u32[]{:S(2)}, u32[]{:S(2)}) collective-permute-start(f32[8,128]{1,0:T(8,128)S(1)} %get-tuple-element.41), channel_id=1, source_target_pairs={{1,2},{2,1},{5,6},{6,5},{9,10},{10,9},{13,14},{14,13},{17,18},{18,... | collective-permute-start | bytes 12296 | tf_op jit(solution)/shard_map/ppermute | solution.py:44
  36.6 0.0 collective-permute-done.4.got_even.wye
  36.6 2.5 %collective-permute-done.5.got_odd.wyo = f32[8,128]{1,0:T(8,128)S(1)} collective-permute-done((f32[8,128]{1,0:T(8,128)S(1)}, f32[8,128]{1,0:T(8,128)S(1)}, u32[]{:S(2)}, u32[]{:S(2)}) %collective-permute-start.5) | collective-permute-done | bytes 4128 | tf_op jit(solution)/shard_map/ppermute | solution.py:44
  39.1 1.5 %collective-permute-start.6 = (f32[24,128]{1,0:T(8,128)S(1)}, f32[24,128]{1,0:T(8,128)S(1)}, u32[]{:S(2)}, u32[]{:S(2)}) collective-permute-start(f32[24,128]{1,0:T(8,128)S(1)} %get-tuple-element.42), channel_id=1, source_target_pairs={{0,4},{4,0},{8,12},{12,8},{16,20},{20,16},{24,28},{28,24},{1,5},{5... | collective-permute-start | bytes 36872 | tf_op jit(solution)/shard_map/ppermute | solution.py:45
  40.6 2.5 %collective-permute-start.7 = (f32[24,128]{1,0:T(8,128)S(1)}, f32[24,128]{1,0:T(8,128)S(1)}, u32[]{:S(2)}, u32[]{:S(2)}) collective-permute-start(f32[24,128]{1,0:T(8,128)S(1)} %get-tuple-element.43), channel_id=1, source_target_pairs={{4,8},{8,4},{12,16},{16,12},{20,24},{24,20},{5,9},{9,5},{13,17},{1... | collective-permute-start | bytes 36872 | tf_op jit(solution)/shard_map/ppermute | solution.py:44
  43.1 0.0 collective-permute-done.6.fxe
  43.1 4.0 %collective-permute-done.7.fxo = f32[24,128]{1,0:T(8,128)S(1)} collective-permute-done((f32[24,128]{1,0:T(8,128)S(1)}, f32[24,128]{1,0:T(8,128)S(1)}, u32[]{:S(2)}, u32[]{:S(2)}) %collective-permute-start.7) | collective-permute-done | bytes 12320 | tf_op jit(solution)/shard_map/ppermute | solution.py:44
  47.1 0.0 all-to-all-done.got
  47.1 1.7 %wall_last.1 = (f32[3,2,4,128]{3,2,1,0:T(4,128)}, f32[3,2,4,128]{3,2,1,0:T(4,128)}) custom-call(f32[2,4,40,8,128]{4,3,2,1,0:T(8,128)S(1)} %get-tuple-element.28.weights, f32[2,4,40,8,128]{4,3,2,1,0:T(8,128)S(1)} %get-tuple-element.35.end_weights, f32[32,32,128]{2,1,0:T(8,128)S(1)} %all-to-all-done.got, f32[3,2,4,128]{3,2,1,0:T(4,128)S(1)} %get-tuple-element.37.base1, ...), custom_call_target="tpu_custom_call" | custom-call | tf_op jit(solution)/shard_map/wall_last/pallas_call | solution.py:656
  (6 shorter events, 0.0 us)
Async XLA Ops:
  2.6 25.8 %copy-start.3 = (f32[3,3,2,4,128]{4,3,2,1,0:T(4,128)S(1)}, f32[3,3,2,4,128]{4,3,2,1,0:T(4,128)}, u32[]{:S(2)}) copy-start(f32[3,3,2,4,128]{4,3,2,1,0:T(4,128)} %get-tuple-element.25.wall) | copy-start | bytes 110596
  2.6 2.6 %collective-permute-start = (f32[80,128]{1,0:T(8,128)}, f32[80,128]{1,0:T(8,128)S(1)}, u32[]{:S(2)}, u32[]{:S(2)}) collective-permute-start(f32[80,128]{1,0:T(8,128)} %get-tuple-element.26), channel_id=1, source_target_pairs={{0,1},{1,0},{2,3},{3,2},{4,5},{5,4},{6,7},{7,6},{8,9},{9,8},{10,11... | collective-permute-start | bytes 122888 | tf_op jit(solution)/shard_map/ppermute | solution.py:45
  2.6 5.5 %collective-permute-start.1 = (f32[80,128]{1,0:T(8,128)}, f32[80,128]{1,0:T(8,128)S(1)}, u32[]{:S(2)}, u32[]{:S(2)}) collective-permute-start(f32[80,128]{1,0:T(8,128)} %get-tuple-element.27), channel_id=1, source_target_pairs={{1,2},{2,1},{5,6},{6,5},{9,10},{10,9},{13,14},{14,13},{17,18},{18,... | collective-permute-start | bytes 122888 | tf_op jit(solution)/shard_map/ppermute | solution.py:44
  8.2 0.9 %copy-start.4 = (f32[168,128]{1,0:T(8,128)S(1)}, f32[168,128]{1,0:T(8,128)}, u32[]{:S(2)}) copy-start(f32[168,128]{1,0:T(8,128)} %get-tuple-element.29.part_even) | copy-start | bytes 258052
  9.1 0.9 %copy-start.5 = (f32[168,128]{1,0:T(8,128)S(1)}, f32[168,128]{1,0:T(8,128)}, u32[]{:S(2)}) copy-start(f32[168,128]{1,0:T(8,128)} %get-tuple-element.30.part_odd) | copy-start | bytes 258052
  10.0 4.6 %collective-permute-start.2 = (f32[168,128]{1,0:T(8,128)S(1)}, f32[168,128]{1,0:T(8,128)S(1)}, u32[]{:S(2)}, u32[]{:S(2)}) collective-permute-start(f32[168,128]{1,0:T(8,128)S(1)} %get-tuple-element.31), channel_id=1, source_target_pairs={{0,4},{4,0},{8,12},{12,8},{16,20},{20,16},{24,28},{28,24},{1,5},{5... | collective-permute-start | bytes 258056 | tf_op jit(solution)/shard_map/ppermute | solution.py:45
  11.5 7.3 %collective-permute-start.3 = (f32[168,128]{1,0:T(8,128)S(1)}, f32[168,128]{1,0:T(8,128)S(1)}, u32[]{:S(2)}, u32[]{:S(2)}) collective-permute-start(f32[168,128]{1,0:T(8,128)S(1)} %get-tuple-element.32), channel_id=1, source_target_pairs={{4,8},{8,4},{12,16},{16,12},{20,24},{24,20},{5,9},{9,5},{13,17},{1... | collective-permute-start | bytes 258056 | tf_op jit(solution)/shard_map/ppermute | solution.py:44
  18.8 1.0 %copy-start = (f32[16,32,128]{2,1,0:T(8,128)S(1)}, f32[16,32,128]{2,1,0:T(8,128)}, u32[]{:S(2)}) copy-start(f32[16,32,128]{2,1,0:T(8,128)} %p.3) | copy-start | bytes 786436
  19.8 0.9 %copy-start.1 = (f32[16,32,128]{2,1,0:T(8,128)S(1)}, f32[16,32,128]{2,1,0:T(8,128)}, u32[]{:S(2)}) copy-start(f32[16,32,128]{2,1,0:T(8,128)} %q.3) | copy-start | bytes 786436
  20.7 0.9 %copy-start.2 = (f32[16,32,128]{2,1,0:T(8,128)S(1)}, f32[16,32,128]{2,1,0:T(8,128)}, u32[]{:S(2)}) copy-start(f32[16,32,128]{2,1,0:T(8,128)} %s.3) | copy-start | bytes 786436
  23.3 23.8 %all-to-all-start = ((f32[32,32,128]{2,1,0:T(8,128)}), f32[32,32,128]{2,1,0:T(8,128)S(1)}, u32[]{:S(2)}, u32[]{:S(2)}) async-start(f32[32,32,128]{2,1,0:T(8,128)} %get-tuple-element.36), calls=%async_computation | async-start | bytes 1048576 | tf_op jit(solution)/shard_map/all_to_all | solution.py:702
  33.9 2.6 %collective-permute-start.4 = (f32[8,128]{1,0:T(8,128)S(1)}, f32[8,128]{1,0:T(8,128)S(1)}, u32[]{:S(2)}, u32[]{:S(2)}) collective-permute-start(f32[8,128]{1,0:T(8,128)S(1)} %get-tuple-element.40), channel_id=1, source_target_pairs={{0,1},{1,0},{2,3},{3,2},{4,5},{5,4},{6,7},{7,6},{8,9},{9,8},{10,11... | collective-permute-start | bytes 12296 | tf_op jit(solution)/shard_map/ppermute | solution.py:45
  34.2 4.9 %collective-permute-start.5 = (f32[8,128]{1,0:T(8,128)S(1)}, f32[8,128]{1,0:T(8,128)S(1)}, u32[]{:S(2)}, u32[]{:S(2)}) collective-permute-start(f32[8,128]{1,0:T(8,128)S(1)} %get-tuple-element.41), channel_id=1, source_target_pairs={{1,2},{2,1},{5,6},{6,5},{9,10},{10,9},{13,14},{14,13},{17,18},{18,... | collective-permute-start | bytes 12296 | tf_op jit(solution)/shard_map/ppermute | solution.py:44
  39.1 4.0 %collective-permute-start.6 = (f32[24,128]{1,0:T(8,128)S(1)}, f32[24,128]{1,0:T(8,128)S(1)}, u32[]{:S(2)}, u32[]{:S(2)}) collective-permute-start(f32[24,128]{1,0:T(8,128)S(1)} %get-tuple-element.42), channel_id=1, source_target_pairs={{0,4},{4,0},{8,12},{12,8},{16,20},{20,16},{24,28},{28,24},{1,5},{5... | collective-permute-start | bytes 36872 | tf_op jit(solution)/shard_map/ppermute | solution.py:45
  40.6 6.5 %collective-permute-start.7 = (f32[24,128]{1,0:T(8,128)S(1)}, f32[24,128]{1,0:T(8,128)S(1)}, u32[]{:S(2)}, u32[]{:S(2)}) collective-permute-start(f32[24,128]{1,0:T(8,128)S(1)} %get-tuple-element.43), channel_id=1, source_target_pairs={{4,8},{8,4},{12,16},{16,12},{20,24},{24,20},{5,9},{9,5},{13,17},{1... | collective-permute-start | bytes 36872 | tf_op jit(solution)/shard_map/ppermute | solution.py:44

commit v4 on v3

--- a/solution.py
+++ b/solution.py
@@ -13,7 +13,6 @@
 LANES = 128
 SUB = 8
 VMEM_BYTES = 48 * 1024 * 1024
-ALL_VMEM = 67_000_000
 HBM = pl.BlockSpec(memory_space=pltpu.HBM)
 
 F32 = jnp.float32
@@ -24,8 +23,12 @@
     return pl.BlockSpec(memory_space=pltpu.VMEM)
 
 
-def params(limit=VMEM_BYTES):
-    return pltpu.CompilerParams(vmem_limit_bytes=limit)
+def params():
+    return pltpu.CompilerParams(vmem_limit_bytes=VMEM_BYTES)
+
+
+def vmem(*shape):
+    return pltpu.VMEM(shape, F32)
 
 
 def even_at(axis):
@@ -127,6 +130,10 @@
     place_edges(even_at("fx"), end(0, 0, 1, 0), end(1, 1, 0, rows - 1), fx_even, fx_odd)
 
 
+def in_hbm(*arrays):
+    return [pltpu.with_memory_space_constraint(v, pltpu.HBM) for v in arrays]
+
+
 def pad8(count):
     return (count + 7) // 8 * 8
 
@@ -134,21 +141,21 @@
 def pack_wy(p, q, s, jit, disp, vel):
     cx, cy = p.shape[0], p.shape[1]
     rows, cols = jit.shape[1], jit.shape[2]
-    wy_out = jax.ShapeDtypeStruct((pad8(4 * cx + 6 * rows), LANES), F32)
-    fx_out = jax.ShapeDtypeStruct((pad8(4 * cy + 6 * (cols + 2) + 2), LANES), F32)
+    wy_out = vmem(pad8(4 * cx + 6 * rows), LANES)
+    fx_out = vmem(pad8(4 * cy + 6 * (cols + 2) + 2), LANES)
     return pl.pallas_call(
         pack_wy_kernel,
         in_specs=[HBM] * 6,
         out_specs=[whole()] * 5,
-        out_shape=[wy_out, wy_out, fx_out, fx_out, jax.ShapeDtypeStruct((3,) + jit.shape, F32)],
+        out_shape=[wy_out, wy_out, fx_out, fx_out, vmem(3, *jit.shape)],
         scratch_shapes=[
             pltpu.VMEM((6, cx, SUB, LANES), F32),
             pltpu.VMEM((2, 4, cy, LANES), F32),
             pltpu.SemaphoreType.DMA((15,)),
         ],
-        compiler_params=params(ALL_VMEM),
+        compiler_params=params(),
         name="pack_wy",
-    )(p, q, s, jit, disp, vel)
+    )(*in_hbm(p, q, s, jit, disp, vel))
 
 
 def pack_fx_kernel(cx, cy, rows, cols, part_even, part_odd, got_even, got_odd, to_even, to_odd):
@@ -173,7 +180,7 @@
 
 
 def pack_fx(sizes, parts, got):
-    out = jax.ShapeDtypeStruct(parts[0].shape, F32)
+    out = vmem(*parts[0].shape)
     return pl.pallas_call(
         functools.partial(pack_fx_kernel, *sizes),
         in_specs=[whole()] * 4,
@@ -286,7 +293,7 @@
         out_specs=[whole()] * 2,
         out_shape=[
             jax.ShapeDtypeStruct(p.shape, F32),
-            jax.ShapeDtypeStruct((devices, 4 * SUB, LANES), F32),
+            vmem(devices, 4 * SUB, LANES),
         ],
         scratch_shapes=[
             pltpu.VMEM((cx + 2, cy + 2 * SUB, LANES), F32),
@@ -410,16 +417,21 @@
 
 
 def center_kernel(
-    cx, masks_in, wall, wye, wyo, weights, acc, end_masks, jpad, dpad, masks, sems
+    masks_in, p_in, q_in, s_in, wall, wye, wyo, weights, acc, end_masks, p, q, s,
+    jpad, dpad, masks, sems,
 ):
     rows, cols = wall.shape[2], wall.shape[3]
+    cx = p.shape[0]
     copies = {}
+    for k, pair in enumerate(((p_in, p), (q_in, q), (s_in, s))):
+        copies[k] = pltpu.make_async_copy(*pair, sems.at[rows * cols + k])
     for h in range(cols):
         for l in range(rows):
             copies[l, h] = pltpu.make_async_copy(
                 masks_in.at[l, h], masks.at[l, h], sems.at[l * cols + h]
             )
-            copies[l, h].start()
+    for copy in copies.values():
+        copy.start()
     first_sub = lax.broadcasted_iota(jnp.int32, (SUB, LANES), 0) < SUB // 2
     before, after = before_after(even_at("wy"), wye, wyo)
     fill_y(jpad, wall.at[0], before, after, 4 * cx)
@@ -450,25 +462,27 @@
         for l in range(rows):
             copies[l, h].wait()
             one_tile(l, h)
-
-
-def wall_center(cx, masks, wall, wy_got):
+    for k in range(3):
+        copies[k].wait()
+
+
+def wall_center(masks, grids, wall, wy_got):
     rows, cols = wall.shape[2], wall.shape[3]
-    stored = jax.ShapeDtypeStruct((rows, cols, STORED, SUB, LANES), F32)
+    stored = vmem(rows, cols, STORED, SUB, LANES)
     return pl.pallas_call(
-        functools.partial(center_kernel, cx),
-        in_specs=[HBM] + [whole()] * 3,
-        out_specs=[whole()] * 3,
-        out_shape=[stored, jax.ShapeDtypeStruct((rows, cols, 4, LANES, LANES), F32), stored],
+        center_kernel,
+        in_specs=[HBM] * 4 + [whole()] * 3,
+        out_specs=[whole()] * 6,
+        out_shape=[stored, vmem(rows, cols, 4, LANES, LANES), stored] + [vmem(*grids[0].shape)] * 3,
         scratch_shapes=[
-            pltpu.VMEM((3, rows + 2, SUB, LANES), F32),
-            pltpu.VMEM((3, rows + 2, SUB, LANES), F32),
+            vmem(3, rows + 2, SUB, LANES),
+            vmem(3, rows + 2, SUB, LANES),
             pltpu.VMEM(masks.shape, jnp.int32),
-            pltpu.SemaphoreType.DMA((rows * cols,)),
+            pltpu.SemaphoreType.DMA((rows * cols + 3,)),
         ],
         compiler_params=params(),
         name="wall_center",
-    )(masks, wall, *wy_got)
+    )(*in_hbm(masks, *grids), wall, *wy_got)
 
 
 def wall_kernel(
@@ -534,18 +548,18 @@
 def wall_first(cx, cy, wall, wy_got, fx_got, part, end_masks):
     rows, cols = wall.shape[2], wall.shape[3]
     edge = (pad8(3 * rows), LANES)
-    field = jax.ShapeDtypeStruct(wall.shape[1:], F32)
+    field = vmem(*wall.shape[1:])
     return pl.pallas_call(
         functools.partial(wall_kernel, cx, cy),
         in_specs=[whole()] * 7,
         out_specs=[whole()] * 6,
         out_shape=[
-            jax.ShapeDtypeStruct((rows, cols, STORED, SUB, LANES), F32),
+            vmem(rows, cols, STORED, SUB, LANES),
             field,
             field,
-            jax.ShapeDtypeStruct((rows, cols, LANES), F32),
-            jax.ShapeDtypeStruct(edge, F32),
-            jax.ShapeDtypeStruct(edge, F32),
+            vmem(rows, cols, LANES),
+            vmem(*edge),
+            vmem(*edge),
         ],
         scratch_shapes=[
             pltpu.VMEM((3, rows + 2, SUB, LANES), F32),
@@ -580,7 +594,7 @@
 
 def pack_base(base1, got):
     cols = base1.shape[2]
-    out = jax.ShapeDtypeStruct((pad8(3 * (cols + 2)), LANES), F32)
+    out = vmem(pad8(3 * (cols + 2)), LANES)
     return pl.pallas_call(
         pack_base_kernel,
         in_specs=[whole()] * 3,
@@ -695,10 +709,9 @@
     wy_got = exchange("wy", *sends)
     sends = pack_fx((cx, cy, rows, cols), (part_even, part_odd), wy_got)
     fx_got = exchange("fx", *sends)
-    weights, part, end_masks = wall_center(cx, bond_masks, wall, wy_got)
-    pressure_out, slots = grid_steps(
-        pressure, pressure_prev, speed_sq, wy_got, fx_got, target, fx_count, wy_count
-    )
+    grids = (pressure, pressure_prev, speed_sq)
+    weights, part, end_masks, *grids = wall_center(bond_masks, grids, wall, wy_got)
+    pressure_out, slots = grid_steps(*grids, wy_got, fx_got, target, fx_count, wy_count)
     got = lax.all_to_all(slots, ("fx", "wy"), split_axis=0, concat_axis=0, tiled=True)
     end_weights, vel1, base1, totals, *sends = wall_first(
         cx, cy, wall, wy_got, fx_got, part, end_masks

time: 49.3 us -> 47.9 us (0.972)
  waiting for transfers between devices: 13.7 us -> 9.31 us
  local copies, waits for them, and re-layouts: 4.63 us -> 7.11 us
  starting transfers between devices: 18.2 us -> 19.1 us
    ppermute x4, waiting for transfers between devices: 13.7 us -> 9.29 us  [exchange(): got_odd = lax.ppermute(to_odd, axis, pair_list(count, 1))]
    unnamed x12, local copies, waits for them, and re-layouts: 4.63 us -> 7.11 us
    all_to_all x1, starting transfers between devices: 5.06 us -> 6.1 us  [per_device(): lax.all_to_all(slots, ('fx', 'wy'), split_axis=0, concat_axis=0, tiled=True)]
    pallas_call x1, Pallas kernels: 1.92 us -> 1.23 us  [pack_wy(): pl.pallas_call(pack_wy_kernel, in_specs=[HBM] * 6, out_specs=[whole()] *...]
  transfers between devices with their start and end apart: 9 -> 9, of which waited for: 4 -> 3; matrix products, arithmetic and copies ran while one was open for 1% -> 2% of each run, Pallas kernels for 11% -> 12%
where the time goes in v4:
time: 47.9 us; the launch traced here: 47.4 us
  starting transfers between devices  19.1 us (40%)
  Pallas kernels  10.4 us (22%)
  waiting for transfers between devices  9.31 us (19%)
  local copies, waits for them, and re-layouts  7.11 us (15%)
  between operations  0.78 us (2%)
  other arithmetic  0.71 us (1%)
    ppermute x4, starting transfers between devices, exchange(): got_odd = lax.ppermute(to_odd, axis, pair_list(count, 1))  9.7 us
    ppermute x4, waiting for transfers between devices, exchange(): got_odd = lax.ppermute(to_odd, axis, pair_list(count, 1))  9.29 us
    unnamed x12, local copies, waits for them, and re-layouts  7.11 us
    all_to_all x1, starting transfers between devices, per_device(): lax.all_to_all(slots, ('fx', 'wy'), split_axis=0, concat_axis=0, tiled=True)  6.1 us
    pallas_call x1, Pallas kernels, wall_center(): pl.pallas_call(center_kernel, in_specs=[HBM] * 4 + [whole()] * 3, out_spe...  3.56 us
    ppermute x4, starting transfers between devices, exchange(): got_even = lax.ppermute(to_even, axis, pair_list(count, 0))  3.32 us
    pallas_call x1, Pallas kernels, wall_first(): pl.pallas_call(functools.partial(wall_kernel, cx, cy), in_specs=[whole()]...  2.26 us
    pallas_call x1, Pallas kernels, wall_last(): pl.pallas_call(last_kernel, in_specs=[whole()] * 10, out_specs=[whole()]...  1.67 us
  transfers between devices with their start and end apart: 9, of which 3 were waited for; matrix products, arithmetic and copies ran while one was open for 2% of the time, Pallas kernels for 12%

profile of v4, /device:TPU:12, one launch (start us, length us, event | category | flops | bytes accessed | tf_op | source)
XLA Modules:
  0.0 47.4 jit_solution(14249601201730209557)
XLA Ops:
  0.6 1.2 %pack_wy.1 = (f32[80,128]{1,0:T(8,128)S(1)}, f32[80,128]{1,0:T(8,128)S(1)}, f32[168,128]{1,0:T(8,128)S(1)}, f32[168,128]{1,0:T(8,128)S(1)}, f32[3,3,2,4,128]{4,3,2,1,0:T(4,128)S(1)}) custom-call(f32[16,32,128]{2,1,0:T(8,128)} %p_in.1, f32[16,32,128]{2,1,0:T(8,128)} %q_in.1, f32[16,32,128]{2,1,0:T(8,128)} %s_in.1, f32[3,2,4,128]{3,2,1,0:T(4,128)} %jit_in.1, ...), custom_call_target="tpu_custom_call" | custom-call | tf_op jit(solution)/shard_map/pack_wy/pallas_call | solution.py:146
  1.9 0.1 collective-permute-start
  1.9 2.5 %collective-permute-start.1 = (f32[80,128]{1,0:T(8,128)S(1)}, f32[80,128]{1,0:T(8,128)S(1)}, u32[]{:S(2)}, u32[]{:S(2)}) collective-permute-start(f32[80,128]{1,0:T(8,128)S(1)} %get-tuple-element.30), channel_id=1, source_target_pairs={{1,2},{2,1},{5,6},{6,5},{9,10},{10,9},{13,14},{14,13},{17,18},{18,... | collective-permute-start | bytes 122888 | tf_op jit(solution)/shard_map/ppermute | solution.py:47
  4.5 0.0 collective-permute-done.wye.got_even
  4.5 2.8 %collective-permute-done.1.wyo.got_odd = f32[80,128]{1,0:T(8,128)S(1)} collective-permute-done((f32[80,128]{1,0:T(8,128)S(1)}, f32[80,128]{1,0:T(8,128)S(1)}, u32[]{:S(2)}, u32[]{:S(2)}) %collective-permute-start.1) | collective-permute-done | bytes 40992 | tf_op jit(solution)/shard_map/ppermute | solution.py:47
  7.3 1.6 %collective-permute-start.2 = (f32[168,128]{1,0:T(8,128)S(1)}, f32[168,128]{1,0:T(8,128)S(1)}, u32[]{:S(2)}, u32[]{:S(2)}) collective-permute-start(f32[168,128]{1,0:T(8,128)S(1)} %get-tuple-element.34), channel_id=1, source_target_pairs={{0,4},{4,0},{8,12},{12,8},{16,20},{20,16},{24,28},{28,24},{1,5},{5... | collective-permute-start | bytes 258056 | tf_op jit(solution)/shard_map/ppermute | solution.py:48
  8.9 2.3 %collective-permute-start.3 = (f32[168,128]{1,0:T(8,128)S(1)}, f32[168,128]{1,0:T(8,128)S(1)}, u32[]{:S(2)}, u32[]{:S(2)}) collective-permute-start(f32[168,128]{1,0:T(8,128)S(1)} %get-tuple-element.35), channel_id=1, source_target_pairs={{4,8},{8,4},{12,16},{16,12},{20,24},{24,20},{5,9},{9,5},{13,17},{1... | collective-permute-start | bytes 258056 | tf_op jit(solution)/shard_map/ppermute | solution.py:47
  11.2 0.7 %fusion.3.target = s32[4,128]{1,0:T(4,128)S(1)} fusion(s32[4,128]{1,0:T(4,128)} %bitcast.17, s32[512]{0:T(512)} %param.17), kind=kLoop, calls=%fused_computation.13 | loop fusion | flops 22528 | bytes 6144 | tf_op jit(solution)/shard_map/add | solution.py:702
  11.9 3.6 %wall_center.1 = (f32[2,4,40,8,128]{4,3,2,1,0:T(8,128)S(1)}, f32[2,4,4,128,128]{4,3,2,1,0:T(8,128)S(1)}, f32[2,4,40,8,128]{4,3,2,1,0:T(8,128)S(1)}, f32[16,32,12...) custom-call(s32[2,4,9,128,128]{4,3,2,1,0:T(8,128)} %masks_in.1, f32[16,32,128]{2,1,0:T(8,128)} %p_in.1, ...), custom_call_target="tpu_custom_call" | custom-call | tf_op jit(solution)/shard_map/wall_center/pallas_call | solution.py:472
  15.5 1.1 %copy-done = f32[2,4,40,8,128]{4,3,2,1,0:T(8,128)} copy-done((f32[2,4,40,8,128]{4,3,2,1,0:T(8,128)}, f32[2,4,40,8,128]{4,3,2,1,0:T(8,128)S(1)}, u32[]{:S(2)}) %copy-start) | copy-done | bytes 1310744
  16.5 1.1 %copy-done.4 = f32[2,4,40,8,128]{4,3,2,1,0:T(8,128)} copy-done((f32[2,4,40,8,128]{4,3,2,1,0:T(8,128)}, f32[2,4,40,8,128]{4,3,2,1,0:T(8,128)S(1)}, u32[]{:S(2)}) %copy-start.4) | copy-done | bytes 1310744
  17.6 0.0 collective-permute-done.2.fxe
  17.6 0.0 collective-permute-done.3.fxo
  17.6 1.6 %grid_steps.1 = (f32[16,32,128]{2,1,0:T(8,128)}, f32[32,32,128]{2,1,0:T(8,128)}) custom-call(f32[16,32,128]{2,1,0:T(8,128)S(1)} %get-tuple-element.39.p, f32[16,32,128]{2,1,0:T(8,128)S(1)} %get-tuple-element.40.q, f32[16,32,128]{2,1,0:T(8,128)S(1)} %get-tuple-element.41.s, f32[80,128]{1,0:T(8,128)S(1)} %collective-permute-done.wye.got_even, ...), custom_call_target="tpu_custom_call" | custom-call | tf_op jit(solution)/shard_map/grid_steps/pallas_call | solution.py:290
  19.2 6.1 %all-to-all-start = ((f32[32,32,128]{2,1,0:T(8,128)}), f32[32,32,128]{2,1,0:T(8,128)S(1)}, u32[]{:S(2)}, u32[]{:S(2)}) async-start(f32[32,32,128]{2,1,0:T(8,128)} %get-tuple-element.42), calls=%async_computation | async-start | bytes 1048576 | tf_op jit(solution)/shard_map/all_to_all | solution.py:715
  25.4 0.0 copy-start.5
  25.4 1.3 %copy-done.5 = f32[2,4,40,8,128]{4,3,2,1,0:T(8,128)S(1)} copy-done((f32[2,4,40,8,128]{4,3,2,1,0:T(8,128)S(1)}, f32[2,4,40,8,128]{4,3,2,1,0:T(8,128)}, u32[]{:S(2)}) %copy-start.5) | copy-done | bytes 1310744
  26.7 2.3 %wall_first.1 = (f32[2,4,40,8,128]{4,3,2,1,0:T(8,128)S(1)}, f32[3,2,4,128]{3,2,1,0:T(4,128)S(1)}, f32[3,2,4,128]{3,2,1,0:T(4,128)S(1)}, f32[2,4,128]{2,1,0:T(4,1...) custom-call(f32[3,3,2,4,128]{4,3,2,1,0:T(4,128)S(1)} %get-tuple-element.28.wall, ...), custom_call_target="tpu_custom_call" | custom-call | tf_op jit(solution)/shard_map/wall_first/pallas_call | solution.py:552
  28.9 0.0 copy-start.2
  29.0 1.0 %copy-done.2 = f32[2,4,40,8,128]{4,3,2,1,0:T(8,128)} copy-done((f32[2,4,40,8,128]{4,3,2,1,0:T(8,128)}, f32[2,4,40,8,128]{4,3,2,1,0:T(8,128)S(1)}, u32[]{:S(2)}) %copy-start.2) | copy-done | bytes 1310744
  30.0 0.1 collective-permute-start.4
  30.2 2.4 %collective-permute-start.5 = (f32[8,128]{1,0:T(8,128)S(1)}, f32[8,128]{1,0:T(8,128)S(1)}, u32[]{:S(2)}, u32[]{:S(2)}) collective-permute-start(f32[8,128]{1,0:T(8,128)S(1)} %get-tuple-element.47), channel_id=1, source_target_pairs={{1,2},{2,1},{5,6},{6,5},{9,10},{10,9},{13,14},{14,13},{17,18},{18,... | collective-permute-start | bytes 12296 | tf_op jit(solution)/shard_map/ppermute | solution.py:47
  32.6 0.0 collective-permute-done.4.got_even.wye
  32.6 2.5 %collective-permute-done.5.got_odd.wyo = f32[8,128]{1,0:T(8,128)S(1)} collective-permute-done((f32[8,128]{1,0:T(8,128)S(1)}, f32[8,128]{1,0:T(8,128)S(1)}, u32[]{:S(2)}, u32[]{:S(2)}) %collective-permute-start.5) | collective-permute-done | bytes 4128 | tf_op jit(solution)/shard_map/ppermute | solution.py:47
  35.1 1.5 %collective-permute-start.6 = (f32[24,128]{1,0:T(8,128)S(1)}, f32[24,128]{1,0:T(8,128)S(1)}, u32[]{:S(2)}, u32[]{:S(2)}) collective-permute-start(f32[24,128]{1,0:T(8,128)S(1)} %get-tuple-element.48), channel_id=1, source_target_pairs={{0,4},{4,0},{8,12},{12,8},{16,20},{20,16},{24,28},{28,24},{1,5},{5... | collective-permute-start | bytes 36872 | tf_op jit(solution)/shard_map/ppermute | solution.py:48
  36.6 2.5 %collective-permute-start.7 = (f32[24,128]{1,0:T(8,128)S(1)}, f32[24,128]{1,0:T(8,128)S(1)}, u32[]{:S(2)}, u32[]{:S(2)}) collective-permute-start(f32[24,128]{1,0:T(8,128)S(1)} %get-tuple-element.49), channel_id=1, source_target_pairs={{4,8},{8,4},{12,16},{16,12},{20,24},{24,20},{5,9},{9,5},{13,17},{1... | collective-permute-start | bytes 36872 | tf_op jit(solution)/shard_map/ppermute | solution.py:47
  39.1 0.0 collective-permute-done.6.fxe
  39.1 4.0 %collective-permute-done.7.fxo = f32[24,128]{1,0:T(8,128)S(1)} collective-permute-done((f32[24,128]{1,0:T(8,128)S(1)}, f32[24,128]{1,0:T(8,128)S(1)}, u32[]{:S(2)}, u32[]{:S(2)}) %collective-permute-start.7) | collective-permute-done | bytes 12320 | tf_op jit(solution)/shard_map/ppermute | solution.py:47
  43.1 0.0 all-to-all-done.got
  43.1 1.3 %copy-done.1 = f32[2,4,40,8,128]{4,3,2,1,0:T(8,128)S(1)} copy-done((f32[2,4,40,8,128]{4,3,2,1,0:T(8,128)S(1)}, f32[2,4,40,8,128]{4,3,2,1,0:T(8,128)}, u32[]{:S(2)}) %copy-start.1) | copy-done | bytes 1310744
  44.4 1.3 %copy-done.3 = f32[2,4,40,8,128]{4,3,2,1,0:T(8,128)S(1)} copy-done((f32[2,4,40,8,128]{4,3,2,1,0:T(8,128)S(1)}, f32[2,4,40,8,128]{4,3,2,1,0:T(8,128)}, u32[]{:S(2)}) %copy-start.3) | copy-done | bytes 1310744
  45.8 1.7 %wall_last.1 = (f32[3,2,4,128]{3,2,1,0:T(4,128)}, f32[3,2,4,128]{3,2,1,0:T(4,128)}) custom-call(f32[2,4,40,8,128]{4,3,2,1,0:T(8,128)S(1)} %copy-done.1, f32[2,4,40,8,128]{4,3,2,1,0:T(8,128)S(1)} %copy-done.3, f32[32,32,128]{2,1,0:T(8,128)S(1)} %all-to-all-done.got, f32[3,2,4,128]{3,2,1,0:T(4,128)S(1)} %get-tuple-element.43.base1, ...), custom_call_target="tpu_custom_call" | custom-call | tf_op jit(solution)/shard_map/wall_last/pallas_call | solution.py:670
  (6 shorter events, 0.0 us)
Async XLA Ops:
  1.9 2.6 %collective-permute-start = (f32[80,128]{1,0:T(8,128)S(1)}, f32[80,128]{1,0:T(8,128)S(1)}, u32[]{:S(2)}, u32[]{:S(2)}) collective-permute-start(f32[80,128]{1,0:T(8,128)S(1)} %get-tuple-element.29), channel_id=1, source_target_pairs={{0,1},{1,0},{2,3},{3,2},{4,5},{5,4},{6,7},{7,6},{8,9},{9,8},{10,11... | collective-permute-start | bytes 122888 | tf_op jit(solution)/shard_map/ppermute | solution.py:48
  1.9 5.3 %collective-permute-start.1 = (f32[80,128]{1,0:T(8,128)S(1)}, f32[80,128]{1,0:T(8,128)S(1)}, u32[]{:S(2)}, u32[]{:S(2)}) collective-permute-start(f32[80,128]{1,0:T(8,128)S(1)} %get-tuple-element.30), channel_id=1, source_target_pairs={{1,2},{2,1},{5,6},{6,5},{9,10},{10,9},{13,14},{14,13},{17,18},{18,... | collective-permute-start | bytes 122888 | tf_op jit(solution)/shard_map/ppermute | solution.py:47
  7.3 10.3 %collective-permute-start.2 = (f32[168,128]{1,0:T(8,128)S(1)}, f32[168,128]{1,0:T(8,128)S(1)}, u32[]{:S(2)}, u32[]{:S(2)}) collective-permute-start(f32[168,128]{1,0:T(8,128)S(1)} %get-tuple-element.34), channel_id=1, source_target_pairs={{0,4},{4,0},{8,12},{12,8},{16,20},{20,16},{24,28},{28,24},{1,5},{5... | collective-permute-start | bytes 258056 | tf_op jit(solution)/shard_map/ppermute | solution.py:48
  8.9 8.7 %collective-permute-start.3 = (f32[168,128]{1,0:T(8,128)S(1)}, f32[168,128]{1,0:T(8,128)S(1)}, u32[]{:S(2)}, u32[]{:S(2)}) collective-permute-start(f32[168,128]{1,0:T(8,128)S(1)} %get-tuple-element.35), channel_id=1, source_target_pairs={{4,8},{8,4},{12,16},{16,12},{20,24},{24,20},{5,9},{9,5},{13,17},{1... | collective-permute-start | bytes 258056 | tf_op jit(solution)/shard_map/ppermute | solution.py:47
  15.5 1.1 %copy-start = (f32[2,4,40,8,128]{4,3,2,1,0:T(8,128)}, f32[2,4,40,8,128]{4,3,2,1,0:T(8,128)S(1)}, u32[]{:S(2)}) copy-start(f32[2,4,40,8,128]{4,3,2,1,0:T(8,128)S(1)} %get-tuple-element.31.weights) | copy-start | bytes 3932164
  16.5 1.1 %copy-start.4 = (f32[2,4,40,8,128]{4,3,2,1,0:T(8,128)}, f32[2,4,40,8,128]{4,3,2,1,0:T(8,128)S(1)}, u32[]{:S(2)}) copy-start(f32[2,4,40,8,128]{4,3,2,1,0:T(8,128)S(1)} %get-tuple-element.37.end_masks) | copy-start | bytes 3932164
  19.2 23.9 %all-to-all-start = ((f32[32,32,128]{2,1,0:T(8,128)}), f32[32,32,128]{2,1,0:T(8,128)S(1)}, u32[]{:S(2)}, u32[]{:S(2)}) async-start(f32[32,32,128]{2,1,0:T(8,128)} %get-tuple-element.42), calls=%async_computation | async-start | bytes 1048576 | tf_op jit(solution)/shard_map/all_to_all | solution.py:715
  25.4 1.3 %copy-start.5 = (f32[2,4,40,8,128]{4,3,2,1,0:T(8,128)S(1)}, f32[2,4,40,8,128]{4,3,2,1,0:T(8,128)}, u32[]{:S(2)}) copy-start(f32[2,4,40,8,128]{4,3,2,1,0:T(8,128)} %copy-done.4) | copy-start | bytes 3932164
  28.9 1.1 %copy-start.2 = (f32[2,4,40,8,128]{4,3,2,1,0:T(8,128)}, f32[2,4,40,8,128]{4,3,2,1,0:T(8,128)S(1)}, u32[]{:S(2)}) copy-start(f32[2,4,40,8,128]{4,3,2,1,0:T(8,128)S(1)} %get-tuple-element.38.end_weights) | copy-start | bytes 3932164
  30.0 2.6 %collective-permute-start.4 = (f32[8,128]{1,0:T(8,128)S(1)}, f32[8,128]{1,0:T(8,128)S(1)}, u32[]{:S(2)}, u32[]{:S(2)}) collective-permute-start(f32[8,128]{1,0:T(8,128)S(1)} %get-tuple-element.46), channel_id=1, source_target_pairs={{0,1},{1,0},{2,3},{3,2},{4,5},{5,4},{6,7},{7,6},{8,9},{9,8},{10,11... | collective-permute-start | bytes 12296 | tf_op jit(solution)/shard_map/ppermute | solution.py:48
  30.2 4.9 %collective-permute-start.5 = (f32[8,128]{1,0:T(8,128)S(1)}, f32[8,128]{1,0:T(8,128)S(1)}, u32[]{:S(2)}, u32[]{:S(2)}) collective-permute-start(f32[8,128]{1,0:T(8,128)S(1)} %get-tuple-element.47), channel_id=1, source_target_pairs={{1,2},{2,1},{5,6},{6,5},{9,10},{10,9},{13,14},{14,13},{17,18},{18,... | collective-permute-start | bytes 12296 | tf_op jit(solution)/shard_map/ppermute | solution.py:47
  35.1 4.0 %collective-permute-start.6 = (f32[24,128]{1,0:T(8,128)S(1)}, f32[24,128]{1,0:T(8,128)S(1)}, u32[]{:S(2)}, u32[]{:S(2)}) collective-permute-start(f32[24,128]{1,0:T(8,128)S(1)} %get-tuple-element.48), channel_id=1, source_target_pairs={{0,4},{4,0},{8,12},{12,8},{16,20},{20,16},{24,28},{28,24},{1,5},{5... | collective-permute-start | bytes 36872 | tf_op jit(solution)/shard_map/ppermute | solution.py:48
  36.6 6.5 %collective-permute-start.7 = (f32[24,128]{1,0:T(8,128)S(1)}, f32[24,128]{1,0:T(8,128)S(1)}, u32[]{:S(2)}, u32[]{:S(2)}) collective-permute-start(f32[24,128]{1,0:T(8,128)S(1)} %get-tuple-element.49), channel_id=1, source_target_pairs={{4,8},{8,4},{12,16},{16,12},{20,24},{24,20},{5,9},{9,5},{13,17},{1... | collective-permute-start | bytes 36872 | tf_op jit(solution)/shard_map/ppermute | solution.py:47
  43.1 1.3 %copy-start.1 = (f32[2,4,40,8,128]{4,3,2,1,0:T(8,128)S(1)}, f32[2,4,40,8,128]{4,3,2,1,0:T(8,128)}, u32[]{:S(2)}) copy-start(f32[2,4,40,8,128]{4,3,2,1,0:T(8,128)} %copy-done) | copy-start | bytes 3932164
  44.4 1.3 %copy-start.3 = (f32[2,4,40,8,128]{4,3,2,1,0:T(8,128)S(1)}, f32[2,4,40,8,128]{4,3,2,1,0:T(8,128)}, u32[]{:S(2)}) copy-start(f32[2,4,40,8,128]{4,3,2,1,0:T(8,128)} %copy-done.2) | copy-start | bytes 3932164

commit v5 on v4

--- a/solution.py
+++ b/solution.py
@@ -12,7 +12,7 @@
 REACH = 3.0
 LANES = 128
 SUB = 8
-VMEM_BYTES = 48 * 1024 * 1024
+VMEM_BYTES = 32 * 1024 * 1024
 HBM = pl.BlockSpec(memory_space=pltpu.HBM)
 
 F32 = jnp.float32
@@ -468,12 +468,13 @@
 
 def wall_center(masks, grids, wall, wy_got):
     rows, cols = wall.shape[2], wall.shape[3]
-    stored = vmem(rows, cols, STORED, SUB, LANES)
+    stored = jax.ShapeDtypeStruct((rows, cols, STORED, SUB, LANES), F32)
+    sums = jax.ShapeDtypeStruct((rows, cols, 4, LANES, LANES), F32)
     return pl.pallas_call(
         center_kernel,
         in_specs=[HBM] * 4 + [whole()] * 3,
         out_specs=[whole()] * 6,
-        out_shape=[stored, vmem(rows, cols, 4, LANES, LANES), stored] + [vmem(*grids[0].shape)] * 3,
+        out_shape=[stored, sums, stored] + [vmem(*grids[0].shape)] * 3,
         scratch_shapes=[
             vmem(3, rows + 2, SUB, LANES),
             vmem(3, rows + 2, SUB, LANES),
@@ -554,7 +555,7 @@
         in_specs=[whole()] * 7,
         out_specs=[whole()] * 6,
         out_shape=[
-            vmem(rows, cols, STORED, SUB, LANES),
+            jax.ShapeDtypeStruct((rows, cols, STORED, SUB, LANES), F32),
             field,
             field,
             vmem(rows, cols, LANES),

time: 47.9 us -> 47.9 us (level)
  no operation moved by 1% of the time
where the time goes in v5:
time: 47.9 us; the launch traced here: 47.4 us
  starting transfers between devices  19.1 us (40%)
  Pallas kernels  10.4 us (22%)
  waiting for transfers between devices  9.31 us (19%)
  local copies, waits for them, and re-layouts  7.11 us (15%)
  between operations  0.78 us (2%)
  other arithmetic  0.71 us (1%)
    ppermute x4, starting transfers between devices, exchange(): got_odd = lax.ppermute(to_odd, axis, pair_list(count, 1))  9.7 us
    ppermute x4, waiting for transfers between devices, exchange(): got_odd = lax.ppermute(to_odd, axis, pair_list(count, 1))  9.29 us
    unnamed x12, local copies, waits for them, and re-layouts  7.11 us
    all_to_all x1, starting transfers between devices, per_device(): lax.all_to_all(slots, ('fx', 'wy'), split_axis=0, concat_axis=0, tiled=True)  6.1 us
    pallas_call x1, Pallas kernels, wall_center(): pl.pallas_call(center_kernel, in_specs=[HBM] * 4 + [whole()] * 3, out_spe...  3.56 us
    ppermute x4, starting transfers between devices, exchange(): got_even = lax.ppermute(to_even, axis, pair_list(count, 0))  3.32 us
    pallas_call x1, Pallas kernels, wall_first(): pl.pallas_call(functools.partial(wall_kernel, cx, cy), in_specs=[whole()]...  2.26 us
    pallas_call x1, Pallas kernels, wall_last(): pl.pallas_call(last_kernel, in_specs=[whole()] * 10, out_specs=[whole()]...  1.67 us
  transfers between devices with their start and end apart: 9, of which 3 were waited for; matrix products, arithmetic and copies ran while one was open for 2% of the time, Pallas kernels for 12%

profile of v5, /device:TPU:12, one launch (start us, length us, event | category | flops | bytes accessed | tf_op | source)
XLA Modules:
  0.0 47.4 jit_solution(6194208234730273990)
XLA Ops:
  0.6 1.2 %pack_wy.1 = (f32[80,128]{1,0:T(8,128)S(1)}, f32[80,128]{1,0:T(8,128)S(1)}, f32[168,128]{1,0:T(8,128)S(1)}, f32[168,128]{1,0:T(8,128)S(1)}, f32[3,3,2,4,128]{4,3,2,1,0:T(4,128)S(1)}) custom-call(f32[16,32,128]{2,1,0:T(8,128)} %p_in.1, f32[16,32,128]{2,1,0:T(8,128)} %q_in.1, f32[16,32,128]{2,1,0:T(8,128)} %s_in.1, f32[3,2,4,128]{3,2,1,0:T(4,128)} %jit_in.1, ...), custom_call_target="tpu_custom_call" | custom-call | tf_op jit(solution)/shard_map/pack_wy/pallas_call | solution.py:146
  1.9 0.1 collective-permute-start
  1.9 2.5 %collective-permute-start.1 = (f32[80,128]{1,0:T(8,128)S(1)}, f32[80,128]{1,0:T(8,128)S(1)}, u32[]{:S(2)}, u32[]{:S(2)}) collective-permute-start(f32[80,128]{1,0:T(8,128)S(1)} %get-tuple-element.30), channel_id=1, source_target_pairs={{1,2},{2,1},{5,6},{6,5},{9,10},{10,9},{13,14},{14,13},{17,18},{18,... | collective-permute-start | bytes 122888 | tf_op jit(solution)/shard_map/ppermute | solution.py:47
  4.5 0.0 collective-permute-done.wye.got_even
  4.5 2.8 %collective-permute-done.1.wyo.got_odd = f32[80,128]{1,0:T(8,128)S(1)} collective-permute-done((f32[80,128]{1,0:T(8,128)S(1)}, f32[80,128]{1,0:T(8,128)S(1)}, u32[]{:S(2)}, u32[]{:S(2)}) %collective-permute-start.1) | collective-permute-done | bytes 40992 | tf_op jit(solution)/shard_map/ppermute | solution.py:47
  7.3 1.6 %collective-permute-start.2 = (f32[168,128]{1,0:T(8,128)S(1)}, f32[168,128]{1,0:T(8,128)S(1)}, u32[]{:S(2)}, u32[]{:S(2)}) collective-permute-start(f32[168,128]{1,0:T(8,128)S(1)} %get-tuple-element.34), channel_id=1, source_target_pairs={{0,4},{4,0},{8,12},{12,8},{16,20},{20,16},{24,28},{28,24},{1,5},{5... | collective-permute-start | bytes 258056 | tf_op jit(solution)/shard_map/ppermute | solution.py:48
  8.9 2.3 %collective-permute-start.3 = (f32[168,128]{1,0:T(8,128)S(1)}, f32[168,128]{1,0:T(8,128)S(1)}, u32[]{:S(2)}, u32[]{:S(2)}) collective-permute-start(f32[168,128]{1,0:T(8,128)S(1)} %get-tuple-element.35), channel_id=1, source_target_pairs={{4,8},{8,4},{12,16},{16,12},{20,24},{24,20},{5,9},{9,5},{13,17},{1... | collective-permute-start | bytes 258056 | tf_op jit(solution)/shard_map/ppermute | solution.py:47
  11.2 0.7 %fusion.3.target = s32[4,128]{1,0:T(4,128)S(1)} fusion(s32[4,128]{1,0:T(4,128)} %bitcast.17, s32[512]{0:T(512)} %param.17), kind=kLoop, calls=%fused_computation.13 | loop fusion | flops 22528 | bytes 6144 | tf_op jit(solution)/shard_map/add | solution.py:703
  11.9 3.6 %wall_center.1 = (f32[2,4,40,8,128]{4,3,2,1,0:T(8,128)S(1)}, f32[2,4,4,128,128]{4,3,2,1,0:T(8,128)S(1)}, f32[2,4,40,8,128]{4,3,2,1,0:T(8,128)S(1)}, f32[16,32,12...) custom-call(s32[2,4,9,128,128]{4,3,2,1,0:T(8,128)} %masks_in.1, f32[16,32,128]{2,1,0:T(8,128)} %p_in.1, ...), custom_call_target="tpu_custom_call" | custom-call | tf_op jit(solution)/shard_map/wall_center/pallas_call | solution.py:473
  15.5 1.1 %copy-done = f32[2,4,40,8,128]{4,3,2,1,0:T(8,128)} copy-done((f32[2,4,40,8,128]{4,3,2,1,0:T(8,128)}, f32[2,4,40,8,128]{4,3,2,1,0:T(8,128)S(1)}, u32[]{:S(2)}) %copy-start) | copy-done | bytes 1310744
  16.5 1.1 %copy-done.4 = f32[2,4,40,8,128]{4,3,2,1,0:T(8,128)} copy-done((f32[2,4,40,8,128]{4,3,2,1,0:T(8,128)}, f32[2,4,40,8,128]{4,3,2,1,0:T(8,128)S(1)}, u32[]{:S(2)}) %copy-start.4) | copy-done | bytes 1310744
  17.6 0.0 collective-permute-done.2.fxe
  17.6 0.0 collective-permute-done.3.fxo
  17.6 1.6 %grid_steps.1 = (f32[16,32,128]{2,1,0:T(8,128)}, f32[32,32,128]{2,1,0:T(8,128)}) custom-call(f32[16,32,128]{2,1,0:T(8,128)S(1)} %get-tuple-element.39.p, f32[16,32,128]{2,1,0:T(8,128)S(1)} %get-tuple-element.40.q, f32[16,32,128]{2,1,0:T(8,128)S(1)} %get-tuple-element.41.s, f32[80,128]{1,0:T(8,128)S(1)} %collective-permute-done.wye.got_even, ...), custom_call_target="tpu_custom_call" | custom-call | tf_op jit(solution)/shard_map/grid_steps/pallas_call | solution.py:290
  19.2 6.1 %all-to-all-start = ((f32[32,32,128]{2,1,0:T(8,128)}), f32[32,32,128]{2,1,0:T(8,128)S(1)}, u32[]{:S(2)}, u32[]{:S(2)}) async-start(f32[32,32,128]{2,1,0:T(8,128)} %get-tuple-element.42), calls=%async_computation | async-start | bytes 1048576 | tf_op jit(solution)/shard_map/all_to_all | solution.py:716
  25.4 0.0 copy-start.5
  25.4 1.3 %copy-done.5 = f32[2,4,40,8,128]{4,3,2,1,0:T(8,128)S(1)} copy-done((f32[2,4,40,8,128]{4,3,2,1,0:T(8,128)S(1)}, f32[2,4,40,8,128]{4,3,2,1,0:T(8,128)}, u32[]{:S(2)}) %copy-start.5) | copy-done | bytes 1310744
  26.7 2.3 %wall_first.1 = (f32[2,4,40,8,128]{4,3,2,1,0:T(8,128)S(1)}, f32[3,2,4,128]{3,2,1,0:T(4,128)S(1)}, f32[3,2,4,128]{3,2,1,0:T(4,128)S(1)}, f32[2,4,128]{2,1,0:T(4,1...) custom-call(f32[3,3,2,4,128]{4,3,2,1,0:T(4,128)S(1)} %get-tuple-element.28.wall, ...), custom_call_target="tpu_custom_call" | custom-call | tf_op jit(solution)/shard_map/wall_first/pallas_call | solution.py:553
  28.9 0.0 copy-start.2
  29.0 1.0 %copy-done.2 = f32[2,4,40,8,128]{4,3,2,1,0:T(8,128)} copy-done((f32[2,4,40,8,128]{4,3,2,1,0:T(8,128)}, f32[2,4,40,8,128]{4,3,2,1,0:T(8,128)S(1)}, u32[]{:S(2)}) %copy-start.2) | copy-done | bytes 1310744
  30.0 0.1 collective-permute-start.4
  30.2 2.4 %collective-permute-start.5 = (f32[8,128]{1,0:T(8,128)S(1)}, f32[8,128]{1,0:T(8,128)S(1)}, u32[]{:S(2)}, u32[]{:S(2)}) collective-permute-start(f32[8,128]{1,0:T(8,128)S(1)} %get-tuple-element.47), channel_id=1, source_target_pairs={{1,2},{2,1},{5,6},{6,5},{9,10},{10,9},{13,14},{14,13},{17,18},{18,... | collective-permute-start | bytes 12296 | tf_op jit(solution)/shard_map/ppermute | solution.py:47
  32.6 0.0 collective-permute-done.4.got_even.wye
  32.6 2.5 %collective-permute-done.5.got_odd.wyo = f32[8,128]{1,0:T(8,128)S(1)} collective-permute-done((f32[8,128]{1,0:T(8,128)S(1)}, f32[8,128]{1,0:T(8,128)S(1)}, u32[]{:S(2)}, u32[]{:S(2)}) %collective-permute-start.5) | collective-permute-done | bytes 4128 | tf_op jit(solution)/shard_map/ppermute | solution.py:47
  35.1 1.5 %collective-permute-start.6 = (f32[24,128]{1,0:T(8,128)S(1)}, f32[24,128]{1,0:T(8,128)S(1)}, u32[]{:S(2)}, u32[]{:S(2)}) collective-permute-start(f32[24,128]{1,0:T(8,128)S(1)} %get-tuple-element.48), channel_id=1, source_target_pairs={{0,4},{4,0},{8,12},{12,8},{16,20},{20,16},{24,28},{28,24},{1,5},{5... | collective-permute-start | bytes 36872 | tf_op jit(solution)/shard_map/ppermute | solution.py:48
  36.6 2.5 %collective-permute-start.7 = (f32[24,128]{1,0:T(8,128)S(1)}, f32[24,128]{1,0:T(8,128)S(1)}, u32[]{:S(2)}, u32[]{:S(2)}) collective-permute-start(f32[24,128]{1,0:T(8,128)S(1)} %get-tuple-element.49), channel_id=1, source_target_pairs={{4,8},{8,4},{12,16},{16,12},{20,24},{24,20},{5,9},{9,5},{13,17},{1... | collective-permute-start | bytes 36872 | tf_op jit(solution)/shard_map/ppermute | solution.py:47
  39.1 0.0 collective-permute-done.6.fxe
  39.1 4.0 %collective-permute-done.7.fxo = f32[24,128]{1,0:T(8,128)S(1)} collective-permute-done((f32[24,128]{1,0:T(8,128)S(1)}, f32[24,128]{1,0:T(8,128)S(1)}, u32[]{:S(2)}, u32[]{:S(2)}) %collective-permute-start.7) | collective-permute-done | bytes 12320 | tf_op jit(solution)/shard_map/ppermute | solution.py:47
  43.1 0.0 all-to-all-done.got
  43.1 1.3 %copy-done.1 = f32[2,4,40,8,128]{4,3,2,1,0:T(8,128)S(1)} copy-done((f32[2,4,40,8,128]{4,3,2,1,0:T(8,128)S(1)}, f32[2,4,40,8,128]{4,3,2,1,0:T(8,128)}, u32[]{:S(2)}) %copy-start.1) | copy-done | bytes 1310744
  44.4 1.3 %copy-done.3 = f32[2,4,40,8,128]{4,3,2,1,0:T(8,128)S(1)} copy-done((f32[2,4,40,8,128]{4,3,2,1,0:T(8,128)S(1)}, f32[2,4,40,8,128]{4,3,2,1,0:T(8,128)}, u32[]{:S(2)}) %copy-start.3) | copy-done | bytes 1310744
  45.8 1.7 %wall_last.1 = (f32[3,2,4,128]{3,2,1,0:T(4,128)}, f32[3,2,4,128]{3,2,1,0:T(4,128)}) custom-call(f32[2,4,40,8,128]{4,3,2,1,0:T(8,128)S(1)} %copy-done.1, f32[2,4,40,8,128]{4,3,2,1,0:T(8,128)S(1)} %copy-done.3, f32[32,32,128]{2,1,0:T(8,128)S(1)} %all-to-all-done.got, f32[3,2,4,128]{3,2,1,0:T(4,128)S(1)} %get-tuple-element.43.base1, ...), custom_call_target="tpu_custom_call" | custom-call | tf_op jit(solution)/shard_map/wall_last/pallas_call | solution.py:671
  (6 shorter events, 0.0 us)
Async XLA Ops:
  1.9 2.6 %collective-permute-start = (f32[80,128]{1,0:T(8,128)S(1)}, f32[80,128]{1,0:T(8,128)S(1)}, u32[]{:S(2)}, u32[]{:S(2)}) collective-permute-start(f32[80,128]{1,0:T(8,128)S(1)} %get-tuple-element.29), channel_id=1, source_target_pairs={{0,1},{1,0},{2,3},{3,2},{4,5},{5,4},{6,7},{7,6},{8,9},{9,8},{10,11... | collective-permute-start | bytes 122888 | tf_op jit(solution)/shard_map/ppermute | solution.py:48
  1.9 5.3 %collective-permute-start.1 = (f32[80,128]{1,0:T(8,128)S(1)}, f32[80,128]{1,0:T(8,128)S(1)}, u32[]{:S(2)}, u32[]{:S(2)}) collective-permute-start(f32[80,128]{1,0:T(8,128)S(1)} %get-tuple-element.30), channel_id=1, source_target_pairs={{1,2},{2,1},{5,6},{6,5},{9,10},{10,9},{13,14},{14,13},{17,18},{18,... | collective-permute-start | bytes 122888 | tf_op jit(solution)/shard_map/ppermute | solution.py:47
  7.3 10.3 %collective-permute-start.2 = (f32[168,128]{1,0:T(8,128)S(1)}, f32[168,128]{1,0:T(8,128)S(1)}, u32[]{:S(2)}, u32[]{:S(2)}) collective-permute-start(f32[168,128]{1,0:T(8,128)S(1)} %get-tuple-element.34), channel_id=1, source_target_pairs={{0,4},{4,0},{8,12},{12,8},{16,20},{20,16},{24,28},{28,24},{1,5},{5... | collective-permute-start | bytes 258056 | tf_op jit(solution)/shard_map/ppermute | solution.py:48
  8.9 8.7 %collective-permute-start.3 = (f32[168,128]{1,0:T(8,128)S(1)}, f32[168,128]{1,0:T(8,128)S(1)}, u32[]{:S(2)}, u32[]{:S(2)}) collective-permute-start(f32[168,128]{1,0:T(8,128)S(1)} %get-tuple-element.35), channel_id=1, source_target_pairs={{4,8},{8,4},{12,16},{16,12},{20,24},{24,20},{5,9},{9,5},{13,17},{1... | collective-permute-start | bytes 258056 | tf_op jit(solution)/shard_map/ppermute | solution.py:47
  15.5 1.1 %copy-start = (f32[2,4,40,8,128]{4,3,2,1,0:T(8,128)}, f32[2,4,40,8,128]{4,3,2,1,0:T(8,128)S(1)}, u32[]{:S(2)}) copy-start(f32[2,4,40,8,128]{4,3,2,1,0:T(8,128)S(1)} %get-tuple-element.31.weights) | copy-start | bytes 3932164
  16.5 1.1 %copy-start.4 = (f32[2,4,40,8,128]{4,3,2,1,0:T(8,128)}, f32[2,4,40,8,128]{4,3,2,1,0:T(8,128)S(1)}, u32[]{:S(2)}) copy-start(f32[2,4,40,8,128]{4,3,2,1,0:T(8,128)S(1)} %get-tuple-element.37.end_masks) | copy-start | bytes 3932164
  19.2 23.9 %all-to-all-start = ((f32[32,32,128]{2,1,0:T(8,128)}), f32[32,32,128]{2,1,0:T(8,128)S(1)}, u32[]{:S(2)}, u32[]{:S(2)}) async-start(f32[32,32,128]{2,1,0:T(8,128)} %get-tuple-element.42), calls=%async_computation | async-start | bytes 1048576 | tf_op jit(solution)/shard_map/all_to_all | solution.py:716
  25.4 1.3 %copy-start.5 = (f32[2,4,40,8,128]{4,3,2,1,0:T(8,128)S(1)}, f32[2,4,40,8,128]{4,3,2,1,0:T(8,128)}, u32[]{:S(2)}) copy-start(f32[2,4,40,8,128]{4,3,2,1,0:T(8,128)} %copy-done.4) | copy-start | bytes 3932164
  28.9 1.1 %copy-start.2 = (f32[2,4,40,8,128]{4,3,2,1,0:T(8,128)}, f32[2,4,40,8,128]{4,3,2,1,0:T(8,128)S(1)}, u32[]{:S(2)}) copy-start(f32[2,4,40,8,128]{4,3,2,1,0:T(8,128)S(1)} %get-tuple-element.38.end_weights) | copy-start | bytes 3932164
  30.0 2.6 %collective-permute-start.4 = (f32[8,128]{1,0:T(8,128)S(1)}, f32[8,128]{1,0:T(8,128)S(1)}, u32[]{:S(2)}, u32[]{:S(2)}) collective-permute-start(f32[8,128]{1,0:T(8,128)S(1)} %get-tuple-element.46), channel_id=1, source_target_pairs={{0,1},{1,0},{2,3},{3,2},{4,5},{5,4},{6,7},{7,6},{8,9},{9,8},{10,11... | collective-permute-start | bytes 12296 | tf_op jit(solution)/shard_map/ppermute | solution.py:48
  30.2 4.9 %collective-permute-start.5 = (f32[8,128]{1,0:T(8,128)S(1)}, f32[8,128]{1,0:T(8,128)S(1)}, u32[]{:S(2)}, u32[]{:S(2)}) collective-permute-start(f32[8,128]{1,0:T(8,128)S(1)} %get-tuple-element.47), channel_id=1, source_target_pairs={{1,2},{2,1},{5,6},{6,5},{9,10},{10,9},{13,14},{14,13},{17,18},{18,... | collective-permute-start | bytes 12296 | tf_op jit(solution)/shard_map/ppermute | solution.py:47
  35.1 4.0 %collective-permute-start.6 = (f32[24,128]{1,0:T(8,128)S(1)}, f32[24,128]{1,0:T(8,128)S(1)}, u32[]{:S(2)}, u32[]{:S(2)}) collective-permute-start(f32[24,128]{1,0:T(8,128)S(1)} %get-tuple-element.48), channel_id=1, source_target_pairs={{0,4},{4,0},{8,12},{12,8},{16,20},{20,16},{24,28},{28,24},{1,5},{5... | collective-permute-start | bytes 36872 | tf_op jit(solution)/shard_map/ppermute | solution.py:48
  36.6 6.5 %collective-permute-start.7 = (f32[24,128]{1,0:T(8,128)S(1)}, f32[24,128]{1,0:T(8,128)S(1)}, u32[]{:S(2)}, u32[]{:S(2)}) collective-permute-start(f32[24,128]{1,0:T(8,128)S(1)} %get-tuple-element.49), channel_id=1, source_target_pairs={{4,8},{8,4},{12,16},{16,12},{20,24},{24,20},{5,9},{9,5},{13,17},{1... | collective-permute-start | bytes 36872 | tf_op jit(solution)/shard_map/ppermute | solution.py:47
  43.1 1.3 %copy-start.1 = (f32[2,4,40,8,128]{4,3,2,1,0:T(8,128)S(1)}, f32[2,4,40,8,128]{4,3,2,1,0:T(8,128)}, u32[]{:S(2)}) copy-start(f32[2,4,40,8,128]{4,3,2,1,0:T(8,128)} %copy-done) | copy-start | bytes 3932164
  44.4 1.3 %copy-start.3 = (f32[2,4,40,8,128]{4,3,2,1,0:T(8,128)S(1)}, f32[2,4,40,8,128]{4,3,2,1,0:T(8,128)}, u32[]{:S(2)}) copy-start(f32[2,4,40,8,128]{4,3,2,1,0:T(8,128)} %copy-done.2) | copy-start | bytes 3932164

commit v6 on v5

--- a/solution.py
+++ b/solution.py
@@ -42,11 +42,11 @@
     return pairs
 
 
-def exchange(axis, to_even, to_odd):
+def exchange(axis, to_odd, to_even):
     count = lax.axis_size(axis)
     got_odd = lax.ppermute(to_odd, axis, pair_list(count, 1))
     got_even = lax.ppermute(to_even, axis, pair_list(count, 0))
-    return got_even, got_odd
+    return got_odd, got_even
 
 
 def place_edges(even, low, high, to_even, to_odd):
@@ -67,7 +67,7 @@
 
 
 def pack_wy_kernel(
-    p, q, s, jit_in, disp_in, vel_in, wy_even, wy_odd, fx_even, fx_odd, wall, edges, ends, sems
+    p, q, s, jit_in, disp_in, vel_in, wy_odd, wy_even, fx_odd, fx_even, wall, edges, ends, sems
 ):
     cx, cy = p.shape[0], p.shape[1]
     rows, cols = jit_in.shape[1], jit_in.shape[2]
@@ -158,7 +158,7 @@
     )(*in_hbm(p, q, s, jit, disp, vel))
 
 
-def pack_fx_kernel(cx, cy, rows, cols, part_even, part_odd, got_even, got_odd, to_even, to_odd):
+def pack_fx_kernel(cx, cy, rows, cols, part_odd, part_even, got_odd, got_even, to_odd, to_even):
     before, after = before_after(even_at("wy"), got_even, got_odd)
     to_even[...] = part_even[...]
     to_odd[...] = part_odd[...]
@@ -207,7 +207,7 @@
     return high, (v - high.astype(F32)).astype(BF16)
 
 
-def grid_kernel(p, q, s, wye, wyo, fxe, fxo, target, out, slots, s0, s1, rhs, part1, part2):
+def grid_kernel(p, q, s, wyo, wye, fxo, fxe, target, out, slots, s0, s1, rhs, part1, part2):
     cx, cy = p.shape[0], p.shape[1]
     ahead, behind = SUB, SUB + cy
     fx_count = part1.shape[0] // 2 - 1
@@ -272,15 +272,52 @@
         l = first // high
         part1[1 + l : 1 + l + chunk // high, SUB : SUB + high, :] = one.reshape(-1, high, LANES)
         part2[l : l + chunk // high, SUB : SUB + high, :] = two.reshape(-1, high, LANES)
-    lower = lax.broadcasted_iota(jnp.int32, (SUB, LANES), 0) < cols + 2
+    sub = lax.broadcasted_iota(jnp.int32, (SUB, LANES), 0)
+    lane = lax.broadcasted_iota(jnp.int32, (SUB, LANES), 1)
+    step1 = sub < cols + 2
     for a in range(fx_count):
         for b in range(wy_count):
-            for l in range(4):
-                h = SUB + cols * b
-                one = part1[2 * a + l, h - 1 : h - 1 + SUB, :]
-                h = h + 2 * (l % 2) - 6
-                two = part2[2 * a + l // 2, h : h + SUB, :]
-                slots[a * wy_count + b, l * SUB : (l + 1) * SUB, :] = jnp.where(lower, one, two)
+            h = SUB + cols * b
+            slot = a * wy_count + b
+            one = [part1[2 * a + l, h - 1 : h - 1 + SUB, :] for l in range(4)]
+            ends = jnp.where(lane % 8 < 4, one[3], one[0])
+            two = [
+                part2[2 * a + l, h + at - 6 : h + at - 6 + SUB, :]
+                for l, at in ((0, 0), (0, 2), (1, 0))
+            ]
+            x = jnp.broadcast_to(part2[2 * a + 1, h + 2 : h + 3, :], (SUB, LANES))
+            y = jnp.broadcast_to(part2[2 * a + 1, h + 3 : h + 4, :], (SUB, LANES))
+            for r in range(4):
+                moved = pltpu.roll(y, (3 - 2 * r) % LANES, 1)
+                ends = jnp.where((sub == 1 + r) & free_ends(lane), moved, ends)
+            low, high_free = (sub == 0) & (lane // 8 % 4 == 0), (sub == cols + 1) & (lane // 8 % 4 == 3)
+            own0 = jnp.where(low | high_free, x, one[1])
+            own1 = jnp.where(low, pltpu.roll(x, LANES - 8, 1), one[2])
+            own1 = jnp.where(high_free, pltpu.roll(x, 8, 1), own1)
+            for k, group in enumerate((ends, own0, own1)):
+                slots[slot, k * SUB : (k + 1) * SUB, :] = jnp.where(step1, group, two[k])
+
+
+def free_ends(lane):
+    return (lane % 8 == 3) | (lane % 8 == 4)
+
+
+def unpack_slots(total, cols):
+    ends, own0, own1 = [total[k * SUB : (k + 1) * SUB] for k in range(3)]
+    lane = lax.broadcasted_iota(jnp.int32, (1, LANES), 1)
+    two = [[ends[6:7], ends[7:8], own0[6:7], own0[7:8]], [own1[6:7], own1[7:8]]]
+    q = lane // 8 % 4
+    last = cols + 1
+    x = jnp.where(q == 0, own0[0:1], own0[last : last + 1])
+    x = jnp.where(q == 1, pltpu.roll(own1[0:1], 8, 1), x)
+    x = jnp.where(q == 2, pltpu.roll(own1[last : last + 1], LANES - 8, 1), x)
+    y = None
+    for r in range(4):
+        moved = pltpu.roll(ends[1 + r : 2 + r], (2 * r - 3) % LANES, 1)
+        y = moved if y is None else jnp.where(lane % 8 // 2 == r, moved, y)
+    two[1].extend([x, y])
+    two = [jnp.concatenate(v, axis=0) for v in two]
+    return (ends, own0, own1, ends), two
 
 
 def grid_steps(p, q, s, wy_got, fx_got, target, fx_count, wy_count):
@@ -293,7 +330,7 @@
         out_specs=[whole()] * 2,
         out_shape=[
             jax.ShapeDtypeStruct(p.shape, F32),
-            vmem(devices, 4 * SUB, LANES),
+            vmem(devices, 3 * SUB, LANES),
         ],
         scratch_shapes=[
             pltpu.VMEM((cx + 2, cy + 2 * SUB, LANES), F32),
@@ -380,15 +417,15 @@
     return jnp.maximum(weight, 0.0)
 
 
-def tile_pass(l, h, columns, others, pulls, mask_at, weights, sums_in, acc):
+def tile_pass(l, h, columns, others, pulls, weight_of, weights, acc):
     place = 0
     for g in range(LANES // SUB):
         span = slice(g * SUB, (g + 1) * SUB)
         mine = [jnp.broadcast_to(columns[span, c : c + 1], (SUB, LANES)) for c in range(3)]
-        sums = [None if sums_in is None else sums_in[l, h, c, span, :] for c in range(4)]
-        for dh in reached(g):
+        sums = [None] * 4
+        for order, dh in enumerate(reached(g)):
             here = [others[c][dh] for c in range(3)]
-            weight = bond_row(mask_at(dh, span, place), here, mine)
+            weight = weight_of(g, order, dh, here, mine)
             weights[l, h, place] = weight
             place += 1
             terms = [weight * pulls[c][dh] for c in range(3)] + [weight]
@@ -416,14 +453,20 @@
     return [jnp.concatenate(parts, axis=0) for parts in result]
 
 
+def quotient(v, n):
+    return ((v.astype(F32) + 0.5) * (1.0 / n)).astype(jnp.int32)
+
+
 def center_kernel(
-    masks_in, p_in, q_in, s_in, wall, wye, wyo, weights, acc, end_masks, p, q, s,
-    jpad, dpad, masks, sems,
+    wy_count, masks_in, p_in, q_in, s_in, device_in, tile_in, wall, wyo, wye,
+    weights, part, bits, target, p, q, s, jpad, dpad, acc, masks, route, sems,
 ):
     rows, cols = wall.shape[2], wall.shape[3]
     cx = p.shape[0]
     copies = {}
-    for k, pair in enumerate(((p_in, p), (q_in, q), (s_in, s))):
+    pairs = [(device_in, route.at[0]), (tile_in, route.at[1])]
+    pairs = [(p_in, p), (q_in, q), (s_in, s)] + pairs
+    for k, pair in enumerate(pairs):
         copies[k] = pltpu.make_async_copy(*pair, sems.at[rows * cols + k])
     for h in range(cols):
         for l in range(rows):
@@ -433,6 +476,12 @@
     for copy in copies.values():
         copy.start()
     first_sub = lax.broadcasted_iota(jnp.int32, (SUB, LANES), 0) < SUB // 2
+    copies[3].wait()
+    copies[4].wait()
+    device, tile = route[0], route[1]
+    a, t = quotient(device, wy_count), quotient(tile, cols)
+    b, u = device - a * wy_count, tile - t * cols
+    target[...] = (a * rows + t) * (wy_count * cols) + b * cols + u
     before, after = before_after(even_at("wy"), wye, wyo)
     fill_y(jpad, wall.at[0], before, after, 4 * cx)
     fill_y(dpad, wall.at[1], before, after, 4 * cx + 3 * rows)
@@ -450,44 +499,56 @@
             others.append(mid)
         pulls = [mid_rows(dpad, c, l, h) for c in range(3)]
 
-        def mask_at(dh, span, place):
+        def weight_of(g, order, dh, here, mine):
+            span = slice(g * SUB, (g + 1) * SUB)
             before = masks[l, h, 1 + dh, span, :]
             after = masks[l, h, 7 + dh, span, :]
-            end_masks[l, h, place] = jnp.where(first_sub, before, after).astype(F32)
-            return masks[l, h, 4 + dh, span, :].astype(F32)
-
-        tile_pass(l, h, columns, others, pulls, mask_at, weights, None, acc)
+            bit = jnp.where(first_sub, before, after) * (1 << order)
+            bits[l, h, g] = bit if order == 0 else bits[l, h, g] + bit
+            return bond_row(masks[l, h, 4 + dh, span, :].astype(F32), here, mine)
+
+        tile_pass(l, h, columns, others, pulls, weight_of, weights, acc)
 
     for h in range(cols):
         for l in range(rows):
             copies[l, h].wait()
             one_tile(l, h)
+    for l in range(rows):
+        for c, sums in enumerate(lane_sums(acc, l, cols, 4)):
+            part[l, c] = sums
     for k in range(3):
         copies[k].wait()
 
 
-def wall_center(masks, grids, wall, wy_got):
+def wall_center(wy_count, masks, grids, device, tile, wall, wy_got):
     rows, cols = wall.shape[2], wall.shape[3]
-    stored = jax.ShapeDtypeStruct((rows, cols, STORED, SUB, LANES), F32)
-    sums = jax.ShapeDtypeStruct((rows, cols, 4, LANES, LANES), F32)
+    groups = LANES // SUB
     return pl.pallas_call(
-        center_kernel,
-        in_specs=[HBM] * 4 + [whole()] * 3,
-        out_specs=[whole()] * 6,
-        out_shape=[stored, sums, stored] + [vmem(*grids[0].shape)] * 3,
+        functools.partial(center_kernel, wy_count),
+        in_specs=[HBM] * 6 + [whole()] * 3,
+        out_specs=[whole()] * 7,
+        out_shape=[
+            jax.ShapeDtypeStruct((rows, cols, STORED, SUB, LANES), F32),
+            vmem(rows, 4, cols, LANES),
+            jax.ShapeDtypeStruct((rows, cols, groups, SUB, LANES), jnp.int32),
+            pltpu.VMEM(device.shape, jnp.int32),
+        ]
+        + [vmem(*grids[0].shape)] * 3,
         scratch_shapes=[
             vmem(3, rows + 2, SUB, LANES),
             vmem(3, rows + 2, SUB, LANES),
+            vmem(rows, cols, 4, LANES, LANES),
             pltpu.VMEM(masks.shape, jnp.int32),
-            pltpu.SemaphoreType.DMA((rows * cols + 3,)),
+            pltpu.VMEM((2,) + device.shape, jnp.int32),
+            pltpu.SemaphoreType.DMA((rows * cols + 5,)),
         ],
         compiler_params=params(),
         name="wall_center",
-    )(*in_hbm(masks, *grids), wall, *wy_got)
+    )(*in_hbm(masks, *grids, device, tile), wall, *wy_got)
 
 
 def wall_kernel(
-    cx, cy, wall, wye, wyo, fxe, fxo, part, end_masks, weights, vel1, base1, totals, to_even, to_odd,
+    cx, cy, wall, wyo, wye, fxo, fxe, part, bits, weights, vel1, base1, totals, to_odd, to_even,
     jpad, dpad, acc,
 ):
     rows, cols = wall.shape[2], wall.shape[3]
@@ -514,10 +575,11 @@
             others.append(ends)
         pulls = [end_rows(dpad, c, l, h, first_sub) for c in range(3)]
 
-        def mask_at(dh, span, place):
-            return end_masks[l, h, place]
-
-        tile_pass(l, h, columns, others, pulls, mask_at, weights, part, acc)
+        def weight_of(g, order, dh, here, mine):
+            bonded = (bits[l, h, g] & (1 << order)) != 0
+            return jnp.where(bonded, bond_row(1.0, here, mine), 0.0)
+
+        tile_pass(l, h, columns, others, pulls, weight_of, weights, acc)
 
     @pl.loop(0, cols)
     def _(h):
@@ -525,7 +587,7 @@
             one_tile(l, h)
 
     for l in range(rows):
-        pulled = lane_sums(acc, l, cols, 4)
+        pulled = [v + part[l, c] for c, v in enumerate(lane_sums(acc, l, cols, 4))]
         totals[l] = pulled[3]
         for c in range(3):
             mine = wall[1, c, l]
@@ -546,7 +608,7 @@
     place_edges(even_at("wy"), edge(0), edge(cols - 1), to_even, to_odd)
 
 
-def wall_first(cx, cy, wall, wy_got, fx_got, part, end_masks):
+def wall_first(cx, cy, wall, wy_got, fx_got, part, bits):
     rows, cols = wall.shape[2], wall.shape[3]
     edge = (pad8(3 * rows), LANES)
     field = vmem(*wall.shape[1:])
@@ -569,10 +631,10 @@
         ],
         compiler_params=params(),
         name="wall_first",
-    )(wall, *wy_got, *fx_got, part, end_masks)
-
-
-def pack_base_kernel(base1, got_even, got_odd, to_even, to_odd):
+    )(wall, *wy_got, *fx_got, part, bits)
+
+
+def pack_base_kernel(base1, got_odd, got_even, to_odd, to_even):
     rows, cols = base1.shape[1], base1.shape[2]
     before, after = before_after(even_at("wy"), got_even, got_odd)
 
@@ -607,8 +669,8 @@
 
 
 def last_kernel(
-    weights, end_weights, got, base1, vel1, totals, wye, wyo, fxe, fxo, disp_out, vel_out,
-    dpad, loads, acc,
+    weights, end_weights, got, base1, vel1, totals, wyo, wye, fxo, fxe, disp_out, vel_out,
+    dpad, acc,
 ):
     rows, cols = base1.shape[1], base1.shape[2]
     first_sub = lax.broadcasted_iota(jnp.int32, (SUB, LANES), 0) < SUB // 2
@@ -619,10 +681,10 @@
     total = got[0]
     for d in range(1, got.shape[0]):
         total = total + got[d]
-    loads[...] = total
+    one, two = unpack_slots(total, cols)
     for k in range(rows + 2):
-        here = total[k * SUB : k * SUB + cols + 2, :]
-        dpad[0, k, 0 : cols + 2, :] = dpad[0, k, 0 : cols + 2, :] + LOADING * here
+        here = dpad[0, k, 0 : cols + 2, :] + LOADING * one[k][0 : cols + 2]
+        dpad[0, k, 0 : cols + 2, :] = here
 
     def one_tile(l, h):
         mids = [mid_rows(dpad, c, l, h) for c in range(3)]
@@ -651,19 +713,10 @@
             mine = dpad[c, l + 1, 1 : cols + 1, :]
             force = STIFFNESS * (pulled[c] - totals[l] * mine)
             if c == 0:
-                at = (l + 1) * SUB + 1
-                force = force + LOADING * loads[at : at + cols, :]
-                for half in range(2):
-                    at = (2 * l + half) * SUB + cols + 2
-                    two = loads[at : at + 2, :]
-                    span = slice(2 * half, 2 * half + 2)
-                    fresh = vel1[c, l, span, :] + force[span] + LOADING * two
-                    vel_out[c, l, span, :] = fresh
-                    disp_out[c, l, span, :] = mine[span] + fresh
-            else:
-                fresh = vel1[c, l] + force
-                vel_out[c, l] = fresh
-                disp_out[c, l] = mine + fresh
+                force = force + LOADING * (one[l + 1][1 : cols + 1] + two[l])
+            fresh = vel1[c, l] + force
+            vel_out[c, l] = fresh
+            disp_out[c, l] = mine + fresh
 
 
 def wall_last(weights, end_weights, got, base1, vel1, totals, wy_got, fx_got):
@@ -675,7 +728,6 @@
         out_shape=[jax.ShapeDtypeStruct(base1.shape, F32)] * 2,
         scratch_shapes=[
             pltpu.VMEM((3, rows + 2, SUB, LANES), F32),
-            pltpu.VMEM((4 * SUB, LANES), F32),
             pltpu.VMEM((rows, cols, 3, LANES, LANES), F32),
         ],
         compiler_params=params(),
@@ -698,24 +750,22 @@
     cols = displacement.shape[2]
     device = route_device.reshape(-1, LANES)
     tile = route_tile.reshape(-1, LANES)
-    length = (device // wy_count) * 2 + tile // cols
-    height = (device % wy_count) * cols + tile % cols
-    target = length * (wy_count * cols) + height
-
     cx, cy = pressure.shape[0], pressure.shape[1]
     rows = displacement.shape[1]
-    *sends, part_even, part_odd, wall = pack_wy(
+    *sends, part_odd, part_even, wall = pack_wy(
         pressure, pressure_prev, speed_sq, jitter, displacement, velocity
     )
     wy_got = exchange("wy", *sends)
-    sends = pack_fx((cx, cy, rows, cols), (part_even, part_odd), wy_got)
+    sends = pack_fx((cx, cy, rows, cols), (part_odd, part_even), wy_got)
     fx_got = exchange("fx", *sends)
     grids = (pressure, pressure_prev, speed_sq)
-    weights, part, end_masks, *grids = wall_center(bond_masks, grids, wall, wy_got)
+    weights, part, bits, target, *grids = wall_center(
+        wy_count, bond_masks, grids, device, tile, wall, wy_got
+    )
     pressure_out, slots = grid_steps(*grids, wy_got, fx_got, target, fx_count, wy_count)
     got = lax.all_to_all(slots, ("fx", "wy"), split_axis=0, concat_axis=0, tiled=True)
     end_weights, vel1, base1, totals, *sends = wall_first(
-        cx, cy, wall, wy_got, fx_got, part, end_masks
+        cx, cy, wall, wy_got, fx_got, part, bits
     )
     base_wy = exchange("wy", *sends)
     sends = pack_base(base1, base_wy)

time: 47.9 us -> 41.8 us (0.87)
  the two profiles are of different devices: /device:TPU:12 before, /device:TPU:0 now
where the time goes in v6:
time: 41.8 us; the launch traced here: 41.5 us
  starting transfers between devices  24.4 us (58%)
  Pallas kernels  11 us (26%)
  waiting for transfers between devices  3.48 us (8%)
  local copies, waits for them, and re-layouts  1.83 us (4%)
  between operations  0.73 us (2%)
    ppermute x4, starting transfers between devices, exchange(): got_even = lax.ppermute(to_even, axis, pair_list(count, 0))  16.2 us
    all_to_all x1, starting transfers between devices, per_device(): lax.all_to_all(slots, ('fx', 'wy'), split_axis=0, concat_axis=0, tiled=True)  5.56 us
    pallas_call x1, Pallas kernels, wall_center(): pl.pallas_call(functools.partial(center_kernel, wy_count), in_specs=[HBM]...  4.02 us
    ppermute x4, waiting for transfers between devices, exchange(): got_even = lax.ppermute(to_even, axis, pair_list(count, 0))  3.47 us
    ppermute x4, starting transfers between devices, exchange(): got_odd = lax.ppermute(to_odd, axis, pair_list(count, 1))  2.65 us
    pallas_call x1, Pallas kernels, wall_first(): pl.pallas_call(functools.partial(wall_kernel, cx, cy), in_specs=[whole()]...  2.27 us
    unnamed x4, local copies, waits for them, and re-layouts  1.83 us
    pallas_call x1, Pallas kernels, wall_last(): pl.pallas_call(last_kernel, in_specs=[whole()] * 10, out_specs=[whole()]...  1.74 us
  transfers between devices with their start and end apart: 9, of which 3 were waited for; matrix products, arithmetic and copies ran while one was open for 0% of the time, Pallas kernels for 15%

profile of v6, /device:TPU:0, one launch (start us, length us, event | category | flops | bytes accessed | tf_op | source)
XLA Modules:
  0.0 41.5 jit_solution(5615064588563187085)
XLA Ops:
  0.6 1.2 %pack_wy.1 = (f32[80,128]{1,0:T(8,128)S(1)}, f32[80,128]{1,0:T(8,128)S(1)}, f32[168,128]{1,0:T(8,128)S(1)}, f32[168,128]{1,0:T(8,128)S(1)}, f32[3,3,2,4,128]{4,3,2,1,0:T(4,128)S(1)}) custom-call(f32[16,32,128]{2,1,0:T(8,128)} %p_in.1, f32[16,32,128]{2,1,0:T(8,128)} %q_in.1, f32[16,32,128]{2,1,0:T(8,128)} %s_in.1, f32[3,2,4,128]{3,2,1,0:T(4,128)} %jit_in.1, ...), custom_call_target="tpu_custom_call" | custom-call | tf_op jit(solution)/shard_map/pack_wy/pallas_call | solution.py:146
  1.9 0.7 %collective-permute-start = (f32[80,128]{1,0:T(8,128)S(1)}, f32[80,128]{1,0:T(8,128)S(1)}, u32[]{:S(2)}, u32[]{:S(2)}) collective-permute-start(f32[80,128]{1,0:T(8,128)S(1)} %get-tuple-element.30), channel_id=1, source_target_pairs={{1,2},{2,1},{5,6},{6,5},{9,10},{10,9},{13,14},{14,13},{17,18},{18,... | collective-permute-start | bytes 122888 | tf_op jit(solution)/shard_map/ppermute | solution.py:47
  2.5 4.4 %collective-permute-start.1 = (f32[80,128]{1,0:T(8,128)S(1)}, f32[80,128]{1,0:T(8,128)S(1)}, u32[]{:S(2)}, u32[]{:S(2)}) collective-permute-start(f32[80,128]{1,0:T(8,128)S(1)} %get-tuple-element.31), channel_id=1, source_target_pairs={{0,1},{1,0},{2,3},{3,2},{4,5},{5,4},{6,7},{7,6},{8,9},{9,8},{10,11... | collective-permute-start | bytes 122888 | tf_op jit(solution)/shard_map/ppermute | solution.py:48
  6.9 0.0 collective-permute-done.wyo.got_odd
  6.9 0.9 %collective-permute-done.1.wye.got_even = f32[80,128]{1,0:T(8,128)S(1)} collective-permute-done((f32[80,128]{1,0:T(8,128)S(1)}, f32[80,128]{1,0:T(8,128)S(1)}, u32[]{:S(2)}, u32[]{:S(2)}) %collective-permute-start.1) | collective-permute-done | bytes 40992 | tf_op jit(solution)/shard_map/ppermute | solution.py:48
  7.8 0.7 %collective-permute-start.2 = (f32[168,128]{1,0:T(8,128)S(1)}, f32[168,128]{1,0:T(8,128)S(1)}, u32[]{:S(2)}, u32[]{:S(2)}) collective-permute-start(f32[168,128]{1,0:T(8,128)S(1)} %get-tuple-element.35), channel_id=1, source_target_pairs={{4,8},{8,4},{12,16},{16,12},{20,24},{24,20},{5,9},{9,5},{13,17},{1... | collective-permute-start | bytes 258056 | tf_op jit(solution)/shard_map/ppermute | solution.py:47
  8.5 4.3 %collective-permute-start.3 = (f32[168,128]{1,0:T(8,128)S(1)}, f32[168,128]{1,0:T(8,128)S(1)}, u32[]{:S(2)}, u32[]{:S(2)}) collective-permute-start(f32[168,128]{1,0:T(8,128)S(1)} %get-tuple-element.36), channel_id=1, source_target_pairs={{0,4},{4,0},{8,12},{12,8},{16,20},{20,16},{24,28},{28,24},{1,5},{5... | collective-permute-start | bytes 258056 | tf_op jit(solution)/shard_map/ppermute | solution.py:48
  12.9 4.0 %wall_center.1 = (f32[2,4,40,8,128]{4,3,2,1,0:T(8,128)S(1)}, f32[2,4,4,128]{3,2,1,0:T(4,128)S(1)}, s32[2,4,16,8,128]{4,3,2,1,0:T(8,128)S(1)}, s32[4,128]{1,0:T(4...) custom-call(s32[2,4,9,128,128]{4,3,2,1,0:T(8,128)} %masks_in.1, ...), custom_call_target="tpu_custom_call" | custom-call | tf_op jit(solution)/shard_map/wall_center/pallas_call | solution.py:526
  16.9 0.0 copy-start
  16.9 0.8 %copy-done = s32[2,4,16,8,128]{4,3,2,1,0:T(8,128)} copy-done((s32[2,4,16,8,128]{4,3,2,1,0:T(8,128)}, s32[2,4,16,8,128]{4,3,2,1,0:T(8,128)S(1)}, u32[]{:S(2)}) %copy-start) | copy-done | bytes 524312
  17.7 0.0 collective-permute-done.2.fxo
  17.7 0.0 collective-permute-done.3.fxe
  17.7 1.7 %grid_steps.1 = (f32[16,32,128]{2,1,0:T(8,128)}, f32[32,24,128]{2,1,0:T(8,128)}) custom-call(f32[16,32,128]{2,1,0:T(8,128)S(1)} %get-tuple-element.40.p, f32[16,32,128]{2,1,0:T(8,128)S(1)} %get-tuple-element.41.q, f32[16,32,128]{2,1,0:T(8,128)S(1)} %get-tuple-element.42.s, f32[80,128]{1,0:T(8,128)S(1)} %collective-permute-done.wyo.got_odd, ...), custom_call_target="tpu_custom_call" | custom-call | tf_op jit(solution)/shard_map/grid_steps/pallas_call | solution.py:327
  19.4 5.6 %all-to-all-start = ((f32[32,24,128]{2,1,0:T(8,128)}), f32[32,24,128]{2,1,0:T(8,128)S(1)}, u32[]{:S(2)}, u32[]{:S(2)}) async-start(f32[32,24,128]{2,1,0:T(8,128)} %get-tuple-element.44), calls=%async_computation | async-start | bytes 786432 | tf_op jit(solution)/shard_map/all_to_all | solution.py:766
  25.0 0.0 copy-start.1
  25.0 1.0 %copy-done.1 = s32[2,4,16,8,128]{4,3,2,1,0:T(8,128)S(1)} copy-done((s32[2,4,16,8,128]{4,3,2,1,0:T(8,128)S(1)}, s32[2,4,16,8,128]{4,3,2,1,0:T(8,128)}, u32[]{:S(2)}) %copy-start.1) | copy-done | bytes 524312
  26.0 2.3 %wall_first.1 = (f32[2,4,40,8,128]{4,3,2,1,0:T(8,128)S(1)}, f32[3,2,4,128]{3,2,1,0:T(4,128)S(1)}, f32[3,2,4,128]{3,2,1,0:T(4,128)S(1)}, f32[2,4,128]{2,1,0:T(4,1...) custom-call(f32[3,3,2,4,128]{4,3,2,1,0:T(4,128)S(1)} %get-tuple-element.29.wall, ...), custom_call_target="tpu_custom_call" | custom-call | tf_op jit(solution)/shard_map/wall_first/pallas_call | solution.py:615
  28.3 0.7 %collective-permute-start.4 = (f32[8,128]{1,0:T(8,128)S(1)}, f32[8,128]{1,0:T(8,128)S(1)}, u32[]{:S(2)}, u32[]{:S(2)}) collective-permute-start(f32[8,128]{1,0:T(8,128)S(1)} %get-tuple-element.48), channel_id=1, source_target_pairs={{1,2},{2,1},{5,6},{6,5},{9,10},{10,9},{13,14},{14,13},{17,18},{18,... | collective-permute-start | bytes 12296 | tf_op jit(solution)/shard_map/ppermute | solution.py:47
  29.0 3.2 %collective-permute-start.5 = (f32[8,128]{1,0:T(8,128)S(1)}, f32[8,128]{1,0:T(8,128)S(1)}, u32[]{:S(2)}, u32[]{:S(2)}) collective-permute-start(f32[8,128]{1,0:T(8,128)S(1)} %get-tuple-element.49), channel_id=1, source_target_pairs={{0,1},{1,0},{2,3},{3,2},{4,5},{5,4},{6,7},{7,6},{8,9},{9,8},{10,11... | collective-permute-start | bytes 12296 | tf_op jit(solution)/shard_map/ppermute | solution.py:48
  32.2 0.0 collective-permute-done.4.got_odd.wyo
  32.2 0.8 %collective-permute-done.5.got_even.wye = f32[8,128]{1,0:T(8,128)S(1)} collective-permute-done((f32[8,128]{1,0:T(8,128)S(1)}, f32[8,128]{1,0:T(8,128)S(1)}, u32[]{:S(2)}, u32[]{:S(2)}) %collective-permute-start.5) | collective-permute-done | bytes 4128 | tf_op jit(solution)/shard_map/ppermute | solution.py:48
  33.0 0.7 %collective-permute-start.6 = (f32[24,128]{1,0:T(8,128)S(1)}, f32[24,128]{1,0:T(8,128)S(1)}, u32[]{:S(2)}, u32[]{:S(2)}) collective-permute-start(f32[24,128]{1,0:T(8,128)S(1)} %get-tuple-element.50), channel_id=1, source_target_pairs={{4,8},{8,4},{12,16},{16,12},{20,24},{24,20},{5,9},{9,5},{13,17},{1... | collective-permute-start | bytes 36872 | tf_op jit(solution)/shard_map/ppermute | solution.py:47
  33.7 4.2 %collective-permute-start.7 = (f32[24,128]{1,0:T(8,128)S(1)}, f32[24,128]{1,0:T(8,128)S(1)}, u32[]{:S(2)}, u32[]{:S(2)}) collective-permute-start(f32[24,128]{1,0:T(8,128)S(1)} %get-tuple-element.51), channel_id=1, source_target_pairs={{0,4},{4,0},{8,12},{12,8},{16,20},{20,16},{24,28},{28,24},{1,5},{5... | collective-permute-start | bytes 36872 | tf_op jit(solution)/shard_map/ppermute | solution.py:48
  37.9 0.0 collective-permute-done.6.fxo
  37.9 1.8 %collective-permute-done.7.fxe = f32[24,128]{1,0:T(8,128)S(1)} collective-permute-done((f32[24,128]{1,0:T(8,128)S(1)}, f32[24,128]{1,0:T(8,128)S(1)}, u32[]{:S(2)}, u32[]{:S(2)}) %collective-permute-start.7) | collective-permute-done | bytes 12320 | tf_op jit(solution)/shard_map/ppermute | solution.py:48
  39.7 0.0 all-to-all-done.got
  39.7 1.7 %wall_last.1 = (f32[3,2,4,128]{3,2,1,0:T(4,128)}, f32[3,2,4,128]{3,2,1,0:T(4,128)}) custom-call(f32[2,4,40,8,128]{4,3,2,1,0:T(8,128)S(1)} %get-tuple-element.32.weights, f32[2,4,40,8,128]{4,3,2,1,0:T(8,128)S(1)} %get-tuple-element.39.end_weights, f32[32,24,128]{2,1,0:T(8,128)S(1)} %all-to-all-done.got, f32[3,2,4,128]{3,2,1,0:T(4,128)S(1)} %get-tuple-element.45.base1, ...), custom_call_target="tpu_custom_call" | custom-call | tf_op jit(solution)/shard_map/wall_last/pallas_call | solution.py:724
  (2 shorter events, 0.0 us)
Async XLA Ops:
  1.9 5.1 %collective-permute-start = (f32[80,128]{1,0:T(8,128)S(1)}, f32[80,128]{1,0:T(8,128)S(1)}, u32[]{:S(2)}, u32[]{:S(2)}) collective-permute-start(f32[80,128]{1,0:T(8,128)S(1)} %get-tuple-element.30), channel_id=1, source_target_pairs={{1,2},{2,1},{5,6},{6,5},{9,10},{10,9},{13,14},{14,13},{17,18},{18,... | collective-permute-start | bytes 122888 | tf_op jit(solution)/shard_map/ppermute | solution.py:47
  2.5 5.3 %collective-permute-start.1 = (f32[80,128]{1,0:T(8,128)S(1)}, f32[80,128]{1,0:T(8,128)S(1)}, u32[]{:S(2)}, u32[]{:S(2)}) collective-permute-start(f32[80,128]{1,0:T(8,128)S(1)} %get-tuple-element.31), channel_id=1, source_target_pairs={{0,1},{1,0},{2,3},{3,2},{4,5},{5,4},{6,7},{7,6},{8,9},{9,8},{10,11... | collective-permute-start | bytes 122888 | tf_op jit(solution)/shard_map/ppermute | solution.py:48
  7.8 9.9 %collective-permute-start.2 = (f32[168,128]{1,0:T(8,128)S(1)}, f32[168,128]{1,0:T(8,128)S(1)}, u32[]{:S(2)}, u32[]{:S(2)}) collective-permute-start(f32[168,128]{1,0:T(8,128)S(1)} %get-tuple-element.35), channel_id=1, source_target_pairs={{4,8},{8,4},{12,16},{16,12},{20,24},{24,20},{5,9},{9,5},{13,17},{1... | collective-permute-start | bytes 258056 | tf_op jit(solution)/shard_map/ppermute | solution.py:47
  8.5 9.2 %collective-permute-start.3 = (f32[168,128]{1,0:T(8,128)S(1)}, f32[168,128]{1,0:T(8,128)S(1)}, u32[]{:S(2)}, u32[]{:S(2)}) collective-permute-start(f32[168,128]{1,0:T(8,128)S(1)} %get-tuple-element.36), channel_id=1, source_target_pairs={{0,4},{4,0},{8,12},{12,8},{16,20},{20,16},{24,28},{28,24},{1,5},{5... | collective-permute-start | bytes 258056 | tf_op jit(solution)/shard_map/ppermute | solution.py:48
  16.9 0.8 %copy-start = (s32[2,4,16,8,128]{4,3,2,1,0:T(8,128)}, s32[2,4,16,8,128]{4,3,2,1,0:T(8,128)S(1)}, u32[]{:S(2)}) copy-start(s32[2,4,16,8,128]{4,3,2,1,0:T(8,128)S(1)} %get-tuple-element.38.bits) | copy-start | bytes 1572868
  19.4 20.3 %all-to-all-start = ((f32[32,24,128]{2,1,0:T(8,128)}), f32[32,24,128]{2,1,0:T(8,128)S(1)}, u32[]{:S(2)}, u32[]{:S(2)}) async-start(f32[32,24,128]{2,1,0:T(8,128)} %get-tuple-element.44), calls=%async_computation | async-start | bytes 786432 | tf_op jit(solution)/shard_map/all_to_all | solution.py:766
  25.0 1.0 %copy-start.1 = (s32[2,4,16,8,128]{4,3,2,1,0:T(8,128)S(1)}, s32[2,4,16,8,128]{4,3,2,1,0:T(8,128)}, u32[]{:S(2)}) copy-start(s32[2,4,16,8,128]{4,3,2,1,0:T(8,128)} %copy-done) | copy-start | bytes 1572868
  28.3 3.9 %collective-permute-start.4 = (f32[8,128]{1,0:T(8,128)S(1)}, f32[8,128]{1,0:T(8,128)S(1)}, u32[]{:S(2)}, u32[]{:S(2)}) collective-permute-start(f32[8,128]{1,0:T(8,128)S(1)} %get-tuple-element.48), channel_id=1, source_target_pairs={{1,2},{2,1},{5,6},{6,5},{9,10},{10,9},{13,14},{14,13},{17,18},{18,... | collective-permute-start | bytes 12296 | tf_op jit(solution)/shard_map/ppermute | solution.py:47
  29.0 4.0 %collective-permute-start.5 = (f32[8,128]{1,0:T(8,128)S(1)}, f32[8,128]{1,0:T(8,128)S(1)}, u32[]{:S(2)}, u32[]{:S(2)}) collective-permute-start(f32[8,128]{1,0:T(8,128)S(1)} %get-tuple-element.49), channel_id=1, source_target_pairs={{0,1},{1,0},{2,3},{3,2},{4,5},{5,4},{6,7},{7,6},{8,9},{9,8},{10,11... | collective-permute-start | bytes 12296 | tf_op jit(solution)/shard_map/ppermute | solution.py:48
  33.0 4.9 %collective-permute-start.6 = (f32[24,128]{1,0:T(8,128)S(1)}, f32[24,128]{1,0:T(8,128)S(1)}, u32[]{:S(2)}, u32[]{:S(2)}) collective-permute-start(f32[24,128]{1,0:T(8,128)S(1)} %get-tuple-element.50), channel_id=1, source_target_pairs={{4,8},{8,4},{12,16},{16,12},{20,24},{24,20},{5,9},{9,5},{13,17},{1... | collective-permute-start | bytes 36872 | tf_op jit(solution)/shard_map/ppermute | solution.py:47
  33.7 6.0 %collective-permute-start.7 = (f32[24,128]{1,0:T(8,128)S(1)}, f32[24,128]{1,0:T(8,128)S(1)}, u32[]{:S(2)}, u32[]{:S(2)}) collective-permute-start(f32[24,128]{1,0:T(8,128)S(1)} %get-tuple-element.51), channel_id=1, source_target_pairs={{0,4},{4,0},{8,12},{12,8},{16,20},{20,16},{24,28},{28,24},{1,5},{5... | collective-permute-start | bytes 36872 | tf_op jit(solution)/shard_map/ppermute | solution.py:48

commit v7 on v6

--- a/solution.py
+++ b/solution.py
@@ -39,6 +39,8 @@
     pairs = []
     for low in range(first, count - 1, 2):
         pairs.extend([(low, low + 1), (low + 1, low)])
+    if first == 1 and count % 2 == 0 and count > 2:
+        pairs.extend([(0, count - 1), (count - 1, 0)])
     return pairs
 
 
@@ -61,9 +63,13 @@
         high(to_odd)
 
 
-def before_after(even, got_even, got_odd):
+def before_after(axis, got_even, got_odd):
+    even = even_at(axis)
+    place, last = lax.axis_index(axis), lax.axis_size(axis) - 1
     a, b = got_even[...], got_odd[...]
-    return jnp.where(even, b, a), jnp.where(even, a, b)
+    before = jnp.where(place == 0, 0.0, jnp.where(even, b, a))
+    after = jnp.where(place == last, 0.0, jnp.where(even, a, b))
+    return before, after
 
 
 def pack_wy_kernel(
@@ -159,7 +165,7 @@
 
 
 def pack_fx_kernel(cx, cy, rows, cols, part_odd, part_even, got_odd, got_even, to_odd, to_even):
-    before, after = before_after(even_at("wy"), got_even, got_odd)
+    before, after = before_after("wy", got_even, got_odd)
     to_even[...] = part_even[...]
     to_odd[...] = part_odd[...]
 
@@ -215,8 +221,8 @@
     tall = part2.shape[0]
     high = part1.shape[1] - 2 * SUB
     wy_count = high // cols
-    before_y, after_y = before_after(even_at("wy"), wye, wyo)
-    before_x, after_x = before_after(even_at("fx"), fxe, fxo)
+    before_y, after_y = before_after("wy", wye, wyo)
+    before_x, after_x = before_after("fx", fxe, fxo)
     corner = 4 * cy + 6 * (cols + 2)
 
     s0[1 : cx + 1, ahead:behind, :] = p[...]
@@ -482,7 +488,7 @@
     a, t = quotient(device, wy_count), quotient(tile, cols)
     b, u = device - a * wy_count, tile - t * cols
     target[...] = (a * rows + t) * (wy_count * cols) + b * cols + u
-    before, after = before_after(even_at("wy"), wye, wyo)
+    before, after = before_after("wy", wye, wyo)
     fill_y(jpad, wall.at[0], before, after, 4 * cx)
     fill_y(dpad, wall.at[1], before, after, 4 * cx + 3 * rows)
     lattice = lattice_rows()
@@ -498,16 +504,19 @@
                     mid[dh] = mid[dh] + RISE * dh
             others.append(mid)
         pulls = [mid_rows(dpad, c, l, h) for c in range(3)]
+        words = [jnp.zeros((SUB, LANES), jnp.int32) for _ in range(2)]
 
         def weight_of(g, order, dh, here, mine):
             span = slice(g * SUB, (g + 1) * SUB)
             before = masks[l, h, 1 + dh, span, :]
             after = masks[l, h, 7 + dh, span, :]
-            bit = jnp.where(first_sub, before, after) * (1 << order)
-            bits[l, h, g] = bit if order == 0 else bits[l, h, g] + bit
+            place = 3 * (g % 8) + order
+            words[g // 8] = words[g // 8] + jnp.where(first_sub, before, after) * (1 << place)
             return bond_row(masks[l, h, 4 + dh, span, :].astype(F32), here, mine)
 
         tile_pass(l, h, columns, others, pulls, weight_of, weights, acc)
+        for k in range(2):
+            bits[l, h, k] = words[k]
 
     for h in range(cols):
         for l in range(rows):
@@ -522,7 +531,6 @@
 
 def wall_center(wy_count, masks, grids, device, tile, wall, wy_got):
     rows, cols = wall.shape[2], wall.shape[3]
-    groups = LANES // SUB
     return pl.pallas_call(
         functools.partial(center_kernel, wy_count),
         in_specs=[HBM] * 6 + [whole()] * 3,
@@ -530,7 +538,7 @@
         out_shape=[
             jax.ShapeDtypeStruct((rows, cols, STORED, SUB, LANES), F32),
             vmem(rows, 4, cols, LANES),
-            jax.ShapeDtypeStruct((rows, cols, groups, SUB, LANES), jnp.int32),
+            pltpu.VMEM((rows, cols, 2, SUB, LANES), jnp.int32),
             pltpu.VMEM(device.shape, jnp.int32),
         ]
         + [vmem(*grids[0].shape)] * 3,
@@ -553,10 +561,10 @@
 ):
     rows, cols = wall.shape[2], wall.shape[3]
     first_sub = lax.broadcasted_iota(jnp.int32, (SUB, LANES), 0) < SUB // 2
-    before, after = before_after(even_at("wy"), wye, wyo)
+    before, after = before_after("wy", wye, wyo)
     fill_y(jpad, wall.at[0], before, after, 4 * cx)
     fill_y(dpad, wall.at[1], before, after, 4 * cx + 3 * rows)
-    before, after = before_after(even_at("fx"), fxe, fxo)
+    before, after = before_after("fx", fxe, fxo)
     fill_x(jpad, rows, cols, before, after, 4 * cy)
     fill_x(dpad, rows, cols, before, after, 4 * cy + 3 * (cols + 2))
     lattice = lattice_rows()
@@ -576,7 +584,7 @@
         pulls = [end_rows(dpad, c, l, h, first_sub) for c in range(3)]
 
         def weight_of(g, order, dh, here, mine):
-            bonded = (bits[l, h, g] & (1 << order)) != 0
+            bonded = (bits[l, h, g // 8] & (1 << (3 * (g % 8) + order))) != 0
             return jnp.where(bonded, bond_row(1.0, here, mine), 0.0)
 
         tile_pass(l, h, columns, others, pulls, weight_of, weights, acc)
@@ -636,7 +644,7 @@
 
 def pack_base_kernel(base1, got_odd, got_even, to_odd, to_even):
     rows, cols = base1.shape[1], base1.shape[2]
-    before, after = before_after(even_at("wy"), got_even, got_odd)
+    before, after = before_after("wy", got_even, got_odd)
 
     def edge(l):
         def write(out):
@@ -674,9 +682,9 @@
 ):
     rows, cols = base1.shape[1], base1.shape[2]
     first_sub = lax.broadcasted_iota(jnp.int32, (SUB, LANES), 0) < SUB // 2
-    before, after = before_after(even_at("wy"), wye, wyo)
+    before, after = before_after("wy", wye, wyo)
     fill_y(dpad, base1, before, after, 0)
-    before, after = before_after(even_at("fx"), fxe, fxo)
+    before, after = before_after("fx", fxe, fxo)
     fill_x(dpad, rows, cols, before, after, 0)
     total = got[0]
     for d in range(1, got.shape[0]):

time: 41.8 us -> 38.4 us (0.919)
  starting transfers between devices: 24.4 us -> 19.6 us
  waiting for transfers between devices: 3.48 us -> 6.8 us
  local copies, waits for them, and re-layouts: 1.83 us -> 0 us
    ppermute x4, starting transfers between devices: 16.2 us -> 1.04 us  [exchange(): got_even = lax.ppermute(to_even, axis, pair_list(count, 0))]
    ppermute x4, starting transfers between devices: 2.65 us -> 14.5 us  [exchange(): got_odd = lax.ppermute(to_odd, axis, pair_list(count, 1))]
    ppermute x4, waiting for transfers between devices: 0.01 us -> 4.22 us  [exchange(): got_odd = lax.ppermute(to_odd, axis, pair_list(count, 1))]
    unnamed x4 -> x0, local copies, waits for them, and re-layouts: 1.83 us -> none
    all_to_all x1, starting transfers between devices: 5.56 us -> 3.98 us  [per_device(): lax.all_to_all(slots, ('fx', 'wy'), split_axis=0, concat_axis=0, tiled=True)]
    ppermute x4, waiting for transfers between devices: 3.47 us -> 2.58 us  [exchange(): got_even = lax.ppermute(to_even, axis, pair_list(count, 0))]
  transfers between devices with their start and end apart: 9 -> 9, of which waited for: 3 -> 5; matrix products, arithmetic and copies ran while one was open for 0% -> 0% of each run, Pallas kernels for 15% -> 17%
where the time goes in v7:
time: 38.4 us; the launch traced here: 38.1 us
  starting transfers between devices  19.6 us (51%)
  Pallas kernels  11 us (29%)
  waiting for transfers between devices  6.8 us (18%)
  between operations  0.69 us (2%)
    ppermute x4, starting transfers between devices, exchange(): got_odd = lax.ppermute(to_odd, axis, pair_list(count, 1))  14.5 us
    ppermute x4, waiting for transfers between devices, exchange(): got_odd = lax.ppermute(to_odd, axis, pair_list(count, 1))  4.22 us
    pallas_call x1, Pallas kernels, wall_center(): pl.pallas_call(functools.partial(center_kernel, wy_count), in_specs=[HBM]...  4 us
    all_to_all x1, starting transfers between devices, per_device(): lax.all_to_all(slots, ('fx', 'wy'), split_axis=0, concat_axis=0, tiled=True)  3.98 us
    ppermute x4, waiting for transfers between devices, exchange(): got_even = lax.ppermute(to_even, axis, pair_list(count, 0))  2.58 us
    pallas_call x1, Pallas kernels, wall_first(): pl.pallas_call(functools.partial(wall_kernel, cx, cy), in_specs=[whole()]...  2.27 us
    pallas_call x1, Pallas kernels, grid_steps(): pl.pallas_call(grid_kernel, in_specs=[whole()] * 8, out_specs=[whole()] *...  1.75 us
    pallas_call x1, Pallas kernels, wall_last(): pl.pallas_call(last_kernel, in_specs=[whole()] * 10, out_specs=[whole()]...  1.74 us
  transfers between devices with their start and end apart: 9, of which 5 were waited for; matrix products, arithmetic and copies ran while one was open for 0% of the time, Pallas kernels for 17%

profile of v7, /device:TPU:0, one launch (start us, length us, event | category | flops | bytes accessed | tf_op | source)
XLA Modules:
  0.0 38.1 jit_solution(9536147701756472277)
XLA Ops:
  0.6 1.2 %pack_wy.1 = (f32[80,128]{1,0:T(8,128)S(1)}, f32[80,128]{1,0:T(8,128)S(1)}, f32[168,128]{1,0:T(8,128)S(1)}, f32[168,128]{1,0:T(8,128)S(1)}, f32[3,3,2,4,128]{4,3,2,1,0:T(4,128)S(1)}) custom-call(f32[16,32,128]{2,1,0:T(8,128)} %p_in.1, f32[16,32,128]{2,1,0:T(8,128)} %q_in.1, f32[16,32,128]{2,1,0:T(8,128)} %s_in.1, f32[3,2,4,128]{3,2,1,0:T(4,128)} %jit_in.1, ...), custom_call_target="tpu_custom_call" | custom-call | tf_op jit(solution)/shard_map/pack_wy/pallas_call | solution.py:152
  1.9 2.5 %collective-permute-start = (f32[80,128]{1,0:T(8,128)S(1)}, f32[80,128]{1,0:T(8,128)S(1)}, u32[]{:S(2)}, u32[]{:S(2)}) collective-permute-start(f32[80,128]{1,0:T(8,128)S(1)} %get-tuple-element.30), channel_id=1, source_target_pairs={{1,2},{2,1},{0,3},{3,0},{5,6},{6,5},{4,7},{7,4},{9,10},{10,9},{8,1... | collective-permute-start | bytes 122888 | tf_op jit(solution)/shard_map/ppermute | solution.py:49
  4.3 0.7 %collective-permute-start.1 = (f32[80,128]{1,0:T(8,128)S(1)}, f32[80,128]{1,0:T(8,128)S(1)}, u32[]{:S(2)}, u32[]{:S(2)}) collective-permute-start(f32[80,128]{1,0:T(8,128)S(1)} %get-tuple-element.31), channel_id=1, source_target_pairs={{0,1},{1,0},{2,3},{3,2},{4,5},{5,4},{6,7},{7,6},{8,9},{9,8},{10,11... | collective-permute-start | bytes 122888 | tf_op jit(solution)/shard_map/ppermute | solution.py:50
  5.0 1.3 %collective-permute-done.wyo.got_odd = f32[80,128]{1,0:T(8,128)S(1)} collective-permute-done((f32[80,128]{1,0:T(8,128)S(1)}, f32[80,128]{1,0:T(8,128)S(1)}, u32[]{:S(2)}, u32[]{:S(2)}) %collective-permute-start) | collective-permute-done | bytes 40992 | tf_op jit(solution)/shard_map/ppermute | solution.py:49
  6.3 0.0 collective-permute-done.1.wye.got_even
  6.3 5.5 %collective-permute-start.2 = (f32[168,128]{1,0:T(8,128)S(1)}, f32[168,128]{1,0:T(8,128)S(1)}, u32[]{:S(2)}, u32[]{:S(2)}) collective-permute-start(f32[168,128]{1,0:T(8,128)S(1)} %get-tuple-element.35), channel_id=1, source_target_pairs={{4,8},{8,4},{12,16},{16,12},{20,24},{24,20},{0,28},{28,0},{5,9},{9... | collective-permute-start | bytes 258056 | tf_op jit(solution)/shard_map/ppermute | solution.py:49
  11.8 0.0 collective-permute-start.3
  11.8 4.0 %wall_center.1 = (f32[2,4,40,8,128]{4,3,2,1,0:T(8,128)S(1)}, f32[2,4,4,128]{3,2,1,0:T(4,128)S(1)}, s32[2,4,2,8,128]{4,3,2,1,0:T(8,128)S(1)}, s32[4,128]{1,0:T(4,...) custom-call(s32[2,4,9,128,128]{4,3,2,1,0:T(8,128)} %masks_in.1, ...), custom_call_target="tpu_custom_call" | custom-call | tf_op jit(solution)/shard_map/wall_center/pallas_call | solution.py:534
  15.8 0.0 collective-permute-done.2.fxo
  15.8 0.6 %collective-permute-done.3.fxe = f32[168,128]{1,0:T(8,128)S(1)} collective-permute-done((f32[168,128]{1,0:T(8,128)S(1)}, f32[168,128]{1,0:T(8,128)S(1)}, u32[]{:S(2)}, u32[]{:S(2)}) %collective-permute-start.3) | collective-permute-done | bytes 86048 | tf_op jit(solution)/shard_map/ppermute | solution.py:50
  16.5 1.8 %grid_steps.1 = (f32[16,32,128]{2,1,0:T(8,128)}, f32[32,24,128]{2,1,0:T(8,128)}) custom-call(f32[16,32,128]{2,1,0:T(8,128)S(1)} %get-tuple-element.40.p, f32[16,32,128]{2,1,0:T(8,128)S(1)} %get-tuple-element.41.q, f32[16,32,128]{2,1,0:T(8,128)S(1)} %get-tuple-element.42.s, f32[80,128]{1,0:T(8,128)S(1)} %collective-permute-done.wyo.got_odd, ...), custom_call_target="tpu_custom_call" | custom-call | tf_op jit(solution)/shard_map/grid_steps/pallas_call | solution.py:333
  18.2 4.0 %all-to-all-start = ((f32[32,24,128]{2,1,0:T(8,128)}), f32[32,24,128]{2,1,0:T(8,128)S(1)}, u32[]{:S(2)}, u32[]{:S(2)}) async-start(f32[32,24,128]{2,1,0:T(8,128)} %get-tuple-element.44), calls=%async_computation | async-start | bytes 786432 | tf_op jit(solution)/shard_map/all_to_all | solution.py:774
  22.2 2.3 %wall_first.1 = (f32[2,4,40,8,128]{4,3,2,1,0:T(8,128)S(1)}, f32[3,2,4,128]{3,2,1,0:T(4,128)S(1)}, f32[3,2,4,128]{3,2,1,0:T(4,128)S(1)}, f32[2,4,128]{2,1,0:T(4,1...) custom-call(f32[3,3,2,4,128]{4,3,2,1,0:T(4,128)S(1)} %get-tuple-element.29.wall, ...), custom_call_target="tpu_custom_call" | custom-call | tf_op jit(solution)/shard_map/wall_first/pallas_call | solution.py:623
  24.5 1.6 %collective-permute-start.4 = (f32[8,128]{1,0:T(8,128)S(1)}, f32[8,128]{1,0:T(8,128)S(1)}, u32[]{:S(2)}, u32[]{:S(2)}) collective-permute-start(f32[8,128]{1,0:T(8,128)S(1)} %get-tuple-element.48), channel_id=1, source_target_pairs={{1,2},{2,1},{0,3},{3,0},{5,6},{6,5},{4,7},{7,4},{9,10},{10,9},{8,1... | collective-permute-start | bytes 12296 | tf_op jit(solution)/shard_map/ppermute | solution.py:49
  26.1 0.4 collective-permute-start.5
  26.4 1.2 %collective-permute-done.4.got_odd.wyo = f32[8,128]{1,0:T(8,128)S(1)} collective-permute-done((f32[8,128]{1,0:T(8,128)S(1)}, f32[8,128]{1,0:T(8,128)S(1)}, u32[]{:S(2)}, u32[]{:S(2)}) %collective-permute-start.4) | collective-permute-done | bytes 4128 | tf_op jit(solution)/shard_map/ppermute | solution.py:49
  27.6 0.0 collective-permute-done.5.got_even.wye
  27.6 5.0 %collective-permute-start.6 = (f32[24,128]{1,0:T(8,128)S(1)}, f32[24,128]{1,0:T(8,128)S(1)}, u32[]{:S(2)}, u32[]{:S(2)}) collective-permute-start(f32[24,128]{1,0:T(8,128)S(1)} %get-tuple-element.50), channel_id=1, source_target_pairs={{4,8},{8,4},{12,16},{16,12},{20,24},{24,20},{0,28},{28,0},{5,9},{9... | collective-permute-start | bytes 36872 | tf_op jit(solution)/shard_map/ppermute | solution.py:49
  32.7 0.0 collective-permute-start.7
  32.7 1.7 %collective-permute-done.6.fxo = f32[24,128]{1,0:T(8,128)S(1)} collective-permute-done((f32[24,128]{1,0:T(8,128)S(1)}, f32[24,128]{1,0:T(8,128)S(1)}, u32[]{:S(2)}, u32[]{:S(2)}) %collective-permute-start.6) | collective-permute-done | bytes 12320 | tf_op jit(solution)/shard_map/ppermute | solution.py:49
  34.4 1.9 %collective-permute-done.7.fxe = f32[24,128]{1,0:T(8,128)S(1)} collective-permute-done((f32[24,128]{1,0:T(8,128)S(1)}, f32[24,128]{1,0:T(8,128)S(1)}, u32[]{:S(2)}, u32[]{:S(2)}) %collective-permute-start.7) | collective-permute-done | bytes 12320 | tf_op jit(solution)/shard_map/ppermute | solution.py:50
  36.4 0.0 all-to-all-done.got
  36.4 1.7 %wall_last.1 = (f32[3,2,4,128]{3,2,1,0:T(4,128)}, f32[3,2,4,128]{3,2,1,0:T(4,128)}) custom-call(f32[2,4,40,8,128]{4,3,2,1,0:T(8,128)S(1)} %get-tuple-element.32.weights, f32[2,4,40,8,128]{4,3,2,1,0:T(8,128)S(1)} %get-tuple-element.39.end_weights, f32[32,24,128]{2,1,0:T(8,128)S(1)} %all-to-all-done.got, f32[3,2,4,128]{3,2,1,0:T(4,128)S(1)} %get-tuple-element.45.base1, ...), custom_call_target="tpu_custom_call" | custom-call | tf_op jit(solution)/shard_map/wall_last/pallas_call | solution.py:732
  (2 shorter events, 0.0 us)
Async XLA Ops:
  1.9 4.4 %collective-permute-start = (f32[80,128]{1,0:T(8,128)S(1)}, f32[80,128]{1,0:T(8,128)S(1)}, u32[]{:S(2)}, u32[]{:S(2)}) collective-permute-start(f32[80,128]{1,0:T(8,128)S(1)} %get-tuple-element.30), channel_id=1, source_target_pairs={{1,2},{2,1},{0,3},{3,0},{5,6},{6,5},{4,7},{7,4},{9,10},{10,9},{8,1... | collective-permute-start | bytes 122888 | tf_op jit(solution)/shard_map/ppermute | solution.py:49
  4.3 2.0 %collective-permute-start.1 = (f32[80,128]{1,0:T(8,128)S(1)}, f32[80,128]{1,0:T(8,128)S(1)}, u32[]{:S(2)}, u32[]{:S(2)}) collective-permute-start(f32[80,128]{1,0:T(8,128)S(1)} %get-tuple-element.31), channel_id=1, source_target_pairs={{0,1},{1,0},{2,3},{3,2},{4,5},{5,4},{6,7},{7,6},{8,9},{9,8},{10,11... | collective-permute-start | bytes 122888 | tf_op jit(solution)/shard_map/ppermute | solution.py:50
  6.3 9.5 %collective-permute-start.2 = (f32[168,128]{1,0:T(8,128)S(1)}, f32[168,128]{1,0:T(8,128)S(1)}, u32[]{:S(2)}, u32[]{:S(2)}) collective-permute-start(f32[168,128]{1,0:T(8,128)S(1)} %get-tuple-element.35), channel_id=1, source_target_pairs={{4,8},{8,4},{12,16},{16,12},{20,24},{24,20},{0,28},{28,0},{5,9},{9... | collective-permute-start | bytes 258056 | tf_op jit(solution)/shard_map/ppermute | solution.py:49
  11.8 4.7 %collective-permute-start.3 = (f32[168,128]{1,0:T(8,128)S(1)}, f32[168,128]{1,0:T(8,128)S(1)}, u32[]{:S(2)}, u32[]{:S(2)}) collective-permute-start(f32[168,128]{1,0:T(8,128)S(1)} %get-tuple-element.36), channel_id=1, source_target_pairs={{0,4},{4,0},{8,12},{12,8},{16,20},{20,16},{24,28},{28,24},{1,5},{5... | collective-permute-start | bytes 258056 | tf_op jit(solution)/shard_map/ppermute | solution.py:50
  18.2 18.1 %all-to-all-start = ((f32[32,24,128]{2,1,0:T(8,128)}), f32[32,24,128]{2,1,0:T(8,128)S(1)}, u32[]{:S(2)}, u32[]{:S(2)}) async-start(f32[32,24,128]{2,1,0:T(8,128)} %get-tuple-element.44), calls=%async_computation | async-start | bytes 786432 | tf_op jit(solution)/shard_map/all_to_all | solution.py:774
  24.5 3.1 %collective-permute-start.4 = (f32[8,128]{1,0:T(8,128)S(1)}, f32[8,128]{1,0:T(8,128)S(1)}, u32[]{:S(2)}, u32[]{:S(2)}) collective-permute-start(f32[8,128]{1,0:T(8,128)S(1)} %get-tuple-element.48), channel_id=1, source_target_pairs={{1,2},{2,1},{0,3},{3,0},{5,6},{6,5},{4,7},{7,4},{9,10},{10,9},{8,1... | collective-permute-start | bytes 12296 | tf_op jit(solution)/shard_map/ppermute | solution.py:49
  26.1 1.6 %collective-permute-start.5 = (f32[8,128]{1,0:T(8,128)S(1)}, f32[8,128]{1,0:T(8,128)S(1)}, u32[]{:S(2)}, u32[]{:S(2)}) collective-permute-start(f32[8,128]{1,0:T(8,128)S(1)} %get-tuple-element.49), channel_id=1, source_target_pairs={{0,1},{1,0},{2,3},{3,2},{4,5},{5,4},{6,7},{7,6},{8,9},{9,8},{10,11... | collective-permute-start | bytes 12296 | tf_op jit(solution)/shard_map/ppermute | solution.py:50
  27.6 6.8 %collective-permute-start.6 = (f32[24,128]{1,0:T(8,128)S(1)}, f32[24,128]{1,0:T(8,128)S(1)}, u32[]{:S(2)}, u32[]{:S(2)}) collective-permute-start(f32[24,128]{1,0:T(8,128)S(1)} %get-tuple-element.50), channel_id=1, source_target_pairs={{4,8},{8,4},{12,16},{16,12},{20,24},{24,20},{0,28},{28,0},{5,9},{9... | collective-permute-start | bytes 36872 | tf_op jit(solution)/shard_map/ppermute | solution.py:49
  32.7 3.7 %collective-permute-start.7 = (f32[24,128]{1,0:T(8,128)S(1)}, f32[24,128]{1,0:T(8,128)S(1)}, u32[]{:S(2)}, u32[]{:S(2)}) collective-permute-start(f32[24,128]{1,0:T(8,128)S(1)} %get-tuple-element.51), channel_id=1, source_target_pairs={{0,4},{4,0},{8,12},{12,8},{16,20},{20,16},{24,28},{28,24},{1,5},{5... | collective-permute-start | bytes 36872 | tf_op jit(solution)/shard_map/ppermute | solution.py:50

commit v8 on v7

--- a/solution.py
+++ b/solution.py
@@ -35,19 +35,35 @@
     return lax.rem(lax.axis_index(axis), 2) == 0
 
 
-def pair_list(count, first):
+def swap_pairs(axis, sizes, first):
+    count, others = sizes[axis], sizes[1 - axis]
     pairs = []
+
+    def join(*two):
+        a, b = [place * sizes[1] + other for place, other in two]
+        pairs.extend([(a, b), (b, a)])
+
+    def at(place, other):
+        return (place, other) if axis == 0 else (other, place)
+
+    met = set()
     for low in range(first, count - 1, 2):
-        pairs.extend([(low, low + 1), (low + 1, low)])
-    if first == 1 and count % 2 == 0 and count > 2:
-        pairs.extend([(0, count - 1), (count - 1, 0)])
+        met.update((low, low + 1))
+        for other in range(others):
+            join(at(low, other), at(low + 1, other))
+    for place in range(count):
+        if place not in met and others % 2 == 0:
+            for other in range(0, others, 2):
+                join(at(place, other), at(place, other + 1))
     return pairs
 
 
 def exchange(axis, to_odd, to_even):
-    count = lax.axis_size(axis)
-    got_odd = lax.ppermute(to_odd, axis, pair_list(count, 1))
-    got_even = lax.ppermute(to_even, axis, pair_list(count, 0))
+    names = ("fx", "wy")
+    sizes = [lax.axis_size(name) for name in names]
+    along = names.index(axis)
+    got_odd = lax.ppermute(to_odd, names, swap_pairs(along, sizes, 1))
+    got_even = lax.ppermute(to_even, names, swap_pairs(along, sizes, 0))
     return got_odd, got_even
 
 

time: 38.4 us -> 35.7 us (0.930)
  starting transfers between devices: 19.6 us -> 15.9 us
  waiting for transfers between devices: 6.8 us -> 7.74 us
    ppermute x8, starting transfers between devices: 15.6 us -> 11.8 us  [the longest x4 6.67 us: exchange(): got_even = lax.ppermute(to_even, names, swap_pairs(along, sizes, 0))]
    all_to_all x1, waiting for transfers between devices: 0.01 us -> 2.14 us  [per_device(): lax.all_to_all(slots, ('fx', 'wy'), split_axis=0, concat_axis=0, tiled=True)]
    ppermute x8, waiting for transfers between devices: 6.8 us -> 5.6 us  [the longest x4 3.83 us: exchange(): got_odd = lax.ppermute(to_odd, names, swap_pairs(along, sizes, 1))]
  transfers between devices with their start and end apart: 9 -> 9, of which waited for: 5 -> 4; matrix products, arithmetic and copies ran while one was open for 0% -> 0% of each run, Pallas kernels for 17% -> 18%
where the time goes in v8:
time: 35.7 us; the launch traced here: 35.4 us
  starting transfers between devices  15.9 us (45%)
  Pallas kernels  11 us (31%)
  waiting for transfers between devices  7.74 us (22%)
  between operations  0.71 us (2%)
    ppermute x4, starting transfers between devices, exchange(): got_even = lax.ppermute(to_even, names, swap_pairs(along, sizes, 0))  6.67 us
    ppermute x4, starting transfers between devices, exchange(): got_odd = lax.ppermute(to_odd, names, swap_pairs(along, sizes, 1))  5.09 us
    all_to_all x1, starting transfers between devices, per_device(): lax.all_to_all(slots, ('fx', 'wy'), split_axis=0, concat_axis=0, tiled=True)  4.15 us
    pallas_call x1, Pallas kernels, wall_center(): pl.pallas_call(functools.partial(center_kernel, wy_count), in_specs=[HBM]...  4 us
    ppermute x4, waiting for transfers between devices, exchange(): got_odd = lax.ppermute(to_odd, names, swap_pairs(along, sizes, 1))  3.83 us
    pallas_call x1, Pallas kernels, wall_first(): pl.pallas_call(functools.partial(wall_kernel, cx, cy), in_specs=[whole()]...  2.27 us
    all_to_all x1, waiting for transfers between devices, per_device(): lax.all_to_all(slots, ('fx', 'wy'), split_axis=0, concat_axis=0, tiled=True)  2.14 us
    ppermute x4, waiting for transfers between devices, exchange(): got_even = lax.ppermute(to_even, names, swap_pairs(along, sizes, 0))  1.76 us
  transfers between devices with their start and end apart: 9, of which 4 were waited for; matrix products, arithmetic and copies ran while one was open for 0% of the time, Pallas kernels for 18%

profile of v8, /device:TPU:0, one launch (start us, length us, event | category | flops | bytes accessed | tf_op | source)
XLA Modules:
  0.0 35.4 jit_solution(15170006131820915805)
XLA Ops:
  0.6 1.2 %pack_wy.1 = (f32[80,128]{1,0:T(8,128)S(1)}, f32[80,128]{1,0:T(8,128)S(1)}, f32[168,128]{1,0:T(8,128)S(1)}, f32[168,128]{1,0:T(8,128)S(1)}, f32[3,3,2,4,128]{4,3,2,1,0:T(4,128)S(1)}) custom-call(f32[16,32,128]{2,1,0:T(8,128)} %p_in.1, f32[16,32,128]{2,1,0:T(8,128)} %q_in.1, f32[16,32,128]{2,1,0:T(8,128)} %s_in.1, f32[3,2,4,128]{3,2,1,0:T(4,128)} %jit_in.1, ...), custom_call_target="tpu_custom_call" | custom-call | tf_op jit(solution)/shard_map/pack_wy/pallas_call | solution.py:168
  1.9 3.0 %collective-permute-start = (f32[80,128]{1,0:T(8,128)S(1)}, f32[80,128]{1,0:T(8,128)S(1)}, u32[]{:S(2)}, u32[]{:S(2)}) collective-permute-start(f32[80,128]{1,0:T(8,128)S(1)} %get-tuple-element.30), channel_id=1, source_target_pairs={{1,2},{2,1},{5,6},{6,5},{9,10},{10,9},{13,14},{14,13},{17,18},{18,... | collective-permute-start | bytes 122888 | tf_op jit(solution)/shard_map/ppermute | solution.py:65
  4.9 0.1 collective-permute-start.1
  5.0 1.8 %collective-permute-done.wyo.got_odd = f32[80,128]{1,0:T(8,128)S(1)} collective-permute-done((f32[80,128]{1,0:T(8,128)S(1)}, f32[80,128]{1,0:T(8,128)S(1)}, u32[]{:S(2)}, u32[]{:S(2)}) %collective-permute-start) | collective-permute-done | bytes 40992 | tf_op jit(solution)/shard_map/ppermute | solution.py:65
  6.9 0.0 collective-permute-done.1.wye.got_even
  6.9 0.2 collective-permute-start.2
  7.1 3.5 %collective-permute-start.3 = (f32[168,128]{1,0:T(8,128)S(1)}, f32[168,128]{1,0:T(8,128)S(1)}, u32[]{:S(2)}, u32[]{:S(2)}) collective-permute-start(f32[168,128]{1,0:T(8,128)S(1)} %get-tuple-element.36), channel_id=1, source_target_pairs={{0,4},{4,0},{1,5},{5,1},{2,6},{6,2},{3,7},{7,3},{8,12},{12,8},{9,1... | collective-permute-start | bytes 258056 | tf_op jit(solution)/shard_map/ppermute | solution.py:66
  10.5 4.0 %wall_center.1 = (f32[2,4,40,8,128]{4,3,2,1,0:T(8,128)S(1)}, f32[2,4,4,128]{3,2,1,0:T(4,128)S(1)}, s32[2,4,2,8,128]{4,3,2,1,0:T(8,128)S(1)}, s32[4,128]{1,0:T(4,...) custom-call(s32[2,4,9,128,128]{4,3,2,1,0:T(8,128)} %masks_in.1, ...), custom_call_target="tpu_custom_call" | custom-call | tf_op jit(solution)/shard_map/wall_center/pallas_call | solution.py:550
  14.5 0.0 collective-permute-done.2.fxo
  14.5 0.0 collective-permute-done.3.fxe
  14.6 1.8 %grid_steps.1 = (f32[16,32,128]{2,1,0:T(8,128)}, f32[32,24,128]{2,1,0:T(8,128)}) custom-call(f32[16,32,128]{2,1,0:T(8,128)S(1)} %get-tuple-element.40.p, f32[16,32,128]{2,1,0:T(8,128)S(1)} %get-tuple-element.41.q, f32[16,32,128]{2,1,0:T(8,128)S(1)} %get-tuple-element.42.s, f32[80,128]{1,0:T(8,128)S(1)} %collective-permute-done.wyo.got_odd, ...), custom_call_target="tpu_custom_call" | custom-call | tf_op jit(solution)/shard_map/grid_steps/pallas_call | solution.py:349
  16.3 4.1 %all-to-all-start = ((f32[32,24,128]{2,1,0:T(8,128)}), f32[32,24,128]{2,1,0:T(8,128)S(1)}, u32[]{:S(2)}, u32[]{:S(2)}) async-start(f32[32,24,128]{2,1,0:T(8,128)} %get-tuple-element.44), calls=%async_computation | async-start | bytes 786432 | tf_op jit(solution)/shard_map/all_to_all | solution.py:790
  20.5 2.3 %wall_first.1 = (f32[2,4,40,8,128]{4,3,2,1,0:T(8,128)S(1)}, f32[3,2,4,128]{3,2,1,0:T(4,128)S(1)}, f32[3,2,4,128]{3,2,1,0:T(4,128)S(1)}, f32[2,4,128]{2,1,0:T(4,1...) custom-call(f32[3,3,2,4,128]{4,3,2,1,0:T(4,128)S(1)} %get-tuple-element.29.wall, ...), custom_call_target="tpu_custom_call" | custom-call | tf_op jit(solution)/shard_map/wall_first/pallas_call | solution.py:639
  22.7 1.8 %collective-permute-start.4 = (f32[8,128]{1,0:T(8,128)S(1)}, f32[8,128]{1,0:T(8,128)S(1)}, u32[]{:S(2)}, u32[]{:S(2)}) collective-permute-start(f32[8,128]{1,0:T(8,128)S(1)} %get-tuple-element.48), channel_id=1, source_target_pairs={{1,2},{2,1},{5,6},{6,5},{9,10},{10,9},{13,14},{14,13},{17,18},{18,... | collective-permute-start | bytes 12296 | tf_op jit(solution)/shard_map/ppermute | solution.py:65
  24.6 0.1 collective-permute-start.5
  24.7 2.0 %collective-permute-done.4.got_odd.wyo = f32[8,128]{1,0:T(8,128)S(1)} collective-permute-done((f32[8,128]{1,0:T(8,128)S(1)}, f32[8,128]{1,0:T(8,128)S(1)}, u32[]{:S(2)}, u32[]{:S(2)}) %collective-permute-start.4) | collective-permute-done | bytes 4128 | tf_op jit(solution)/shard_map/ppermute | solution.py:65
  26.7 0.0 collective-permute-done.5.got_even.wye
  26.7 0.1 collective-permute-start.6
  26.8 3.0 %collective-permute-start.7 = (f32[24,128]{1,0:T(8,128)S(1)}, f32[24,128]{1,0:T(8,128)S(1)}, u32[]{:S(2)}, u32[]{:S(2)}) collective-permute-start(f32[24,128]{1,0:T(8,128)S(1)} %get-tuple-element.51), channel_id=1, source_target_pairs={{0,4},{4,0},{1,5},{5,1},{2,6},{6,2},{3,7},{7,3},{8,12},{12,8},{9,1... | collective-permute-start | bytes 36872 | tf_op jit(solution)/shard_map/ppermute | solution.py:66
  29.7 0.0 collective-permute-done.6.fxo
  29.7 1.8 %collective-permute-done.7.fxe = f32[24,128]{1,0:T(8,128)S(1)} collective-permute-done((f32[24,128]{1,0:T(8,128)S(1)}, f32[24,128]{1,0:T(8,128)S(1)}, u32[]{:S(2)}, u32[]{:S(2)}) %collective-permute-start.7) | collective-permute-done | bytes 12320 | tf_op jit(solution)/shard_map/ppermute | solution.py:66
  31.5 2.1 %all-to-all-done.got = f32[32,24,128]{2,1,0:T(8,128)S(1)} async-done(((f32[32,24,128]{2,1,0:T(8,128)}), f32[32,24,128]{2,1,0:T(8,128)S(1)}, u32[]{:S(2)}, u32[]{:S(2)}) %all-to-all-start) | async-done | bytes 393248 | tf_op jit(solution)/shard_map/all_to_all | solution.py:790
  33.6 1.7 %wall_last.1 = (f32[3,2,4,128]{3,2,1,0:T(4,128)}, f32[3,2,4,128]{3,2,1,0:T(4,128)}) custom-call(f32[2,4,40,8,128]{4,3,2,1,0:T(8,128)S(1)} %get-tuple-element.32.weights, f32[2,4,40,8,128]{4,3,2,1,0:T(8,128)S(1)} %get-tuple-element.39.end_weights, f32[32,24,128]{2,1,0:T(8,128)S(1)} %all-to-all-done.got, f32[3,2,4,128]{3,2,1,0:T(4,128)S(1)} %get-tuple-element.45.base1, ...), custom_call_target="tpu_custom_call" | custom-call | tf_op jit(solution)/shard_map/wall_last/pallas_call | solution.py:748
  (2 shorter events, 0.0 us)
Async XLA Ops:
  1.9 5.0 %collective-permute-start = (f32[80,128]{1,0:T(8,128)S(1)}, f32[80,128]{1,0:T(8,128)S(1)}, u32[]{:S(2)}, u32[]{:S(2)}) collective-permute-start(f32[80,128]{1,0:T(8,128)S(1)} %get-tuple-element.30), channel_id=1, source_target_pairs={{1,2},{2,1},{5,6},{6,5},{9,10},{10,9},{13,14},{14,13},{17,18},{18,... | collective-permute-start | bytes 122888 | tf_op jit(solution)/shard_map/ppermute | solution.py:65
  4.9 2.0 %collective-permute-start.1 = (f32[80,128]{1,0:T(8,128)S(1)}, f32[80,128]{1,0:T(8,128)S(1)}, u32[]{:S(2)}, u32[]{:S(2)}) collective-permute-start(f32[80,128]{1,0:T(8,128)S(1)} %get-tuple-element.31), channel_id=1, source_target_pairs={{0,1},{1,0},{4,5},{5,4},{8,9},{9,8},{12,13},{13,12},{16,17},{17,16... | collective-permute-start | bytes 122888 | tf_op jit(solution)/shard_map/ppermute | solution.py:66
  6.9 7.6 %collective-permute-start.2 = (f32[168,128]{1,0:T(8,128)S(1)}, f32[168,128]{1,0:T(8,128)S(1)}, u32[]{:S(2)}, u32[]{:S(2)}) collective-permute-start(f32[168,128]{1,0:T(8,128)S(1)} %get-tuple-element.35), channel_id=1, source_target_pairs={{4,8},{8,4},{5,9},{9,5},{6,10},{10,6},{7,11},{11,7},{12,16},{16,12... | collective-permute-start | bytes 258056 | tf_op jit(solution)/shard_map/ppermute | solution.py:65
  7.1 7.5 %collective-permute-start.3 = (f32[168,128]{1,0:T(8,128)S(1)}, f32[168,128]{1,0:T(8,128)S(1)}, u32[]{:S(2)}, u32[]{:S(2)}) collective-permute-start(f32[168,128]{1,0:T(8,128)S(1)} %get-tuple-element.36), channel_id=1, source_target_pairs={{0,4},{4,0},{1,5},{5,1},{2,6},{6,2},{3,7},{7,3},{8,12},{12,8},{9,1... | collective-permute-start | bytes 258056 | tf_op jit(solution)/shard_map/ppermute | solution.py:66
  16.3 17.3 %all-to-all-start = ((f32[32,24,128]{2,1,0:T(8,128)}), f32[32,24,128]{2,1,0:T(8,128)S(1)}, u32[]{:S(2)}, u32[]{:S(2)}) async-start(f32[32,24,128]{2,1,0:T(8,128)} %get-tuple-element.44), calls=%async_computation | async-start | bytes 786432 | tf_op jit(solution)/shard_map/all_to_all | solution.py:790
  22.7 3.9 %collective-permute-start.4 = (f32[8,128]{1,0:T(8,128)S(1)}, f32[8,128]{1,0:T(8,128)S(1)}, u32[]{:S(2)}, u32[]{:S(2)}) collective-permute-start(f32[8,128]{1,0:T(8,128)S(1)} %get-tuple-element.48), channel_id=1, source_target_pairs={{1,2},{2,1},{5,6},{6,5},{9,10},{10,9},{13,14},{14,13},{17,18},{18,... | collective-permute-start | bytes 12296 | tf_op jit(solution)/shard_map/ppermute | solution.py:65
  24.6 2.1 %collective-permute-start.5 = (f32[8,128]{1,0:T(8,128)S(1)}, f32[8,128]{1,0:T(8,128)S(1)}, u32[]{:S(2)}, u32[]{:S(2)}) collective-permute-start(f32[8,128]{1,0:T(8,128)S(1)} %get-tuple-element.49), channel_id=1, source_target_pairs={{0,1},{1,0},{4,5},{5,4},{8,9},{9,8},{12,13},{13,12},{16,17},{17,16... | collective-permute-start | bytes 12296 | tf_op jit(solution)/shard_map/ppermute | solution.py:66
  26.7 3.0 %collective-permute-start.6 = (f32[24,128]{1,0:T(8,128)S(1)}, f32[24,128]{1,0:T(8,128)S(1)}, u32[]{:S(2)}, u32[]{:S(2)}) collective-permute-start(f32[24,128]{1,0:T(8,128)S(1)} %get-tuple-element.50), channel_id=1, source_target_pairs={{4,8},{8,4},{5,9},{9,5},{6,10},{10,6},{7,11},{11,7},{12,16},{16,12... | collective-permute-start | bytes 36872 | tf_op jit(solution)/shard_map/ppermute | solution.py:65
  26.8 4.7 %collective-permute-start.7 = (f32[24,128]{1,0:T(8,128)S(1)}, f32[24,128]{1,0:T(8,128)S(1)}, u32[]{:S(2)}, u32[]{:S(2)}) collective-permute-start(f32[24,128]{1,0:T(8,128)S(1)} %get-tuple-element.51), channel_id=1, source_target_pairs={{0,4},{4,0},{1,5},{5,1},{2,6},{6,2},{3,7},{7,3},{8,12},{12,8},{9,1... | collective-permute-start | bytes 36872 | tf_op jit(solution)/shard_map/ppermute | solution.py:66

commit v9 on v8

--- a/solution.py
+++ b/solution.py
@@ -89,7 +89,7 @@
 
 
 def pack_wy_kernel(
-    p, q, s, jit_in, disp_in, vel_in, wy_odd, wy_even, fx_odd, fx_even, wall, edges, ends, sems
+    p, q, s, jit_in, disp_in, vel_in, wy_odd, wy_even, ends, wall, edges, sems
 ):
     cx, cy = p.shape[0], p.shape[1]
     rows, cols = jit_in.shape[1], jit_in.shape[2]
@@ -135,22 +135,6 @@
         wy_odd,
     )
 
-    def end(side, near, far, l):
-        def write(out):
-            out[0:cy, :] = ends[side, near]
-            out[cy : 2 * cy, :] = ends[side, far]
-            out[2 * cy : 3 * cy, :] = ends[side, 2]
-            out[3 * cy : 4 * cy, :] = ends[side, 3]
-            at = 4 * cy
-            for field in range(2):
-                for c in range(3):
-                    out[at + 1 : at + 1 + cols, :] = wall[field, c, l]
-                    at += cols + 2
-
-        return write
-
-    place_edges(even_at("fx"), end(0, 0, 1, 0), end(1, 1, 0, rows - 1), fx_even, fx_odd)
-
 
 def in_hbm(*arrays):
     return [pltpu.with_memory_space_constraint(v, pltpu.HBM) for v in arrays]
@@ -162,17 +146,15 @@
 
 def pack_wy(p, q, s, jit, disp, vel):
     cx, cy = p.shape[0], p.shape[1]
-    rows, cols = jit.shape[1], jit.shape[2]
+    rows = jit.shape[1]
     wy_out = vmem(pad8(4 * cx + 6 * rows), LANES)
-    fx_out = vmem(pad8(4 * cy + 6 * (cols + 2) + 2), LANES)
     return pl.pallas_call(
         pack_wy_kernel,
         in_specs=[HBM] * 6,
-        out_specs=[whole()] * 5,
-        out_shape=[wy_out, wy_out, fx_out, fx_out, vmem(3, *jit.shape)],
+        out_specs=[whole()] * 4,
+        out_shape=[wy_out, wy_out, vmem(2, 4, cy, LANES), vmem(3, *jit.shape)],
         scratch_shapes=[
             pltpu.VMEM((6, cx, SUB, LANES), F32),
-            pltpu.VMEM((2, 4, cy, LANES), F32),
             pltpu.SemaphoreType.DMA((15,)),
         ],
         compiler_params=params(),
@@ -180,37 +162,60 @@
     )(*in_hbm(p, q, s, jit, disp, vel))
 
 
-def pack_fx_kernel(cx, cy, rows, cols, part_odd, part_even, got_odd, got_even, to_odd, to_even):
+def wall_lanes(field, low):
+    lane = lax.broadcasted_iota(jnp.int32, field.shape, 1) % 8
+    return lane < 3 if low else lane > 4
+
+
+def pack_fx_kernel(cx, ends, wall, got_odd, got_even, to_odd, to_even, line):
+    cy = ends.shape[2]
+    rows, cols = wall.shape[2], wall.shape[3]
     before, after = before_after("wy", got_even, got_odd)
-    to_even[...] = part_even[...]
-    to_odd[...] = part_odd[...]
-
-    def corners(x, l):
+
+    def edge(side, near, far, x, l):
         def write(out):
-            at = 4 * cy
-            for k in range(6):
-                side = 4 * cx + k * rows + l
-                out[at : at + 1, :] = before[side : side + 1]
-                out[at + 1 + cols : at + 2 + cols, :] = after[side : side + 1]
+            line[SUB - 1 : SUB, :] = before[x : x + 1]
+            line[SUB : SUB + cy, :] = ends[side, near]
+            line[SUB + cy : SUB + cy + 1, :] = after[x : x + 1]
+            mine, speed = ends[side, near], ends[side, 3]
+            beside = ends[side, far] + line[SUB - 1 : SUB - 1 + cy, :] + line[SUB + 1 : SUB + 1 + cy, :]
+            out[0:cy, :] = mine
+            out[cy : 2 * cy, :] = update(mine, ends[side, 2], speed, beside)
+            out[2 * cy : 3 * cy, :] = speed
+            at = 3 * cy
+            for c in range(3):
+                pair = []
+                for field in range(2):
+                    row = 4 * cx + (field * 3 + c) * rows + l
+                    parts = (before[row : row + 1], wall[field, c, l], after[row : row + 1])
+                    pair.append(jnp.concatenate(parts, axis=0))
+                moved = pltpu.roll(pair[1], 3 if side == 0 else LANES - 3, 1)
+                out[at : at + cols + 2, :] = jnp.where(wall_lanes(moved, side == 0), pair[0], moved)
                 at += cols + 2
             out[at : at + 1, :] = before[x : x + 1]
             out[at + 1 : at + 2, :] = after[x : x + 1]
+            for spare in range(at + 2, out.shape[0]):
+                out[spare : spare + 1, :] = jnp.zeros((1, LANES), F32)
 
         return write
 
-    place_edges(even_at("fx"), corners(0, 0), corners(cx - 1, rows - 1), to_even, to_odd)
-
-
-def pack_fx(sizes, parts, got):
-    out = vmem(*parts[0].shape)
+    place_edges(
+        even_at("fx"), edge(0, 0, 1, 0, 0), edge(1, 1, 0, cx - 1, rows - 1), to_even, to_odd
+    )
+
+
+def pack_fx(cx, ends, wall, got):
+    cy, cols = ends.shape[2], wall.shape[3]
+    out = vmem(pad8(3 * cy + 3 * (cols + 2) + 2), LANES)
     return pl.pallas_call(
-        functools.partial(pack_fx_kernel, *sizes),
+        functools.partial(pack_fx_kernel, cx),
         in_specs=[whole()] * 4,
         out_specs=[whole()] * 2,
         out_shape=[out, out],
+        scratch_shapes=[vmem(cy + 2 * SUB, LANES)],
         compiler_params=params(),
         name="pack_fx",
-    )(*parts, *got)
+    )(ends, wall, *got)
 
 
 def along_z(v):
@@ -239,7 +244,7 @@
     wy_count = high // cols
     before_y, after_y = before_after("wy", wye, wyo)
     before_x, after_x = before_after("fx", fxe, fxo)
-    corner = 4 * cy + 6 * (cols + 2)
+    corner = 3 * cy + 3 * (cols + 2)
 
     s0[1 : cx + 1, ahead:behind, :] = p[...]
     for x, side in ((0, before_x), (cx + 1, after_x)):
@@ -255,11 +260,8 @@
         beside = s0[0:cx, y, :] + s0[2 : cx + 2, y, :] + far + s0[1 : cx + 1, inner, :]
         s1[1 : cx + 1, y, :] = update(near, old, speed, beside)
     for side, x, inner in ((before_x, 0, 1), (after_x, cx + 1, cx)):
-        near, far = side[0:cy], side[cy : 2 * cy]
-        old, speed = side[2 * cy : 3 * cy], side[3 * cy : 4 * cy]
-        beside = s0[x, ahead - 1 : behind - 1, :] + s0[x, ahead + 1 : behind + 1, :]
-        beside = beside + far + s0[inner, ahead:behind, :]
-        s1[x, ahead:behind, :] = update(near, old, speed, beside)
+        part, speed = side[cy : 2 * cy], side[2 * cy : 3 * cy]
+        s1[x, ahead:behind, :] = part + speed * s0[inner, ahead:behind, :]
 
     def sweep(now, old, x):
         beside = now[x, ahead:behind, :] + now[x + 2, ahead:behind, :]
@@ -413,6 +415,16 @@
         pad[c, rows + 1, 0 : cols + 2, :] = after[row : row + cols + 2]
 
 
+def fill_x_shared(jpad, dpad, rows, cols, before, after, at):
+    for c in range(3):
+        row = at + c * (cols + 2)
+        for message, l, low in ((before, 0, False), (after, rows + 1, True)):
+            both = message[row : row + cols + 2]
+            jpad[c, l, 0 : cols + 2, :] = jnp.where(wall_lanes(both, low), both, 0.0)
+            moved = pltpu.roll(both, LANES - 3 if low else 3, 1)
+            dpad[c, l, 0 : cols + 2, :] = moved
+
+
 def lattice_rows():
     index = lax.broadcasted_iota(jnp.int32, (1, LANES), 1)
     places = (index % 8, index // 8 % 4, index // 32)
@@ -423,13 +435,22 @@
 RISE = 4.0 / REACH
 
 
-def mine_columns(ref, lattice, l, h):
-    sub = lax.broadcasted_iota(jnp.int32, (SUB, LANES), 0)
+def spread_mine(ref, lattice, l, h):
     own = []
     for c in range(3):
-        row = ref[c, l + 1, pl.ds(h + 1, 1), :] * (1.0 / REACH) + lattice[c]
-        own.append(jnp.broadcast_to(row, (SUB, LANES)))
-    return jnp.transpose(jnp.where(sub == 0, own[0], jnp.where(sub == 1, own[1], own[2])))
+        own.append(ref[c, l + 1, pl.ds(h + 1, 1), :] * (1.0 / REACH) + lattice[c])
+    rest = jnp.concatenate(own + [jnp.zeros((1, LANES), F32)], axis=0)
+    terms = []
+    for _ in range(3):
+        term = rest.astype(BF16).astype(F32)
+        terms.append(term)
+        rest = rest - term
+    terms.append(jnp.zeros((4, LANES), F32))
+    columns = jnp.transpose(jnp.concatenate(terms, axis=0)).astype(BF16)
+    row = lax.broadcasted_iota(jnp.int32, (16, 3 * LANES), 0)
+    lane = lax.broadcasted_iota(jnp.int32, (16, 3 * LANES), 1)
+    ones = jnp.where((row % 4 == lane // LANES) & (row < 12), 1.0, 0.0).astype(BF16)
+    return jnp.dot(columns, ones, preferred_element_type=F32)
 
 
 def bond_row(weight, others, mine):
@@ -443,7 +464,7 @@
     place = 0
     for g in range(LANES // SUB):
         span = slice(g * SUB, (g + 1) * SUB)
-        mine = [jnp.broadcast_to(columns[span, c : c + 1], (SUB, LANES)) for c in range(3)]
+        mine = [columns[span, c * LANES : (c + 1) * LANES] for c in range(3)]
         sums = [None] * 4
         for order, dh in enumerate(reached(g)):
             here = [others[c][dh] for c in range(3)]
@@ -456,23 +477,21 @@
             acc[l, h, c, span, :] = sums[c]
 
 
+def tile_sums(acc, l, h, count):
+    ones = jnp.ones((2 * SUB, 2 * LANES), BF16)
+    terms = [jnp.concatenate(two_terms(acc[l, h, c]), axis=1) for c in range(count)]
+    sums = lax.dot_general(
+        ones,
+        jnp.concatenate(terms, axis=0),
+        (((1,), (1,)), ((), ())),
+        preferred_element_type=F32,
+    )[0:1]
+    return [sums[:, c * LANES : (c + 1) * LANES] for c in range(count)]
+
+
 def lane_sums(acc, l, cols, count):
-    ones = jnp.ones((2 * SUB, LANES), BF16)
-    result = [[] for _ in range(count)]
-    for h in range(cols):
-        terms = []
-        for c in range(count):
-            terms.extend(two_terms(acc[l, h, c]))
-        sums = lax.dot_general(
-            ones,
-            jnp.concatenate(terms, axis=0),
-            (((1,), (1,)), ((), ())),
-            preferred_element_type=F32,
-        )[0:1]
-        for c in range(count):
-            at = 2 * c * LANES
-            result[c].append(sums[:, at : at + LANES] + sums[:, at + LANES : at + 2 * LANES])
-    return [jnp.concatenate(parts, axis=0) for parts in result]
+    tiles = [tile_sums(acc, l, h, count) for h in range(cols)]
+    return [jnp.concatenate(rows, axis=0) for rows in zip(*tiles)]
 
 
 def quotient(v, n):
@@ -489,13 +508,21 @@
     pairs = [(device_in, route.at[0]), (tile_in, route.at[1])]
     pairs = [(p_in, p), (q_in, q), (s_in, s)] + pairs
     for k, pair in enumerate(pairs):
-        copies[k] = pltpu.make_async_copy(*pair, sems.at[rows * cols + k])
-    for h in range(cols):
-        for l in range(rows):
-            copies[l, h] = pltpu.make_async_copy(
-                masks_in.at[l, h], masks.at[l, h], sems.at[l * cols + h]
+        copies[k] = pltpu.make_async_copy(*pair, sems.at[k])
+    tiles = [(l, h) for h in range(cols) for l in range(rows)]
+    at = rows * cols
+    for k, first in enumerate((3, 0, 6)):
+        for n, (l, h) in enumerate(tiles):
+            copies[l, h, first] = pltpu.make_async_copy(
+                masks_in.at[l, h, first : first + 3],
+                masks.at[l, h, first : first + 3],
+                sems.at[5 + k * at + n],
             )
-    for copy in copies.values():
+    order = [copies[k] for k in (3, 4)]
+    order += [copies[l, h, 3] for l, h in tiles]
+    order += [copies[l, h, first] for l, h in tiles for first in (0, 6)]
+    order += [copies[k] for k in range(3)]
+    for copy in order:
         copy.start()
     first_sub = lax.broadcasted_iota(jnp.int32, (SUB, LANES), 0) < SUB // 2
     copies[3].wait()
@@ -510,7 +537,7 @@
     lattice = lattice_rows()
 
     def one_tile(l, h):
-        columns = mine_columns(jpad, lattice, l, h)
+        columns = spread_mine(jpad, lattice, l, h)
         others = []
         for c in range(3):
             mid = mid_rows(jpad, c, l, h)
@@ -520,27 +547,39 @@
                     mid[dh] = mid[dh] + RISE * dh
             others.append(mid)
         pulls = [mid_rows(dpad, c, l, h) for c in range(3)]
-        words = [jnp.zeros((SUB, LANES), jnp.int32) for _ in range(2)]
 
         def weight_of(g, order, dh, here, mine):
             span = slice(g * SUB, (g + 1) * SUB)
-            before = masks[l, h, 1 + dh, span, :]
-            after = masks[l, h, 7 + dh, span, :]
-            place = 3 * (g % 8) + order
-            words[g // 8] = words[g // 8] + jnp.where(first_sub, before, after) * (1 << place)
             return bond_row(masks[l, h, 4 + dh, span, :].astype(F32), here, mine)
 
         tile_pass(l, h, columns, others, pulls, weight_of, weights, acc)
+
+    def put_sums(l, h):
+        for c, sums in enumerate(tile_sums(acc, l, h, 4)):
+            part[l, c, h : h + 1, :] = sums
+
+    def put_bits(l, h):
+        words = [jnp.zeros((SUB, LANES), jnp.int32) for _ in range(2)]
+        for g in range(LANES // SUB):
+            span = slice(g * SUB, (g + 1) * SUB)
+            for order, dh in enumerate(reached(g)):
+                before = masks[l, h, 1 + dh, span, :]
+                after = masks[l, h, 7 + dh, span, :]
+                place = 3 * (g % 8) + order
+                words[g // 8] = words[g // 8] + jnp.where(first_sub, before, after) * (1 << place)
         for k in range(2):
             bits[l, h, k] = words[k]
 
-    for h in range(cols):
-        for l in range(rows):
-            copies[l, h].wait()
-            one_tile(l, h)
-    for l in range(rows):
-        for c, sums in enumerate(lane_sums(acc, l, cols, 4)):
-            part[l, c] = sums
+    for n, (l, h) in enumerate(tiles):
+        copies[l, h, 3].wait()
+        one_tile(l, h)
+        if n > 0:
+            put_sums(*tiles[n - 1])
+    put_sums(*tiles[-1])
+    for l, h in tiles:
+        copies[l, h, 0].wait()
+        copies[l, h, 6].wait()
+        put_bits(l, h)
     for k in range(3):
         copies[k].wait()
 
@@ -564,7 +603,7 @@
             vmem(rows, cols, 4, LANES, LANES),
             pltpu.VMEM(masks.shape, jnp.int32),
             pltpu.VMEM((2,) + device.shape, jnp.int32),
-            pltpu.SemaphoreType.DMA((rows * cols + 5,)),
+            pltpu.SemaphoreType.DMA((5 + 3 * rows * cols,)),
         ],
         compiler_params=params(),
         name="wall_center",
@@ -581,12 +620,11 @@
     fill_y(jpad, wall.at[0], before, after, 4 * cx)
     fill_y(dpad, wall.at[1], before, after, 4 * cx + 3 * rows)
     before, after = before_after("fx", fxe, fxo)
-    fill_x(jpad, rows, cols, before, after, 4 * cy)
-    fill_x(dpad, rows, cols, before, after, 4 * cy + 3 * (cols + 2))
+    fill_x_shared(jpad, dpad, rows, cols, before, after, 3 * cy)
     lattice = lattice_rows()
 
     def one_tile(l, h):
-        columns = mine_columns(jpad, lattice, l, h)
+        columns = spread_mine(jpad, lattice, l, h)
         others = []
         for c in range(3):
             ends = end_rows(jpad, c, l, h, first_sub)
@@ -775,12 +813,11 @@
     device = route_device.reshape(-1, LANES)
     tile = route_tile.reshape(-1, LANES)
     cx, cy = pressure.shape[0], pressure.shape[1]
-    rows = displacement.shape[1]
-    *sends, part_odd, part_even, wall = pack_wy(
+    *sends, ends, wall = pack_wy(
         pressure, pressure_prev, speed_sq, jitter, displacement, velocity
     )
     wy_got = exchange("wy", *sends)
-    sends = pack_fx((cx, cy, rows, cols), (part_odd, part_even), wy_got)
+    sends = pack_fx(cx, ends, wall, wy_got)
     fx_got = exchange("fx", *sends)
     grids = (pressure, pressure_prev, speed_sq)
     weights, part, bits, target, *grids = wall_center(

time: 35.7 us -> 35.8 us (level)
  waiting for transfers between devices: 7.74 us -> 7.35 us
where the time goes in v9:
time: 35.8 us; the launch traced here: 35.5 us
  starting transfers between devices  16.1 us (45%)
  Pallas kernels  11.3 us (32%)
  waiting for transfers between devices  7.35 us (21%)
  between operations  0.7 us (2%)
    ppermute x4, starting transfers between devices, exchange(): got_even = lax.ppermute(to_even, names, swap_pairs(along, sizes, 0))  6.61 us
    ppermute x4, starting transfers between devices, exchange(): got_odd = lax.ppermute(to_odd, names, swap_pairs(along, sizes, 1))  5.36 us
    all_to_all x1, starting transfers between devices, per_device(): lax.all_to_all(slots, ('fx', 'wy'), split_axis=0, concat_axis=0, tiled=True)  4.14 us
    pallas_call x1, Pallas kernels, wall_center(): pl.pallas_call(functools.partial(center_kernel, wy_count), in_specs=[HBM]...  4.05 us
    ppermute x4, waiting for transfers between devices, exchange(): got_odd = lax.ppermute(to_odd, names, swap_pairs(along, sizes, 1))  3.66 us
    pallas_call x1, Pallas kernels, wall_first(): pl.pallas_call(functools.partial(wall_kernel, cx, cy), in_specs=[whole()]...  2.45 us
    all_to_all x1, waiting for transfers between devices, per_device(): lax.all_to_all(slots, ('fx', 'wy'), split_axis=0, concat_axis=0, tiled=True)  1.92 us
    ppermute x4, waiting for transfers between devices, exchange(): got_even = lax.ppermute(to_even, names, swap_pairs(along, sizes, 0))  1.77 us
  transfers between devices with their start and end apart: 9, of which 4 were waited for; matrix products, arithmetic and copies ran while one was open for 0% of the time, Pallas kernels for 18%

profile of v9, /device:TPU:0, one launch (start us, length us, event | category | flops | bytes accessed | tf_op | source)
XLA Modules:
  0.0 35.5 jit_solution(3009555339193424262)
XLA Ops:
  0.6 1.2 %pack_wy.1 = (f32[80,128]{1,0:T(8,128)S(1)}, f32[80,128]{1,0:T(8,128)S(1)}, f32[2,4,32,128]{3,2,1,0:T(8,128)S(1)}, f32[3,3,2,4,128]{4,3,2,1,0:T(4,128)S(1)}) custom-call(f32[16,32,128]{2,1,0:T(8,128)} %p_in.1, f32[16,32,128]{2,1,0:T(8,128)} %q_in.1, f32[16,32,128]{2,1,0:T(8,128)} %s_in.1, f32[3,2,4,128]{3,2,1,0:T(4,128)} %jit_in.1, ...), custom_call_target="tpu_custom_call" | custom-call | tf_op jit(solution)/shard_map/pack_wy/pallas_call | solution.py:151
  1.8 3.0 %collective-permute-start = (f32[80,128]{1,0:T(8,128)S(1)}, f32[80,128]{1,0:T(8,128)S(1)}, u32[]{:S(2)}, u32[]{:S(2)}) collective-permute-start(f32[80,128]{1,0:T(8,128)S(1)} %get-tuple-element.29), channel_id=1, source_target_pairs={{1,2},{2,1},{5,6},{6,5},{9,10},{10,9},{13,14},{14,13},{17,18},{18,... | collective-permute-start | bytes 122888 | tf_op jit(solution)/shard_map/ppermute | solution.py:65
  4.8 0.1 collective-permute-start.1
  5.0 1.8 %collective-permute-done.wyo.got_odd = f32[80,128]{1,0:T(8,128)S(1)} collective-permute-done((f32[80,128]{1,0:T(8,128)S(1)}, f32[80,128]{1,0:T(8,128)S(1)}, u32[]{:S(2)}, u32[]{:S(2)}) %collective-permute-start) | collective-permute-done | bytes 40992 | tf_op jit(solution)/shard_map/ppermute | solution.py:65
  6.8 0.0 collective-permute-done.1.wye.got_even
  6.8 0.1 pack_fx.1
  6.9 0.2 collective-permute-start.2
  7.1 3.5 %collective-permute-start.3 = (f32[120,128]{1,0:T(8,128)S(1)}, f32[120,128]{1,0:T(8,128)S(1)}, u32[]{:S(2)}, u32[]{:S(2)}) collective-permute-start(f32[120,128]{1,0:T(8,128)S(1)} %get-tuple-element.34), channel_id=1, source_target_pairs={{0,4},{4,0},{1,5},{5,1},{2,6},{6,2},{3,7},{7,3},{8,12},{12,8},{9,1... | collective-permute-start | bytes 184328 | tf_op jit(solution)/shard_map/ppermute | solution.py:66
  10.6 4.0 %wall_center.1 = (f32[2,4,40,8,128]{4,3,2,1,0:T(8,128)S(1)}, f32[2,4,4,128]{3,2,1,0:T(4,128)S(1)}, s32[2,4,2,8,128]{4,3,2,1,0:T(8,128)S(1)}, s32[4,128]{1,0:T(4,...) custom-call(s32[2,4,9,128,128]{4,3,2,1,0:T(8,128)} %masks_in.1, ...), custom_call_target="tpu_custom_call" | custom-call | tf_op jit(solution)/shard_map/wall_center/pallas_call | solution.py:589
  14.6 0.0 collective-permute-done.2.fxo
  14.6 0.0 collective-permute-done.3.fxe
  14.7 1.7 %grid_steps.1 = (f32[16,32,128]{2,1,0:T(8,128)}, f32[32,24,128]{2,1,0:T(8,128)}) custom-call(f32[16,32,128]{2,1,0:T(8,128)S(1)} %get-tuple-element.38.p, f32[16,32,128]{2,1,0:T(8,128)S(1)} %get-tuple-element.39.q, f32[16,32,128]{2,1,0:T(8,128)S(1)} %get-tuple-element.40.s, f32[80,128]{1,0:T(8,128)S(1)} %collective-permute-done.wyo.got_odd, ...), custom_call_target="tpu_custom_call" | custom-call | tf_op jit(solution)/shard_map/grid_steps/pallas_call | solution.py:351
  16.4 4.1 %all-to-all-start = ((f32[32,24,128]{2,1,0:T(8,128)}), f32[32,24,128]{2,1,0:T(8,128)S(1)}, u32[]{:S(2)}, u32[]{:S(2)}) async-start(f32[32,24,128]{2,1,0:T(8,128)} %get-tuple-element.42), calls=%async_computation | async-start | bytes 786432 | tf_op jit(solution)/shard_map/all_to_all | solution.py:827
  20.5 2.4 %wall_first.1 = (f32[2,4,40,8,128]{4,3,2,1,0:T(8,128)S(1)}, f32[3,2,4,128]{3,2,1,0:T(4,128)S(1)}, f32[3,2,4,128]{3,2,1,0:T(4,128)S(1)}, f32[2,4,128]{2,1,0:T(4,1...) custom-call(f32[3,3,2,4,128]{4,3,2,1,0:T(4,128)S(1)} %get-tuple-element.28.wall, ...), custom_call_target="tpu_custom_call" | custom-call | tf_op jit(solution)/shard_map/wall_first/pallas_call | solution.py:677
  23.0 1.8 %collective-permute-start.4 = (f32[8,128]{1,0:T(8,128)S(1)}, f32[8,128]{1,0:T(8,128)S(1)}, u32[]{:S(2)}, u32[]{:S(2)}) collective-permute-start(f32[8,128]{1,0:T(8,128)S(1)} %get-tuple-element.46), channel_id=1, source_target_pairs={{1,2},{2,1},{5,6},{6,5},{9,10},{10,9},{13,14},{14,13},{17,18},{18,... | collective-permute-start | bytes 12296 | tf_op jit(solution)/shard_map/ppermute | solution.py:65
  24.8 0.1 collective-permute-start.5
  24.9 1.8 %collective-permute-done.4.got_odd.wyo = f32[8,128]{1,0:T(8,128)S(1)} collective-permute-done((f32[8,128]{1,0:T(8,128)S(1)}, f32[8,128]{1,0:T(8,128)S(1)}, u32[]{:S(2)}, u32[]{:S(2)}) %collective-permute-start.4) | collective-permute-done | bytes 4128 | tf_op jit(solution)/shard_map/ppermute | solution.py:65
  26.8 0.0 collective-permute-done.5.got_even.wye
  26.8 0.3 collective-permute-start.6
  27.1 2.9 %collective-permute-start.7 = (f32[24,128]{1,0:T(8,128)S(1)}, f32[24,128]{1,0:T(8,128)S(1)}, u32[]{:S(2)}, u32[]{:S(2)}) collective-permute-start(f32[24,128]{1,0:T(8,128)S(1)} %get-tuple-element.49), channel_id=1, source_target_pairs={{0,4},{4,0},{1,5},{5,1},{2,6},{6,2},{3,7},{7,3},{8,12},{12,8},{9,1... | collective-permute-start | bytes 36872 | tf_op jit(solution)/shard_map/ppermute | solution.py:66
  30.0 0.0 collective-permute-done.6.fxo
  30.0 1.8 %collective-permute-done.7.fxe = f32[24,128]{1,0:T(8,128)S(1)} collective-permute-done((f32[24,128]{1,0:T(8,128)S(1)}, f32[24,128]{1,0:T(8,128)S(1)}, u32[]{:S(2)}, u32[]{:S(2)}) %collective-permute-start.7) | collective-permute-done | bytes 12320 | tf_op jit(solution)/shard_map/ppermute | solution.py:66
  31.8 1.9 %all-to-all-done.got = f32[32,24,128]{2,1,0:T(8,128)S(1)} async-done(((f32[32,24,128]{2,1,0:T(8,128)}), f32[32,24,128]{2,1,0:T(8,128)S(1)}, u32[]{:S(2)}, u32[]{:S(2)}) %all-to-all-start) | async-done | bytes 393248 | tf_op jit(solution)/shard_map/all_to_all | solution.py:827
  33.7 1.7 %wall_last.1 = (f32[3,2,4,128]{3,2,1,0:T(4,128)}, f32[3,2,4,128]{3,2,1,0:T(4,128)}) custom-call(f32[2,4,40,8,128]{4,3,2,1,0:T(8,128)S(1)} %get-tuple-element.31.weights, f32[2,4,40,8,128]{4,3,2,1,0:T(8,128)S(1)} %get-tuple-element.37.end_weights, f32[32,24,128]{2,1,0:T(8,128)S(1)} %all-to-all-done.got, f32[3,2,4,128]{3,2,1,0:T(4,128)S(1)} %get-tuple-element.43.base1, ...), custom_call_target="tpu_custom_call" | custom-call | tf_op jit(solution)/shard_map/wall_last/pallas_call | solution.py:786
  (1 shorter events, 0.0 us)
Async XLA Ops:
  1.8 5.0 %collective-permute-start = (f32[80,128]{1,0:T(8,128)S(1)}, f32[80,128]{1,0:T(8,128)S(1)}, u32[]{:S(2)}, u32[]{:S(2)}) collective-permute-start(f32[80,128]{1,0:T(8,128)S(1)} %get-tuple-element.29), channel_id=1, source_target_pairs={{1,2},{2,1},{5,6},{6,5},{9,10},{10,9},{13,14},{14,13},{17,18},{18,... | collective-permute-start | bytes 122888 | tf_op jit(solution)/shard_map/ppermute | solution.py:65
  4.8 2.0 %collective-permute-start.1 = (f32[80,128]{1,0:T(8,128)S(1)}, f32[80,128]{1,0:T(8,128)S(1)}, u32[]{:S(2)}, u32[]{:S(2)}) collective-permute-start(f32[80,128]{1,0:T(8,128)S(1)} %get-tuple-element.30), channel_id=1, source_target_pairs={{0,1},{1,0},{4,5},{5,4},{8,9},{9,8},{12,13},{13,12},{16,17},{17,16... | collective-permute-start | bytes 122888 | tf_op jit(solution)/shard_map/ppermute | solution.py:66
  6.9 7.7 %collective-permute-start.2 = (f32[120,128]{1,0:T(8,128)S(1)}, f32[120,128]{1,0:T(8,128)S(1)}, u32[]{:S(2)}, u32[]{:S(2)}) collective-permute-start(f32[120,128]{1,0:T(8,128)S(1)} %get-tuple-element.33), channel_id=1, source_target_pairs={{4,8},{8,4},{5,9},{9,5},{6,10},{10,6},{7,11},{11,7},{12,16},{16,12... | collective-permute-start | bytes 184328 | tf_op jit(solution)/shard_map/ppermute | solution.py:65
  7.1 7.5 %collective-permute-start.3 = (f32[120,128]{1,0:T(8,128)S(1)}, f32[120,128]{1,0:T(8,128)S(1)}, u32[]{:S(2)}, u32[]{:S(2)}) collective-permute-start(f32[120,128]{1,0:T(8,128)S(1)} %get-tuple-element.34), channel_id=1, source_target_pairs={{0,4},{4,0},{1,5},{5,1},{2,6},{6,2},{3,7},{7,3},{8,12},{12,8},{9,1... | collective-permute-start | bytes 184328 | tf_op jit(solution)/shard_map/ppermute | solution.py:66
  16.4 17.3 %all-to-all-start = ((f32[32,24,128]{2,1,0:T(8,128)}), f32[32,24,128]{2,1,0:T(8,128)S(1)}, u32[]{:S(2)}, u32[]{:S(2)}) async-start(f32[32,24,128]{2,1,0:T(8,128)} %get-tuple-element.42), calls=%async_computation | async-start | bytes 786432 | tf_op jit(solution)/shard_map/all_to_all | solution.py:827
  23.0 3.8 %collective-permute-start.4 = (f32[8,128]{1,0:T(8,128)S(1)}, f32[8,128]{1,0:T(8,128)S(1)}, u32[]{:S(2)}, u32[]{:S(2)}) collective-permute-start(f32[8,128]{1,0:T(8,128)S(1)} %get-tuple-element.46), channel_id=1, source_target_pairs={{1,2},{2,1},{5,6},{6,5},{9,10},{10,9},{13,14},{14,13},{17,18},{18,... | collective-permute-start | bytes 12296 | tf_op jit(solution)/shard_map/ppermute | solution.py:65
  24.8 1.9 %collective-permute-start.5 = (f32[8,128]{1,0:T(8,128)S(1)}, f32[8,128]{1,0:T(8,128)S(1)}, u32[]{:S(2)}, u32[]{:S(2)}) collective-permute-start(f32[8,128]{1,0:T(8,128)S(1)} %get-tuple-element.47), channel_id=1, source_target_pairs={{0,1},{1,0},{4,5},{5,4},{8,9},{9,8},{12,13},{13,12},{16,17},{17,16... | collective-permute-start | bytes 12296 | tf_op jit(solution)/shard_map/ppermute | solution.py:66
  26.8 3.2 %collective-permute-start.6 = (f32[24,128]{1,0:T(8,128)S(1)}, f32[24,128]{1,0:T(8,128)S(1)}, u32[]{:S(2)}, u32[]{:S(2)}) collective-permute-start(f32[24,128]{1,0:T(8,128)S(1)} %get-tuple-element.48), channel_id=1, source_target_pairs={{4,8},{8,4},{5,9},{9,5},{6,10},{10,6},{7,11},{11,7},{12,16},{16,12... | collective-permute-start | bytes 36872 | tf_op jit(solution)/shard_map/ppermute | solution.py:65
  27.1 4.7 %collective-permute-start.7 = (f32[24,128]{1,0:T(8,128)S(1)}, f32[24,128]{1,0:T(8,128)S(1)}, u32[]{:S(2)}, u32[]{:S(2)}) collective-permute-start(f32[24,128]{1,0:T(8,128)S(1)} %get-tuple-element.49), channel_id=1, source_target_pairs={{0,4},{4,0},{1,5},{5,1},{2,6},{6,2},{3,7},{7,3},{8,12},{12,8},{9,1... | collective-permute-start | bytes 36872 | tf_op jit(solution)/shard_map/ppermute | solution.py:66

commit v10 on v9

--- a/solution.py
+++ b/solution.py
@@ -435,22 +435,16 @@
 RISE = 4.0 / REACH
 
 
-def spread_mine(ref, lattice, l, h):
-    own = []
-    for c in range(3):
-        own.append(ref[c, l + 1, pl.ds(h + 1, 1), :] * (1.0 / REACH) + lattice[c])
-    rest = jnp.concatenate(own + [jnp.zeros((1, LANES), F32)], axis=0)
-    terms = []
-    for _ in range(3):
-        term = rest.astype(BF16).astype(F32)
-        terms.append(term)
-        rest = rest - term
-    terms.append(jnp.zeros((4, LANES), F32))
-    columns = jnp.transpose(jnp.concatenate(terms, axis=0)).astype(BF16)
-    row = lax.broadcasted_iota(jnp.int32, (16, 3 * LANES), 0)
-    lane = lax.broadcasted_iota(jnp.int32, (16, 3 * LANES), 1)
-    ones = jnp.where((row % 4 == lane // LANES) & (row < 12), 1.0, 0.0).astype(BF16)
-    return jnp.dot(columns, ones, preferred_element_type=F32)
+def own_columns(ref, lattice, rows, cols):
+    places = []
+    for l in range(rows):
+        for h in range(cols):
+            for c in range(3):
+                places.append(ref[c, l + 1, h + 1 : h + 2, :] * (1.0 / REACH) + lattice[c])
+    spare = -len(places) % SUB
+    if spare:
+        places.append(jnp.zeros((spare, LANES), F32))
+    return jnp.transpose(jnp.concatenate(places, axis=0))
 
 
 def bond_row(weight, others, mine):
@@ -460,11 +454,12 @@
     return jnp.maximum(weight, 0.0)
 
 
-def tile_pass(l, h, columns, others, pulls, weight_of, weights, acc):
+def tile_pass(l, h, cols, columns, others, pulls, weight_of, weights, acc):
     place = 0
+    first = 3 * (l * cols + h)
     for g in range(LANES // SUB):
         span = slice(g * SUB, (g + 1) * SUB)
-        mine = [columns[span, c * LANES : (c + 1) * LANES] for c in range(3)]
+        mine = [jnp.broadcast_to(columns[span, first + c : first + c + 1], (SUB, LANES)) for c in range(3)]
         sums = [None] * 4
         for order, dh in enumerate(reached(g)):
             here = [others[c][dh] for c in range(3)]
@@ -489,8 +484,7 @@
     return [sums[:, c * LANES : (c + 1) * LANES] for c in range(count)]
 
 
-def lane_sums(acc, l, cols, count):
-    tiles = [tile_sums(acc, l, h, count) for h in range(cols)]
+def by_quantity(tiles):
     return [jnp.concatenate(rows, axis=0) for rows in zip(*tiles)]
 
 
@@ -500,7 +494,7 @@
 
 def center_kernel(
     wy_count, masks_in, p_in, q_in, s_in, device_in, tile_in, wall, wyo, wye,
-    weights, part, bits, target, p, q, s, jpad, dpad, acc, masks, route, sems,
+    weights, part, bits, target, columns, p, q, s, jpad, dpad, acc, masks, route, sems,
 ):
     rows, cols = wall.shape[2], wall.shape[3]
     cx = p.shape[0]
@@ -509,21 +503,14 @@
     pairs = [(p_in, p), (q_in, q), (s_in, s)] + pairs
     for k, pair in enumerate(pairs):
         copies[k] = pltpu.make_async_copy(*pair, sems.at[k])
-    tiles = [(l, h) for h in range(cols) for l in range(rows)]
-    at = rows * cols
     for k, first in enumerate((3, 0, 6)):
-        for n, (l, h) in enumerate(tiles):
-            copies[l, h, first] = pltpu.make_async_copy(
-                masks_in.at[l, h, first : first + 3],
-                masks.at[l, h, first : first + 3],
-                sems.at[5 + k * at + n],
-            )
-    order = [copies[k] for k in (3, 4)]
-    order += [copies[l, h, 3] for l, h in tiles]
-    order += [copies[l, h, first] for l, h in tiles for first in (0, 6)]
-    order += [copies[k] for k in range(3)]
-    for copy in order:
-        copy.start()
+        span = slice(first, first + 3)
+        copies["masks", first] = pltpu.make_async_copy(
+            masks_in.at[:, :, span], masks.at[:, :, span], sems.at[5 + k]
+        )
+    order = [3, 4, ("masks", 3), ("masks", 0), ("masks", 6), 0, 1, 2]
+    for k in order:
+        copies[k].start()
     first_sub = lax.broadcasted_iota(jnp.int32, (SUB, LANES), 0) < SUB // 2
     copies[3].wait()
     copies[4].wait()
@@ -535,9 +522,9 @@
     fill_y(jpad, wall.at[0], before, after, 4 * cx)
     fill_y(dpad, wall.at[1], before, after, 4 * cx + 3 * rows)
     lattice = lattice_rows()
+    columns[...] = own_columns(jpad, lattice, rows, cols)
 
     def one_tile(l, h):
-        columns = spread_mine(jpad, lattice, l, h)
         others = []
         for c in range(3):
             mid = mid_rows(jpad, c, l, h)
@@ -552,7 +539,7 @@
             span = slice(g * SUB, (g + 1) * SUB)
             return bond_row(masks[l, h, 4 + dh, span, :].astype(F32), here, mine)
 
-        tile_pass(l, h, columns, others, pulls, weight_of, weights, acc)
+        tile_pass(l, h, cols, columns, others, pulls, weight_of, weights, acc)
 
     def put_sums(l, h):
         for c, sums in enumerate(tile_sums(acc, l, h, 4)):
@@ -570,15 +557,14 @@
         for k in range(2):
             bits[l, h, k] = words[k]
 
-    for n, (l, h) in enumerate(tiles):
-        copies[l, h, 3].wait()
+    tiles = [(l, h) for l in range(rows) for h in range(cols)]
+    copies["masks", 3].wait()
+    for l, h in tiles:
         one_tile(l, h)
-        if n > 0:
-            put_sums(*tiles[n - 1])
-    put_sums(*tiles[-1])
+        put_sums(l, h)
+    copies["masks", 0].wait()
+    copies["masks", 6].wait()
     for l, h in tiles:
-        copies[l, h, 0].wait()
-        copies[l, h, 6].wait()
         put_bits(l, h)
     for k in range(3):
         copies[k].wait()
@@ -589,12 +575,13 @@
     return pl.pallas_call(
         functools.partial(center_kernel, wy_count),
         in_specs=[HBM] * 6 + [whole()] * 3,
-        out_specs=[whole()] * 7,
+        out_specs=[whole()] * 8,
         out_shape=[
             jax.ShapeDtypeStruct((rows, cols, STORED, SUB, LANES), F32),
             vmem(rows, 4, cols, LANES),
             pltpu.VMEM((rows, cols, 2, SUB, LANES), jnp.int32),
             pltpu.VMEM(device.shape, jnp.int32),
+            vmem(LANES, pad8(3 * rows * cols)),
         ]
         + [vmem(*grids[0].shape)] * 3,
         scratch_shapes=[
@@ -603,7 +590,7 @@
             vmem(rows, cols, 4, LANES, LANES),
             pltpu.VMEM(masks.shape, jnp.int32),
             pltpu.VMEM((2,) + device.shape, jnp.int32),
-            pltpu.SemaphoreType.DMA((5 + 3 * rows * cols,)),
+            pltpu.SemaphoreType.DMA((8,)),
         ],
         compiler_params=params(),
         name="wall_center",
@@ -611,7 +598,7 @@
 
 
 def wall_kernel(
-    cx, cy, wall, wyo, wye, fxo, fxe, part, bits, weights, vel1, base1, totals, to_odd, to_even,
+    cx, cy, wall, wyo, wye, fxo, fxe, part, bits, columns, weights, vel1, base1, totals, to_odd, to_even,
     jpad, dpad, acc,
 ):
     rows, cols = wall.shape[2], wall.shape[3]
@@ -624,7 +611,6 @@
     lattice = lattice_rows()
 
     def one_tile(l, h):
-        columns = spread_mine(jpad, lattice, l, h)
         others = []
         for c in range(3):
             ends = end_rows(jpad, c, l, h, first_sub)
@@ -641,15 +627,14 @@
             bonded = (bits[l, h, g // 8] & (1 << (3 * (g % 8) + order))) != 0
             return jnp.where(bonded, bond_row(1.0, here, mine), 0.0)
 
-        tile_pass(l, h, columns, others, pulls, weight_of, weights, acc)
-
-    @pl.loop(0, cols)
-    def _(h):
-        for l in range(rows):
+        tile_pass(l, h, cols, columns, others, pulls, weight_of, weights, acc)
+
+    for l in range(rows):
+        sums = []
+        for h in range(cols):
             one_tile(l, h)
-
-    for l in range(rows):
-        pulled = [v + part[l, c] for c, v in enumerate(lane_sums(acc, l, cols, 4))]
+            sums.append(tile_sums(acc, l, h, 4))
+        pulled = [v + part[l, c] for c, v in enumerate(by_quantity(sums))]
         totals[l] = pulled[3]
         for c in range(3):
             mine = wall[1, c, l]
@@ -670,13 +655,13 @@
     place_edges(even_at("wy"), edge(0), edge(cols - 1), to_even, to_odd)
 
 
-def wall_first(cx, cy, wall, wy_got, fx_got, part, bits):
+def wall_first(cx, cy, wall, wy_got, fx_got, part, bits, columns):
     rows, cols = wall.shape[2], wall.shape[3]
     edge = (pad8(3 * rows), LANES)
     field = vmem(*wall.shape[1:])
     return pl.pallas_call(
         functools.partial(wall_kernel, cx, cy),
-        in_specs=[whole()] * 7,
+        in_specs=[whole()] * 8,
         out_specs=[whole()] * 6,
         out_shape=[
             jax.ShapeDtypeStruct((rows, cols, STORED, SUB, LANES), F32),
@@ -693,7 +678,7 @@
         ],
         compiler_params=params(),
         name="wall_first",
-    )(wall, *wy_got, *fx_got, part, bits)
+    )(wall, *wy_got, *fx_got, part, bits, columns)
 
 
 def pack_base_kernel(base1, got_odd, got_even, to_odd, to_even):
@@ -764,13 +749,12 @@
             for c in range(3):
                 acc[l, h, c, g * SUB : (g + 1) * SUB, :] = sums[c]
 
-    @pl.loop(0, cols)
-    def _(h):
-        for l in range(rows):
+    for l in range(rows):
+        sums = []
+        for h in range(cols):
             one_tile(l, h)
-
-    for l in range(rows):
-        pulled = lane_sums(acc, l, cols, 3)
+            sums.append(tile_sums(acc, l, h, 3))
+        pulled = by_quantity(sums)
         for c in range(3):
             mine = dpad[c, l + 1, 1 : cols + 1, :]
             force = STIFFNESS * (pulled[c] - totals[l] * mine)
@@ -820,13 +804,13 @@
     sends = pack_fx(cx, ends, wall, wy_got)
     fx_got = exchange("fx", *sends)
     grids = (pressure, pressure_prev, speed_sq)
-    weights, part, bits, target, *grids = wall_center(
+    weights, part, bits, target, columns, *grids = wall_center(
         wy_count, bond_masks, grids, device, tile, wall, wy_got
     )
     pressure_out, slots = grid_steps(*grids, wy_got, fx_got, target, fx_count, wy_count)
     got = lax.all_to_all(slots, ("fx", "wy"), split_axis=0, concat_axis=0, tiled=True)
     end_weights, vel1, base1, totals, *sends = wall_first(
-        cx, cy, wall, wy_got, fx_got, part, bits
+        cx, cy, wall, wy_got, fx_got, part, bits, columns
     )
     base_wy = exchange("wy", *sends)
     sends = pack_base(base1, base_wy)

time: 35.8 us -> 34.3 us (0.958)
  Pallas kernels: 11.3 us -> 8.59 us
  waiting for transfers between devices: 7.35 us -> 8.5 us
    all_to_all x1, waiting for transfers between devices: 1.92 us -> 3.22 us  [per_device(): lax.all_to_all(slots, ('fx', 'wy'), split_axis=0, concat_axis=0, tiled=True)]
    pallas_call x1, Pallas kernels: 4.05 us -> 2.81 us  [wall_center(): pl.pallas_call(functools.partial(center_kernel, wy_count), in_specs=[HBM]...]
    pallas_call x1, Pallas kernels: 2.45 us -> 1.28 us  [wall_first(): pl.pallas_call(functools.partial(wall_kernel, cx, cy), in_specs=[whole()]...]
  transfers between devices with their start and end apart: 9 -> 9, of which waited for: 4 -> 4; matrix products, arithmetic and copies ran while one was open for 0% -> 0% of each run, Pallas kernels for 18% -> 12%
where the time goes in v10:
time: 34.3 us; the launch traced here: 34 us
  starting transfers between devices  16.2 us (47%)
  Pallas kernels  8.59 us (25%)
  waiting for transfers between devices  8.5 us (25%)
  between operations  0.71 us (2%)
    ppermute x4, starting transfers between devices, exchange(): got_even = lax.ppermute(to_even, names, swap_pairs(along, sizes, 0))  6.89 us
    ppermute x4, starting transfers between devices, exchange(): got_odd = lax.ppermute(to_odd, names, swap_pairs(along, sizes, 1))  5.09 us
    all_to_all x1, starting transfers between devices, per_device(): lax.all_to_all(slots, ('fx', 'wy'), split_axis=0, concat_axis=0, tiled=True)  4.25 us
    ppermute x4, waiting for transfers between devices, exchange(): got_odd = lax.ppermute(to_odd, names, swap_pairs(along, sizes, 1))  3.61 us
    all_to_all x1, waiting for transfers between devices, per_device(): lax.all_to_all(slots, ('fx', 'wy'), split_axis=0, concat_axis=0, tiled=True)  3.22 us
    pallas_call x1, Pallas kernels, wall_center(): pl.pallas_call(functools.partial(center_kernel, wy_count), in_specs=[HBM]...  2.81 us
    pallas_call x1, Pallas kernels, grid_steps(): pl.pallas_call(grid_kernel, in_specs=[whole()] * 8, out_specs=[whole()] *...  1.74 us
    ppermute x4, waiting for transfers between devices, exchange(): got_even = lax.ppermute(to_even, names, swap_pairs(along, sizes, 0))  1.68 us
  transfers between devices with their start and end apart: 9, of which 4 were waited for; matrix products, arithmetic and copies ran while one was open for 0% of the time, Pallas kernels for 12%

profile of v10, /device:TPU:0, one launch (start us, length us, event | category | flops | bytes accessed | tf_op | source)
XLA Modules:
  0.0 34.0 jit_solution(3743957366253302005)
XLA Ops:
  0.6 1.2 %pack_wy.1 = (f32[80,128]{1,0:T(8,128)S(1)}, f32[80,128]{1,0:T(8,128)S(1)}, f32[2,4,32,128]{3,2,1,0:T(8,128)S(1)}, f32[3,3,2,4,128]{4,3,2,1,0:T(4,128)S(1)}) custom-call(f32[16,32,128]{2,1,0:T(8,128)} %p_in.1, f32[16,32,128]{2,1,0:T(8,128)} %q_in.1, f32[16,32,128]{2,1,0:T(8,128)} %s_in.1, f32[3,2,4,128]{3,2,1,0:T(4,128)} %jit_in.1, ...), custom_call_target="tpu_custom_call" | custom-call | tf_op jit(solution)/shard_map/pack_wy/pallas_call | solution.py:151
  1.8 3.0 %collective-permute-start = (f32[80,128]{1,0:T(8,128)S(1)}, f32[80,128]{1,0:T(8,128)S(1)}, u32[]{:S(2)}, u32[]{:S(2)}) collective-permute-start(f32[80,128]{1,0:T(8,128)S(1)} %get-tuple-element.30), channel_id=1, source_target_pairs={{1,2},{2,1},{5,6},{6,5},{9,10},{10,9},{13,14},{14,13},{17,18},{18,... | collective-permute-start | bytes 122888 | tf_op jit(solution)/shard_map/ppermute | solution.py:65
  4.8 0.1 collective-permute-start.1
  5.0 1.8 %collective-permute-done.wyo.got_odd = f32[80,128]{1,0:T(8,128)S(1)} collective-permute-done((f32[80,128]{1,0:T(8,128)S(1)}, f32[80,128]{1,0:T(8,128)S(1)}, u32[]{:S(2)}, u32[]{:S(2)}) %collective-permute-start) | collective-permute-done | bytes 40992 | tf_op jit(solution)/shard_map/ppermute | solution.py:65
  6.8 0.0 collective-permute-done.1.wye.got_even
  6.8 0.1 pack_fx.1
  6.9 0.2 collective-permute-start.2
  7.1 3.5 %collective-permute-start.3 = (f32[120,128]{1,0:T(8,128)S(1)}, f32[120,128]{1,0:T(8,128)S(1)}, u32[]{:S(2)}, u32[]{:S(2)}) collective-permute-start(f32[120,128]{1,0:T(8,128)S(1)} %get-tuple-element.35), channel_id=1, source_target_pairs={{0,4},{4,0},{1,5},{5,1},{2,6},{6,2},{3,7},{7,3},{8,12},{12,8},{9,1... | collective-permute-start | bytes 184328 | tf_op jit(solution)/shard_map/ppermute | solution.py:66
  10.6 2.8 %wall_center.1 = (f32[2,4,40,8,128]{4,3,2,1,0:T(8,128)S(1)}, f32[2,4,4,128]{3,2,1,0:T(4,128)S(1)}, s32[2,4,2,8,128]{4,3,2,1,0:T(8,128)S(1)}, s32[4,128]{1,0:T(4,...) custom-call(s32[2,4,9,128,128]{4,3,2,1,0:T(8,128)} %masks_in.1, ...), custom_call_target="tpu_custom_call" | custom-call | tf_op jit(solution)/shard_map/wall_center/pallas_call | solution.py:575
  13.4 0.0 collective-permute-done.2.fxo
  13.4 0.0 collective-permute-done.3.fxe
  13.4 1.7 %grid_steps.1 = (f32[16,32,128]{2,1,0:T(8,128)}, f32[32,24,128]{2,1,0:T(8,128)}) custom-call(f32[16,32,128]{2,1,0:T(8,128)S(1)} %get-tuple-element.40.p, f32[16,32,128]{2,1,0:T(8,128)S(1)} %get-tuple-element.41.q, f32[16,32,128]{2,1,0:T(8,128)S(1)} %get-tuple-element.42.s, f32[80,128]{1,0:T(8,128)S(1)} %collective-permute-done.wyo.got_odd, ...), custom_call_target="tpu_custom_call" | custom-call | tf_op jit(solution)/shard_map/grid_steps/pallas_call | solution.py:351
  15.2 4.2 %all-to-all-start = ((f32[32,24,128]{2,1,0:T(8,128)}), f32[32,24,128]{2,1,0:T(8,128)S(1)}, u32[]{:S(2)}, u32[]{:S(2)}) async-start(f32[32,24,128]{2,1,0:T(8,128)} %get-tuple-element.44), calls=%async_computation | async-start | bytes 786432 | tf_op jit(solution)/shard_map/all_to_all | solution.py:811
  19.4 1.3 %wall_first.1 = (f32[2,4,40,8,128]{4,3,2,1,0:T(8,128)S(1)}, f32[3,2,4,128]{3,2,1,0:T(4,128)S(1)}, f32[3,2,4,128]{3,2,1,0:T(4,128)S(1)}, f32[2,4,128]{2,1,0:T(4,1...) custom-call(f32[3,3,2,4,128]{4,3,2,1,0:T(4,128)S(1)} %get-tuple-element.29.wall, ...), custom_call_target="tpu_custom_call" | custom-call | tf_op jit(solution)/shard_map/wall_first/pallas_call | solution.py:662
  20.7 1.8 %collective-permute-start.4 = (f32[8,128]{1,0:T(8,128)S(1)}, f32[8,128]{1,0:T(8,128)S(1)}, u32[]{:S(2)}, u32[]{:S(2)}) collective-permute-start(f32[8,128]{1,0:T(8,128)S(1)} %get-tuple-element.48), channel_id=1, source_target_pairs={{1,2},{2,1},{5,6},{6,5},{9,10},{10,9},{13,14},{14,13},{17,18},{18,... | collective-permute-start | bytes 12296 | tf_op jit(solution)/shard_map/ppermute | solution.py:65
  22.5 0.1 collective-permute-start.5
  22.6 1.8 %collective-permute-done.4.got_odd.wyo = f32[8,128]{1,0:T(8,128)S(1)} collective-permute-done((f32[8,128]{1,0:T(8,128)S(1)}, f32[8,128]{1,0:T(8,128)S(1)}, u32[]{:S(2)}, u32[]{:S(2)}) %collective-permute-start.4) | collective-permute-done | bytes 4128 | tf_op jit(solution)/shard_map/ppermute | solution.py:65
  24.4 0.0 collective-permute-done.5.got_even.wye
  24.4 0.1 collective-permute-start.6
  24.5 3.2 %collective-permute-start.7 = (f32[24,128]{1,0:T(8,128)S(1)}, f32[24,128]{1,0:T(8,128)S(1)}, u32[]{:S(2)}, u32[]{:S(2)}) collective-permute-start(f32[24,128]{1,0:T(8,128)S(1)} %get-tuple-element.51), channel_id=1, source_target_pairs={{0,4},{4,0},{1,5},{5,1},{2,6},{6,2},{3,7},{7,3},{8,12},{12,8},{9,1... | collective-permute-start | bytes 36872 | tf_op jit(solution)/shard_map/ppermute | solution.py:66
  27.7 0.0 collective-permute-done.6.fxo
  27.7 1.7 %collective-permute-done.7.fxe = f32[24,128]{1,0:T(8,128)S(1)} collective-permute-done((f32[24,128]{1,0:T(8,128)S(1)}, f32[24,128]{1,0:T(8,128)S(1)}, u32[]{:S(2)}, u32[]{:S(2)}) %collective-permute-start.7) | collective-permute-done | bytes 12320 | tf_op jit(solution)/shard_map/ppermute | solution.py:66
  29.4 3.2 %all-to-all-done.got = f32[32,24,128]{2,1,0:T(8,128)S(1)} async-done(((f32[32,24,128]{2,1,0:T(8,128)}), f32[32,24,128]{2,1,0:T(8,128)S(1)}, u32[]{:S(2)}, u32[]{:S(2)}) %all-to-all-start) | async-done | bytes 393248 | tf_op jit(solution)/shard_map/all_to_all | solution.py:811
  32.6 1.4 %wall_last.1 = (f32[3,2,4,128]{3,2,1,0:T(4,128)}, f32[3,2,4,128]{3,2,1,0:T(4,128)}) custom-call(f32[2,4,40,8,128]{4,3,2,1,0:T(8,128)S(1)} %get-tuple-element.32.weights, f32[2,4,40,8,128]{4,3,2,1,0:T(8,128)S(1)} %get-tuple-element.39.end_weights, f32[32,24,128]{2,1,0:T(8,128)S(1)} %all-to-all-done.got, f32[3,2,4,128]{3,2,1,0:T(4,128)S(1)} %get-tuple-element.45.base1, ...), custom_call_target="tpu_custom_call" | custom-call | tf_op jit(solution)/shard_map/wall_last/pallas_call | solution.py:770
  (1 shorter events, 0.0 us)
Async XLA Ops:
  1.8 5.0 %collective-permute-start = (f32[80,128]{1,0:T(8,128)S(1)}, f32[80,128]{1,0:T(8,128)S(1)}, u32[]{:S(2)}, u32[]{:S(2)}) collective-permute-start(f32[80,128]{1,0:T(8,128)S(1)} %get-tuple-element.30), channel_id=1, source_target_pairs={{1,2},{2,1},{5,6},{6,5},{9,10},{10,9},{13,14},{14,13},{17,18},{18,... | collective-permute-start | bytes 122888 | tf_op jit(solution)/shard_map/ppermute | solution.py:65
  4.8 2.0 %collective-permute-start.1 = (f32[80,128]{1,0:T(8,128)S(1)}, f32[80,128]{1,0:T(8,128)S(1)}, u32[]{:S(2)}, u32[]{:S(2)}) collective-permute-start(f32[80,128]{1,0:T(8,128)S(1)} %get-tuple-element.31), channel_id=1, source_target_pairs={{0,1},{1,0},{4,5},{5,4},{8,9},{9,8},{12,13},{13,12},{16,17},{17,16... | collective-permute-start | bytes 122888 | tf_op jit(solution)/shard_map/ppermute | solution.py:66
  6.9 6.5 %collective-permute-start.2 = (f32[120,128]{1,0:T(8,128)S(1)}, f32[120,128]{1,0:T(8,128)S(1)}, u32[]{:S(2)}, u32[]{:S(2)}) collective-permute-start(f32[120,128]{1,0:T(8,128)S(1)} %get-tuple-element.34), channel_id=1, source_target_pairs={{4,8},{8,4},{5,9},{9,5},{6,10},{10,6},{7,11},{11,7},{12,16},{16,12... | collective-permute-start | bytes 184328 | tf_op jit(solution)/shard_map/ppermute | solution.py:65
  7.1 6.3 %collective-permute-start.3 = (f32[120,128]{1,0:T(8,128)S(1)}, f32[120,128]{1,0:T(8,128)S(1)}, u32[]{:S(2)}, u32[]{:S(2)}) collective-permute-start(f32[120,128]{1,0:T(8,128)S(1)} %get-tuple-element.35), channel_id=1, source_target_pairs={{0,4},{4,0},{1,5},{5,1},{2,6},{6,2},{3,7},{7,3},{8,12},{12,8},{9,1... | collective-permute-start | bytes 184328 | tf_op jit(solution)/shard_map/ppermute | solution.py:66
  15.2 17.4 %all-to-all-start = ((f32[32,24,128]{2,1,0:T(8,128)}), f32[32,24,128]{2,1,0:T(8,128)S(1)}, u32[]{:S(2)}, u32[]{:S(2)}) async-start(f32[32,24,128]{2,1,0:T(8,128)} %get-tuple-element.44), calls=%async_computation | async-start | bytes 786432 | tf_op jit(solution)/shard_map/all_to_all | solution.py:811
  20.7 3.7 %collective-permute-start.4 = (f32[8,128]{1,0:T(8,128)S(1)}, f32[8,128]{1,0:T(8,128)S(1)}, u32[]{:S(2)}, u32[]{:S(2)}) collective-permute-start(f32[8,128]{1,0:T(8,128)S(1)} %get-tuple-element.48), channel_id=1, source_target_pairs={{1,2},{2,1},{5,6},{6,5},{9,10},{10,9},{13,14},{14,13},{17,18},{18,... | collective-permute-start | bytes 12296 | tf_op jit(solution)/shard_map/ppermute | solution.py:65
  22.5 1.9 %collective-permute-start.5 = (f32[8,128]{1,0:T(8,128)S(1)}, f32[8,128]{1,0:T(8,128)S(1)}, u32[]{:S(2)}, u32[]{:S(2)}) collective-permute-start(f32[8,128]{1,0:T(8,128)S(1)} %get-tuple-element.49), channel_id=1, source_target_pairs={{0,1},{1,0},{4,5},{5,4},{8,9},{9,8},{12,13},{13,12},{16,17},{17,16... | collective-permute-start | bytes 12296 | tf_op jit(solution)/shard_map/ppermute | solution.py:66
  24.4 3.3 %collective-permute-start.6 = (f32[24,128]{1,0:T(8,128)S(1)}, f32[24,128]{1,0:T(8,128)S(1)}, u32[]{:S(2)}, u32[]{:S(2)}) collective-permute-start(f32[24,128]{1,0:T(8,128)S(1)} %get-tuple-element.50), channel_id=1, source_target_pairs={{4,8},{8,4},{5,9},{9,5},{6,10},{10,6},{7,11},{11,7},{12,16},{16,12... | collective-permute-start | bytes 36872 | tf_op jit(solution)/shard_map/ppermute | solution.py:65
  24.5 4.8 %collective-permute-start.7 = (f32[24,128]{1,0:T(8,128)S(1)}, f32[24,128]{1,0:T(8,128)S(1)}, u32[]{:S(2)}, u32[]{:S(2)}) collective-permute-start(f32[24,128]{1,0:T(8,128)S(1)} %get-tuple-element.51), channel_id=1, source_target_pairs={{0,4},{4,0},{1,5},{5,1},{2,6},{6,2},{3,7},{7,3},{8,12},{12,8},{9,1... | collective-permute-start | bytes 36872 | tf_op jit(solution)/shard_map/ppermute | solution.py:66

commit v11 on v10

--- a/solution.py
+++ b/solution.py
@@ -234,7 +234,9 @@
     return high, (v - high.astype(F32)).astype(BF16)
 
 
-def grid_kernel(p, q, s, wyo, wye, fxo, fxe, target, out, slots, s0, s1, rhs, part1, part2):
+def grid_kernel(
+    p, q, s, wyo, wye, fxo, fxe, target, out_to, slots_to, s0, s1, rhs, part1, part2, out, slots, sems
+):
     cx, cy = p.shape[0], p.shape[1]
     ahead, behind = SUB, SUB + cy
     fx_count = part1.shape[0] // 2 - 1
@@ -281,6 +283,9 @@
         a, b = two_terms(fresh)
         rhs[x * cy : (x + 1) * cy, 2 * LANES : 3 * LANES] = a
         rhs[x * cy : (x + 1) * cy, 3 * LANES : 4 * LANES] = b
+
+    out_copy = pltpu.make_async_copy(out, out_to, sems.at[0])
+    out_copy.start()
 
     part1[...] = jnp.zeros(part1.shape, F32)
     part2[:, 0:SUB, :] = jnp.zeros((tall, SUB, LANES), F32)
@@ -299,6 +304,8 @@
     sub = lax.broadcasted_iota(jnp.int32, (SUB, LANES), 0)
     lane = lax.broadcasted_iota(jnp.int32, (SUB, LANES), 1)
     step1 = sub < cols + 2
+    copies = [out_copy]
+    batch = max(1, fx_count // 4)
     for a in range(fx_count):
         for b in range(wy_count):
             h = SUB + cols * b
@@ -320,6 +327,14 @@
             own1 = jnp.where(high_free, pltpu.roll(x, 8, 1), own1)
             for k, group in enumerate((ends, own0, own1)):
                 slots[slot, k * SUB : (k + 1) * SUB, :] = jnp.where(step1, group, two[k])
+        if a % batch == batch - 1 or a == fx_count - 1:
+            done = (a + 1) * wy_count
+            span = slice((a // batch) * batch * wy_count, done)
+            sem = sems.at[len(copies)]
+            copies.append(pltpu.make_async_copy(slots.at[span], slots_to.at[span], sem))
+            copies[-1].start()
+    for copy in copies:
+        copy.wait()
 
 
 def free_ends(lane):
@@ -351,10 +366,10 @@
     return pl.pallas_call(
         grid_kernel,
         in_specs=[whole()] * 8,
-        out_specs=[whole()] * 2,
+        out_specs=[HBM] * 2,
         out_shape=[
             jax.ShapeDtypeStruct(p.shape, F32),
-            vmem(devices, 3 * SUB, LANES),
+            jax.ShapeDtypeStruct((devices, 3 * SUB, LANES), F32),
         ],
         scratch_shapes=[
             pltpu.VMEM((cx + 2, cy + 2 * SUB, LANES), F32),
@@ -362,6 +377,9 @@
             pltpu.VMEM((cx * cy, 4 * LANES), BF16),
             pltpu.VMEM((tall + 2, high + 2 * SUB, LANES), F32),
             pltpu.VMEM((tall, high + 2 * SUB, LANES), F32),
+            vmem(*p.shape),
+            vmem(devices, 3 * SUB, LANES),
+            pltpu.SemaphoreType.DMA((8,)),
         ],
         compiler_params=params(),
         name="grid_steps",

time: 34.3 us -> 34.3 us (level)
  no operation moved by 1% of the time
where the time goes in v11:
time: 34.3 us; the launch traced here: 34 us
  starting transfers between devices  16.2 us (47%)
  Pallas kernels  8.53 us (25%)
  waiting for transfers between devices  8.5 us (25%)
  between operations  0.72 us (2%)
    ppermute x4, starting transfers between devices, exchange(): got_even = lax.ppermute(to_even, names, swap_pairs(along, sizes, 0))  6.89 us
    ppermute x4, starting transfers between devices, exchange(): got_odd = lax.ppermute(to_odd, names, swap_pairs(along, sizes, 1))  5.09 us
    all_to_all x1, starting transfers between devices, per_device(): lax.all_to_all(slots, ('fx', 'wy'), split_axis=0, concat_axis=0, tiled=True)  4.25 us
    ppermute x4, waiting for transfers between devices, exchange(): got_odd = lax.ppermute(to_odd, names, swap_pairs(along, sizes, 1))  3.61 us
    all_to_all x1, waiting for transfers between devices, per_device(): lax.all_to_all(slots, ('fx', 'wy'), split_axis=0, concat_axis=0, tiled=True)  3.22 us
    pallas_call x1, Pallas kernels, wall_center(): pl.pallas_call(functools.partial(center_kernel, wy_count), in_specs=[HBM]...  2.81 us
    pallas_call x1, Pallas kernels, grid_steps(): pl.pallas_call(grid_kernel, in_specs=[whole()] * 8, out_specs=[HBM] * 2,...  1.68 us
    ppermute x4, waiting for transfers between devices, exchange(): got_even = lax.ppermute(to_even, names, swap_pairs(along, sizes, 0))  1.68 us
  transfers between devices with their start and end apart: 9, of which 4 were waited for; matrix products, arithmetic and copies ran while one was open for 0% of the time, Pallas kernels for 12%

profile of v11, /device:TPU:0, one launch (start us, length us, event | category | flops | bytes accessed | tf_op | source)
XLA Modules:
  0.0 34.0 jit_solution(5434000616478861868)
XLA Ops:
  0.6 1.2 %pack_wy.1 = (f32[80,128]{1,0:T(8,128)S(1)}, f32[80,128]{1,0:T(8,128)S(1)}, f32[2,4,32,128]{3,2,1,0:T(8,128)S(1)}, f32[3,3,2,4,128]{4,3,2,1,0:T(4,128)S(1)}) custom-call(f32[16,32,128]{2,1,0:T(8,128)} %p_in.1, f32[16,32,128]{2,1,0:T(8,128)} %q_in.1, f32[16,32,128]{2,1,0:T(8,128)} %s_in.1, f32[3,2,4,128]{3,2,1,0:T(4,128)} %jit_in.1, ...), custom_call_target="tpu_custom_call" | custom-call | tf_op jit(solution)/shard_map/pack_wy/pallas_call | solution.py:151
  1.8 3.0 %collective-permute-start = (f32[80,128]{1,0:T(8,128)S(1)}, f32[80,128]{1,0:T(8,128)S(1)}, u32[]{:S(2)}, u32[]{:S(2)}) collective-permute-start(f32[80,128]{1,0:T(8,128)S(1)} %get-tuple-element.30), channel_id=1, source_target_pairs={{1,2},{2,1},{5,6},{6,5},{9,10},{10,9},{13,14},{14,13},{17,18},{18,... | collective-permute-start | bytes 122888 | tf_op jit(solution)/shard_map/ppermute | solution.py:65
  4.8 0.1 collective-permute-start.1
  5.0 1.8 %collective-permute-done.wyo.got_odd = f32[80,128]{1,0:T(8,128)S(1)} collective-permute-done((f32[80,128]{1,0:T(8,128)S(1)}, f32[80,128]{1,0:T(8,128)S(1)}, u32[]{:S(2)}, u32[]{:S(2)}) %collective-permute-start) | collective-permute-done | bytes 40992 | tf_op jit(solution)/shard_map/ppermute | solution.py:65
  6.8 0.0 collective-permute-done.1.wye.got_even
  6.8 0.1 pack_fx.1
  6.9 0.2 collective-permute-start.2
  7.1 3.5 %collective-permute-start.3 = (f32[120,128]{1,0:T(8,128)S(1)}, f32[120,128]{1,0:T(8,128)S(1)}, u32[]{:S(2)}, u32[]{:S(2)}) collective-permute-start(f32[120,128]{1,0:T(8,128)S(1)} %get-tuple-element.35), channel_id=1, source_target_pairs={{0,4},{4,0},{1,5},{5,1},{2,6},{6,2},{3,7},{7,3},{8,12},{12,8},{9,1... | collective-permute-start | bytes 184328 | tf_op jit(solution)/shard_map/ppermute | solution.py:66
  10.6 2.8 %wall_center.1 = (f32[2,4,40,8,128]{4,3,2,1,0:T(8,128)S(1)}, f32[2,4,4,128]{3,2,1,0:T(4,128)S(1)}, s32[2,4,2,8,128]{4,3,2,1,0:T(8,128)S(1)}, s32[4,128]{1,0:T(4,...) custom-call(s32[2,4,9,128,128]{4,3,2,1,0:T(8,128)} %masks_in.1, ...), custom_call_target="tpu_custom_call" | custom-call | tf_op jit(solution)/shard_map/wall_center/pallas_call | solution.py:593
  13.4 0.0 collective-permute-done.2.fxo
  13.4 0.0 collective-permute-done.3.fxe
  13.4 1.7 %grid_steps.1 = (f32[16,32,128]{2,1,0:T(8,128)}, f32[32,24,128]{2,1,0:T(8,128)}) custom-call(f32[16,32,128]{2,1,0:T(8,128)S(1)} %get-tuple-element.40.p, f32[16,32,128]{2,1,0:T(8,128)S(1)} %get-tuple-element.41.q, f32[16,32,128]{2,1,0:T(8,128)S(1)} %get-tuple-element.42.s, f32[80,128]{1,0:T(8,128)S(1)} %collective-permute-done.wyo.got_odd, ...), custom_call_target="tpu_custom_call" | custom-call | tf_op jit(solution)/shard_map/grid_steps/pallas_call | solution.py:366
  15.1 4.3 %all-to-all-start = ((f32[32,24,128]{2,1,0:T(8,128)}), f32[32,24,128]{2,1,0:T(8,128)S(1)}, u32[]{:S(2)}, u32[]{:S(2)}) async-start(f32[32,24,128]{2,1,0:T(8,128)} %get-tuple-element.44), calls=%async_computation | async-start | bytes 786432 | tf_op jit(solution)/shard_map/all_to_all | solution.py:829
  19.4 1.3 %wall_first.1 = (f32[2,4,40,8,128]{4,3,2,1,0:T(8,128)S(1)}, f32[3,2,4,128]{3,2,1,0:T(4,128)S(1)}, f32[3,2,4,128]{3,2,1,0:T(4,128)S(1)}, f32[2,4,128]{2,1,0:T(4,1...) custom-call(f32[3,3,2,4,128]{4,3,2,1,0:T(4,128)S(1)} %get-tuple-element.29.wall, ...), custom_call_target="tpu_custom_call" | custom-call | tf_op jit(solution)/shard_map/wall_first/pallas_call | solution.py:680
  20.6 1.8 %collective-permute-start.4 = (f32[8,128]{1,0:T(8,128)S(1)}, f32[8,128]{1,0:T(8,128)S(1)}, u32[]{:S(2)}, u32[]{:S(2)}) collective-permute-start(f32[8,128]{1,0:T(8,128)S(1)} %get-tuple-element.48), channel_id=1, source_target_pairs={{1,2},{2,1},{5,6},{6,5},{9,10},{10,9},{13,14},{14,13},{17,18},{18,... | collective-permute-start | bytes 12296 | tf_op jit(solution)/shard_map/ppermute | solution.py:65
  22.5 0.1 collective-permute-start.5
  22.6 1.8 %collective-permute-done.4.got_odd.wyo = f32[8,128]{1,0:T(8,128)S(1)} collective-permute-done((f32[8,128]{1,0:T(8,128)S(1)}, f32[8,128]{1,0:T(8,128)S(1)}, u32[]{:S(2)}, u32[]{:S(2)}) %collective-permute-start.4) | collective-permute-done | bytes 4128 | tf_op jit(solution)/shard_map/ppermute | solution.py:65
  24.4 0.0 collective-permute-done.5.got_even.wye
  24.4 0.1 collective-permute-start.6
  24.5 3.2 %collective-permute-start.7 = (f32[24,128]{1,0:T(8,128)S(1)}, f32[24,128]{1,0:T(8,128)S(1)}, u32[]{:S(2)}, u32[]{:S(2)}) collective-permute-start(f32[24,128]{1,0:T(8,128)S(1)} %get-tuple-element.51), channel_id=1, source_target_pairs={{0,4},{4,0},{1,5},{5,1},{2,6},{6,2},{3,7},{7,3},{8,12},{12,8},{9,1... | collective-permute-start | bytes 36872 | tf_op jit(solution)/shard_map/ppermute | solution.py:66
  27.6 0.0 collective-permute-done.6.fxo
  27.6 1.7 %collective-permute-done.7.fxe = f32[24,128]{1,0:T(8,128)S(1)} collective-permute-done((f32[24,128]{1,0:T(8,128)S(1)}, f32[24,128]{1,0:T(8,128)S(1)}, u32[]{:S(2)}, u32[]{:S(2)}) %collective-permute-start.7) | collective-permute-done | bytes 12320 | tf_op jit(solution)/shard_map/ppermute | solution.py:66
  29.3 3.2 %all-to-all-done.got = f32[32,24,128]{2,1,0:T(8,128)S(1)} async-done(((f32[32,24,128]{2,1,0:T(8,128)}), f32[32,24,128]{2,1,0:T(8,128)S(1)}, u32[]{:S(2)}, u32[]{:S(2)}) %all-to-all-start) | async-done | bytes 393248 | tf_op jit(solution)/shard_map/all_to_all | solution.py:829
  32.5 1.4 %wall_last.1 = (f32[3,2,4,128]{3,2,1,0:T(4,128)}, f32[3,2,4,128]{3,2,1,0:T(4,128)}) custom-call(f32[2,4,40,8,128]{4,3,2,1,0:T(8,128)S(1)} %get-tuple-element.32.weights, f32[2,4,40,8,128]{4,3,2,1,0:T(8,128)S(1)} %get-tuple-element.39.end_weights, f32[32,24,128]{2,1,0:T(8,128)S(1)} %all-to-all-done.got, f32[3,2,4,128]{3,2,1,0:T(4,128)S(1)} %get-tuple-element.45.base1, ...), custom_call_target="tpu_custom_call" | custom-call | tf_op jit(solution)/shard_map/wall_last/pallas_call | solution.py:788
  (1 shorter events, 0.0 us)
Async XLA Ops:
  1.8 5.0 %collective-permute-start = (f32[80,128]{1,0:T(8,128)S(1)}, f32[80,128]{1,0:T(8,128)S(1)}, u32[]{:S(2)}, u32[]{:S(2)}) collective-permute-start(f32[80,128]{1,0:T(8,128)S(1)} %get-tuple-element.30), channel_id=1, source_target_pairs={{1,2},{2,1},{5,6},{6,5},{9,10},{10,9},{13,14},{14,13},{17,18},{18,... | collective-permute-start | bytes 122888 | tf_op jit(solution)/shard_map/ppermute | solution.py:65
  4.8 2.0 %collective-permute-start.1 = (f32[80,128]{1,0:T(8,128)S(1)}, f32[80,128]{1,0:T(8,128)S(1)}, u32[]{:S(2)}, u32[]{:S(2)}) collective-permute-start(f32[80,128]{1,0:T(8,128)S(1)} %get-tuple-element.31), channel_id=1, source_target_pairs={{0,1},{1,0},{4,5},{5,4},{8,9},{9,8},{12,13},{13,12},{16,17},{17,16... | collective-permute-start | bytes 122888 | tf_op jit(solution)/shard_map/ppermute | solution.py:66
  6.9 6.5 %collective-permute-start.2 = (f32[120,128]{1,0:T(8,128)S(1)}, f32[120,128]{1,0:T(8,128)S(1)}, u32[]{:S(2)}, u32[]{:S(2)}) collective-permute-start(f32[120,128]{1,0:T(8,128)S(1)} %get-tuple-element.34), channel_id=1, source_target_pairs={{4,8},{8,4},{5,9},{9,5},{6,10},{10,6},{7,11},{11,7},{12,16},{16,12... | collective-permute-start | bytes 184328 | tf_op jit(solution)/shard_map/ppermute | solution.py:65
  7.1 6.3 %collective-permute-start.3 = (f32[120,128]{1,0:T(8,128)S(1)}, f32[120,128]{1,0:T(8,128)S(1)}, u32[]{:S(2)}, u32[]{:S(2)}) collective-permute-start(f32[120,128]{1,0:T(8,128)S(1)} %get-tuple-element.35), channel_id=1, source_target_pairs={{0,4},{4,0},{1,5},{5,1},{2,6},{6,2},{3,7},{7,3},{8,12},{12,8},{9,1... | collective-permute-start | bytes 184328 | tf_op jit(solution)/shard_map/ppermute | solution.py:66
  15.1 17.4 %all-to-all-start = ((f32[32,24,128]{2,1,0:T(8,128)}), f32[32,24,128]{2,1,0:T(8,128)S(1)}, u32[]{:S(2)}, u32[]{:S(2)}) async-start(f32[32,24,128]{2,1,0:T(8,128)} %get-tuple-element.44), calls=%async_computation | async-start | bytes 786432 | tf_op jit(solution)/shard_map/all_to_all | solution.py:829
  20.6 3.7 %collective-permute-start.4 = (f32[8,128]{1,0:T(8,128)S(1)}, f32[8,128]{1,0:T(8,128)S(1)}, u32[]{:S(2)}, u32[]{:S(2)}) collective-permute-start(f32[8,128]{1,0:T(8,128)S(1)} %get-tuple-element.48), channel_id=1, source_target_pairs={{1,2},{2,1},{5,6},{6,5},{9,10},{10,9},{13,14},{14,13},{17,18},{18,... | collective-permute-start | bytes 12296 | tf_op jit(solution)/shard_map/ppermute | solution.py:65
  22.5 1.9 %collective-permute-start.5 = (f32[8,128]{1,0:T(8,128)S(1)}, f32[8,128]{1,0:T(8,128)S(1)}, u32[]{:S(2)}, u32[]{:S(2)}) collective-permute-start(f32[8,128]{1,0:T(8,128)S(1)} %get-tuple-element.49), channel_id=1, source_target_pairs={{0,1},{1,0},{4,5},{5,4},{8,9},{9,8},{12,13},{13,12},{16,17},{17,16... | collective-permute-start | bytes 12296 | tf_op jit(solution)/shard_map/ppermute | solution.py:66
  24.4 3.3 %collective-permute-start.6 = (f32[24,128]{1,0:T(8,128)S(1)}, f32[24,128]{1,0:T(8,128)S(1)}, u32[]{:S(2)}, u32[]{:S(2)}) collective-permute-start(f32[24,128]{1,0:T(8,128)S(1)} %get-tuple-element.50), channel_id=1, source_target_pairs={{4,8},{8,4},{5,9},{9,5},{6,10},{10,6},{7,11},{11,7},{12,16},{16,12... | collective-permute-start | bytes 36872 | tf_op jit(solution)/shard_map/ppermute | solution.py:65
  24.5 4.8 %collective-permute-start.7 = (f32[24,128]{1,0:T(8,128)S(1)}, f32[24,128]{1,0:T(8,128)S(1)}, u32[]{:S(2)}, u32[]{:S(2)}) collective-permute-start(f32[24,128]{1,0:T(8,128)S(1)} %get-tuple-element.51), channel_id=1, source_target_pairs={{0,4},{4,0},{1,5},{5,1},{2,6},{6,2},{3,7},{7,3},{8,12},{12,8},{9,1... | collective-permute-start | bytes 36872 | tf_op jit(solution)/shard_map/ppermute | solution.py:66

commit v12 on v10

--- a/solution.py
+++ b/solution.py
@@ -234,7 +234,9 @@
     return high, (v - high.astype(F32)).astype(BF16)
 
 
-def grid_kernel(p, q, s, wyo, wye, fxo, fxe, target, out, slots, s0, s1, rhs, part1, part2):
+def grid_kernel(
+    p, q, s, wyo, wye, fxo, fxe, target, out_to, keep, send, s0, s1, rhs, part1, part2, out, slots, sem
+):
     cx, cy = p.shape[0], p.shape[1]
     ahead, behind = SUB, SUB + cy
     fx_count = part1.shape[0] // 2 - 1
@@ -281,6 +283,9 @@
         a, b = two_terms(fresh)
         rhs[x * cy : (x + 1) * cy, 2 * LANES : 3 * LANES] = a
         rhs[x * cy : (x + 1) * cy, 3 * LANES : 4 * LANES] = b
+
+    out_copy = pltpu.make_async_copy(out, out_to, sem)
+    out_copy.start()
 
     part1[...] = jnp.zeros(part1.shape, F32)
     part2[:, 0:SUB, :] = jnp.zeros((tall, SUB, LANES), F32)
@@ -302,7 +307,7 @@
     for a in range(fx_count):
         for b in range(wy_count):
             h = SUB + cols * b
-            slot = a * wy_count + b
+            slot = a * (wy_count // 2) + b // 2
             one = [part1[2 * a + l, h - 1 : h - 1 + SUB, :] for l in range(4)]
             ends = jnp.where(lane % 8 < 4, one[3], one[0])
             two = [
@@ -319,7 +324,19 @@
             own1 = jnp.where(low, pltpu.roll(x, LANES - 8, 1), one[2])
             own1 = jnp.where(high_free, pltpu.roll(x, 8, 1), own1)
             for k, group in enumerate((ends, own0, own1)):
-                slots[slot, k * SUB : (k + 1) * SUB, :] = jnp.where(step1, group, two[k])
+                slots[b % 2, slot, k * SUB : (k + 1) * SUB, :] = jnp.where(step1, group, two[k])
+
+    @pl.when(even_at("wy"))
+    def _():
+        keep[...] = slots[0]
+        send[...] = slots[1]
+
+    @pl.when(jnp.logical_not(even_at("wy")))
+    def _():
+        keep[...] = slots[1]
+        send[...] = slots[0]
+
+    out_copy.wait()
 
 
 def free_ends(lane):
@@ -347,14 +364,15 @@
 def grid_steps(p, q, s, wy_got, fx_got, target, fx_count, wy_count):
     cx, cy = p.shape[0], p.shape[1]
     tall, high = fx_count * 2, wy_count * 4
-    devices = fx_count * wy_count
+    half = (fx_count * wy_count // 2, 3 * SUB, LANES)
     return pl.pallas_call(
         grid_kernel,
         in_specs=[whole()] * 8,
-        out_specs=[whole()] * 2,
+        out_specs=[HBM, whole(), whole()],
         out_shape=[
             jax.ShapeDtypeStruct(p.shape, F32),
-            vmem(devices, 3 * SUB, LANES),
+            vmem(*half),
+            vmem(*half),
         ],
         scratch_shapes=[
             pltpu.VMEM((cx + 2, cy + 2 * SUB, LANES), F32),
@@ -362,10 +380,33 @@
             pltpu.VMEM((cx * cy, 4 * LANES), BF16),
             pltpu.VMEM((tall + 2, high + 2 * SUB, LANES), F32),
             pltpu.VMEM((tall, high + 2 * SUB, LANES), F32),
+            vmem(*p.shape),
+            vmem(2, *half),
+            pltpu.SemaphoreType.DMA(()),
         ],
         compiler_params=params(),
         name="grid_steps",
     )(p, q, s, *wy_got, *fx_got, target)
+
+
+def pair_sum_kernel(keep, got, after, out):
+    out[...] = keep[...] + got[...]
+
+
+def pair_sum(keep, got, after):
+    return pl.pallas_call(
+        pair_sum_kernel,
+        in_specs=[whole()] * 3,
+        out_specs=whole(),
+        out_shape=jax.ShapeDtypeStruct(keep.shape, F32),
+        compiler_params=params(),
+        name="pair_sum",
+    )(keep, got, after)
+
+
+def parity_groups(fx_count, wy_count):
+    whole_row = range(fx_count * wy_count)
+    return [[d for d in whole_row if d % wy_count % 2 == parity] for parity in range(2)]
 
 
 def reached(g):
@@ -807,10 +848,20 @@
     weights, part, bits, target, columns, *grids = wall_center(
         wy_count, bond_masks, grids, device, tile, wall, wy_got
     )
-    pressure_out, slots = grid_steps(*grids, wy_got, fx_got, target, fx_count, wy_count)
-    got = lax.all_to_all(slots, ("fx", "wy"), split_axis=0, concat_axis=0, tiled=True)
+    pressure_out, keep, send = grid_steps(*grids, wy_got, fx_got, target, fx_count, wy_count)
+    names = ("fx", "wy")
+    other = lax.ppermute(send, names, swap_pairs(1, (fx_count, wy_count), 0))
     end_weights, vel1, base1, totals, *sends = wall_first(
         cx, cy, wall, wy_got, fx_got, part, bits, columns
+    )
+    slots = pair_sum(keep, other, totals)
+    got = lax.all_to_all(
+        slots,
+        names,
+        split_axis=0,
+        concat_axis=0,
+        tiled=True,
+        axis_index_groups=parity_groups(fx_count, wy_count),
     )
     base_wy = exchange("wy", *sends)
     sends = pack_base(base1, base_wy)

time: 34.3 us -> 33.4 us (0.974)
  waiting for transfers between devices: 8.5 us -> 6.21 us
  starting transfers between devices: 16.2 us -> 17 us
  Pallas kernels: 8.59 us -> 9.12 us
    all_to_all x1, waiting for transfers between devices: 3.22 us -> 0.35 us  [per_device(): lax.all_to_all(slots, names, split_axis=0, concat_axis=0, tiled=True, axi...]
    all_to_all x1, starting transfers between devices: 4.25 us -> 5.28 us  [per_device(): lax.all_to_all(slots, names, split_axis=0, concat_axis=0, tiled=True, axi...]
    pallas_call x1 -> x2, Pallas kernels: 1.74 us -> 2.3 us  [the longest x1 1.61 us: grid_steps(): pl.pallas_call(grid_kernel, in_specs=[whole()] * 8, out_specs=[HBM, whole...]
    ppermute x4, waiting for transfers between devices: 3.61 us -> 4.04 us  [exchange(): got_odd = lax.ppermute(to_odd, names, swap_pairs(along, sizes, 1))]
    ppermute x4, starting transfers between devices: 6.89 us -> 6.5 us  [exchange(): got_even = lax.ppermute(to_even, names, swap_pairs(along, sizes, 0))]
  transfers between devices with their start and end apart: 9 -> 10, of which waited for: 4 -> 5; matrix products, arithmetic and copies ran while one was open for 0% -> 0% of each run, Pallas kernels for 12% -> 12%
where the time goes in v12:
time: 33.4 us; the launch traced here: 33.1 us
  starting transfers between devices  17 us (51%)
  Pallas kernels  9.12 us (27%)
  waiting for transfers between devices  6.21 us (19%)
  between operations  0.73 us (2%)
    ppermute x4, starting transfers between devices, exchange(): got_even = lax.ppermute(to_even, names, swap_pairs(along, sizes, 0))  6.5 us
    all_to_all x1, starting transfers between devices, per_device(): lax.all_to_all(slots, names, split_axis=0, concat_axis=0, tiled=True, axi...  5.28 us
    ppermute x4, starting transfers between devices, exchange(): got_odd = lax.ppermute(to_odd, names, swap_pairs(along, sizes, 1))  5.18 us
    ppermute x4, waiting for transfers between devices, exchange(): got_odd = lax.ppermute(to_odd, names, swap_pairs(along, sizes, 1))  4.04 us
    pallas_call x1, Pallas kernels, wall_center(): pl.pallas_call(functools.partial(center_kernel, wy_count), in_specs=[HBM]...  2.81 us
    ppermute x4, waiting for transfers between devices, exchange(): got_even = lax.ppermute(to_even, names, swap_pairs(along, sizes, 0))  1.68 us
    pallas_call x1, Pallas kernels, grid_steps(): pl.pallas_call(grid_kernel, in_specs=[whole()] * 8, out_specs=[HBM, whole...  1.61 us
    pallas_call x1, Pallas kernels, wall_last(): pl.pallas_call(last_kernel, in_specs=[whole()] * 10, out_specs=[whole()]...  1.42 us
  transfers between devices with their start and end apart: 10, of which 5 were waited for; matrix products, arithmetic and copies ran while one was open for 0% of the time, Pallas kernels for 12%

profile of v12, /device:TPU:0, one launch (start us, length us, event | category | flops | bytes accessed | tf_op | source)
XLA Modules:
  0.0 33.1 jit_solution(13828720176438790520)
XLA Ops:
  0.6 1.2 %pack_wy.1 = (f32[80,128]{1,0:T(8,128)S(1)}, f32[80,128]{1,0:T(8,128)S(1)}, f32[2,4,32,128]{3,2,1,0:T(8,128)S(1)}, f32[3,3,2,4,128]{4,3,2,1,0:T(4,128)S(1)}) custom-call(f32[16,32,128]{2,1,0:T(8,128)} %p_in.1, f32[16,32,128]{2,1,0:T(8,128)} %q_in.1, f32[16,32,128]{2,1,0:T(8,128)} %s_in.1, f32[3,2,4,128]{3,2,1,0:T(4,128)} %jit_in.1, ...), custom_call_target="tpu_custom_call" | custom-call | tf_op jit(solution)/shard_map/pack_wy/pallas_call | solution.py:151
  1.8 3.0 %collective-permute-start = (f32[80,128]{1,0:T(8,128)S(1)}, f32[80,128]{1,0:T(8,128)S(1)}, u32[]{:S(2)}, u32[]{:S(2)}) collective-permute-start(f32[80,128]{1,0:T(8,128)S(1)} %get-tuple-element.31), channel_id=1, source_target_pairs={{1,2},{2,1},{5,6},{6,5},{9,10},{10,9},{13,14},{14,13},{17,18},{18,... | collective-permute-start | bytes 122888 | tf_op jit(solution)/shard_map/ppermute | solution.py:65
  4.8 0.1 collective-permute-start.1
  5.0 1.8 %collective-permute-done.wyo.got_odd = f32[80,128]{1,0:T(8,128)S(1)} collective-permute-done((f32[80,128]{1,0:T(8,128)S(1)}, f32[80,128]{1,0:T(8,128)S(1)}, u32[]{:S(2)}, u32[]{:S(2)}) %collective-permute-start) | collective-permute-done | bytes 40992 | tf_op jit(solution)/shard_map/ppermute | solution.py:65
  6.8 0.0 collective-permute-done.1.wye.got_even
  6.8 0.1 pack_fx.1
  6.9 0.2 collective-permute-start.2
  7.1 3.5 %collective-permute-start.3 = (f32[120,128]{1,0:T(8,128)S(1)}, f32[120,128]{1,0:T(8,128)S(1)}, u32[]{:S(2)}, u32[]{:S(2)}) collective-permute-start(f32[120,128]{1,0:T(8,128)S(1)} %get-tuple-element.36), channel_id=1, source_target_pairs={{0,4},{4,0},{1,5},{5,1},{2,6},{6,2},{3,7},{7,3},{8,12},{12,8},{9,1... | collective-permute-start | bytes 184328 | tf_op jit(solution)/shard_map/ppermute | solution.py:66
  10.6 2.8 %wall_center.1 = (f32[2,4,40,8,128]{4,3,2,1,0:T(8,128)S(1)}, f32[2,4,4,128]{3,2,1,0:T(4,128)S(1)}, s32[2,4,2,8,128]{4,3,2,1,0:T(8,128)S(1)}, s32[4,128]{1,0:T(4,...) custom-call(s32[2,4,9,128,128]{4,3,2,1,0:T(8,128)} %masks_in.1, ...), custom_call_target="tpu_custom_call" | custom-call | tf_op jit(solution)/shard_map/wall_center/pallas_call | solution.py:616
  13.4 0.0 collective-permute-done.2.fxo
  13.4 0.0 collective-permute-done.3.fxe
  13.4 1.6 %grid_steps.1 = (f32[16,32,128]{2,1,0:T(8,128)}, f32[16,24,128]{2,1,0:T(8,128)S(1)}, f32[16,24,128]{2,1,0:T(8,128)S(1)}) custom-call(f32[16,32,128]{2,1,0:T(8,128)S(1)} %get-tuple-element.41.p, f32[16,32,128]{2,1,0:T(8,128)S(1)} %get-tuple-element.42.q, f32[16,32,128]{2,1,0:T(8,128)S(1)} %get-tuple-element.43.s, ...), custom_call_target="tpu_custom_call" | custom-call | tf_op jit(solution)/shard_map/grid_steps/pallas_call | solution.py:368
  15.0 0.1 collective-permute-start.4
  15.1 1.3 %wall_first.1 = (f32[2,4,40,8,128]{4,3,2,1,0:T(8,128)S(1)}, f32[3,2,4,128]{3,2,1,0:T(4,128)S(1)}, f32[3,2,4,128]{3,2,1,0:T(4,128)S(1)}, f32[2,4,128]{2,1,0:T(4,1...) custom-call(f32[3,3,2,4,128]{4,3,2,1,0:T(4,128)S(1)} %get-tuple-element.30.wall, ...), custom_call_target="tpu_custom_call" | custom-call | tf_op jit(solution)/shard_map/wall_first/pallas_call | solution.py:703
  16.4 0.1 collective-permute-done.4.got
  16.5 0.7 %pair_sum.1 = f32[16,24,128]{2,1,0:T(8,128)} custom-call(f32[16,24,128]{2,1,0:T(8,128)S(1)} %get-tuple-element.45.keep, f32[16,24,128]{2,1,0:T(8,128)S(1)} %collective-permute-done.4.got, f32[2,4,128]{2,1,0:T(4,128)S(1)} %get-tuple-element.47.after.totals), custom_call_target="tpu_custom_call" | custom-call | tf_op jit(solution)/shard_map/pair_sum/pallas_call | solution.py:397
  17.2 5.3 %all-to-all-start = ((f32[16,24,128]{2,1,0:T(8,128)}), f32[16,24,128]{2,1,0:T(8,128)S(1)}, u32[]{:S(2)}, u32[]{:S(2)}) async-start(f32[16,24,128]{2,1,0:T(8,128)} %pair_sum.1), calls=%async_computation | async-start | bytes 393216 | tf_op jit(solution)/shard_map/all_to_all | solution.py:858
  22.5 1.9 %collective-permute-start.5 = (f32[8,128]{1,0:T(8,128)S(1)}, f32[8,128]{1,0:T(8,128)S(1)}, u32[]{:S(2)}, u32[]{:S(2)}) collective-permute-start(f32[8,128]{1,0:T(8,128)S(1)} %get-tuple-element.50), channel_id=1, source_target_pairs={{1,2},{2,1},{5,6},{6,5},{9,10},{10,9},{13,14},{14,13},{17,18},{18,... | collective-permute-start | bytes 12296 | tf_op jit(solution)/shard_map/ppermute | solution.py:65
  24.4 0.1 collective-permute-start.6
  24.6 2.2 %collective-permute-done.5.got_odd.wyo = f32[8,128]{1,0:T(8,128)S(1)} collective-permute-done((f32[8,128]{1,0:T(8,128)S(1)}, f32[8,128]{1,0:T(8,128)S(1)}, u32[]{:S(2)}, u32[]{:S(2)}) %collective-permute-start.5) | collective-permute-done | bytes 4128 | tf_op jit(solution)/shard_map/ppermute | solution.py:65
  26.7 0.0 collective-permute-done.6.got_even.wye
  26.8 0.1 collective-permute-start.7
  26.9 2.8 %collective-permute-start.8 = (f32[24,128]{1,0:T(8,128)S(1)}, f32[24,128]{1,0:T(8,128)S(1)}, u32[]{:S(2)}, u32[]{:S(2)}) collective-permute-start(f32[24,128]{1,0:T(8,128)S(1)} %get-tuple-element.53), channel_id=1, source_target_pairs={{0,4},{4,0},{1,5},{5,1},{2,6},{6,2},{3,7},{7,3},{8,12},{12,8},{9,1... | collective-permute-start | bytes 36872 | tf_op jit(solution)/shard_map/ppermute | solution.py:66
  29.6 0.0 collective-permute-done.7.fxo
  29.6 1.7 %collective-permute-done.8.fxe = f32[24,128]{1,0:T(8,128)S(1)} collective-permute-done((f32[24,128]{1,0:T(8,128)S(1)}, f32[24,128]{1,0:T(8,128)S(1)}, u32[]{:S(2)}, u32[]{:S(2)}) %collective-permute-start.8) | collective-permute-done | bytes 12320 | tf_op jit(solution)/shard_map/ppermute | solution.py:66
  31.3 0.3 %all-to-all-done.got = f32[16,24,128]{2,1,0:T(8,128)S(1)} async-done(((f32[16,24,128]{2,1,0:T(8,128)}), f32[16,24,128]{2,1,0:T(8,128)S(1)}, u32[]{:S(2)}, u32[]{:S(2)}) %all-to-all-start) | async-done | bytes 196640 | tf_op jit(solution)/shard_map/all_to_all | solution.py:858
  31.7 1.4 %wall_last.1 = (f32[3,2,4,128]{3,2,1,0:T(4,128)}, f32[3,2,4,128]{3,2,1,0:T(4,128)}) custom-call(f32[2,4,40,8,128]{4,3,2,1,0:T(8,128)S(1)} %get-tuple-element.33.weights, f32[2,4,40,8,128]{4,3,2,1,0:T(8,128)S(1)} %get-tuple-element.40.end_weights, f32[16,24,128]{2,1,0:T(8,128)S(1)} %all-to-all-done.got, f32[3,2,4,128]{3,2,1,0:T(4,128)S(1)} %get-tuple-element.48.base1, ...), custom_call_target="tpu_custom_call" | custom-call | tf_op jit(solution)/shard_map/wall_last/pallas_call | solution.py:811
  (1 shorter events, 0.0 us)
Async XLA Ops:
  1.8 5.0 %collective-permute-start = (f32[80,128]{1,0:T(8,128)S(1)}, f32[80,128]{1,0:T(8,128)S(1)}, u32[]{:S(2)}, u32[]{:S(2)}) collective-permute-start(f32[80,128]{1,0:T(8,128)S(1)} %get-tuple-element.31), channel_id=1, source_target_pairs={{1,2},{2,1},{5,6},{6,5},{9,10},{10,9},{13,14},{14,13},{17,18},{18,... | collective-permute-start | bytes 122888 | tf_op jit(solution)/shard_map/ppermute | solution.py:65
  4.8 2.0 %collective-permute-start.1 = (f32[80,128]{1,0:T(8,128)S(1)}, f32[80,128]{1,0:T(8,128)S(1)}, u32[]{:S(2)}, u32[]{:S(2)}) collective-permute-start(f32[80,128]{1,0:T(8,128)S(1)} %get-tuple-element.32), channel_id=1, source_target_pairs={{0,1},{1,0},{4,5},{5,4},{8,9},{9,8},{12,13},{13,12},{16,17},{17,16... | collective-permute-start | bytes 122888 | tf_op jit(solution)/shard_map/ppermute | solution.py:66
  6.9 6.5 %collective-permute-start.2 = (f32[120,128]{1,0:T(8,128)S(1)}, f32[120,128]{1,0:T(8,128)S(1)}, u32[]{:S(2)}, u32[]{:S(2)}) collective-permute-start(f32[120,128]{1,0:T(8,128)S(1)} %get-tuple-element.35), channel_id=1, source_target_pairs={{4,8},{8,4},{5,9},{9,5},{6,10},{10,6},{7,11},{11,7},{12,16},{16,12... | collective-permute-start | bytes 184328 | tf_op jit(solution)/shard_map/ppermute | solution.py:65
  7.1 6.3 %collective-permute-start.3 = (f32[120,128]{1,0:T(8,128)S(1)}, f32[120,128]{1,0:T(8,128)S(1)}, u32[]{:S(2)}, u32[]{:S(2)}) collective-permute-start(f32[120,128]{1,0:T(8,128)S(1)} %get-tuple-element.36), channel_id=1, source_target_pairs={{0,4},{4,0},{1,5},{5,1},{2,6},{6,2},{3,7},{7,3},{8,12},{12,8},{9,1... | collective-permute-start | bytes 184328 | tf_op jit(solution)/shard_map/ppermute | solution.py:66
  15.0 1.5 %collective-permute-start.4 = (f32[16,24,128]{2,1,0:T(8,128)S(1)}, f32[16,24,128]{2,1,0:T(8,128)S(1)}, u32[]{:S(2)}, u32[]{:S(2)}) collective-permute-start(f32[16,24,128]{2,1,0:T(8,128)S(1)} %get-tuple-element.46), channel_id=1, source_target_pairs={{0,1},{1,0},{4,5},{5,4},{8,9},{9,8},{12,13},{13,12},{16,17},{17,16... | collective-permute-start | bytes 589832 | tf_op jit(solution)/shard_map/ppermute | solution.py:853
  17.2 14.4 %all-to-all-start = ((f32[16,24,128]{2,1,0:T(8,128)}), f32[16,24,128]{2,1,0:T(8,128)S(1)}, u32[]{:S(2)}, u32[]{:S(2)}) async-start(f32[16,24,128]{2,1,0:T(8,128)} %pair_sum.1), calls=%async_computation | async-start | bytes 393216 | tf_op jit(solution)/shard_map/all_to_all | solution.py:858
  22.5 4.2 %collective-permute-start.5 = (f32[8,128]{1,0:T(8,128)S(1)}, f32[8,128]{1,0:T(8,128)S(1)}, u32[]{:S(2)}, u32[]{:S(2)}) collective-permute-start(f32[8,128]{1,0:T(8,128)S(1)} %get-tuple-element.50), channel_id=1, source_target_pairs={{1,2},{2,1},{5,6},{6,5},{9,10},{10,9},{13,14},{14,13},{17,18},{18,... | collective-permute-start | bytes 12296 | tf_op jit(solution)/shard_map/ppermute | solution.py:65
  24.4 2.3 %collective-permute-start.6 = (f32[8,128]{1,0:T(8,128)S(1)}, f32[8,128]{1,0:T(8,128)S(1)}, u32[]{:S(2)}, u32[]{:S(2)}) collective-permute-start(f32[8,128]{1,0:T(8,128)S(1)} %get-tuple-element.51), channel_id=1, source_target_pairs={{0,1},{1,0},{4,5},{5,4},{8,9},{9,8},{12,13},{13,12},{16,17},{17,16... | collective-permute-start | bytes 12296 | tf_op jit(solution)/shard_map/ppermute | solution.py:66
  26.8 2.9 %collective-permute-start.7 = (f32[24,128]{1,0:T(8,128)S(1)}, f32[24,128]{1,0:T(8,128)S(1)}, u32[]{:S(2)}, u32[]{:S(2)}) collective-permute-start(f32[24,128]{1,0:T(8,128)S(1)} %get-tuple-element.52), channel_id=1, source_target_pairs={{4,8},{8,4},{5,9},{9,5},{6,10},{10,6},{7,11},{11,7},{12,16},{16,12... | collective-permute-start | bytes 36872 | tf_op jit(solution)/shard_map/ppermute | solution.py:65
  26.9 4.5 %collective-permute-start.8 = (f32[24,128]{1,0:T(8,128)S(1)}, f32[24,128]{1,0:T(8,128)S(1)}, u32[]{:S(2)}, u32[]{:S(2)}) collective-permute-start(f32[24,128]{1,0:T(8,128)S(1)} %get-tuple-element.53), channel_id=1, source_target_pairs={{0,4},{4,0},{1,5},{5,1},{2,6},{6,2},{3,7},{7,3},{8,12},{12,8},{9,1... | collective-permute-start | bytes 36872 | tf_op jit(solution)/shard_map/ppermute | solution.py:66

commit v13 on v12

--- a/solution.py
+++ b/solution.py
@@ -235,7 +235,7 @@
 
 
 def grid_kernel(
-    p, q, s, wyo, wye, fxo, fxe, target, out_to, keep, send, s0, s1, rhs, part1, part2, out, slots, sem
+    p, q, s, wyo, wye, fxo, fxe, target, out, keep, send, s0, s1, rhs, part1, part2, slots
 ):
     cx, cy = p.shape[0], p.shape[1]
     ahead, behind = SUB, SUB + cy
@@ -283,9 +283,6 @@
         a, b = two_terms(fresh)
         rhs[x * cy : (x + 1) * cy, 2 * LANES : 3 * LANES] = a
         rhs[x * cy : (x + 1) * cy, 3 * LANES : 4 * LANES] = b
-
-    out_copy = pltpu.make_async_copy(out, out_to, sem)
-    out_copy.start()
 
     part1[...] = jnp.zeros(part1.shape, F32)
     part2[:, 0:SUB, :] = jnp.zeros((tall, SUB, LANES), F32)
@@ -336,8 +333,6 @@
         keep[...] = slots[1]
         send[...] = slots[0]
 
-    out_copy.wait()
-
 
 def free_ends(lane):
     return (lane % 8 == 3) | (lane % 8 == 4)
@@ -368,9 +363,9 @@
     return pl.pallas_call(
         grid_kernel,
         in_specs=[whole()] * 8,
-        out_specs=[HBM, whole(), whole()],
+        out_specs=[whole()] * 3,
         out_shape=[
-            jax.ShapeDtypeStruct(p.shape, F32),
+            vmem(*p.shape),
             vmem(*half),
             vmem(*half),
         ],
@@ -380,9 +375,7 @@
             pltpu.VMEM((cx * cy, 4 * LANES), BF16),
             pltpu.VMEM((tall + 2, high + 2 * SUB, LANES), F32),
             pltpu.VMEM((tall, high + 2 * SUB, LANES), F32),
-            vmem(*p.shape),
             vmem(2, *half),
-            pltpu.SemaphoreType.DMA(()),
         ],
         compiler_params=params(),
         name="grid_steps",
@@ -639,10 +632,12 @@
 
 
 def wall_kernel(
-    cx, cy, wall, wyo, wye, fxo, fxe, part, bits, columns, weights, vel1, base1, totals, to_odd, to_even,
-    jpad, dpad, acc,
+    cx, cy, wall, wyo, wye, fxo, fxe, part, bits, columns, pressure,
+    weights, vel1, base1, totals, to_odd, to_even, pressure_out, jpad, dpad, acc, sem,
 ):
     rows, cols = wall.shape[2], wall.shape[3]
+    copy = pltpu.make_async_copy(pressure, pressure_out, sem)
+    copy.start()
     first_sub = lax.broadcasted_iota(jnp.int32, (SUB, LANES), 0) < SUB // 2
     before, after = before_after("wy", wye, wyo)
     fill_y(jpad, wall.at[0], before, after, 4 * cx)
@@ -694,16 +689,18 @@
         return write
 
     place_edges(even_at("wy"), edge(0), edge(cols - 1), to_even, to_odd)
-
-
-def wall_first(cx, cy, wall, wy_got, fx_got, part, bits, columns):
+    copy.wait()
+
+
+def wall_first(wall, wy_got, fx_got, part, bits, columns, pressure):
+    cx, cy = pressure.shape[0], pressure.shape[1]
     rows, cols = wall.shape[2], wall.shape[3]
     edge = (pad8(3 * rows), LANES)
     field = vmem(*wall.shape[1:])
     return pl.pallas_call(
         functools.partial(wall_kernel, cx, cy),
-        in_specs=[whole()] * 8,
-        out_specs=[whole()] * 6,
+        in_specs=[whole()] * 9,
+        out_specs=[whole()] * 6 + [HBM],
         out_shape=[
             jax.ShapeDtypeStruct((rows, cols, STORED, SUB, LANES), F32),
             field,
@@ -711,15 +708,17 @@
             vmem(rows, cols, LANES),
             vmem(*edge),
             vmem(*edge),
+            jax.ShapeDtypeStruct(pressure.shape, F32),
         ],
         scratch_shapes=[
             pltpu.VMEM((3, rows + 2, SUB, LANES), F32),
             pltpu.VMEM((3, rows + 2, SUB, LANES), F32),
             pltpu.VMEM((rows, cols, 4, LANES, LANES), F32),
+            pltpu.SemaphoreType.DMA(()),
         ],
         compiler_params=params(),
         name="wall_first",
-    )(wall, *wy_got, *fx_got, part, bits, columns)
+    )(wall, *wy_got, *fx_got, part, bits, columns, pressure)
 
 
 def pack_base_kernel(base1, got_odd, got_even, to_odd, to_even):
@@ -837,7 +836,7 @@
     cols = displacement.shape[2]
     device = route_device.reshape(-1, LANES)
     tile = route_tile.reshape(-1, LANES)
-    cx, cy = pressure.shape[0], pressure.shape[1]
+    cx = pressure.shape[0]
     *sends, ends, wall = pack_wy(
         pressure, pressure_prev, speed_sq, jitter, displacement, velocity
     )
@@ -848,11 +847,11 @@
     weights, part, bits, target, columns, *grids = wall_center(
         wy_count, bond_masks, grids, device, tile, wall, wy_got
     )
-    pressure_out, keep, send = grid_steps(*grids, wy_got, fx_got, target, fx_count, wy_count)
+    fresh, keep, send = grid_steps(*grids, wy_got, fx_got, target, fx_count, wy_count)
     names = ("fx", "wy")
     other = lax.ppermute(send, names, swap_pairs(1, (fx_count, wy_count), 0))
-    end_weights, vel1, base1, totals, *sends = wall_first(
-        cx, cy, wall, wy_got, fx_got, part, bits, columns
+    end_weights, vel1, base1, totals, *sends, pressure_out = wall_first(
+        wall, wy_got, fx_got, part, bits, columns, fresh
     )
     slots = pair_sum(keep, other, totals)
     got = lax.all_to_all(

time: 33.4 us -> 32.8 us (0.982)
  Pallas kernels: 9.12 us -> 8.53 us
    pallas_call x1, Pallas kernels: 1.61 us -> 0.99 us  [grid_steps(): pl.pallas_call(grid_kernel, in_specs=[whole()] * 8, out_specs=[whole()] *...]
  transfers between devices with their start and end apart: 10 -> 10, of which waited for: 5 -> 5; matrix products, arithmetic and copies ran while one was open for 0% -> 0% of each run, Pallas kernels for 12% -> 13%
where the time goes in v13:
time: 32.8 us; the launch traced here: 32.5 us
  starting transfers between devices  17 us (52%)
  Pallas kernels  8.53 us (26%)
  waiting for transfers between devices  6.2 us (19%)
  between operations  0.73 us (2%)
    ppermute x4, starting transfers between devices, exchange(): got_even = lax.ppermute(to_even, names, swap_pairs(along, sizes, 0))  6.5 us
    all_to_all x1, starting transfers between devices, per_device(): lax.all_to_all(slots, names, split_axis=0, concat_axis=0, tiled=True, axi...  5.28 us
    ppermute x4, starting transfers between devices, exchange(): got_odd = lax.ppermute(to_odd, names, swap_pairs(along, sizes, 1))  5.18 us
    ppermute x4, waiting for transfers between devices, exchange(): got_odd = lax.ppermute(to_odd, names, swap_pairs(along, sizes, 1))  4.04 us
    pallas_call x1, Pallas kernels, wall_center(): pl.pallas_call(functools.partial(center_kernel, wy_count), in_specs=[HBM]...  2.81 us
    ppermute x4, waiting for transfers between devices, exchange(): got_even = lax.ppermute(to_even, names, swap_pairs(along, sizes, 0))  1.68 us
    pallas_call x1, Pallas kernels, wall_last(): pl.pallas_call(last_kernel, in_specs=[whole()] * 10, out_specs=[whole()]...  1.42 us
    pallas_call x1, Pallas kernels, wall_first(): pl.pallas_call(functools.partial(wall_kernel, cx, cy), in_specs=[whole()]...  1.29 us
  transfers between devices with their start and end apart: 10, of which 5 were waited for; matrix products, arithmetic and copies ran while one was open for 0% of the time, Pallas kernels for 13%

profile of v13, /device:TPU:0, one launch (start us, length us, event | category | flops | bytes accessed | tf_op | source)
XLA Modules:
  0.0 32.5 jit_solution(14382344504616054835)
XLA Ops:
  0.6 1.2 %pack_wy.1 = (f32[80,128]{1,0:T(8,128)S(1)}, f32[80,128]{1,0:T(8,128)S(1)}, f32[2,4,32,128]{3,2,1,0:T(8,128)S(1)}, f32[3,3,2,4,128]{4,3,2,1,0:T(4,128)S(1)}) custom-call(f32[16,32,128]{2,1,0:T(8,128)} %p_in.1, f32[16,32,128]{2,1,0:T(8,128)} %q_in.1, f32[16,32,128]{2,1,0:T(8,128)} %s_in.1, f32[3,2,4,128]{3,2,1,0:T(4,128)} %jit_in.1, ...), custom_call_target="tpu_custom_call" | custom-call | tf_op jit(solution)/shard_map/pack_wy/pallas_call | solution.py:151
  1.8 3.0 %collective-permute-start = (f32[80,128]{1,0:T(8,128)S(1)}, f32[80,128]{1,0:T(8,128)S(1)}, u32[]{:S(2)}, u32[]{:S(2)}) collective-permute-start(f32[80,128]{1,0:T(8,128)S(1)} %get-tuple-element.32), channel_id=1, source_target_pairs={{1,2},{2,1},{5,6},{6,5},{9,10},{10,9},{13,14},{14,13},{17,18},{18,... | collective-permute-start | bytes 122888 | tf_op jit(solution)/shard_map/ppermute | solution.py:65
  4.8 0.1 collective-permute-start.1
  5.0 1.8 %collective-permute-done.wyo.got_odd = f32[80,128]{1,0:T(8,128)S(1)} collective-permute-done((f32[80,128]{1,0:T(8,128)S(1)}, f32[80,128]{1,0:T(8,128)S(1)}, u32[]{:S(2)}, u32[]{:S(2)}) %collective-permute-start) | collective-permute-done | bytes 40992 | tf_op jit(solution)/shard_map/ppermute | solution.py:65
  6.8 0.0 collective-permute-done.1.wye.got_even
  6.8 0.1 pack_fx.1
  6.9 0.2 collective-permute-start.2
  7.1 3.5 %collective-permute-start.3 = (f32[120,128]{1,0:T(8,128)S(1)}, f32[120,128]{1,0:T(8,128)S(1)}, u32[]{:S(2)}, u32[]{:S(2)}) collective-permute-start(f32[120,128]{1,0:T(8,128)S(1)} %get-tuple-element.37), channel_id=1, source_target_pairs={{0,4},{4,0},{1,5},{5,1},{2,6},{6,2},{3,7},{7,3},{8,12},{12,8},{9,1... | collective-permute-start | bytes 184328 | tf_op jit(solution)/shard_map/ppermute | solution.py:66
  10.6 2.8 %wall_center.1 = (f32[2,4,40,8,128]{4,3,2,1,0:T(8,128)S(1)}, f32[2,4,4,128]{3,2,1,0:T(4,128)S(1)}, s32[2,4,2,8,128]{4,3,2,1,0:T(8,128)S(1)}, s32[4,128]{1,0:T(4,...) custom-call(s32[2,4,9,128,128]{4,3,2,1,0:T(8,128)} %masks_in.1, ...), custom_call_target="tpu_custom_call" | custom-call | tf_op jit(solution)/shard_map/wall_center/pallas_call | solution.py:609
  13.4 0.0 collective-permute-done.2.fxo
  13.4 0.0 collective-permute-done.3.fxe
  13.4 1.0 %grid_steps.1 = (f32[16,32,128]{2,1,0:T(8,128)S(1)}, f32[16,24,128]{2,1,0:T(8,128)S(1)}, f32[16,24,128]{2,1,0:T(8,128)S(1)}) custom-call(f32[16,32,128]{2,1,0:T(8,128)S(1)} %get-tuple-element.41.p, f32[16,32,128]{2,1,0:T(8,128)S(1)} %get-tuple-element.42.q, f32[16,32,128]{2,1,0:T(8,128)S(1)} %get-tuple-element.43.s, ...), custom_call_target="tpu_custom_call" | custom-call | tf_op jit(solution)/shard_map/grid_steps/pallas_call | solution.py:363
  14.4 0.1 collective-permute-start.4
  14.5 1.3 %wall_first.1 = (f32[2,4,40,8,128]{4,3,2,1,0:T(8,128)S(1)}, f32[3,2,4,128]{3,2,1,0:T(4,128)S(1)}, f32[3,2,4,128]{3,2,1,0:T(4,128)S(1)}, f32[2,4,128]{2,1,0:T(4,1...) custom-call(f32[3,3,2,4,128]{4,3,2,1,0:T(4,128)S(1)} %get-tuple-element.31.wall, ...), custom_call_target="tpu_custom_call" | custom-call | tf_op jit(solution)/shard_map/wall_first/pallas_call | solution.py:700
  15.8 0.1 collective-permute-done.4.got
  15.9 0.7 %pair_sum.1 = f32[16,24,128]{2,1,0:T(8,128)} custom-call(f32[16,24,128]{2,1,0:T(8,128)S(1)} %get-tuple-element.47.keep, f32[16,24,128]{2,1,0:T(8,128)S(1)} %collective-permute-done.4.got, f32[2,4,128]{2,1,0:T(4,128)S(1)} %get-tuple-element.49.after.totals), custom_call_target="tpu_custom_call" | custom-call | tf_op jit(solution)/shard_map/pair_sum/pallas_call | solution.py:390
  16.6 5.3 %all-to-all-start = ((f32[16,24,128]{2,1,0:T(8,128)}), f32[16,24,128]{2,1,0:T(8,128)S(1)}, u32[]{:S(2)}, u32[]{:S(2)}) async-start(f32[16,24,128]{2,1,0:T(8,128)} %pair_sum.1), calls=%async_computation | async-start | bytes 393216 | tf_op jit(solution)/shard_map/all_to_all | solution.py:857
  21.9 1.9 %collective-permute-start.5 = (f32[8,128]{1,0:T(8,128)S(1)}, f32[8,128]{1,0:T(8,128)S(1)}, u32[]{:S(2)}, u32[]{:S(2)}) collective-permute-start(f32[8,128]{1,0:T(8,128)S(1)} %get-tuple-element.52), channel_id=1, source_target_pairs={{1,2},{2,1},{5,6},{6,5},{9,10},{10,9},{13,14},{14,13},{17,18},{18,... | collective-permute-start | bytes 12296 | tf_op jit(solution)/shard_map/ppermute | solution.py:65
  23.8 0.1 collective-permute-start.6
  23.9 2.2 %collective-permute-done.5.got_odd.wyo = f32[8,128]{1,0:T(8,128)S(1)} collective-permute-done((f32[8,128]{1,0:T(8,128)S(1)}, f32[8,128]{1,0:T(8,128)S(1)}, u32[]{:S(2)}, u32[]{:S(2)}) %collective-permute-start.5) | collective-permute-done | bytes 4128 | tf_op jit(solution)/shard_map/ppermute | solution.py:65
  26.1 0.0 collective-permute-done.6.got_even.wye
  26.2 0.1 collective-permute-start.7
  26.3 2.8 %collective-permute-start.8 = (f32[24,128]{1,0:T(8,128)S(1)}, f32[24,128]{1,0:T(8,128)S(1)}, u32[]{:S(2)}, u32[]{:S(2)}) collective-permute-start(f32[24,128]{1,0:T(8,128)S(1)} %get-tuple-element.55), channel_id=1, source_target_pairs={{0,4},{4,0},{1,5},{5,1},{2,6},{6,2},{3,7},{7,3},{8,12},{12,8},{9,1... | collective-permute-start | bytes 36872 | tf_op jit(solution)/shard_map/ppermute | solution.py:66
  29.0 0.0 collective-permute-done.7.fxo
  29.1 1.7 %collective-permute-done.8.fxe = f32[24,128]{1,0:T(8,128)S(1)} collective-permute-done((f32[24,128]{1,0:T(8,128)S(1)}, f32[24,128]{1,0:T(8,128)S(1)}, u32[]{:S(2)}, u32[]{:S(2)}) %collective-permute-start.8) | collective-permute-done | bytes 12320 | tf_op jit(solution)/shard_map/ppermute | solution.py:66
  30.7 0.4 %all-to-all-done.got = f32[16,24,128]{2,1,0:T(8,128)S(1)} async-done(((f32[16,24,128]{2,1,0:T(8,128)}), f32[16,24,128]{2,1,0:T(8,128)S(1)}, u32[]{:S(2)}, u32[]{:S(2)}) %all-to-all-start) | async-done | bytes 196640 | tf_op jit(solution)/shard_map/all_to_all | solution.py:857
  31.1 1.4 %wall_last.1 = (f32[3,2,4,128]{3,2,1,0:T(4,128)}, f32[3,2,4,128]{3,2,1,0:T(4,128)}) custom-call(f32[2,4,40,8,128]{4,3,2,1,0:T(8,128)S(1)} %get-tuple-element.34.weights, f32[2,4,40,8,128]{4,3,2,1,0:T(8,128)S(1)} %get-tuple-element.46.end_weights, f32[16,24,128]{2,1,0:T(8,128)S(1)} %all-to-all-done.got, f32[3,2,4,128]{3,2,1,0:T(4,128)S(1)} %get-tuple-element.50.base1, ...), custom_call_target="tpu_custom_call" | custom-call | tf_op jit(solution)/shard_map/wall_last/pallas_call | solution.py:810
  (1 shorter events, 0.0 us)
Async XLA Ops:
  1.8 5.0 %collective-permute-start = (f32[80,128]{1,0:T(8,128)S(1)}, f32[80,128]{1,0:T(8,128)S(1)}, u32[]{:S(2)}, u32[]{:S(2)}) collective-permute-start(f32[80,128]{1,0:T(8,128)S(1)} %get-tuple-element.32), channel_id=1, source_target_pairs={{1,2},{2,1},{5,6},{6,5},{9,10},{10,9},{13,14},{14,13},{17,18},{18,... | collective-permute-start | bytes 122888 | tf_op jit(solution)/shard_map/ppermute | solution.py:65
  4.8 2.0 %collective-permute-start.1 = (f32[80,128]{1,0:T(8,128)S(1)}, f32[80,128]{1,0:T(8,128)S(1)}, u32[]{:S(2)}, u32[]{:S(2)}) collective-permute-start(f32[80,128]{1,0:T(8,128)S(1)} %get-tuple-element.33), channel_id=1, source_target_pairs={{0,1},{1,0},{4,5},{5,4},{8,9},{9,8},{12,13},{13,12},{16,17},{17,16... | collective-permute-start | bytes 122888 | tf_op jit(solution)/shard_map/ppermute | solution.py:66
  6.9 6.5 %collective-permute-start.2 = (f32[120,128]{1,0:T(8,128)S(1)}, f32[120,128]{1,0:T(8,128)S(1)}, u32[]{:S(2)}, u32[]{:S(2)}) collective-permute-start(f32[120,128]{1,0:T(8,128)S(1)} %get-tuple-element.36), channel_id=1, source_target_pairs={{4,8},{8,4},{5,9},{9,5},{6,10},{10,6},{7,11},{11,7},{12,16},{16,12... | collective-permute-start | bytes 184328 | tf_op jit(solution)/shard_map/ppermute | solution.py:65
  7.1 6.3 %collective-permute-start.3 = (f32[120,128]{1,0:T(8,128)S(1)}, f32[120,128]{1,0:T(8,128)S(1)}, u32[]{:S(2)}, u32[]{:S(2)}) collective-permute-start(f32[120,128]{1,0:T(8,128)S(1)} %get-tuple-element.37), channel_id=1, source_target_pairs={{0,4},{4,0},{1,5},{5,1},{2,6},{6,2},{3,7},{7,3},{8,12},{12,8},{9,1... | collective-permute-start | bytes 184328 | tf_op jit(solution)/shard_map/ppermute | solution.py:66
  14.4 1.5 %collective-permute-start.4 = (f32[16,24,128]{2,1,0:T(8,128)S(1)}, f32[16,24,128]{2,1,0:T(8,128)S(1)}, u32[]{:S(2)}, u32[]{:S(2)}) collective-permute-start(f32[16,24,128]{2,1,0:T(8,128)S(1)} %get-tuple-element.48), channel_id=1, source_target_pairs={{0,1},{1,0},{4,5},{5,4},{8,9},{9,8},{12,13},{13,12},{16,17},{17,16... | collective-permute-start | bytes 589832 | tf_op jit(solution)/shard_map/ppermute | solution.py:852
  16.6 14.5 %all-to-all-start = ((f32[16,24,128]{2,1,0:T(8,128)}), f32[16,24,128]{2,1,0:T(8,128)S(1)}, u32[]{:S(2)}, u32[]{:S(2)}) async-start(f32[16,24,128]{2,1,0:T(8,128)} %pair_sum.1), calls=%async_computation | async-start | bytes 393216 | tf_op jit(solution)/shard_map/all_to_all | solution.py:857
  21.9 4.2 %collective-permute-start.5 = (f32[8,128]{1,0:T(8,128)S(1)}, f32[8,128]{1,0:T(8,128)S(1)}, u32[]{:S(2)}, u32[]{:S(2)}) collective-permute-start(f32[8,128]{1,0:T(8,128)S(1)} %get-tuple-element.52), channel_id=1, source_target_pairs={{1,2},{2,1},{5,6},{6,5},{9,10},{10,9},{13,14},{14,13},{17,18},{18,... | collective-permute-start | bytes 12296 | tf_op jit(solution)/shard_map/ppermute | solution.py:65
  23.8 2.3 %collective-permute-start.6 = (f32[8,128]{1,0:T(8,128)S(1)}, f32[8,128]{1,0:T(8,128)S(1)}, u32[]{:S(2)}, u32[]{:S(2)}) collective-permute-start(f32[8,128]{1,0:T(8,128)S(1)} %get-tuple-element.53), channel_id=1, source_target_pairs={{0,1},{1,0},{4,5},{5,4},{8,9},{9,8},{12,13},{13,12},{16,17},{17,16... | collective-permute-start | bytes 12296 | tf_op jit(solution)/shard_map/ppermute | solution.py:66
  26.2 2.9 %collective-permute-start.7 = (f32[24,128]{1,0:T(8,128)S(1)}, f32[24,128]{1,0:T(8,128)S(1)}, u32[]{:S(2)}, u32[]{:S(2)}) collective-permute-start(f32[24,128]{1,0:T(8,128)S(1)} %get-tuple-element.54), channel_id=1, source_target_pairs={{4,8},{8,4},{5,9},{9,5},{6,10},{10,6},{7,11},{11,7},{12,16},{16,12... | collective-permute-start | bytes 36872 | tf_op jit(solution)/shard_map/ppermute | solution.py:65
  26.3 4.5 %collective-permute-start.8 = (f32[24,128]{1,0:T(8,128)S(1)}, f32[24,128]{1,0:T(8,128)S(1)}, u32[]{:S(2)}, u32[]{:S(2)}) collective-permute-start(f32[24,128]{1,0:T(8,128)S(1)} %get-tuple-element.55), channel_id=1, source_target_pairs={{0,4},{4,0},{1,5},{5,1},{2,6},{6,2},{3,7},{7,3},{8,12},{12,8},{9,1... | collective-permute-start | bytes 36872 | tf_op jit(solution)/shard_map/ppermute | solution.py:66

commit v14 on v13

--- a/solution.py
+++ b/solution.py
@@ -89,19 +89,11 @@
 
 
 def pack_wy_kernel(
-    p, q, s, jit_in, disp_in, vel_in, wy_odd, wy_even, ends, wall, edges, sems
+    p_in, q_in, s_in, jit_in, disp_in, vel_in, wy_odd, wy_even, p, q, s, wall, sems
 ):
     cx, cy = p.shape[0], p.shape[1]
     rows, cols = jit_in.shape[1], jit_in.shape[2]
-    pairs = []
-    for k, field in enumerate((p, q, s)):
-        for side, first in enumerate((0, cy - SUB)):
-            pairs.append((field.at[:, first : first + SUB, :], edges.at[2 * k + side]))
-    pairs.append((p.at[0:2], ends.at[0, 0:2]))
-    pairs.append((p.at[cx - 2 : cx], ends.at[1, 0:2]))
-    for k, field in enumerate((q, s)):
-        pairs.append((field.at[0], ends.at[0, 2 + k]))
-        pairs.append((field.at[cx - 1], ends.at[1, 2 + k]))
+    pairs = [(p_in, p), (q_in, q), (s_in, s)]
     for k, field in enumerate((jit_in, disp_in, vel_in)):
         pairs.append((field, wall.at[k]))
     copies = [pltpu.make_async_copy(a, b, sems.at[k]) for k, (a, b) in enumerate(pairs)]
@@ -110,12 +102,12 @@
     for copy in copies:
         copy.wait()
 
-    def edge(side, near, far, h):
+    def edge(near, far, h):
         def write(out):
-            out[0:cx, :] = edges[side, :, near, :]
-            out[cx : 2 * cx, :] = edges[side, :, far, :]
-            out[2 * cx : 3 * cx, :] = edges[2 + side, :, near, :]
-            out[3 * cx : 4 * cx, :] = edges[4 + side, :, near, :]
+            out[0:cx, :] = p[:, near, :]
+            out[cx : 2 * cx, :] = p[:, far, :]
+            out[2 * cx : 3 * cx, :] = q[:, near, :]
+            out[3 * cx : 4 * cx, :] = s[:, near, :]
             at = 4 * cx
             for field in range(2):
                 for c in range(3):
@@ -129,8 +121,8 @@
 
     place_edges(
         even_at("wy"),
-        edge(0, 0, 1, 0),
-        edge(1, SUB - 1, SUB - 2, cols - 1),
+        edge(0, 1, 0),
+        edge(cy - 1, cy - 2, cols - 1),
         wy_even,
         wy_odd,
     )
@@ -145,18 +137,13 @@
 
 
 def pack_wy(p, q, s, jit, disp, vel):
-    cx, cy = p.shape[0], p.shape[1]
-    rows = jit.shape[1]
-    wy_out = vmem(pad8(4 * cx + 6 * rows), LANES)
+    message = vmem(pad8(4 * p.shape[0] + 6 * jit.shape[1]), LANES)
     return pl.pallas_call(
         pack_wy_kernel,
         in_specs=[HBM] * 6,
-        out_specs=[whole()] * 4,
-        out_shape=[wy_out, wy_out, vmem(2, 4, cy, LANES), vmem(3, *jit.shape)],
-        scratch_shapes=[
-            pltpu.VMEM((6, cx, SUB, LANES), F32),
-            pltpu.SemaphoreType.DMA((15,)),
-        ],
+        out_specs=[whole()] * 6,
+        out_shape=[message, message] + [vmem(*p.shape)] * 3 + [vmem(3, *jit.shape)],
+        scratch_shapes=[pltpu.SemaphoreType.DMA((6,))],
         compiler_params=params(),
         name="pack_wy",
     )(*in_hbm(p, q, s, jit, disp, vel))
@@ -167,20 +154,20 @@
     return lane < 3 if low else lane > 4
 
 
-def pack_fx_kernel(cx, ends, wall, got_odd, got_even, to_odd, to_even, line):
-    cy = ends.shape[2]
+def pack_fx_kernel(p, q, s, wall, got_odd, got_even, to_odd, to_even, line):
+    cx, cy = p.shape[0], p.shape[1]
     rows, cols = wall.shape[2], wall.shape[3]
     before, after = before_after("wy", got_even, got_odd)
 
-    def edge(side, near, far, x, l):
+    def edge(low, x, far, l):
         def write(out):
             line[SUB - 1 : SUB, :] = before[x : x + 1]
-            line[SUB : SUB + cy, :] = ends[side, near]
+            line[SUB : SUB + cy, :] = p[x]
             line[SUB + cy : SUB + cy + 1, :] = after[x : x + 1]
-            mine, speed = ends[side, near], ends[side, 3]
-            beside = ends[side, far] + line[SUB - 1 : SUB - 1 + cy, :] + line[SUB + 1 : SUB + 1 + cy, :]
+            mine, speed = p[x], s[x]
+            beside = p[far] + line[SUB - 1 : SUB - 1 + cy, :] + line[SUB + 1 : SUB + 1 + cy, :]
             out[0:cy, :] = mine
-            out[cy : 2 * cy, :] = update(mine, ends[side, 2], speed, beside)
+            out[cy : 2 * cy, :] = update(mine, q[x], speed, beside)
             out[2 * cy : 3 * cy, :] = speed
             at = 3 * cy
             for c in range(3):
@@ -189,8 +176,8 @@
                     row = 4 * cx + (field * 3 + c) * rows + l
                     parts = (before[row : row + 1], wall[field, c, l], after[row : row + 1])
                     pair.append(jnp.concatenate(parts, axis=0))
-                moved = pltpu.roll(pair[1], 3 if side == 0 else LANES - 3, 1)
-                out[at : at + cols + 2, :] = jnp.where(wall_lanes(moved, side == 0), pair[0], moved)
+                moved = pltpu.roll(pair[1], 3 if low else LANES - 3, 1)
+                out[at : at + cols + 2, :] = jnp.where(wall_lanes(moved, low), pair[0], moved)
                 at += cols + 2
             out[at : at + 1, :] = before[x : x + 1]
             out[at + 1 : at + 2, :] = after[x : x + 1]
@@ -200,22 +187,22 @@
         return write
 
     place_edges(
-        even_at("fx"), edge(0, 0, 1, 0, 0), edge(1, 1, 0, cx - 1, rows - 1), to_even, to_odd
+        even_at("fx"), edge(True, 0, 1, 0), edge(False, cx - 1, cx - 2, rows - 1), to_even, to_odd
     )
 
 
-def pack_fx(cx, ends, wall, got):
-    cy, cols = ends.shape[2], wall.shape[3]
+def pack_fx(grids, wall, got):
+    cy, cols = grids[0].shape[1], wall.shape[3]
     out = vmem(pad8(3 * cy + 3 * (cols + 2) + 2), LANES)
     return pl.pallas_call(
-        functools.partial(pack_fx_kernel, cx),
-        in_specs=[whole()] * 4,
+        pack_fx_kernel,
+        in_specs=[whole()] * 6,
         out_specs=[whole()] * 2,
         out_shape=[out, out],
         scratch_shapes=[vmem(cy + 2 * SUB, LANES)],
         compiler_params=params(),
         name="pack_fx",
-    )(ends, wall, *got)
+    )(*grids, wall, *got)
 
 
 def along_z(v):
@@ -304,7 +291,7 @@
     for a in range(fx_count):
         for b in range(wy_count):
             h = SUB + cols * b
-            slot = a * (wy_count // 2) + b // 2
+            slot = a * wy_count + b
             one = [part1[2 * a + l, h - 1 : h - 1 + SUB, :] for l in range(4)]
             ends = jnp.where(lane % 8 < 4, one[3], one[0])
             two = [
@@ -321,17 +308,20 @@
             own1 = jnp.where(low, pltpu.roll(x, LANES - 8, 1), one[2])
             own1 = jnp.where(high_free, pltpu.roll(x, 8, 1), own1)
             for k, group in enumerate((ends, own0, own1)):
-                slots[b % 2, slot, k * SUB : (k + 1) * SUB, :] = jnp.where(step1, group, two[k])
+                slots[slot, k * SUB : (k + 1) * SUB, :] = jnp.where(step1, group, two[k])
+
+    def halve(first, second):
+        for to, at in ((first, 0), (second, 3)):
+            for k in range(3):
+                to[:, k] = slots[:, 4 * (at + k) : 4 * (at + k + 1), :]
 
     @pl.when(even_at("wy"))
     def _():
-        keep[...] = slots[0]
-        send[...] = slots[1]
+        halve(keep, send)
 
     @pl.when(jnp.logical_not(even_at("wy")))
     def _():
-        keep[...] = slots[1]
-        send[...] = slots[0]
+        halve(send, keep)
 
 
 def free_ends(lane):
@@ -359,7 +349,8 @@
 def grid_steps(p, q, s, wy_got, fx_got, target, fx_count, wy_count):
     cx, cy = p.shape[0], p.shape[1]
     tall, high = fx_count * 2, wy_count * 4
-    half = (fx_count * wy_count // 2, 3 * SUB, LANES)
+    devices = fx_count * wy_count
+    half = (devices, 3, 4, LANES)
     return pl.pallas_call(
         grid_kernel,
         in_specs=[whole()] * 8,
@@ -375,7 +366,7 @@
             pltpu.VMEM((cx * cy, 4 * LANES), BF16),
             pltpu.VMEM((tall + 2, high + 2 * SUB, LANES), F32),
             pltpu.VMEM((tall, high + 2 * SUB, LANES), F32),
-            vmem(2, *half),
+            vmem(devices, 3 * SUB, LANES),
         ],
         compiler_params=params(),
         name="grid_steps",
@@ -395,11 +386,6 @@
         compiler_params=params(),
         name="pair_sum",
     )(keep, got, after)
-
-
-def parity_groups(fx_count, wy_count):
-    whole_row = range(fx_count * wy_count)
-    return [[d for d in whole_row if d % wy_count % 2 == parity] for parity in range(2)]
 
 
 def reached(g):
@@ -527,27 +513,24 @@
 
 
 def center_kernel(
-    wy_count, masks_in, p_in, q_in, s_in, device_in, tile_in, wall, wyo, wye,
-    weights, part, bits, target, columns, p, q, s, jpad, dpad, acc, masks, route, sems,
+    cx, wy_count, masks_in, device_in, tile_in, wall, wyo, wye,
+    weights, part, bits, target, columns, jpad, dpad, acc, masks, route, sems,
 ):
     rows, cols = wall.shape[2], wall.shape[3]
-    cx = p.shape[0]
     copies = {}
-    pairs = [(device_in, route.at[0]), (tile_in, route.at[1])]
-    pairs = [(p_in, p), (q_in, q), (s_in, s)] + pairs
-    for k, pair in enumerate(pairs):
+    for k, pair in enumerate(((device_in, route.at[0]), (tile_in, route.at[1]))):
         copies[k] = pltpu.make_async_copy(*pair, sems.at[k])
     for k, first in enumerate((3, 0, 6)):
         span = slice(first, first + 3)
         copies["masks", first] = pltpu.make_async_copy(
-            masks_in.at[:, :, span], masks.at[:, :, span], sems.at[5 + k]
+            masks_in.at[:, :, span], masks.at[:, :, span], sems.at[2 + k]
         )
-    order = [3, 4, ("masks", 3), ("masks", 0), ("masks", 6), 0, 1, 2]
+    order = [0, 1, ("masks", 3), ("masks", 0), ("masks", 6)]
     for k in order:
         copies[k].start()
     first_sub = lax.broadcasted_iota(jnp.int32, (SUB, LANES), 0) < SUB // 2
-    copies[3].wait()
-    copies[4].wait()
+    copies[0].wait()
+    copies[1].wait()
     device, tile = route[0], route[1]
     a, t = quotient(device, wy_count), quotient(tile, cols)
     b, u = device - a * wy_count, tile - t * cols
@@ -600,35 +583,32 @@
     copies["masks", 6].wait()
     for l, h in tiles:
         put_bits(l, h)
-    for k in range(3):
-        copies[k].wait()
-
-
-def wall_center(wy_count, masks, grids, device, tile, wall, wy_got):
+
+
+def wall_center(cx, wy_count, masks, device, tile, wall, wy_got):
     rows, cols = wall.shape[2], wall.shape[3]
     return pl.pallas_call(
-        functools.partial(center_kernel, wy_count),
-        in_specs=[HBM] * 6 + [whole()] * 3,
-        out_specs=[whole()] * 8,
+        functools.partial(center_kernel, cx, wy_count),
+        in_specs=[HBM] * 3 + [whole()] * 3,
+        out_specs=[whole()] * 5,
         out_shape=[
             jax.ShapeDtypeStruct((rows, cols, STORED, SUB, LANES), F32),
             vmem(rows, 4, cols, LANES),
             pltpu.VMEM((rows, cols, 2, SUB, LANES), jnp.int32),
             pltpu.VMEM(device.shape, jnp.int32),
             vmem(LANES, pad8(3 * rows * cols)),
-        ]
-        + [vmem(*grids[0].shape)] * 3,
+        ],
         scratch_shapes=[
             vmem(3, rows + 2, SUB, LANES),
             vmem(3, rows + 2, SUB, LANES),
             vmem(rows, cols, 4, LANES, LANES),
             pltpu.VMEM(masks.shape, jnp.int32),
             pltpu.VMEM((2,) + device.shape, jnp.int32),
-            pltpu.SemaphoreType.DMA((8,)),
+            pltpu.SemaphoreType.DMA((5,)),
         ],
         compiler_params=params(),
         name="wall_center",
-    )(*in_hbm(masks, *grids, device, tile), wall, *wy_got)
+    )(*in_hbm(masks, device, tile), wall, *wy_got)
 
 
 def wall_kernel(
@@ -765,9 +745,14 @@
     fill_y(dpad, base1, before, after, 0)
     before, after = before_after("fx", fxe, fxo)
     fill_x(dpad, rows, cols, before, after, 0)
-    total = got[0]
-    for d in range(1, got.shape[0]):
-        total = total + got[d]
+    pieces = []
+    for half in range(2):
+        for k in range(3):
+            total = got[half, k]
+            for d in range(half + 2, got.shape[0], 2):
+                total = total + got[d, k]
+            pieces.append(total)
+    total = jnp.concatenate(pieces, axis=0)
     one, two = unpack_slots(total, cols)
     for k in range(rows + 2):
         here = dpad[0, k, 0 : cols + 2, :] + LOADING * one[k][0 : cols + 2]
@@ -837,15 +822,15 @@
     device = route_device.reshape(-1, LANES)
     tile = route_tile.reshape(-1, LANES)
     cx = pressure.shape[0]
-    *sends, ends, wall = pack_wy(
+    *sends, p, q, s, wall = pack_wy(
         pressure, pressure_prev, speed_sq, jitter, displacement, velocity
     )
+    grids = (p, q, s)
     wy_got = exchange("wy", *sends)
-    sends = pack_fx(cx, ends, wall, wy_got)
+    sends = pack_fx(grids, wall, wy_got)
     fx_got = exchange("fx", *sends)
-    grids = (pressure, pressure_prev, speed_sq)
-    weights, part, bits, target, columns, *grids = wall_center(
-        wy_count, bond_masks, grids, device, tile, wall, wy_got
+    weights, part, bits, target, columns = wall_center(
+        cx, wy_count, bond_masks, device, tile, wall, wy_got
     )
     fresh, keep, send = grid_steps(*grids, wy_got, fx_got, target, fx_count, wy_count)
     names = ("fx", "wy")
@@ -854,14 +839,7 @@
         wall, wy_got, fx_got, part, bits, columns, fresh
     )
     slots = pair_sum(keep, other, totals)
-    got = lax.all_to_all(
-        slots,
-        names,
-        split_axis=0,
-        concat_axis=0,
-        tiled=True,
-        axis_index_groups=parity_groups(fx_count, wy_count),
-    )
+    got = lax.all_to_all(slots, names, split_axis=0, concat_axis=0, tiled=True)
     base_wy = exchange("wy", *sends)
     sends = pack_base(base1, base_wy)
     base_fx = exchange("fx", *sends)

time: 32.8 us -> 31.7 us (0.966)
  starting transfers between devices: 17 us -> 16.4 us
  waiting for transfers between devices: 6.2 us -> 5.6 us
    all_to_all x1, starting transfers between devices: 5.28 us -> 4.31 us  [per_device(): got = lax.all_to_all(slots, names, split_axis=0, concat_axis=0, tiled=True)]
    ppermute x4, waiting for transfers between devices: 4.04 us -> 3.6 us  [exchange(): got_odd = lax.ppermute(to_odd, names, swap_pairs(along, sizes, 1))]
    ppermute x4, starting transfers between devices: 6.5 us -> 6.93 us  [exchange(): got_even = lax.ppermute(to_even, names, swap_pairs(along, sizes, 0))]
where the time goes in v14:
time: 31.7 us; the launch traced here: 31.3 us
  starting transfers between devices  16.4 us (52%)
  Pallas kernels  8.56 us (27%)
  waiting for transfers between devices  5.6 us (18%)
  between operations  0.73 us (2%)
    ppermute x4, starting transfers between devices, exchange(): got_even = lax.ppermute(to_even, names, swap_pairs(along, sizes, 0))  6.93 us
    ppermute x4, starting transfers between devices, exchange(): got_odd = lax.ppermute(to_odd, names, swap_pairs(along, sizes, 1))  5.09 us
    all_to_all x1, starting transfers between devices, per_device(): got = lax.all_to_all(slots, names, split_axis=0, concat_axis=0, tiled=True)  4.31 us
    ppermute x4, waiting for transfers between devices, exchange(): got_odd = lax.ppermute(to_odd, names, swap_pairs(along, sizes, 1))  3.6 us
    pallas_call x1, Pallas kernels, wall_center(): pl.pallas_call(functools.partial(center_kernel, cx, wy_count), in_specs=[...  2.77 us
    ppermute x4, waiting for transfers between devices, exchange(): got_even = lax.ppermute(to_even, names, swap_pairs(along, sizes, 0))  1.68 us
    pallas_call x1, Pallas kernels, wall_last(): pl.pallas_call(last_kernel, in_specs=[whole()] * 10, out_specs=[whole()]...  1.43 us
    pallas_call x1, Pallas kernels, wall_first(): pl.pallas_call(functools.partial(wall_kernel, cx, cy), in_specs=[whole()]...  1.29 us
  transfers between devices with their start and end apart: 10, of which 5 were waited for; matrix products, arithmetic and copies ran while one was open for 0% of the time, Pallas kernels for 13%

profile of v14, /device:TPU:0, one launch (start us, length us, event | category | flops | bytes accessed | tf_op | source)
XLA Modules:
  0.0 31.3 jit_solution(3238306733228139017)
XLA Ops:
  0.6 1.2 %pack_wy.1 = (f32[80,128]{1,0:T(8,128)S(1)}, f32[80,128]{1,0:T(8,128)S(1)}, f32[16,32,128]{2,1,0:T(8,128)S(1)}, f32[16,32,128]{2,1,0:T(8,128)S(1)}, f32[16,32,12...) custom-call(f32[16,32,128]{2,1,0:T(8,128)} %p_in.1, f32[16,32,128]{2,1,0:T(8,128)} %q_in.1, f32[16,32,128]{2,1,0:T(8,128)} %s_in.1, ...), custom_call_target="tpu_custom_call" | custom-call | tf_op jit(solution)/shard_map/pack_wy/pallas_call | solution.py:141
  1.9 3.0 %collective-permute-start = (f32[80,128]{1,0:T(8,128)S(1)}, f32[80,128]{1,0:T(8,128)S(1)}, u32[]{:S(2)}, u32[]{:S(2)}) collective-permute-start(f32[80,128]{1,0:T(8,128)S(1)} %get-tuple-element.31), channel_id=1, source_target_pairs={{1,2},{2,1},{5,6},{6,5},{9,10},{10,9},{13,14},{14,13},{17,18},{18,... | collective-permute-start | bytes 122888 | tf_op jit(solution)/shard_map/ppermute | solution.py:65
  4.9 0.1 collective-permute-start.1
  5.0 1.8 %collective-permute-done.wyo.got_odd = f32[80,128]{1,0:T(8,128)S(1)} collective-permute-done((f32[80,128]{1,0:T(8,128)S(1)}, f32[80,128]{1,0:T(8,128)S(1)}, u32[]{:S(2)}, u32[]{:S(2)}) %collective-permute-start) | collective-permute-done | bytes 40992 | tf_op jit(solution)/shard_map/ppermute | solution.py:65
  6.8 0.0 collective-permute-done.1.wye.got_even
  6.8 0.1 pack_fx.1
  7.0 0.2 collective-permute-start.2
  7.1 3.5 %collective-permute-start.3 = (f32[120,128]{1,0:T(8,128)S(1)}, f32[120,128]{1,0:T(8,128)S(1)}, u32[]{:S(2)}, u32[]{:S(2)}) collective-permute-start(f32[120,128]{1,0:T(8,128)S(1)} %get-tuple-element.38), channel_id=1, source_target_pairs={{0,4},{4,0},{1,5},{5,1},{2,6},{6,2},{3,7},{7,3},{8,12},{12,8},{9,1... | collective-permute-start | bytes 184328 | tf_op jit(solution)/shard_map/ppermute | solution.py:66
  10.6 2.8 %wall_center.1 = (f32[2,4,40,8,128]{4,3,2,1,0:T(8,128)S(1)}, f32[2,4,4,128]{3,2,1,0:T(4,128)S(1)}, s32[2,4,2,8,128]{4,3,2,1,0:T(8,128)S(1)}, s32[4,128]{1,0:T(4,128)S(1)}, f32[128,24]{1,0:T(8,128)S(1)}) custom-call(s32[2,4,9,128,128]{4,3,2,1,0:T(8,128)} %masks_in.1, s32[4,128]{1,0:T(4,128)} %bitcast.2, s32[4,128]{1,0:T(4,128)} %bitcast.3, ...), custom_call_target="tpu_custom_call" | custom-call | tf_op jit(solution)/shard_map/wall_center/pallas_call | solution.py:590
  13.4 0.0 collective-permute-done.2.fxo
  13.4 0.0 collective-permute-done.3.fxe
  13.4 1.0 %grid_steps.1 = (f32[16,32,128]{2,1,0:T(8,128)S(1)}, f32[32,3,4,128]{3,2,1,0:T(4,128)S(1)}, f32[32,3,4,128]{3,2,1,0:T(4,128)S(1)}) custom-call(f32[16,32,128]{2,1,0:T(8,128)S(1)} %get-tuple-element.34.p, f32[16,32,128]{2,1,0:T(8,128)S(1)} %get-tuple-element.35.q, f32[16,32,128]{2,1,0:T(8,128)S(1)} %get-tuple-element.36.s, ...), custom_call_target="tpu_custom_call" | custom-call | tf_op jit(solution)/shard_map/grid_steps/pallas_call | solution.py:354
  14.4 0.1 collective-permute-start.4
  14.5 1.3 %wall_first.1 = (f32[2,4,40,8,128]{4,3,2,1,0:T(8,128)S(1)}, f32[3,2,4,128]{3,2,1,0:T(4,128)S(1)}, f32[3,2,4,128]{3,2,1,0:T(4,128)S(1)}, f32[2,4,128]{2,1,0:T(4,1...) custom-call(f32[3,3,2,4,128]{4,3,2,1,0:T(4,128)S(1)} %get-tuple-element.30.wall, ...), custom_call_target="tpu_custom_call" | custom-call | tf_op jit(solution)/shard_map/wall_first/pallas_call | solution.py:680
  15.8 0.1 collective-permute-done.4.got
  15.9 0.7 %pair_sum.1 = f32[32,3,4,128]{3,2,1,0:T(4,128)} custom-call(f32[32,3,4,128]{3,2,1,0:T(4,128)S(1)} %get-tuple-element.45.keep, f32[32,3,4,128]{3,2,1,0:T(4,128)S(1)} %collective-permute-done.4.got, f32[2,4,128]{2,1,0:T(4,128)S(1)} %get-tuple-element.47.after.totals), custom_call_target="tpu_custom_call" | custom-call | tf_op jit(solution)/shard_map/pair_sum/pallas_call | solution.py:381
  16.6 4.3 %all-to-all-start = ((f32[32,3,4,128]{3,2,1,0:T(4,128)}), f32[32,3,4,128]{3,2,1,0:T(4,128)S(1)}, u32[]{:S(2)}, u32[]{:S(2)}) async-start(f32[32,3,4,128]{3,2,1,0:T(4,128)} %pair_sum.1), calls=%async_computation | async-start | bytes 393216 | tf_op jit(solution)/shard_map/all_to_all | solution.py:842
  21.0 1.8 %collective-permute-start.5 = (f32[8,128]{1,0:T(8,128)S(1)}, f32[8,128]{1,0:T(8,128)S(1)}, u32[]{:S(2)}, u32[]{:S(2)}) collective-permute-start(f32[8,128]{1,0:T(8,128)S(1)} %get-tuple-element.50), channel_id=1, source_target_pairs={{1,2},{2,1},{5,6},{6,5},{9,10},{10,9},{13,14},{14,13},{17,18},{18,... | collective-permute-start | bytes 12296 | tf_op jit(solution)/shard_map/ppermute | solution.py:65
  22.8 0.1 collective-permute-start.6
  22.9 1.8 %collective-permute-done.5.got_odd.wyo = f32[8,128]{1,0:T(8,128)S(1)} collective-permute-done((f32[8,128]{1,0:T(8,128)S(1)}, f32[8,128]{1,0:T(8,128)S(1)}, u32[]{:S(2)}, u32[]{:S(2)}) %collective-permute-start.5) | collective-permute-done | bytes 4128 | tf_op jit(solution)/shard_map/ppermute | solution.py:65
  24.7 0.0 collective-permute-done.6.got_even.wye
  24.7 0.1 collective-permute-start.7
  24.8 3.2 %collective-permute-start.8 = (f32[24,128]{1,0:T(8,128)S(1)}, f32[24,128]{1,0:T(8,128)S(1)}, u32[]{:S(2)}, u32[]{:S(2)}) collective-permute-start(f32[24,128]{1,0:T(8,128)S(1)} %get-tuple-element.53), channel_id=1, source_target_pairs={{0,4},{4,0},{1,5},{5,1},{2,6},{6,2},{3,7},{7,3},{8,12},{12,8},{9,1... | collective-permute-start | bytes 36872 | tf_op jit(solution)/shard_map/ppermute | solution.py:66
  28.0 0.0 collective-permute-done.7.fxo
  28.0 1.7 %collective-permute-done.8.fxe = f32[24,128]{1,0:T(8,128)S(1)} collective-permute-done((f32[24,128]{1,0:T(8,128)S(1)}, f32[24,128]{1,0:T(8,128)S(1)}, u32[]{:S(2)}, u32[]{:S(2)}) %collective-permute-start.8) | collective-permute-done | bytes 12320 | tf_op jit(solution)/shard_map/ppermute | solution.py:66
  29.7 0.2 all-to-all-done.got
  29.8 1.4 %wall_last.1 = (f32[3,2,4,128]{3,2,1,0:T(4,128)}, f32[3,2,4,128]{3,2,1,0:T(4,128)}) custom-call(f32[2,4,40,8,128]{4,3,2,1,0:T(8,128)S(1)} %get-tuple-element.33.weights, f32[2,4,40,8,128]{4,3,2,1,0:T(8,128)S(1)} %get-tuple-element.44.end_weights, f32[32,3,4,128]{3,2,1,0:T(4,128)S(1)} %all-to-all-done.got, f32[3,2,4,128]{3,2,1,0:T(4,128)S(1)} %get-tuple-element.48.base1, ...), custom_call_target="tpu_custom_call" | custom-call | tf_op jit(solution)/shard_map/wall_last/pallas_call | solution.py:795
  (1 shorter events, 0.0 us)
Async XLA Ops:
  1.9 5.0 %collective-permute-start = (f32[80,128]{1,0:T(8,128)S(1)}, f32[80,128]{1,0:T(8,128)S(1)}, u32[]{:S(2)}, u32[]{:S(2)}) collective-permute-start(f32[80,128]{1,0:T(8,128)S(1)} %get-tuple-element.31), channel_id=1, source_target_pairs={{1,2},{2,1},{5,6},{6,5},{9,10},{10,9},{13,14},{14,13},{17,18},{18,... | collective-permute-start | bytes 122888 | tf_op jit(solution)/shard_map/ppermute | solution.py:65
  4.9 2.0 %collective-permute-start.1 = (f32[80,128]{1,0:T(8,128)S(1)}, f32[80,128]{1,0:T(8,128)S(1)}, u32[]{:S(2)}, u32[]{:S(2)}) collective-permute-start(f32[80,128]{1,0:T(8,128)S(1)} %get-tuple-element.32), channel_id=1, source_target_pairs={{0,1},{1,0},{4,5},{5,4},{8,9},{9,8},{12,13},{13,12},{16,17},{17,16... | collective-permute-start | bytes 122888 | tf_op jit(solution)/shard_map/ppermute | solution.py:66
  7.0 6.4 %collective-permute-start.2 = (f32[120,128]{1,0:T(8,128)S(1)}, f32[120,128]{1,0:T(8,128)S(1)}, u32[]{:S(2)}, u32[]{:S(2)}) collective-permute-start(f32[120,128]{1,0:T(8,128)S(1)} %get-tuple-element.37), channel_id=1, source_target_pairs={{4,8},{8,4},{5,9},{9,5},{6,10},{10,6},{7,11},{11,7},{12,16},{16,12... | collective-permute-start | bytes 184328 | tf_op jit(solution)/shard_map/ppermute | solution.py:65
  7.1 6.2 %collective-permute-start.3 = (f32[120,128]{1,0:T(8,128)S(1)}, f32[120,128]{1,0:T(8,128)S(1)}, u32[]{:S(2)}, u32[]{:S(2)}) collective-permute-start(f32[120,128]{1,0:T(8,128)S(1)} %get-tuple-element.38), channel_id=1, source_target_pairs={{0,4},{4,0},{1,5},{5,1},{2,6},{6,2},{3,7},{7,3},{8,12},{12,8},{9,1... | collective-permute-start | bytes 184328 | tf_op jit(solution)/shard_map/ppermute | solution.py:66
  14.4 1.5 %collective-permute-start.4 = (f32[32,3,4,128]{3,2,1,0:T(4,128)S(1)}, f32[32,3,4,128]{3,2,1,0:T(4,128)S(1)}, u32[]{:S(2)}, u32[]{:S(2)}) collective-permute-start(f32[32,3,4,128]{3,2,1,0:T(4,128)S(1)} %get-tuple-element.46), channel_id=1, source_target_pairs={{0,1},{1,0},{4,5},{5,4},{8,9},{9,8},{12,13},{13,12},{16,17},{17,16... | collective-permute-start | bytes 589832 | tf_op jit(solution)/shard_map/ppermute | solution.py:837
  16.6 13.2 %all-to-all-start = ((f32[32,3,4,128]{3,2,1,0:T(4,128)}), f32[32,3,4,128]{3,2,1,0:T(4,128)S(1)}, u32[]{:S(2)}, u32[]{:S(2)}) async-start(f32[32,3,4,128]{3,2,1,0:T(4,128)} %pair_sum.1), calls=%async_computation | async-start | bytes 393216 | tf_op jit(solution)/shard_map/all_to_all | solution.py:842
  21.0 3.7 %collective-permute-start.5 = (f32[8,128]{1,0:T(8,128)S(1)}, f32[8,128]{1,0:T(8,128)S(1)}, u32[]{:S(2)}, u32[]{:S(2)}) collective-permute-start(f32[8,128]{1,0:T(8,128)S(1)} %get-tuple-element.50), channel_id=1, source_target_pairs={{1,2},{2,1},{5,6},{6,5},{9,10},{10,9},{13,14},{14,13},{17,18},{18,... | collective-permute-start | bytes 12296 | tf_op jit(solution)/shard_map/ppermute | solution.py:65
  22.8 1.9 %collective-permute-start.6 = (f32[8,128]{1,0:T(8,128)S(1)}, f32[8,128]{1,0:T(8,128)S(1)}, u32[]{:S(2)}, u32[]{:S(2)}) collective-permute-start(f32[8,128]{1,0:T(8,128)S(1)} %get-tuple-element.51), channel_id=1, source_target_pairs={{0,1},{1,0},{4,5},{5,4},{8,9},{9,8},{12,13},{13,12},{16,17},{17,16... | collective-permute-start | bytes 12296 | tf_op jit(solution)/shard_map/ppermute | solution.py:66
  24.7 3.3 %collective-permute-start.7 = (f32[24,128]{1,0:T(8,128)S(1)}, f32[24,128]{1,0:T(8,128)S(1)}, u32[]{:S(2)}, u32[]{:S(2)}) collective-permute-start(f32[24,128]{1,0:T(8,128)S(1)} %get-tuple-element.52), channel_id=1, source_target_pairs={{4,8},{8,4},{5,9},{9,5},{6,10},{10,6},{7,11},{11,7},{12,16},{16,12... | collective-permute-start | bytes 36872 | tf_op jit(solution)/shard_map/ppermute | solution.py:65
  24.8 4.9 %collective-permute-start.8 = (f32[24,128]{1,0:T(8,128)S(1)}, f32[24,128]{1,0:T(8,128)S(1)}, u32[]{:S(2)}, u32[]{:S(2)}) collective-permute-start(f32[24,128]{1,0:T(8,128)S(1)} %get-tuple-element.53), channel_id=1, source_target_pairs={{0,4},{4,0},{1,5},{5,1},{2,6},{6,2},{3,7},{7,3},{8,12},{12,8},{9,1... | collective-permute-start | bytes 36872 | tf_op jit(solution)/shard_map/ppermute | solution.py:66

commit v15 on v14

--- a/solution.py
+++ b/solution.py
@@ -474,16 +474,16 @@
     return jnp.maximum(weight, 0.0)
 
 
-def tile_pass(l, h, cols, columns, others, pulls, weight_of, weights, acc):
+def tile_pass(l, h, cols, columns, others, pulls, mask_at, weights, acc):
     place = 0
     first = 3 * (l * cols + h)
     for g in range(LANES // SUB):
         span = slice(g * SUB, (g + 1) * SUB)
         mine = [jnp.broadcast_to(columns[span, first + c : first + c + 1], (SUB, LANES)) for c in range(3)]
         sums = [None] * 4
-        for order, dh in enumerate(reached(g)):
+        for dh in reached(g):
             here = [others[c][dh] for c in range(3)]
-            weight = weight_of(g, order, dh, here, mine)
+            weight = bond_row(mask_at(dh, span, place), here, mine)
             weights[l, h, place] = weight
             place += 1
             terms = [weight * pulls[c][dh] for c in range(3)] + [weight]
@@ -514,7 +514,7 @@
 
 def center_kernel(
     cx, wy_count, masks_in, device_in, tile_in, wall, wyo, wye,
-    weights, part, bits, target, columns, jpad, dpad, acc, masks, route, sems,
+    weights, part, end_masks, target, columns, jpad, dpad, acc, masks, route, sems,
 ):
     rows, cols = wall.shape[2], wall.shape[3]
     copies = {}
@@ -552,27 +552,24 @@
             others.append(mid)
         pulls = [mid_rows(dpad, c, l, h) for c in range(3)]
 
-        def weight_of(g, order, dh, here, mine):
-            span = slice(g * SUB, (g + 1) * SUB)
-            return bond_row(masks[l, h, 4 + dh, span, :].astype(F32), here, mine)
-
-        tile_pass(l, h, cols, columns, others, pulls, weight_of, weights, acc)
+        def mask_at(dh, span, place):
+            return masks[l, h, 4 + dh, span, :].astype(F32)
+
+        tile_pass(l, h, cols, columns, others, pulls, mask_at, weights, acc)
 
     def put_sums(l, h):
         for c, sums in enumerate(tile_sums(acc, l, h, 4)):
             part[l, c, h : h + 1, :] = sums
 
-    def put_bits(l, h):
-        words = [jnp.zeros((SUB, LANES), jnp.int32) for _ in range(2)]
+    def put_masks(l, h):
+        place = 0
         for g in range(LANES // SUB):
             span = slice(g * SUB, (g + 1) * SUB)
-            for order, dh in enumerate(reached(g)):
+            for dh in reached(g):
                 before = masks[l, h, 1 + dh, span, :]
                 after = masks[l, h, 7 + dh, span, :]
-                place = 3 * (g % 8) + order
-                words[g // 8] = words[g // 8] + jnp.where(first_sub, before, after) * (1 << place)
-        for k in range(2):
-            bits[l, h, k] = words[k]
+                end_masks[l, h, place] = jnp.where(first_sub, before, after).astype(F32)
+                place += 1
 
     tiles = [(l, h) for l in range(rows) for h in range(cols)]
     copies["masks", 3].wait()
@@ -582,7 +579,7 @@
     copies["masks", 0].wait()
     copies["masks", 6].wait()
     for l, h in tiles:
-        put_bits(l, h)
+        put_masks(l, h)
 
 
 def wall_center(cx, wy_count, masks, device, tile, wall, wy_got):
@@ -594,7 +591,7 @@
         out_shape=[
             jax.ShapeDtypeStruct((rows, cols, STORED, SUB, LANES), F32),
             vmem(rows, 4, cols, LANES),
-            pltpu.VMEM((rows, cols, 2, SUB, LANES), jnp.int32),
+            vmem(rows, cols, STORED, SUB, LANES),
             pltpu.VMEM(device.shape, jnp.int32),
             vmem(LANES, pad8(3 * rows * cols)),
         ],
@@ -612,7 +609,7 @@
 
 
 def wall_kernel(
-    cx, cy, wall, wyo, wye, fxo, fxe, part, bits, columns, pressure,
+    cx, cy, wall, wyo, wye, fxo, fxe, part, end_masks, columns, pressure,
     weights, vel1, base1, totals, to_odd, to_even, pressure_out, jpad, dpad, acc, sem,
 ):
     rows, cols = wall.shape[2], wall.shape[3]
@@ -639,11 +636,10 @@
             others.append(ends)
         pulls = [end_rows(dpad, c, l, h, first_sub) for c in range(3)]
 
-        def weight_of(g, order, dh, here, mine):
-            bonded = (bits[l, h, g // 8] & (1 << (3 * (g % 8) + order))) != 0
-            return jnp.where(bonded, bond_row(1.0, here, mine), 0.0)
-
-        tile_pass(l, h, cols, columns, others, pulls, weight_of, weights, acc)
+        def mask_at(dh, span, place):
+            return end_masks[l, h, place]
+
+        tile_pass(l, h, cols, columns, others, pulls, mask_at, weights, acc)
 
     for l in range(rows):
         sums = []
@@ -672,7 +668,7 @@
     copy.wait()
 
 
-def wall_first(wall, wy_got, fx_got, part, bits, columns, pressure):
+def wall_first(wall, wy_got, fx_got, part, end_masks, columns, pressure):
     cx, cy = pressure.shape[0], pressure.shape[1]
     rows, cols = wall.shape[2], wall.shape[3]
     edge = (pad8(3 * rows), LANES)
@@ -698,7 +694,7 @@
         ],
         compiler_params=params(),
         name="wall_first",
-    )(wall, *wy_got, *fx_got, part, bits, columns, pressure)
+    )(wall, *wy_got, *fx_got, part, end_masks, columns, pressure)
 
 
 def pack_base_kernel(base1, got_odd, got_even, to_odd, to_even):
@@ -735,9 +731,43 @@
     )(base1, *got)
 
 
+def middle_kernel(weights, base1, wyo, wye, after_this, part, dpad, acc):
+    rows, cols = base1.shape[1], base1.shape[2]
+    before, after = before_after("wy", wye, wyo)
+    fill_y(dpad, base1, before, after, 0)
+    for l in range(rows):
+        for h in range(cols):
+            mids = [mid_rows(dpad, c, l, h) for c in range(3)]
+            place = 0
+            for g in range(LANES // SUB):
+                sums = [None] * 3
+                for dh in reached(g):
+                    weight = weights[l, h, place]
+                    terms = [weight * mids[c][dh] for c in range(3)]
+                    sums = [t if v is None else v + t for v, t in zip(sums, terms)]
+                    place += 1
+                for c in range(3):
+                    acc[l, h, c, g * SUB : (g + 1) * SUB, :] = sums[c]
+            for c, row in enumerate(tile_sums(acc, l, h, 3)):
+                part[l, c, h : h + 1, :] = row
+
+
+def wall_middle(weights, base1, wy_got, after):
+    rows, cols = base1.shape[1], base1.shape[2]
+    return pl.pallas_call(
+        middle_kernel,
+        in_specs=[whole()] * 5,
+        out_specs=whole(),
+        out_shape=vmem(rows, 3, cols, LANES),
+        scratch_shapes=[vmem(3, rows + 2, SUB, LANES), vmem(rows, cols, 3, LANES, LANES)],
+        compiler_params=params(),
+        name="wall_middle",
+    )(weights, base1, *wy_got, after)
+
+
 def last_kernel(
-    weights, end_weights, got, base1, vel1, totals, wyo, wye, fxo, fxe, disp_out, vel_out,
-    dpad, acc,
+    weights, end_weights, part, got, base1, vel1, totals, wyo, wye, fxo, fxe, disp_out, vel_out,
+    dpad, load_pad, acc,
 ):
     rows, cols = base1.shape[1], base1.shape[2]
     first_sub = lax.broadcasted_iota(jnp.int32, (SUB, LANES), 0) < SUB // 2
@@ -755,21 +785,21 @@
     total = jnp.concatenate(pieces, axis=0)
     one, two = unpack_slots(total, cols)
     for k in range(rows + 2):
-        here = dpad[0, k, 0 : cols + 2, :] + LOADING * one[k][0 : cols + 2]
-        dpad[0, k, 0 : cols + 2, :] = here
+        loads = LOADING * one[k][0 : cols + 2]
+        load_pad[0, k, 0 : cols + 2, :] = loads
+        dpad[0, k, 0 : cols + 2, :] = dpad[0, k, 0 : cols + 2, :] + loads
 
     def one_tile(l, h):
-        mids = [mid_rows(dpad, c, l, h) for c in range(3)]
+        mid = mid_rows(load_pad, 0, l, h)
         ends = [end_rows(dpad, c, l, h, first_sub) for c in range(3)]
         place = 0
         for g in range(LANES // SUB):
             sums = [None] * 3
             for dh in reached(g):
-                for weight, pulls in (
-                    (weights[l, h, place], mids), (end_weights[l, h, place], ends)
-                ):
-                    terms = [weight * pulls[c][dh] for c in range(3)]
-                    sums = [t if v is None else v + t for v, t in zip(sums, terms)]
+                weight = end_weights[l, h, place]
+                terms = [weight * ends[c][dh] for c in range(3)]
+                terms[0] = terms[0] + weights[l, h, place] * mid[dh]
+                sums = [t if v is None else v + t for v, t in zip(sums, terms)]
                 place += 1
             for c in range(3):
                 acc[l, h, c, g * SUB : (g + 1) * SUB, :] = sums[c]
@@ -782,7 +812,7 @@
         pulled = by_quantity(sums)
         for c in range(3):
             mine = dpad[c, l + 1, 1 : cols + 1, :]
-            force = STIFFNESS * (pulled[c] - totals[l] * mine)
+            force = STIFFNESS * (pulled[c] + part[l, c] - totals[l] * mine)
             if c == 0:
                 force = force + LOADING * (one[l + 1][1 : cols + 1] + two[l])
             fresh = vel1[c, l] + force
@@ -790,20 +820,21 @@
             disp_out[c, l] = mine + fresh
 
 
-def wall_last(weights, end_weights, got, base1, vel1, totals, wy_got, fx_got):
+def wall_last(weights, end_weights, part, got, base1, vel1, totals, wy_got, fx_got):
     rows, cols = base1.shape[1], base1.shape[2]
     return pl.pallas_call(
         last_kernel,
-        in_specs=[whole()] * 10,
+        in_specs=[whole()] * 11,
         out_specs=[whole()] * 2,
         out_shape=[jax.ShapeDtypeStruct(base1.shape, F32)] * 2,
         scratch_shapes=[
-            pltpu.VMEM((3, rows + 2, SUB, LANES), F32),
+            vmem(3, rows + 2, SUB, LANES),
+            vmem(1, rows + 2, SUB, LANES),
             pltpu.VMEM((rows, cols, 3, LANES, LANES), F32),
         ],
         compiler_params=params(),
         name="wall_last",
-    )(weights, end_weights, got, base1, vel1, totals, *wy_got, *fx_got)
+    )(weights, end_weights, part, got, base1, vel1, totals, *wy_got, *fx_got)
 
 
 def per_device(
@@ -829,22 +860,23 @@
     wy_got = exchange("wy", *sends)
     sends = pack_fx(grids, wall, wy_got)
     fx_got = exchange("fx", *sends)
-    weights, part, bits, target, columns = wall_center(
+    weights, part, end_masks, target, columns = wall_center(
         cx, wy_count, bond_masks, device, tile, wall, wy_got
     )
     fresh, keep, send = grid_steps(*grids, wy_got, fx_got, target, fx_count, wy_count)
     names = ("fx", "wy")
     other = lax.ppermute(send, names, swap_pairs(1, (fx_count, wy_count), 0))
     end_weights, vel1, base1, totals, *sends, pressure_out = wall_first(
-        wall, wy_got, fx_got, part, bits, columns, fresh
+        wall, wy_got, fx_got, part, end_masks, columns, fresh
     )
     slots = pair_sum(keep, other, totals)
     got = lax.all_to_all(slots, names, split_axis=0, concat_axis=0, tiled=True)
     base_wy = exchange("wy", *sends)
     sends = pack_base(base1, base_wy)
     base_fx = exchange("fx", *sends)
+    middle = wall_middle(weights, base1, base_wy, sends[0])
     disp_out, vel_out = wall_last(
-        weights, end_weights, got, base1, vel1, totals, base_wy, base_fx
+        weights, end_weights, middle, got, base1, vel1, totals, base_wy, base_fx
     )
     return (disp_out, vel_out, pressure_out)
 

time: 31.7 us -> 31.5 us (level)
  starting transfers between devices: 16.4 us -> 14.9 us
  waiting for transfers between devices: 5.6 us -> 6.63 us
    ppermute x4, starting transfers between devices: 6.93 us -> 5.52 us  [exchange(): got_even = lax.ppermute(to_even, names, swap_pairs(along, sizes, 0))]
    all_to_all x1, waiting for transfers between devices: 0.19 us -> 1.37 us  [per_device(): got = lax.all_to_all(slots, names, split_axis=0, concat_axis=0, tiled=True)]
    pallas_call x1 -> x2, Pallas kernels: 1.43 us -> 1.79 us  [the longest x1 1.25 us: wall_last(): pl.pallas_call(last_kernel, in_specs=[whole()] * 11, out_specs=[whole()]...]
  transfers between devices with their start and end apart: 10 -> 10, of which waited for: 5 -> 5; matrix products, arithmetic and copies ran while one was open for 0% -> 0% of each run, Pallas kernels for 13% -> 15%
where the time goes in v15:
time: 31.5 us; the launch traced here: 31.1 us
  starting transfers between devices  14.9 us (47%)
  Pallas kernels  8.82 us (28%)
  waiting for transfers between devices  6.63 us (21%)
  between operations  0.72 us (2%)
    ppermute x4, starting transfers between devices, exchange(): got_even = lax.ppermute(to_even, names, swap_pairs(along, sizes, 0))  5.52 us
    ppermute x4, starting transfers between devices, exchange(): got_odd = lax.ppermute(to_odd, names, swap_pairs(along, sizes, 1))  5.02 us
    all_to_all x1, starting transfers between devices, per_device(): got = lax.all_to_all(slots, names, split_axis=0, concat_axis=0, tiled=True)  4.28 us
    ppermute x4, waiting for transfers between devices, exchange(): got_odd = lax.ppermute(to_odd, names, swap_pairs(along, sizes, 1))  3.6 us
    pallas_call x1, Pallas kernels, wall_center(): pl.pallas_call(functools.partial(center_kernel, cx, wy_count), in_specs=[...  2.77 us
    ppermute x4, waiting for transfers between devices, exchange(): got_even = lax.ppermute(to_even, names, swap_pairs(along, sizes, 0))  1.43 us
    all_to_all x1, waiting for transfers between devices, per_device(): got = lax.all_to_all(slots, names, split_axis=0, concat_axis=0, tiled=True)  1.37 us
    pallas_call x1, Pallas kernels, wall_last(): pl.pallas_call(last_kernel, in_specs=[whole()] * 11, out_specs=[whole()]...  1.25 us
  transfers between devices with their start and end apart: 10, of which 5 were waited for; matrix products, arithmetic and copies ran while one was open for 0% of the time, Pallas kernels for 15%

profile of v15, /device:TPU:0, one launch (start us, length us, event | category | flops | bytes accessed | tf_op | source)
XLA Modules:
  0.0 31.1 jit_solution(16287597951493440588)
XLA Ops:
  0.6 1.2 %pack_wy.1 = (f32[80,128]{1,0:T(8,128)S(1)}, f32[80,128]{1,0:T(8,128)S(1)}, f32[16,32,128]{2,1,0:T(8,128)S(1)}, f32[16,32,128]{2,1,0:T(8,128)S(1)}, f32[16,32,12...) custom-call(f32[16,32,128]{2,1,0:T(8,128)} %p_in.1, f32[16,32,128]{2,1,0:T(8,128)} %q_in.1, f32[16,32,128]{2,1,0:T(8,128)} %s_in.1, ...), custom_call_target="tpu_custom_call" | custom-call | tf_op jit(solution)/shard_map/pack_wy/pallas_call | solution.py:141
  1.9 3.0 %collective-permute-start = (f32[80,128]{1,0:T(8,128)S(1)}, f32[80,128]{1,0:T(8,128)S(1)}, u32[]{:S(2)}, u32[]{:S(2)}) collective-permute-start(f32[80,128]{1,0:T(8,128)S(1)} %get-tuple-element.31), channel_id=1, source_target_pairs={{1,2},{2,1},{5,6},{6,5},{9,10},{10,9},{13,14},{14,13},{17,18},{18,... | collective-permute-start | bytes 122888 | tf_op jit(solution)/shard_map/ppermute | solution.py:65
  4.9 0.1 collective-permute-start.1
  5.0 1.8 %collective-permute-done.wyo.got_odd = f32[80,128]{1,0:T(8,128)S(1)} collective-permute-done((f32[80,128]{1,0:T(8,128)S(1)}, f32[80,128]{1,0:T(8,128)S(1)}, u32[]{:S(2)}, u32[]{:S(2)}) %collective-permute-start) | collective-permute-done | bytes 40992 | tf_op jit(solution)/shard_map/ppermute | solution.py:65
  6.8 0.0 collective-permute-done.1.wye.got_even
  6.8 0.1 pack_fx.1
  7.0 0.2 collective-permute-start.2
  7.1 3.5 %collective-permute-start.3 = (f32[120,128]{1,0:T(8,128)S(1)}, f32[120,128]{1,0:T(8,128)S(1)}, u32[]{:S(2)}, u32[]{:S(2)}) collective-permute-start(f32[120,128]{1,0:T(8,128)S(1)} %get-tuple-element.38), channel_id=1, source_target_pairs={{0,4},{4,0},{1,5},{5,1},{2,6},{6,2},{3,7},{7,3},{8,12},{12,8},{9,1... | collective-permute-start | bytes 184328 | tf_op jit(solution)/shard_map/ppermute | solution.py:66
  10.6 2.8 %wall_center.1 = (f32[2,4,40,8,128]{4,3,2,1,0:T(8,128)S(1)}, f32[2,4,4,128]{3,2,1,0:T(4,128)S(1)}, f32[2,4,40,8,128]{4,3,2,1,0:T(8,128)S(1)}, s32[4,128]{1,0:T(4,128)S(1)}, f32[128,24]{1,0:T(8,128)S(1)}) custom-call(s32[2,4,9,128,128]{4,3,2,1,0:T(8,128)} %masks_in.1, s32[4,128]{1,0:T(4,128)} %bitcast.2, s32[4,128]{1,0:T(4,128)} %bitcast.3, ...), custom_call_target="tpu_custom_call" | custom-call | tf_op jit(solution)/shard_map/wall_center/pallas_call | solution.py:587
  13.4 0.0 collective-permute-done.2.fxo
  13.4 0.0 collective-permute-done.3.fxe
  13.4 1.0 %grid_steps.1 = (f32[16,32,128]{2,1,0:T(8,128)S(1)}, f32[32,3,4,128]{3,2,1,0:T(4,128)S(1)}, f32[32,3,4,128]{3,2,1,0:T(4,128)S(1)}) custom-call(f32[16,32,128]{2,1,0:T(8,128)S(1)} %get-tuple-element.34.p, f32[16,32,128]{2,1,0:T(8,128)S(1)} %get-tuple-element.35.q, f32[16,32,128]{2,1,0:T(8,128)S(1)} %get-tuple-element.36.s, ...), custom_call_target="tpu_custom_call" | custom-call | tf_op jit(solution)/shard_map/grid_steps/pallas_call | solution.py:354
  14.4 0.1 collective-permute-start.6
  14.5 1.2 %wall_first.1 = (f32[2,4,40,8,128]{4,3,2,1,0:T(8,128)S(1)}, f32[3,2,4,128]{3,2,1,0:T(4,128)S(1)}, f32[3,2,4,128]{3,2,1,0:T(4,128)S(1)}, f32[2,4,128]{2,1,0:T(4,1...) custom-call(f32[3,3,2,4,128]{4,3,2,1,0:T(4,128)S(1)} %get-tuple-element.30.wall, ...), custom_call_target="tpu_custom_call" | custom-call | tf_op jit(solution)/shard_map/wall_first/pallas_call | solution.py:676
  15.7 0.2 collective-permute-done.6.got
  15.9 0.7 %pair_sum.1 = f32[32,3,4,128]{3,2,1,0:T(4,128)} custom-call(f32[32,3,4,128]{3,2,1,0:T(4,128)S(1)} %get-tuple-element.49.keep, f32[32,3,4,128]{3,2,1,0:T(4,128)S(1)} %collective-permute-done.6.got, f32[2,4,128]{2,1,0:T(4,128)S(1)} %get-tuple-element.51.after.totals), custom_call_target="tpu_custom_call" | custom-call | tf_op jit(solution)/shard_map/pair_sum/pallas_call | solution.py:381
  16.6 4.3 %all-to-all-start = ((f32[32,3,4,128]{3,2,1,0:T(4,128)}), f32[32,3,4,128]{3,2,1,0:T(4,128)S(1)}, u32[]{:S(2)}, u32[]{:S(2)}) async-start(f32[32,3,4,128]{3,2,1,0:T(4,128)} %pair_sum.1), calls=%async_computation | async-start | bytes 393216 | tf_op jit(solution)/shard_map/all_to_all | solution.py:873
  20.9 1.8 %collective-permute-start.4 = (f32[8,128]{1,0:T(8,128)S(1)}, f32[8,128]{1,0:T(8,128)S(1)}, u32[]{:S(2)}, u32[]{:S(2)}) collective-permute-start(f32[8,128]{1,0:T(8,128)S(1)} %get-tuple-element.46), channel_id=1, source_target_pairs={{1,2},{2,1},{5,6},{6,5},{9,10},{10,9},{13,14},{14,13},{17,18},{18,... | collective-permute-start | bytes 12296 | tf_op jit(solution)/shard_map/ppermute | solution.py:65
  22.8 0.1 collective-permute-start.5
  22.9 1.8 %collective-permute-done.4.got_odd.wyo = f32[8,128]{1,0:T(8,128)S(1)} collective-permute-done((f32[8,128]{1,0:T(8,128)S(1)}, f32[8,128]{1,0:T(8,128)S(1)}, u32[]{:S(2)}, u32[]{:S(2)}) %collective-permute-start.4) | collective-permute-done | bytes 4128 | tf_op jit(solution)/shard_map/ppermute | solution.py:65
  24.6 0.0 collective-permute-done.5.got_even.wye
  24.7 1.8 %collective-permute-start.8 = (f32[24,128]{1,0:T(8,128)S(1)}, f32[24,128]{1,0:T(8,128)S(1)}, u32[]{:S(2)}, u32[]{:S(2)}) collective-permute-start(f32[24,128]{1,0:T(8,128)S(1)} %get-tuple-element.53), channel_id=1, source_target_pairs={{0,4},{4,0},{1,5},{5,1},{2,6},{6,2},{3,7},{7,3},{8,12},{12,8},{9,1... | collective-permute-start | bytes 36872 | tf_op jit(solution)/shard_map/ppermute | solution.py:66
  26.5 0.0 collective-permute-start.7
  26.5 0.5 %wall_middle.1.part = f32[2,3,4,128]{3,2,1,0:T(4,128)S(1)} custom-call(f32[2,4,40,8,128]{4,3,2,1,0:T(8,128)S(1)} %get-tuple-element.33.weights, f32[3,2,4,128]{3,2,1,0:T(4,128)S(1)} %get-tuple-element.45.base1, f32[8,128]{1,0:T(8,128)S(1)} %collective-permute-done.4.got_odd.wyo, f32[8,128]{1,0:T(8,128)S(1)} %collective-permute-done.5.got_even.wye, ...), custom_call_target="tpu_custom_call" | custom-call | tf_op jit(solution)/shard_map/wall_middle/pallas_call | solution.py:757
  27.0 1.4 %collective-permute-done.8.fxe = f32[24,128]{1,0:T(8,128)S(1)} collective-permute-done((f32[24,128]{1,0:T(8,128)S(1)}, f32[24,128]{1,0:T(8,128)S(1)}, u32[]{:S(2)}, u32[]{:S(2)}) %collective-permute-start.8) | collective-permute-done | bytes 12320 | tf_op jit(solution)/shard_map/ppermute | solution.py:66
  28.5 0.0 collective-permute-done.7.fxo
  28.5 1.4 %all-to-all-done.got = f32[32,3,4,128]{3,2,1,0:T(4,128)S(1)} async-done(((f32[32,3,4,128]{3,2,1,0:T(4,128)}), f32[32,3,4,128]{3,2,1,0:T(4,128)S(1)}, u32[]{:S(2)}, u32[]{:S(2)}) %all-to-all-start) | async-done | bytes 196640 | tf_op jit(solution)/shard_map/all_to_all | solution.py:873
  29.8 1.2 %wall_last.1 = (f32[3,2,4,128]{3,2,1,0:T(4,128)}, f32[3,2,4,128]{3,2,1,0:T(4,128)}) custom-call(f32[2,4,40,8,128]{4,3,2,1,0:T(8,128)S(1)} %get-tuple-element.33.weights, f32[2,4,40,8,128]{4,3,2,1,0:T(8,128)S(1)} %get-tuple-element.44.end_weights, f32[2,3,4,128]{3,2,1,0:T(4,128)S(1)} %wall_middle.1.part, f32[32,3,4,128]{3,2,1,0:T(4,128)S(1)} %all-to-all-done.got, ...), custom_call_target="tpu_custom_call" | custom-call | tf_op jit(solution)/shard_map/wall_last/pallas_call | solution.py:825
  (1 shorter events, 0.0 us)
Async XLA Ops:
  1.9 5.0 %collective-permute-start = (f32[80,128]{1,0:T(8,128)S(1)}, f32[80,128]{1,0:T(8,128)S(1)}, u32[]{:S(2)}, u32[]{:S(2)}) collective-permute-start(f32[80,128]{1,0:T(8,128)S(1)} %get-tuple-element.31), channel_id=1, source_target_pairs={{1,2},{2,1},{5,6},{6,5},{9,10},{10,9},{13,14},{14,13},{17,18},{18,... | collective-permute-start | bytes 122888 | tf_op jit(solution)/shard_map/ppermute | solution.py:65
  4.9 2.0 %collective-permute-start.1 = (f32[80,128]{1,0:T(8,128)S(1)}, f32[80,128]{1,0:T(8,128)S(1)}, u32[]{:S(2)}, u32[]{:S(2)}) collective-permute-start(f32[80,128]{1,0:T(8,128)S(1)} %get-tuple-element.32), channel_id=1, source_target_pairs={{0,1},{1,0},{4,5},{5,4},{8,9},{9,8},{12,13},{13,12},{16,17},{17,16... | collective-permute-start | bytes 122888 | tf_op jit(solution)/shard_map/ppermute | solution.py:66
  7.0 6.4 %collective-permute-start.2 = (f32[120,128]{1,0:T(8,128)S(1)}, f32[120,128]{1,0:T(8,128)S(1)}, u32[]{:S(2)}, u32[]{:S(2)}) collective-permute-start(f32[120,128]{1,0:T(8,128)S(1)} %get-tuple-element.37), channel_id=1, source_target_pairs={{4,8},{8,4},{5,9},{9,5},{6,10},{10,6},{7,11},{11,7},{12,16},{16,12... | collective-permute-start | bytes 184328 | tf_op jit(solution)/shard_map/ppermute | solution.py:65
  7.1 6.2 %collective-permute-start.3 = (f32[120,128]{1,0:T(8,128)S(1)}, f32[120,128]{1,0:T(8,128)S(1)}, u32[]{:S(2)}, u32[]{:S(2)}) collective-permute-start(f32[120,128]{1,0:T(8,128)S(1)} %get-tuple-element.38), channel_id=1, source_target_pairs={{0,4},{4,0},{1,5},{5,1},{2,6},{6,2},{3,7},{7,3},{8,12},{12,8},{9,1... | collective-permute-start | bytes 184328 | tf_op jit(solution)/shard_map/ppermute | solution.py:66
  14.4 1.5 %collective-permute-start.6 = (f32[32,3,4,128]{3,2,1,0:T(4,128)S(1)}, f32[32,3,4,128]{3,2,1,0:T(4,128)S(1)}, u32[]{:S(2)}, u32[]{:S(2)}) collective-permute-start(f32[32,3,4,128]{3,2,1,0:T(4,128)S(1)} %get-tuple-element.50), channel_id=1, source_target_pairs={{0,1},{1,0},{4,5},{5,4},{8,9},{9,8},{12,13},{13,12},{16,17},{17,16... | collective-permute-start | bytes 589832 | tf_op jit(solution)/shard_map/ppermute | solution.py:868
  16.6 13.2 %all-to-all-start = ((f32[32,3,4,128]{3,2,1,0:T(4,128)}), f32[32,3,4,128]{3,2,1,0:T(4,128)S(1)}, u32[]{:S(2)}, u32[]{:S(2)}) async-start(f32[32,3,4,128]{3,2,1,0:T(4,128)} %pair_sum.1), calls=%async_computation | async-start | bytes 393216 | tf_op jit(solution)/shard_map/all_to_all | solution.py:873
  20.9 3.7 %collective-permute-start.4 = (f32[8,128]{1,0:T(8,128)S(1)}, f32[8,128]{1,0:T(8,128)S(1)}, u32[]{:S(2)}, u32[]{:S(2)}) collective-permute-start(f32[8,128]{1,0:T(8,128)S(1)} %get-tuple-element.46), channel_id=1, source_target_pairs={{1,2},{2,1},{5,6},{6,5},{9,10},{10,9},{13,14},{14,13},{17,18},{18,... | collective-permute-start | bytes 12296 | tf_op jit(solution)/shard_map/ppermute | solution.py:65
  22.8 1.9 %collective-permute-start.5 = (f32[8,128]{1,0:T(8,128)S(1)}, f32[8,128]{1,0:T(8,128)S(1)}, u32[]{:S(2)}, u32[]{:S(2)}) collective-permute-start(f32[8,128]{1,0:T(8,128)S(1)} %get-tuple-element.47), channel_id=1, source_target_pairs={{0,1},{1,0},{4,5},{5,4},{8,9},{9,8},{12,13},{13,12},{16,17},{17,16... | collective-permute-start | bytes 12296 | tf_op jit(solution)/shard_map/ppermute | solution.py:66
  24.7 3.8 %collective-permute-start.8 = (f32[24,128]{1,0:T(8,128)S(1)}, f32[24,128]{1,0:T(8,128)S(1)}, u32[]{:S(2)}, u32[]{:S(2)}) collective-permute-start(f32[24,128]{1,0:T(8,128)S(1)} %get-tuple-element.53), channel_id=1, source_target_pairs={{0,4},{4,0},{1,5},{5,1},{2,6},{6,2},{3,7},{7,3},{8,12},{12,8},{9,1... | collective-permute-start | bytes 36872 | tf_op jit(solution)/shard_map/ppermute | solution.py:66
  26.5 2.0 %collective-permute-start.7 = (f32[24,128]{1,0:T(8,128)S(1)}, f32[24,128]{1,0:T(8,128)S(1)}, u32[]{:S(2)}, u32[]{:S(2)}) collective-permute-start(f32[24,128]{1,0:T(8,128)S(1)} %get-tuple-element.48.after_this), channel_id=1, source_target_pairs={{4,8},{8,4},{5,9},{9,5},{6,10},{10,6},{7,11},{11,7},{12,16},{16,12... | collective-permute-start | bytes 36872 | tf_op jit(solution)/shard_map/ppermute | solution.py:65

commit v16 on v15

--- a/solution.py
+++ b/solution.py
@@ -765,16 +765,52 @@
     )(weights, base1, *wy_got, after)
 
 
-def last_kernel(
-    weights, end_weights, part, got, base1, vel1, totals, wyo, wye, fxo, fxe, disp_out, vel_out,
-    dpad, load_pad, acc,
-):
+def ends_kernel(weights, base1, fxo, fxe, wyo, wye, middle, part, dpad, acc):
     rows, cols = base1.shape[1], base1.shape[2]
     first_sub = lax.broadcasted_iota(jnp.int32, (SUB, LANES), 0) < SUB // 2
     before, after = before_after("wy", wye, wyo)
     fill_y(dpad, base1, before, after, 0)
     before, after = before_after("fx", fxe, fxo)
     fill_x(dpad, rows, cols, before, after, 0)
+    for l in range(rows):
+        sums = []
+        for h in range(cols):
+            ends = [end_rows(dpad, c, l, h, first_sub) for c in range(3)]
+            weigh(weights, ends, l, h, acc)
+            sums.append(tile_sums(acc, l, h, 3))
+        for c, rows_c in enumerate(by_quantity(sums)):
+            part[l, c] = middle[l, c] + rows_c
+
+
+def weigh(weights, fields, l, h, acc):
+    place = 0
+    for g in range(LANES // SUB):
+        sums = [None] * len(fields)
+        for dh in reached(g):
+            weight = weights[l, h, place]
+            terms = [weight * field[dh] for field in fields]
+            sums = [t if v is None else v + t for v, t in zip(sums, terms)]
+            place += 1
+        for c, value in enumerate(sums):
+            acc[l, h, c, g * SUB : (g + 1) * SUB, :] = value
+
+
+def wall_ends(weights, base1, wy_got, fx_got, middle):
+    rows, cols = base1.shape[1], base1.shape[2]
+    return pl.pallas_call(
+        ends_kernel,
+        in_specs=[whole()] * 7,
+        out_specs=whole(),
+        out_shape=vmem(rows, 3, cols, LANES),
+        scratch_shapes=[vmem(3, rows + 2, SUB, LANES), vmem(rows, cols, 3, LANES, LANES)],
+        compiler_params=params(),
+        name="wall_ends",
+    )(weights, base1, *fx_got, *wy_got, middle)
+
+
+def last_kernel(weights, end_weights, part, got, base1, vel1, totals, disp_out, vel_out, load_pad, acc):
+    rows, cols = base1.shape[1], base1.shape[2]
+    first_sub = lax.broadcasted_iota(jnp.int32, (SUB, LANES), 0) < SUB // 2
     pieces = []
     for half in range(2):
         for k in range(3):
@@ -782,37 +818,33 @@
             for d in range(half + 2, got.shape[0], 2):
                 total = total + got[d, k]
             pieces.append(total)
-    total = jnp.concatenate(pieces, axis=0)
-    one, two = unpack_slots(total, cols)
+    one, two = unpack_slots(jnp.concatenate(pieces, axis=0), cols)
     for k in range(rows + 2):
-        loads = LOADING * one[k][0 : cols + 2]
-        load_pad[0, k, 0 : cols + 2, :] = loads
-        dpad[0, k, 0 : cols + 2, :] = dpad[0, k, 0 : cols + 2, :] + loads
+        load_pad[0, k, 0 : cols + 2, :] = LOADING * one[k][0 : cols + 2]
 
     def one_tile(l, h):
         mid = mid_rows(load_pad, 0, l, h)
-        ends = [end_rows(dpad, c, l, h, first_sub) for c in range(3)]
+        ends = end_rows(load_pad, 0, l, h, first_sub)
         place = 0
         for g in range(LANES // SUB):
-            sums = [None] * 3
+            total = None
             for dh in reached(g):
-                weight = end_weights[l, h, place]
-                terms = [weight * ends[c][dh] for c in range(3)]
-                terms[0] = terms[0] + weights[l, h, place] * mid[dh]
-                sums = [t if v is None else v + t for v, t in zip(sums, terms)]
+                term = weights[l, h, place] * mid[dh] + end_weights[l, h, place] * ends[dh]
+                total = term if total is None else total + term
                 place += 1
-            for c in range(3):
-                acc[l, h, c, g * SUB : (g + 1) * SUB, :] = sums[c]
+            acc[l, h, 0, g * SUB : (g + 1) * SUB, :] = total
 
     for l in range(rows):
         sums = []
         for h in range(cols):
             one_tile(l, h)
-            sums.append(tile_sums(acc, l, h, 3))
-        pulled = by_quantity(sums)
+            sums.append(tile_sums(acc, l, h, 1))
+        loads = by_quantity(sums)[0]
         for c in range(3):
-            mine = dpad[c, l + 1, 1 : cols + 1, :]
-            force = STIFFNESS * (pulled[c] + part[l, c] - totals[l] * mine)
+            mine, pulled = base1[c, l], part[l, c]
+            if c == 0:
+                mine, pulled = mine + load_pad[0, l + 1, 1 : cols + 1, :], pulled + loads
+            force = STIFFNESS * (pulled - totals[l] * mine)
             if c == 0:
                 force = force + LOADING * (one[l + 1][1 : cols + 1] + two[l])
             fresh = vel1[c, l] + force
@@ -820,21 +852,17 @@
             disp_out[c, l] = mine + fresh
 
 
-def wall_last(weights, end_weights, part, got, base1, vel1, totals, wy_got, fx_got):
+def wall_last(weights, end_weights, part, got, base1, vel1, totals):
     rows, cols = base1.shape[1], base1.shape[2]
     return pl.pallas_call(
         last_kernel,
-        in_specs=[whole()] * 11,
+        in_specs=[whole()] * 7,
         out_specs=[whole()] * 2,
         out_shape=[jax.ShapeDtypeStruct(base1.shape, F32)] * 2,
-        scratch_shapes=[
-            vmem(3, rows + 2, SUB, LANES),
-            vmem(1, rows + 2, SUB, LANES),
-            pltpu.VMEM((rows, cols, 3, LANES, LANES), F32),
-        ],
+        scratch_shapes=[vmem(1, rows + 2, SUB, LANES), vmem(rows, cols, 1, LANES, LANES)],
         compiler_params=params(),
         name="wall_last",
-    )(weights, end_weights, part, got, base1, vel1, totals, *wy_got, *fx_got)
+    )(weights, end_weights, part, got, base1, vel1, totals)
 
 
 def per_device(
@@ -875,9 +903,8 @@
     sends = pack_base(base1, base_wy)
     base_fx = exchange("fx", *sends)
     middle = wall_middle(weights, base1, base_wy, sends[0])
-    disp_out, vel_out = wall_last(
-        weights, end_weights, middle, got, base1, vel1, totals, base_wy, base_fx
-    )
+    part = wall_ends(end_weights, base1, base_wy, base_fx, middle)
+    disp_out, vel_out = wall_last(weights, end_weights, part, got, base1, vel1, totals)
     return (disp_out, vel_out, pressure_out)
 
 

time: 31.5 us -> 31.3 us (level)
  waiting for transfers between devices: 6.63 us -> 6.09 us
    all_to_all x1, waiting for transfers between devices: 1.37 us -> 0.82 us  [per_device(): got = lax.all_to_all(slots, names, split_axis=0, concat_axis=0, tiled=True)]
    pallas_call x1 -> x2, Pallas kernels: 1.25 us -> 1.52 us  [the longest x1 0.97 us: wall_last(): pl.pallas_call(last_kernel, in_specs=[whole()] * 7, out_specs=[whole()] *...]
  transfers between devices with their start and end apart: 10 -> 10, of which waited for: 5 -> 5; matrix products, arithmetic and copies ran while one was open for 0% -> 0% of each run, Pallas kernels for 15% -> 16%
where the time goes in v16:
time: 31.3 us; the launch traced here: 30.8 us
  starting transfers between devices  14.9 us (48%)
  Pallas kernels  9.1 us (29%)
  waiting for transfers between devices  6.09 us (19%)
  between operations  0.72 us (2%)
    ppermute x4, starting transfers between devices, exchange(): got_even = lax.ppermute(to_even, names, swap_pairs(along, sizes, 0))  5.52 us
    ppermute x4, starting transfers between devices, exchange(): got_odd = lax.ppermute(to_odd, names, swap_pairs(along, sizes, 1))  5.02 us
    all_to_all x1, starting transfers between devices, per_device(): got = lax.all_to_all(slots, names, split_axis=0, concat_axis=0, tiled=True)  4.28 us
    ppermute x4, waiting for transfers between devices, exchange(): got_odd = lax.ppermute(to_odd, names, swap_pairs(along, sizes, 1))  3.6 us
    pallas_call x1, Pallas kernels, wall_center(): pl.pallas_call(functools.partial(center_kernel, cx, wy_count), in_specs=[...  2.77 us
    ppermute x4, waiting for transfers between devices, exchange(): got_even = lax.ppermute(to_even, names, swap_pairs(along, sizes, 0))  1.43 us
    pallas_call x1, Pallas kernels, pack_wy(): pl.pallas_call(pack_wy_kernel, in_specs=[HBM] * 6, out_specs=[whole()] *...  1.22 us
    pallas_call x1, Pallas kernels, wall_first(): pl.pallas_call(functools.partial(wall_kernel, cx, cy), in_specs=[whole()]...  1.19 us
  transfers between devices with their start and end apart: 10, of which 5 were waited for; matrix products, arithmetic and copies ran while one was open for 0% of the time, Pallas kernels for 16%

profile of v16, /device:TPU:0, one launch (start us, length us, event | category | flops | bytes accessed | tf_op | source)
XLA Modules:
  0.0 30.8 jit_solution(7615936156462568372)
XLA Ops:
  0.6 1.2 %pack_wy.1 = (f32[80,128]{1,0:T(8,128)S(1)}, f32[80,128]{1,0:T(8,128)S(1)}, f32[16,32,128]{2,1,0:T(8,128)S(1)}, f32[16,32,128]{2,1,0:T(8,128)S(1)}, f32[16,32,12...) custom-call(f32[16,32,128]{2,1,0:T(8,128)} %p_in.1, f32[16,32,128]{2,1,0:T(8,128)} %q_in.1, f32[16,32,128]{2,1,0:T(8,128)} %s_in.1, ...), custom_call_target="tpu_custom_call" | custom-call | tf_op jit(solution)/shard_map/pack_wy/pallas_call | solution.py:141
  1.9 3.0 %collective-permute-start = (f32[80,128]{1,0:T(8,128)S(1)}, f32[80,128]{1,0:T(8,128)S(1)}, u32[]{:S(2)}, u32[]{:S(2)}) collective-permute-start(f32[80,128]{1,0:T(8,128)S(1)} %get-tuple-element.31), channel_id=1, source_target_pairs={{1,2},{2,1},{5,6},{6,5},{9,10},{10,9},{13,14},{14,13},{17,18},{18,... | collective-permute-start | bytes 122888 | tf_op jit(solution)/shard_map/ppermute | solution.py:65
  4.9 0.1 collective-permute-start.1
  5.0 1.8 %collective-permute-done.wyo.got_odd = f32[80,128]{1,0:T(8,128)S(1)} collective-permute-done((f32[80,128]{1,0:T(8,128)S(1)}, f32[80,128]{1,0:T(8,128)S(1)}, u32[]{:S(2)}, u32[]{:S(2)}) %collective-permute-start) | collective-permute-done | bytes 40992 | tf_op jit(solution)/shard_map/ppermute | solution.py:65
  6.8 0.0 collective-permute-done.1.wye.got_even
  6.8 0.1 pack_fx.1
  7.0 0.2 collective-permute-start.2
  7.1 3.5 %collective-permute-start.3 = (f32[120,128]{1,0:T(8,128)S(1)}, f32[120,128]{1,0:T(8,128)S(1)}, u32[]{:S(2)}, u32[]{:S(2)}) collective-permute-start(f32[120,128]{1,0:T(8,128)S(1)} %get-tuple-element.38), channel_id=1, source_target_pairs={{0,4},{4,0},{1,5},{5,1},{2,6},{6,2},{3,7},{7,3},{8,12},{12,8},{9,1... | collective-permute-start | bytes 184328 | tf_op jit(solution)/shard_map/ppermute | solution.py:66
  10.6 2.8 %wall_center.1 = (f32[2,4,40,8,128]{4,3,2,1,0:T(8,128)S(1)}, f32[2,4,4,128]{3,2,1,0:T(4,128)S(1)}, f32[2,4,40,8,128]{4,3,2,1,0:T(8,128)S(1)}, s32[4,128]{1,0:T(4,128)S(1)}, f32[128,24]{1,0:T(8,128)S(1)}) custom-call(s32[2,4,9,128,128]{4,3,2,1,0:T(8,128)} %masks_in.1, s32[4,128]{1,0:T(4,128)} %bitcast.2, s32[4,128]{1,0:T(4,128)} %bitcast.3, ...), custom_call_target="tpu_custom_call" | custom-call | tf_op jit(solution)/shard_map/wall_center/pallas_call | solution.py:587
  13.4 0.0 collective-permute-done.2.fxo
  13.4 0.0 collective-permute-done.3.fxe
  13.4 1.0 %grid_steps.1 = (f32[16,32,128]{2,1,0:T(8,128)S(1)}, f32[32,3,4,128]{3,2,1,0:T(4,128)S(1)}, f32[32,3,4,128]{3,2,1,0:T(4,128)S(1)}) custom-call(f32[16,32,128]{2,1,0:T(8,128)S(1)} %get-tuple-element.34.p, f32[16,32,128]{2,1,0:T(8,128)S(1)} %get-tuple-element.35.q, f32[16,32,128]{2,1,0:T(8,128)S(1)} %get-tuple-element.36.s, ...), custom_call_target="tpu_custom_call" | custom-call | tf_op jit(solution)/shard_map/grid_steps/pallas_call | solution.py:354
  14.4 0.1 collective-permute-start.8
  14.5 1.2 %wall_first.1 = (f32[2,4,40,8,128]{4,3,2,1,0:T(8,128)S(1)}, f32[3,2,4,128]{3,2,1,0:T(4,128)S(1)}, f32[3,2,4,128]{3,2,1,0:T(4,128)S(1)}, f32[2,4,128]{2,1,0:T(4,1...) custom-call(f32[3,3,2,4,128]{4,3,2,1,0:T(4,128)S(1)} %get-tuple-element.30.wall, ...), custom_call_target="tpu_custom_call" | custom-call | tf_op jit(solution)/shard_map/wall_first/pallas_call | solution.py:676
  15.7 0.2 collective-permute-done.8.got
  15.9 0.7 %pair_sum.1 = f32[32,3,4,128]{3,2,1,0:T(4,128)} custom-call(f32[32,3,4,128]{3,2,1,0:T(4,128)S(1)} %get-tuple-element.50.keep, f32[32,3,4,128]{3,2,1,0:T(4,128)S(1)} %collective-permute-done.8.got, f32[2,4,128]{2,1,0:T(4,128)S(1)} %get-tuple-element.52.after.totals), custom_call_target="tpu_custom_call" | custom-call | tf_op jit(solution)/shard_map/pair_sum/pallas_call | solution.py:381
  16.6 4.3 %all-to-all-start = ((f32[32,3,4,128]{3,2,1,0:T(4,128)}), f32[32,3,4,128]{3,2,1,0:T(4,128)S(1)}, u32[]{:S(2)}, u32[]{:S(2)}) async-start(f32[32,3,4,128]{3,2,1,0:T(4,128)} %pair_sum.1), calls=%async_computation | async-start | bytes 393216 | tf_op jit(solution)/shard_map/all_to_all | solution.py:901
  20.9 1.8 %collective-permute-start.4 = (f32[8,128]{1,0:T(8,128)S(1)}, f32[8,128]{1,0:T(8,128)S(1)}, u32[]{:S(2)}, u32[]{:S(2)}) collective-permute-start(f32[8,128]{1,0:T(8,128)S(1)} %get-tuple-element.46), channel_id=1, source_target_pairs={{1,2},{2,1},{5,6},{6,5},{9,10},{10,9},{13,14},{14,13},{17,18},{18,... | collective-permute-start | bytes 12296 | tf_op jit(solution)/shard_map/ppermute | solution.py:65
  22.8 0.1 collective-permute-start.5
  22.9 1.8 %collective-permute-done.4.got_odd.wyo = f32[8,128]{1,0:T(8,128)S(1)} collective-permute-done((f32[8,128]{1,0:T(8,128)S(1)}, f32[8,128]{1,0:T(8,128)S(1)}, u32[]{:S(2)}, u32[]{:S(2)}) %collective-permute-start.4) | collective-permute-done | bytes 4128 | tf_op jit(solution)/shard_map/ppermute | solution.py:65
  24.6 0.0 collective-permute-done.5.got_even.wye
  24.7 1.8 %collective-permute-start.7 = (f32[24,128]{1,0:T(8,128)S(1)}, f32[24,128]{1,0:T(8,128)S(1)}, u32[]{:S(2)}, u32[]{:S(2)}) collective-permute-start(f32[24,128]{1,0:T(8,128)S(1)} %get-tuple-element.49), channel_id=1, source_target_pairs={{0,4},{4,0},{1,5},{5,1},{2,6},{6,2},{3,7},{7,3},{8,12},{12,8},{9,1... | collective-permute-start | bytes 36872 | tf_op jit(solution)/shard_map/ppermute | solution.py:66
  26.5 0.0 collective-permute-start.6
  26.5 0.5 %wall_middle.1.middle = f32[2,3,4,128]{3,2,1,0:T(4,128)S(1)} custom-call(f32[2,4,40,8,128]{4,3,2,1,0:T(8,128)S(1)} %get-tuple-element.33.weights, f32[3,2,4,128]{3,2,1,0:T(4,128)S(1)} %get-tuple-element.45.base1, f32[8,128]{1,0:T(8,128)S(1)} %collective-permute-done.4.got_odd.wyo, f32[8,128]{1,0:T(8,128)S(1)} %collective-permute-done.5.got_even.wye, ...), custom_call_target="tpu_custom_call" | custom-call | tf_op jit(solution)/shard_map/wall_middle/pallas_call | solution.py:757
  27.0 1.4 %collective-permute-done.7.fxe = f32[24,128]{1,0:T(8,128)S(1)} collective-permute-done((f32[24,128]{1,0:T(8,128)S(1)}, f32[24,128]{1,0:T(8,128)S(1)}, u32[]{:S(2)}, u32[]{:S(2)}) %collective-permute-start.7) | collective-permute-done | bytes 12320 | tf_op jit(solution)/shard_map/ppermute | solution.py:66
  28.5 0.0 collective-permute-done.6.fxo
  28.5 0.5 %wall_ends.1.part = f32[2,3,4,128]{3,2,1,0:T(4,128)S(1)} custom-call(f32[2,4,40,8,128]{4,3,2,1,0:T(8,128)S(1)} %get-tuple-element.44.weights.end_weights, f32[3,2,4,128]{3,2,1,0:T(4,128)S(1)} %get-tuple-element.45.base1, f32[24,128]{1,0:T(8,128)S(1)} %collective-permute-done.6.fxo, f32[24,128]{1,0:T(8,128)S(1)} %collective-permute-done.7.fxe, ...), custom_call_target="tpu_custom_call" | custom-call | tf_op jit(solution)/shard_map/wall_ends/pallas_call | solution.py:800
  29.0 0.8 %all-to-all-done.got = f32[32,3,4,128]{3,2,1,0:T(4,128)S(1)} async-done(((f32[32,3,4,128]{3,2,1,0:T(4,128)}), f32[32,3,4,128]{3,2,1,0:T(4,128)S(1)}, u32[]{:S(2)}, u32[]{:S(2)}) %all-to-all-start) | async-done | bytes 196640 | tf_op jit(solution)/shard_map/all_to_all | solution.py:901
  29.8 1.0 %wall_last.1 = (f32[3,2,4,128]{3,2,1,0:T(4,128)}, f32[3,2,4,128]{3,2,1,0:T(4,128)}) custom-call(f32[2,4,40,8,128]{4,3,2,1,0:T(8,128)S(1)} %get-tuple-element.33.weights, f32[2,4,40,8,128]{4,3,2,1,0:T(8,128)S(1)} %get-tuple-element.44.weights.end_weights, f32[2,3,4,128]{3,2,1,0:T(4,128)S(1)} %wall_ends.1.part, f32[32,3,4,128]{3,2,1,0:T(4,128)S(1)} %all-to-all-done.got, ...), custom_call_target="tpu_custom_call" | custom-call | tf_op jit(solution)/shard_map/wall_last/pallas_call | solution.py:857
  (1 shorter events, 0.0 us)
Async XLA Ops:
  1.9 5.0 %collective-permute-start = (f32[80,128]{1,0:T(8,128)S(1)}, f32[80,128]{1,0:T(8,128)S(1)}, u32[]{:S(2)}, u32[]{:S(2)}) collective-permute-start(f32[80,128]{1,0:T(8,128)S(1)} %get-tuple-element.31), channel_id=1, source_target_pairs={{1,2},{2,1},{5,6},{6,5},{9,10},{10,9},{13,14},{14,13},{17,18},{18,... | collective-permute-start | bytes 122888 | tf_op jit(solution)/shard_map/ppermute | solution.py:65
  4.9 2.0 %collective-permute-start.1 = (f32[80,128]{1,0:T(8,128)S(1)}, f32[80,128]{1,0:T(8,128)S(1)}, u32[]{:S(2)}, u32[]{:S(2)}) collective-permute-start(f32[80,128]{1,0:T(8,128)S(1)} %get-tuple-element.32), channel_id=1, source_target_pairs={{0,1},{1,0},{4,5},{5,4},{8,9},{9,8},{12,13},{13,12},{16,17},{17,16... | collective-permute-start | bytes 122888 | tf_op jit(solution)/shard_map/ppermute | solution.py:66
  7.0 6.4 %collective-permute-start.2 = (f32[120,128]{1,0:T(8,128)S(1)}, f32[120,128]{1,0:T(8,128)S(1)}, u32[]{:S(2)}, u32[]{:S(2)}) collective-permute-start(f32[120,128]{1,0:T(8,128)S(1)} %get-tuple-element.37), channel_id=1, source_target_pairs={{4,8},{8,4},{5,9},{9,5},{6,10},{10,6},{7,11},{11,7},{12,16},{16,12... | collective-permute-start | bytes 184328 | tf_op jit(solution)/shard_map/ppermute | solution.py:65
  7.1 6.2 %collective-permute-start.3 = (f32[120,128]{1,0:T(8,128)S(1)}, f32[120,128]{1,0:T(8,128)S(1)}, u32[]{:S(2)}, u32[]{:S(2)}) collective-permute-start(f32[120,128]{1,0:T(8,128)S(1)} %get-tuple-element.38), channel_id=1, source_target_pairs={{0,4},{4,0},{1,5},{5,1},{2,6},{6,2},{3,7},{7,3},{8,12},{12,8},{9,1... | collective-permute-start | bytes 184328 | tf_op jit(solution)/shard_map/ppermute | solution.py:66
  14.4 1.5 %collective-permute-start.8 = (f32[32,3,4,128]{3,2,1,0:T(4,128)S(1)}, f32[32,3,4,128]{3,2,1,0:T(4,128)S(1)}, u32[]{:S(2)}, u32[]{:S(2)}) collective-permute-start(f32[32,3,4,128]{3,2,1,0:T(4,128)S(1)} %get-tuple-element.51), channel_id=1, source_target_pairs={{0,1},{1,0},{4,5},{5,4},{8,9},{9,8},{12,13},{13,12},{16,17},{17,16... | collective-permute-start | bytes 589832 | tf_op jit(solution)/shard_map/ppermute | solution.py:896
  16.6 13.2 %all-to-all-start = ((f32[32,3,4,128]{3,2,1,0:T(4,128)}), f32[32,3,4,128]{3,2,1,0:T(4,128)S(1)}, u32[]{:S(2)}, u32[]{:S(2)}) async-start(f32[32,3,4,128]{3,2,1,0:T(4,128)} %pair_sum.1), calls=%async_computation | async-start | bytes 393216 | tf_op jit(solution)/shard_map/all_to_all | solution.py:901
  20.9 3.7 %collective-permute-start.4 = (f32[8,128]{1,0:T(8,128)S(1)}, f32[8,128]{1,0:T(8,128)S(1)}, u32[]{:S(2)}, u32[]{:S(2)}) collective-permute-start(f32[8,128]{1,0:T(8,128)S(1)} %get-tuple-element.46), channel_id=1, source_target_pairs={{1,2},{2,1},{5,6},{6,5},{9,10},{10,9},{13,14},{14,13},{17,18},{18,... | collective-permute-start | bytes 12296 | tf_op jit(solution)/shard_map/ppermute | solution.py:65
  22.8 1.9 %collective-permute-start.5 = (f32[8,128]{1,0:T(8,128)S(1)}, f32[8,128]{1,0:T(8,128)S(1)}, u32[]{:S(2)}, u32[]{:S(2)}) collective-permute-start(f32[8,128]{1,0:T(8,128)S(1)} %get-tuple-element.47), channel_id=1, source_target_pairs={{0,1},{1,0},{4,5},{5,4},{8,9},{9,8},{12,13},{13,12},{16,17},{17,16... | collective-permute-start | bytes 12296 | tf_op jit(solution)/shard_map/ppermute | solution.py:66
  24.7 3.8 %collective-permute-start.7 = (f32[24,128]{1,0:T(8,128)S(1)}, f32[24,128]{1,0:T(8,128)S(1)}, u32[]{:S(2)}, u32[]{:S(2)}) collective-permute-start(f32[24,128]{1,0:T(8,128)S(1)} %get-tuple-element.49), channel_id=1, source_target_pairs={{0,4},{4,0},{1,5},{5,1},{2,6},{6,2},{3,7},{7,3},{8,12},{12,8},{9,1... | collective-permute-start | bytes 36872 | tf_op jit(solution)/shard_map/ppermute | solution.py:66
  26.5 2.0 %collective-permute-start.6 = (f32[24,128]{1,0:T(8,128)S(1)}, f32[24,128]{1,0:T(8,128)S(1)}, u32[]{:S(2)}, u32[]{:S(2)}) collective-permute-start(f32[24,128]{1,0:T(8,128)S(1)} %get-tuple-element.48.after_this), channel_id=1, source_target_pairs={{4,8},{8,4},{5,9},{9,5},{6,10},{10,6},{7,11},{11,7},{12,16},{16,12... | collective-permute-start | bytes 36872 | tf_op jit(solution)/shard_map/ppermute | solution.py:65
